TPU v7x, 32 devices: a whole 2x2x4 slice. The times are simulated.
32 devices in a mesh: owner: 8 (over z, x), helper: 4 (over y, core).
Axes of the slice: x: 2, y: 2, z: 4, core: 2. Of those that a mesh axis runs over, the one named last changes fastest.
Arguments:
- states: bfloat16 [16, 128, 768], P('owner'), may hold values from -6 to 6
- partners: int32 [16, 5], P('owner'), may hold values from -1 to 15, as said below
- self_proj: bfloat16 [3, 768, 768], P(None, None, 'helper'), may hold values from -0.28867513 to 0.28867513
- self_out: bfloat16 [768, 768], P('helper'), may hold values from -0.21875 to 0.21875
- cross_proj: bfloat16 [3, 768, 768], P(None, None, 'helper'), may hold values from -0.28867513 to 0.28867513
- cross_out: bfloat16 [768, 768], P('helper'), may hold values from -0.21875 to 0.21875
- gains: float32 [3, 768], replicated, may hold values from 0.5 to 1.5
Outputs:
- pair_states: bfloat16 [16, 5, 128, 768], P('owner', None, 'helper')
Inputs may be any that keep to these rules, and one draw needn't show every extreme that they name: Row i lists the images paired with image i, left-aligned, then -1 in the remaining slots. Pairs are symmetric. Images 2 * o and 2 * o + 1 belong to owner o. With M = 8 owners, every pair joins owner o with owner o + k modulo M for k from 1 to 2 or k = M // 2, or with owner o - k modulo M for k from 1 to 2; each of these 5 owners is joined to o by exactly one pair, so the two images of one owner take part in exactly 5 pairs together, and some image has 5 partners.
All inputs are finite; a program needn't handle non-finite values.
Results may differ from a plain program's by a relative error of at most 0.0095.
Values may be sent and summed in bfloat16 or wider, within the bound.
No kernel may reach another device: no remote copies, remote signals or barrier semaphores. Data moves between devices by JAX's collectives and lax.ppermute only.
A program may use at most 128 MiB of HBM per device.

v0:
```python
import jax
import jax.numpy as jnp
from jax import lax
from jax.sharding import PartitionSpec as P

HEAD = 64


def norm_rows(values, gain_row):
    row_mean = jnp.mean(values, -1, keepdims=True)
    centred = values - row_mean
    row_var = jnp.mean(centred * centred, -1, keepdims=True)
    return centred * lax.rsqrt(row_var + 1e-05) * gain_row


def attend(queries, key_rows, value_rows):
    count_n, patch_n, column_n = queries.shape
    head_count = column_n // HEAD
    q_heads = queries.reshape(count_n, patch_n, head_count, HEAD)
    k_heads = key_rows.reshape(count_n, key_rows.shape[1], head_count, HEAD)
    v_heads = value_rows.reshape(count_n, value_rows.shape[1], head_count, HEAD)
    scores = jnp.einsum(
        "nqhe,nkhe->nhqk", q_heads, k_heads, preferred_element_type=jnp.float32
    ) * HEAD ** (-0.5)
    weights = jax.nn.softmax(scores, axis=-1).astype(jnp.bfloat16)
    context = jnp.einsum("nhqk,nkhe->nqhe", weights, v_heads, preferred_element_type=jnp.float32)
    return context.astype(jnp.bfloat16).reshape(count_n, patch_n, column_n)


def local(states, partners, self_proj, self_out, cross_proj, cross_out, gains):
    as_float = states.astype(jnp.float32)
    image_count, patch_count, model_width = states.shape
    normed = norm_rows(as_float, gains[0]).astype(jnp.bfloat16)
    key_norm = norm_rows(as_float, gains[2]).astype(jnp.bfloat16)
    cross_kv = jnp.einsum(
        "ipd,cdf->ipcf", key_norm, cross_proj[1:], preferred_element_type=jnp.float32
    ).astype(jnp.bfloat16)
    head_cols = cross_kv.shape[3]
    cross_kv = cross_kv.reshape(image_count, patch_count, 2 * head_cols)
    owner_count = lax.axis_size("owner")
    is_live = partners >= 0
    partner_owner = jnp.where(is_live, partners // image_count, -1)
    needed = jnp.any(
        partner_owner[:, :, None] == jnp.arange(owner_count, dtype=jnp.int32)[None, None, :], axis=1
    )
    slot_count = partners.shape[1]
    outgoing = jnp.einsum(
        "ed,epc->dpc", needed.astype(jnp.bfloat16), cross_kv, preferred_element_type=jnp.float32
    ).astype(jnp.bfloat16)
    incoming = lax.all_to_all(outgoing, "owner", split_axis=0, concat_axis=0, tiled=True)
    projected = jnp.einsum(
        "ipd,cdf->cipf", normed, self_proj, preferred_element_type=jnp.float32
    ).astype(jnp.bfloat16)
    context = attend(projected[0], projected[1], projected[2])
    own_heads = jnp.einsum("ipf,fd->ipd", context, self_out, preferred_element_type=jnp.float32)
    mixed = as_float + lax.psum(own_heads.astype(jnp.bfloat16), "helper").astype(jnp.float32)
    queries = jnp.einsum(
        "ipd,df->ipf",
        norm_rows(mixed, gains[1]).astype(jnp.bfloat16),
        cross_proj[0],
        preferred_element_type=jnp.float32,
    ).astype(jnp.bfloat16)
    flat_list = partners.reshape(-1)
    side_order = jnp.arange(image_count * slot_count, dtype=jnp.int32)
    side_partner = flat_list[side_order]
    side_image = side_order // slot_count
    side_live = side_partner >= 0
    sender = jnp.where(side_live, side_partner // image_count, 0)
    side_kv = incoming[sender]
    side_context = attend(queries[side_image], side_kv[:, :, :head_cols], side_kv[:, :, head_cols:])
    helper_count = lax.axis_size("helper")
    row_count = patch_count // helper_count
    row_start = lax.axis_index("helper") * row_count
    summed = lax.psum_scatter(
        jnp.einsum(
            "spf,fd->psd", side_context, cross_out, preferred_element_type=jnp.float32
        ).astype(jnp.bfloat16),
        "helper",
        scatter_dimension=0,
        tiled=True,
    ).astype(jnp.float32)
    cross_terms = jnp.transpose(summed, (1, 0, 2))
    own_rows = lax.dynamic_slice_in_dim(mixed, row_start, row_count, 1)
    result = (own_rows[side_image] + cross_terms).astype(jnp.bfloat16)
    result = jnp.where(side_live[:, None, None], result, jnp.zeros((), jnp.bfloat16))
    return result.reshape(image_count, slot_count, row_count, model_width)


def solution(mesh):
    return jax.shard_map(
        local,
        mesh=mesh,
        in_specs=(
            P("owner", None, None),
            P("owner", None),
            P(None, None, "helper"),
            P("helper", None),
            P(None, None, "helper"),
            P("helper", None),
            P(),
        ),
        out_specs=P("owner", None, "helper", None),
        check_vma=False,
    )
```

profile of v0, /device:TPU:0, one launch (start us, length us, event | category | flops | bytes accessed | tf_op | source)
XLA Modules:
  0.0 101.9 jit_solution(2916497154021179233)
XLA Ops:
  6.5 1.2 %convert_reduce_fusion = f32[2,128]{1,0:T(2,128)S(1)} fusion(bf16[2,128,768]{2,1,0:T(8,128)(2,1)} %param.7), kind=kLoop, calls=%fused_computation.20 | loop fusion | flops 392960 | bytes 394240 | tf_op jit(solution)/shard_map/reduce_sum | solution.py:10
  7.8 1.2 %fusion.15 = f32[2,128]{1,0:T(2,128)S(1)} fusion(bf16[2,128,768]{2,1,0:T(8,128)(2,1)} %param.7, f32[2,128]{1,0:T(2,128)S(1)} %broadcast_multiply_fusion.1), kind=kLoop, calls=%fused_computation.35 | loop fusion | flops 786176 | bytes 395264 | tf_op jit(solution)/shard_map/reduce_sum | solution.py:12
  9.0 0.9 slice_reduce_fusion
  9.9 1.5 %fusion.5 = bf16[3,2,128,192]{2,3,0,1:T(8,128)(2,1)S(1)} fusion(bf16[3,768,192]{1,2,0:T(8,128)(2,1)S(1)} %copy-done, bf16[2,128,768]{2,1,0:T(8,128)(2,1)} %param.7, f32[768]{0:T(1024)S(1)} %get-tuple-element.6, f32[2,128]{1,0:T(2,128)S(1)} %add_rsqrt_fusion.1, f32[2,128]{1,0:T(2,128)S(1)} %broadcast_multiply_fusion.1), kind=kOutput, calls=%fused_computation.21 | convolution fusion | flops 227622912 | bytes 1577984 | tf_op jit(solution)/shard_map/ipd,cdf->cipf/dot_general | solution.py:51
  11.5 0.3 convolution_multiply_fusion
  11.7 0.3 fusion.48
  12.1 0.2 convolution_convert_fusion.6
  12.4 1.0 %convolution_convert_fusion.2 = bf16[2,128,768]{2,1,0:T(8,128)(2,1)} fusion(bf16[2,128,192]{1,2,0:T(8,128)(2,1)S(1)} %bitcast.89, bf16[192,768]{1,0:T(8,128)(2,1)S(1)} %copy-done.4), kind=kOutput, calls=%fused_computation.14 | convolution fusion | flops 75694080 | bytes 786432 | tf_op jit(solution)/shard_map/ipf,fd->ipd/dot_general | solution.py:55
  13.5 0.4 convolution_convert_fusion.4
  13.9 0.2 copy.26
  14.1 0.1 fusion.38
  14.2 0.4 convolution_convert_fusion
  14.7 1.0 copy.27
  15.6 7.3 %all-to-all-start = ((bf16[8,128,384]{2,1,0:T(8,128)(2,1)}), bf16[8,128,384]{2,1,0:T(8,128)(2,1)S(1)}, u32[]{:S(2)}, u32[]{:S(2)}) async-start(bf16[8,128,384]{2,1,0:T(8,128)(2,1)} %copy.27), calls=%async_computation | async-start | bytes 1572864 | tf_op jit(solution)/shard_map/all_to_all | solution.py:50
  23.0 0.7 gather_fusion
  23.8 25.2 %all-reduce.2.cloned.1.call-done = bf16[2,128,768]{2,1,0:T(8,128)(2,1)} async-done(((bf16[2,128,768]{2,1,0:T(8,128)(2,1)}), bf16[2,128,768]{2,1,0:T(8,128)(2,1)}) %all-reduce.2.cloned.1.call-update) | async-done | bytes 393232 | tf_op jit(solution)/shard_map/psum | solution.py:56
  48.9 1.2 %fusion.45 = f32[2,128]{1,0:T(2,128)S(1)} fusion(bf16[2,128,768]{2,1,0:T(8,128)(2,1)} %all-reduce.2.cloned.1.call-done, bf16[2,128,768]{2,1,0:T(8,128)(2,1)S(1)} %copy-done.1), kind=kLoop, calls=%fused_computation.95 | loop fusion | flops 786176 | bytes 787456 | tf_op jit(solution)/shard_map/reduce_sum | solution.py:10
  50.2 2.0 %multiply_reduce_fusion.1 = (f32[2,128]{1,0:T(2,128)S(1)}, f32[2,128,768]{2,1,0:T(8,128)}) fusion(f32[2,128]{1,0:T(2,128)S(1)} %broadcast_multiply_fusion, bf16[2,128,768]{2,1,0:T(8,128)(2,1)} %all-reduce.2.cloned.1.call-done, bf16[2,128,768]{2,1,0:T(8,128)(2,1)S(1)} %copy-done.1), kind=kLoop, calls=%fused_computation.37 | loop fusion | flops 1179392 | bytes 1574912 | tf_op jit(solution)/shard_map/reduce_sum | solution.py:12
  52.2 0.4 convolution_convert_fusion.5
  52.6 1.4 %gather_fusion.3 = bf16[10,128,192]{1,2,0:T(8,128)(2,1)} fusion(bf16[2,128,192]{1,2,0:T(8,128)(2,1)S(1)} %convolution_convert_fusion.5, s32[1024]{0:T(1024)S(1)} %pad_clamp_fusion.1), kind=kCustom, calls=%fused_computation.3 | custom fusion | bytes 983080 | tf_op jit(solution)/shard_map/gather | solution.py:70
  54.0 0.8 gather_fusion.2
  54.8 0.3 fusion.46
  55.1 0.3 copy.29
  55.4 0.3 copy.28
  55.8 0.4 copy-done.3
  56.2 2.1 %fusion.49 = (f32[10,3,128]{2,1,0:T(4,128)S(1)}, f32[10,3,128,128]{2,3,1,0:T(8,128)}) fusion(bf16[10,128,3,64]{1,3,2,0:T(8,128)(2,1)S(1)} %bitcast.79, bf16[10,128,3,64]{1,3,2,0:T(8,128)(2,1)S(1)} %bitcast.80), kind=kOutput, calls=%fused_computation.99 | convolution fusion | flops 64389248 | bytes 2964480 | tf_op jit(solution)/shard_map/sub | solution.py:25
  58.3 2.0 %convolution_convert_fusion.1 = bf16[10,3,64,128]{3,2,1,0:T(8,128)(2,1)S(1)} fusion(bf16[10,128,3,64]{1,3,2,0:T(8,128)(2,1)S(1)} %bitcast.81, f32[10,3,128,128]{2,3,1,0:T(8,128)} %get-tuple-element.16, f32[10,3,128]{2,1,0:T(4,128)S(1)} %get-tuple-element.15), kind=kOutput, calls=%fused_computation.12 | convolution fusion | flops 64143360 | bytes 2964480 | tf_op jit(solution)/shard_map/nhqk,nkhe->nqhe/dot_general | solution.py:26
  60.3 2.0 %convert_bitcast_fusion = bf16[128,10,768]{2,0,1:T(8,128)(2,1)} fusion(bf16[10,128,192]{1,2,0:T(8,128)(2,1)S(1)} %bitcast.82, bf16[192,768]{1,0:T(8,128)(2,1)S(1)} %copy-done.5), kind=kOutput, calls=%fused_computation.6 | convolution fusion | flops 378470400 | bytes 2752512 | tf_op jit(solution)/shard_map/spf,fd->psd/dot_general | solution.py:75
  62.3 1.0 constant_dynamic-slice_fusion
  63.3 0.6 gather_fusion.1
  63.9 29.2 %reduce-scatter.2.cloned.1.call-done = bf16[32,10,768]{2,0,1:T(8,128)(2,1)} async-done(((bf16[128,10,768]{2,0,1:T(8,128)(2,1)}), bf16[32,10,768]{2,0,1:T(8,128)(2,1)}) %reduce-scatter.2.cloned.1.call-update) | async-done | bytes 491536 | tf_op jit(solution)/shard_map/reduce_scatter | solution.py:74
  93.1 2.0 %fusion.18 = bf16[10,32,768]{2,1,0:T(8,128)(2,1)} fusion(f32[10,32,768]{2,1,0:T(8,128)S(1)} %gather_fusion.1, bf16[32,10,768]{2,0,1:T(8,128)(2,1)} %reduce-scatter.2.cloned.1.call-done, pred[10]{0:T(512)(128)(4,1)S(1)} %broadcast_compare_fusion), kind=kLoop, calls=%fused_computation.40 | loop fusion | flops 983040 | bytes 1966090 | tf_op jit(solution)/shard_map/jit(_where)/select_n | solution.py:85
  (34 shorter events, 0.3 us)
Async XLA Ops:
  6.5 3.3 %copy-start = (bf16[3,768,192]{1,2,0:T(8,128)(2,1)S(1)}, bf16[3,768,192]{1,2,0:T(8,128)(2,1)}, u32[]{:S(2)}) copy-start(bf16[3,768,192]{1,2,0:T(8,128)(2,1)} %param.9) | copy-start | bytes 2654212
  6.5 42.4 %all-reduce.2.cloned.1.call-start = ((), (), s32[]{:S(2)}) async-start(), calls=%async_computation.2 | async-start | bytes 786432 | tf_op jit(solution)/shard_map/psum | solution.py:56
  11.4 1.0 copy-start.4
  11.4 2.0 %copy-start.1 = (bf16[2,128,768]{2,1,0:T(8,128)(2,1)S(1)}, bf16[2,128,768]{2,1,0:T(8,128)(2,1)}, u32[]{:S(2)}) copy-start(bf16[2,128,768]{2,1,0:T(8,128)(2,1)} %param.7) | copy-start | bytes 1179652
  11.5 2.0 %copy-start.7 = (bf16[3,768,192]{1,2,0:T(8,128)(2,1)S(1)}, bf16[3,768,192]{1,2,0:T(8,128)(2,1)}, u32[]{:S(2)}) copy-start(bf16[3,768,192]{1,2,0:T(8,128)(2,1)} %param.11) | copy-start | bytes 2654212
  12.3 1.8 %copy-start.6 = (s32[2,5]{1,0:T(2,128)S(1)}, s32[2,5]{1,0:T(2,128)}, u32[]{:S(2)}) copy-start(s32[2,5]{1,0:T(2,128)} %param.8) | copy-start | bytes 124
  15.6 38.4 %all-to-all-start = ((bf16[8,128,384]{2,1,0:T(8,128)(2,1)}), bf16[8,128,384]{2,1,0:T(8,128)(2,1)S(1)}, u32[]{:S(2)}, u32[]{:S(2)}) async-start(bf16[8,128,384]{2,1,0:T(8,128)(2,1)} %copy.27), calls=%async_computation | async-start | bytes 1572864 | tf_op jit(solution)/shard_map/all_to_all | solution.py:50
  22.9 70.2 %reduce-scatter.2.cloned.1.call-start = ((), (), s32[]{:S(2)}) async-start(), calls=%async_computation.3 | async-start | bytes 2457600 | tf_op jit(solution)/shard_map/reduce_scatter | solution.py:74
  48.9 3.3 %copy-start.2 = (bf16[2,128,768]{2,1,0:T(8,128)(2,1)S(1)}, bf16[2,128,768]{2,1,0:T(8,128)(2,1)}, u32[]{:S(2)}) copy-start(bf16[2,128,768]{2,1,0:T(8,128)(2,1)} %all-reduce.2.cloned.1.call-done) | copy-start | bytes 1179652
  55.1 1.0 %copy-start.3 = (bf16[10,128,192]{1,2,0:T(8,128)(2,1)S(1)}, bf16[10,128,192]{1,2,0:T(8,128)(2,1)}, u32[]{:S(2)}) copy-start(bf16[10,128,192]{1,2,0:T(8,128)(2,1)} %gather_fusion.3) | copy-start | bytes 1474564
  58.3 2.0 %copy-start.5 = (bf16[192,768]{1,0:T(8,128)(2,1)S(1)}, bf16[192,768]{1,0:T(8,128)(2,1)}, u32[]{:S(2)}) copy-start(bf16[192,768]{1,0:T(8,128)(2,1)} %param.12) | copy-start | bytes 884740
Sparse Core Ops, SparseCore 0:
  13.6 35.3 all-reduce.1
  62.4 30.6 reduce-scatter.1
where the time goes:
time: 102 us
  waiting for transfers between devices  54.4 us (53%)
  between operations  13.6 us (13%)
  matrix products  10.8 us (11%)
  local copies, waits for them, and re-layouts  7.93 us (8%)
  other arithmetic  7.86 us (8%)
  starting transfers between devices  7.29 us (7%)
    reduce_scatter x1, waiting for transfers between devices, local(): lax.psum_scatter(jnp.einsum('spf,fd->psd', side_context, cross_out, prefe...  29.2 us
    psum x1, waiting for transfers between devices, local(): lax.psum(own_heads.astype(jnp.bfloat16), 'helper').astype(jnp.float32)  25.2 us
    all_to_all x1, starting transfers between devices, local(): lax.all_to_all(outgoing, 'owner', split_axis=0, concat_axis=0, tiled=True)  7.25 us
    reduce_sum x2, other arithmetic, norm_rows(): row_var = jnp.mean(centred * centred, -1, keepdims=True)  3.27 us
    sub x2, matrix products, attend(): weights = jax.nn.softmax(scores, axis=-1).astype(jnp.bfloat16)  2.46 us
    reduce_sum x2, other arithmetic, norm_rows(): row_mean = jnp.mean(values, -1, keepdims=True)  2.45 us
    dot_general x2, matrix products, attend(): jnp.einsum('nhqk,nkhe->nqhe', weights, v_heads, preferred_element_type=jn...  2.22 us
  transfers between devices with their start and end apart: 3, of which 2 were waited for; matrix products, arithmetic and copies ran while one was open for 9% of the time, Pallas kernels for 0%

commit v1 on v0

v1 whole, which is shorter than its diff:
```python
import functools

import jax
import jax.numpy as jnp
from jax import lax
from jax.experimental import pallas as pl
from jax.experimental.pallas import tpu as pltpu
from jax.sharding import PartitionSpec as P

HEAD = 64
F32 = jnp.float32
BF16 = jnp.bfloat16
VMEM_BYTES = 24 * 1024 * 1024

VMEM = pl.BlockSpec(memory_space=pltpu.VMEM)
SMEM = pl.BlockSpec(memory_space=pltpu.SMEM)


def owner_offsets(slot_count, owner_count):
    near = (slot_count - 1) // 2
    ups = list(range(1, near + 1))
    return ups + [owner_count - k for k in ups] + [owner_count // 2]


def nn(left, right):
    return lax.dot_general(left, right, (((1,), (0,)), ((), ())), preferred_element_type=F32)


def nt(left, right):
    return lax.dot_general(left, right, (((1,), (1,)), ((), ())), preferred_element_type=F32)


def norm_core(values):
    row_mean = jnp.mean(values, -1, keepdims=True)
    centred = values - row_mean
    row_var = jnp.mean(centred * centred, -1, keepdims=True)
    return centred * lax.rsqrt(row_var + 1e-05)


def attend(queries, keys_t, values_t):
    row_n, column_n = queries.shape
    head_n = column_n // HEAD
    head_of = lax.broadcasted_iota(jnp.int32, (row_n, column_n), 1) // HEAD
    zero = jnp.zeros((), queries.dtype)
    stacked = jnp.concatenate([jnp.where(head_of == h, queries, zero) for h in range(head_n)], 0)
    scores = nn(stacked.astype(BF16), keys_t)
    top = jnp.max(scores, -1, keepdims=True)
    powers = jnp.exp(scores - top)
    weights = (powers * (1.0 / jnp.sum(powers, -1, keepdims=True))).astype(BF16)
    spread = nt(weights, values_t)
    context = spread[(head_n - 1) * row_n :]
    for h in range(head_n - 1):
        context = jnp.where(head_of == h, spread[h * row_n : (h + 1) * row_n], context)
    return context.astype(BF16)


def joined_image(partners_ref, owner, image_n):
    low = owner * image_n
    found = jnp.int32(0)
    for image in range(1, image_n):
        for slot in range(partners_ref.shape[1]):
            gap = partners_ref[image, slot] - low
            found = jnp.where(jnp.logical_and(gap >= 0, gap < image_n), jnp.int32(image), found)
    return found


def key_value_kernel(offsets, owner_n, states, gains, proj_t, partners, *rest):
    outs, held = rest[:-1], rest[-1]
    image_n, patch_n, width = states.shape
    columns = proj_t.shape[1]
    rows = states[...].reshape(image_n * patch_n, width).astype(F32)
    normed = (norm_core(rows) * gains[2:3, :]).astype(BF16)
    both = proj_t[1:3].reshape(2 * columns, width)
    projected = nt(both, normed).astype(BF16)
    for image in range(image_n):
        held[image] = projected[:, image * patch_n : (image + 1) * patch_n]
    me = lax.axis_index("owner")
    for out, offset in zip(outs, offsets):
        target = lax.rem(me + offset, owner_n)
        out[...] = held[joined_image(partners, target, image_n)]


def self_kernel(states, gains, proj_t, out):
    image_n, patch_n, width = states.shape
    columns = proj_t.shape[1]
    rows = states[...].reshape(image_n * patch_n, width).astype(F32)
    normed = (norm_core(rows) * gains[0:1, :]).astype(BF16)
    queries = nt(normed, proj_t[0]).astype(BF16).astype(F32) * HEAD ** (-0.5)
    key_value = nt(proj_t[1:3].reshape(2 * columns, width), normed).astype(BF16)
    for image in range(image_n):
        span = slice(image * patch_n, (image + 1) * patch_n)
        out[span, :] = attend(queries[span], key_value[:columns, span], key_value[columns:, span])


def cross_kernel(offsets, owner_n, helper_n, states, gains, proj_t, partners, *rest):
    contexts, rest = rest[:helper_n], rest[helper_n:]
    weights, rest = rest[:helper_n], rest[helper_n:]
    arrived, rest = rest[: len(offsets)], rest[len(offsets) :]
    outs, rest = rest[:helper_n], rest[helper_n:]
    own_rows, mixed_ref, query_ref, side_ref = rest
    image_n, patch_n, width = states.shape
    row_n = patch_n // helper_n
    columns = proj_t.shape[1]
    mixed = states[...].reshape(image_n * patch_n, width).astype(F32)
    for context, weight in zip(contexts, weights):
        mixed = mixed + nn(context[...], weight[...])
    mixed_ref[...] = mixed.reshape(image_n, patch_n, width)
    normed = (norm_core(mixed) * gains[1:2, :]).astype(BF16)
    queries = nt(normed, proj_t[0]).astype(BF16).astype(F32) * HEAD ** (-0.5)
    query_ref[...] = queries.reshape(image_n, patch_n, columns)
    me = lax.axis_index("owner")
    for at, (offset, block) in enumerate(zip(offsets, arrived)):
        partner_owner = lax.rem(me + offset, owner_n)
        image = joined_image(partners, partner_owner, image_n)
        side_ref[at] = attend(query_ref[image], block[:columns, :], block[columns:, :])
    helper = lax.axis_index("helper")
    start = pl.multiple_of(helper * row_n, row_n)
    own_rows[...] = mixed_ref[:, pl.ds(start, row_n), :]
    for k, out in enumerate(outs):
        target = jnp.bitwise_xor(helper, k)
        start = pl.multiple_of(target * row_n, row_n)
        out[...] = side_ref[:, pl.ds(start, row_n), :].reshape(len(offsets) * row_n, columns)


def out_kernel(offsets, owner_n, helper_n, partners, own_rows, *rest):
    sides, rest = rest[:helper_n], rest[helper_n:]
    weights, rest = rest[:helper_n], rest[helper_n:]
    out, term_ref = rest
    image_n, row_n, width = own_rows.shape
    terms = nn(sides[0][...], weights[0][...])
    for side, weight in zip(sides[1:], weights[1:]):
        terms = terms + nn(side[...], weight[...])
    term_ref[...] = terms.reshape(len(offsets), row_n, width)
    me = lax.axis_index("owner")
    for image in range(image_n):
        for slot in range(partners.shape[1]):
            partner = partners[image, slot]
            which = jnp.int32(0)
            for at, offset in enumerate(offsets):
                gap = partner - lax.rem(me + offset, owner_n) * image_n
                which = jnp.where(jnp.logical_and(gap >= 0, gap < image_n), jnp.int32(at), which)
            value = (own_rows[image] + term_ref[which]).astype(BF16)
            out[image, slot] = jnp.where(partner >= 0, value, jnp.zeros_like(value))


def local(owner_n, helper_n, states, partners, self_proj, self_out, cross_proj, cross_out, gains):
    image_n, patch_n, width = states.shape
    slot_n = partners.shape[1]
    columns = self_proj.shape[2]
    row_n = patch_n // helper_n
    offsets = owner_offsets(slot_n, owner_n)
    pair_n = len(offsets)
    self_proj_t = jnp.swapaxes(self_proj, 1, 2)
    cross_proj_t = jnp.swapaxes(cross_proj, 1, 2)

    def across(value, k):
        return lax.ppermute(value, "helper", [(j, j ^ k) for j in range(helper_n)])

    def gather(value):
        blocks = {0: value}
        bit = helper_n // 2
        while bit:
            blocks.update({k ^ bit: across(block, bit) for k, block in list(blocks.items())})
            bit //= 2
        return [blocks[k] for k in range(helper_n)]

    def call(kernel, out_shape, in_specs, scratch=()):
        return pl.pallas_call(
            kernel,
            out_shape=out_shape,
            in_specs=in_specs,
            out_specs=jax.tree.map(lambda _: VMEM, out_shape),
            scratch_shapes=scratch,
            compiler_params=pltpu.CompilerParams(vmem_limit_bytes=VMEM_BYTES),
        )

    shape = jax.ShapeDtypeStruct
    self_weights = gather(self_out)
    with jax.named_scope("cross_keys_values"):
        outgoing = call(
            functools.partial(key_value_kernel, offsets, owner_n),
            [shape((2 * columns, patch_n), BF16)] * pair_n,
            [VMEM, VMEM, VMEM, SMEM],
            [pltpu.VMEM((image_n, 2 * columns, patch_n), BF16)],
        )(states, gains, cross_proj_t, partners)
    arrived = {}
    for offset, block in zip(offsets, outgoing):
        moved = lax.ppermute(block, "owner", [(o, (o + offset) % owner_n) for o in range(owner_n)])
        arrived[(owner_n - offset) % owner_n] = moved
    arrived = [arrived[offset] for offset in offsets]
    with jax.named_scope("self_attention"):
        context = call(
            self_kernel,
            shape((image_n * patch_n, columns), BF16),
            [VMEM, VMEM, VMEM],
        )(states, gains, self_proj_t)
    contexts = gather(context)
    cross_weights = gather(cross_out)
    with jax.named_scope("cross_attention"):
        *sides, own_rows = call(
            functools.partial(cross_kernel, offsets, owner_n, helper_n),
            [shape((pair_n * row_n, columns), BF16)] * helper_n + [shape((image_n, row_n, width), F32)],
            [VMEM, VMEM, VMEM, SMEM] + [VMEM] * (2 * helper_n + pair_n),
            [
                pltpu.VMEM((image_n, patch_n, width), F32),
                pltpu.VMEM((image_n, patch_n, columns), F32),
                pltpu.VMEM((pair_n, patch_n, columns), BF16),
            ],
        )(states, gains, cross_proj_t, partners, *contexts, *self_weights, *arrived)
    sides = [sides[0]] + [across(sides[k], k) for k in range(1, helper_n)]
    with jax.named_scope("pair_output"):
        return call(
            functools.partial(out_kernel, offsets, owner_n, helper_n),
            shape((image_n, slot_n, row_n, width), BF16),
            [SMEM] + [VMEM] * (1 + 2 * helper_n),
            [pltpu.VMEM((pair_n, row_n, width), F32)],
        )(partners, own_rows, *sides, *cross_weights)


def solution(mesh):
    return jax.shard_map(
        functools.partial(local, mesh.shape["owner"], mesh.shape["helper"]),
        mesh=mesh,
        in_specs=(
            P("owner", None, None),
            P("owner", None),
            P(None, None, "helper"),
            P("helper", None),
            P(None, None, "helper"),
            P("helper", None),
            P(),
        ),
        out_specs=P("owner", None, "helper", None),
        check_vma=False,
    )
```

time: 102 us -> 41.9 us (0.41)
  the two profiles are of different devices: /device:TPU:0 before, /device:TPU:11 now
where the time goes in v1:
time: 41.9 us; the launch traced here: 41.7 us
  starting transfers between devices  18.9 us (45%)
  waiting for transfers between devices  12.2 us (29%)
  Pallas kernels  7.57 us (18%)
  local copies, waits for them, and re-layouts  2.89 us (7%)
    ppermute x12, starting transfers between devices, across(): return lax.ppermute(value, 'helper', [(j, j ^ k) for j in range(helper_n)])  11.2 us
    ppermute x5, starting transfers between devices, local(): lax.ppermute(block, 'owner', [(o, (o + offset) % owner_n) for o in range(...  7.75 us
    ppermute x12, waiting for transfers between devices, across(): return lax.ppermute(value, 'helper', [(j, j ^ k) for j in range(helper_n)])  6.19 us
    ppermute x5, waiting for transfers between devices, local(): lax.ppermute(block, 'owner', [(o, (o + offset) % owner_n) for o in range(...  6.03 us
    pallas_call x1, Pallas kernels, local(): call(functools.partial(cross_kernel, offsets, owner_n, helper_n), [shape(...  3.04 us
    unnamed x16, local copies, waits for them, and re-layouts  2.89 us
    pallas_call x1, Pallas kernels, local(): call(functools.partial(out_kernel, offsets, owner_n, helper_n), shape((im...  1.86 us
    pallas_call x1, Pallas kernels, local(): call(self_kernel, shape((image_n * patch_n, columns), BF16), [VMEM, VMEM,...  1.47 us
  transfers between devices with their start and end apart: 17, of which 5 were waited for; matrix products, arithmetic and copies ran while one was open for 0% of the time, Pallas kernels for 14%

profile of v1, /device:TPU:11, one launch (start us, length us, event | category | flops | bytes accessed | tf_op | source)
XLA Modules:
  0.0 41.7 jit_solution(9378961540342578503)
XLA Ops:
  0.0 1.2 %collective-permute-start.4 = (bf16[192,768]{1,0:T(8,128)(2,1)}, bf16[192,768]{1,0:T(8,128)(2,1)S(1)}, u32[]{:S(2)}, u32[]{:S(2)}) collective-permute-start(bf16[192,768]{1,0:T(8,128)(2,1)} %rest_4_.2), channel_id=1, source_target_pairs={{0,2},{1,3},{2,0},{3,1},{4,6},{5,7},{6,4},{7,5},{8,10},{9,11},{10,... | collective-permute-start | bytes 884744 | tf_op jit(solution)/shard_map/ppermute | solution.py:157
  1.2 0.2 collective-permute-start.15
  1.5 1.2 %copy-done = bf16[3,768,192]{1,2,0:T(8,128)(2,1)S(1)} copy-done((bf16[3,768,192]{1,2,0:T(8,128)(2,1)S(1)}, bf16[3,768,192]{1,2,0:T(8,128)(2,1)}, u32[]{:S(2)}) %copy-start) | copy-done | bytes 884760
  2.6 1.0 %copy-done.2 = bf16[2,128,768]{2,1,0:T(8,128)(2,1)S(1)} copy-done((bf16[2,128,768]{2,1,0:T(8,128)(2,1)S(1)}, bf16[2,128,768]{2,1,0:T(8,128)(2,1)}, u32[]{:S(2)}) %copy-start.2) | copy-done | bytes 393240
  3.6 0.7 %copy-done.6 = f32[3,768]{1,0:T(4,128)S(1)} copy-done((f32[3,768]{1,0:T(4,128)S(1)}, f32[3,768]{1,0:T(4,128)}, u32[]{:S(2)}) %copy-start.6) | copy-done | bytes 9240
  4.3 1.2 %cross_keys_values.1 = (bf16[384,128]{1,0:T(8,128)(2,1)S(1)}, bf16[384,128]{1,0:T(8,128)(2,1)S(1)}, bf16[384,128]{1,0:T(8,128)(2,1)S(1)}, bf16[384,128]{1,0:T(8,128)(2,1)S(1)}, bf16[384,128]{1,0:T(8,128)(2,1)S(1)}) custom-call(bf16[2,128,768]{2,1,0:T(8,128)(2,1)S(1)} %copy-done.2, f32[3,768]{1,0:T(4,128)S(1)} %copy-done.6, bf16[3,192,768]{2,1,0:T(8,128)(2,1)S(1)} %bitcast.2, ...), custom_call_target="tpu_custom_call" | custom-call | tf_op jit(solution)/shard_map/cross_keys_values/pallas_call | solution.py:180
  5.5 0.0 copy-start.1
  5.6 2.4 %collective-permute-start.10 = (bf16[384,128]{1,0:T(8,128)(2,1)S(1)}, bf16[384,128]{1,0:T(8,128)(2,1)S(1)}, u32[]{:S(2)}, u32[]{:S(2)}) collective-permute-start(bf16[384,128]{1,0:T(8,128)(2,1)S(1)} %get-tuple-element.19), channel_id=1, source_target_pairs={{0,16},{4,20},{8,24},{12,28},{16,0},{20,4},{24,8},{28,12},{1,17},{... | collective-permute-start | bytes 294920 | tf_op jit(solution)/shard_map/ppermute | solution.py:188
  8.0 0.2 collective-permute-start.6
  8.2 0.2 collective-permute-start.7
  8.4 6.0 %collective-permute-done.10.rest_12_ = bf16[384,128]{1,0:T(8,128)(2,1)S(1)} collective-permute-done((bf16[384,128]{1,0:T(8,128)(2,1)S(1)}, bf16[384,128]{1,0:T(8,128)(2,1)S(1)}, u32[]{:S(2)}, u32[]{:S(2)}) %collective-permute-start.10) | collective-permute-done | bytes 98336 | tf_op jit(solution)/shard_map/ppermute | solution.py:188
  14.4 0.0 collective-permute-done.6.rest_8_
  14.4 4.9 %collective-permute-start.9 = (bf16[384,128]{1,0:T(8,128)(2,1)S(1)}, bf16[384,128]{1,0:T(8,128)(2,1)S(1)}, u32[]{:S(2)}, u32[]{:S(2)}) collective-permute-start(bf16[384,128]{1,0:T(8,128)(2,1)S(1)} %get-tuple-element.18), channel_id=1, source_target_pairs={{0,8},{4,12},{8,16},{12,20},{16,24},{20,28},{24,0},{28,4},{1,9},{5... | collective-permute-start | bytes 294920 | tf_op jit(solution)/shard_map/ppermute | solution.py:188
  19.3 1.5 %self_attention.1.rest_0_ = bf16[256,192]{1,0:T(8,128)(2,1)S(1)} custom-call(bf16[2,128,768]{2,1,0:T(8,128)(2,1)S(1)} %copy-done.2, f32[3,768]{1,0:T(4,128)S(1)} %copy-done.6, bf16[3,192,768]{2,1,0:T(8,128)(2,1)S(1)} %bitcast.4), custom_call_target="tpu_custom_call" | custom-call | tf_op jit(solution)/shard_map/self_attention/pallas_call | solution.py:192
  20.8 0.0 collective-permute-done.7.rest_9_
  20.8 1.3 %collective-permute-start.1 = (bf16[256,192]{1,0:T(8,128)(2,1)S(1)}, bf16[256,192]{1,0:T(8,128)(2,1)S(1)}, u32[]{:S(2)}, u32[]{:S(2)}) collective-permute-start(bf16[256,192]{1,0:T(8,128)(2,1)S(1)} %self_attention.1.rest_0_), channel_id=1, source_target_pairs={{0,2},{1,3},{2,0},{3,1},{4,6},{5,7},{6,4},{7,5},{8,10},{9,11},{10,... | collective-permute-start | bytes 294920 | tf_op jit(solution)/shard_map/ppermute | solution.py:157
  22.2 0.0 collective-permute-done.8.rest_10_
  22.2 2.4 %collective-permute-start.3 = (bf16[192,768]{1,0:T(8,128)(2,1)S(1)}, bf16[192,768]{1,0:T(8,128)(2,1)S(1)}, u32[]{:S(2)}, u32[]{:S(2)}) collective-permute-start(bf16[192,768]{1,0:T(8,128)(2,1)S(1)} %copy-done.4), channel_id=1, source_target_pairs={{0,1},{1,0},{2,3},{3,2},{4,5},{5,4},{6,7},{7,6},{8,9},{9,8},{10,11... | collective-permute-start | bytes 884744 | tf_op jit(solution)/shard_map/ppermute | solution.py:157
  24.5 0.1 collective-permute-start.5
  24.6 0.4 %collective-permute-start.14 = (bf16[192,768]{1,0:T(8,128)(2,1)S(1)}, bf16[192,768]{1,0:T(8,128)(2,1)S(1)}, u32[]{:S(2)}, u32[]{:S(2)}) collective-permute-start(bf16[192,768]{1,0:T(8,128)(2,1)S(1)} %copy-done.5), channel_id=1, source_target_pairs={{0,1},{1,0},{2,3},{3,2},{4,5},{5,4},{6,7},{7,6},{8,9},{9,8},{10,11... | collective-permute-start | bytes 884744 | tf_op jit(solution)/shard_map/ppermute | solution.py:157
  25.1 0.1 collective-permute-start.16
  25.1 2.8 %collective-permute-start = (bf16[256,192]{1,0:T(8,128)(2,1)S(1)}, bf16[256,192]{1,0:T(8,128)(2,1)S(1)}, u32[]{:S(2)}, u32[]{:S(2)}) collective-permute-start(bf16[256,192]{1,0:T(8,128)(2,1)S(1)} %self_attention.1.rest_0_), channel_id=1, source_target_pairs={{0,1},{1,0},{2,3},{3,2},{4,5},{5,4},{6,7},{7,6},{8,9},{9,8},{10,11... | collective-permute-start | bytes 294920 | tf_op jit(solution)/shard_map/ppermute | solution.py:157
  28.0 1.0 %collective-permute-done.rest_1_ = bf16[256,192]{1,0:T(8,128)(2,1)S(1)} collective-permute-done((bf16[256,192]{1,0:T(8,128)(2,1)S(1)}, bf16[256,192]{1,0:T(8,128)(2,1)S(1)}, u32[]{:S(2)}, u32[]{:S(2)}) %collective-permute-start) | collective-permute-done | bytes 98336 | tf_op jit(solution)/shard_map/ppermute | solution.py:157
  29.0 0.4 collective-permute-start.2
  29.3 1.0 %collective-permute-done.2.rest_3_ = bf16[256,192]{1,0:T(8,128)(2,1)S(1)} collective-permute-done((bf16[256,192]{1,0:T(8,128)(2,1)S(1)}, bf16[256,192]{1,0:T(8,128)(2,1)S(1)}, u32[]{:S(2)}, u32[]{:S(2)}) %collective-permute-start.2) | collective-permute-done | bytes 98336 | tf_op jit(solution)/shard_map/ppermute | solution.py:157
  30.3 3.0 %cross_attention.1 = (bf16[160,192]{1,0:T(8,128)(2,1)S(1)}, bf16[160,192]{1,0:T(8,128)(2,1)S(1)}, bf16[160,192]{1,0:T(8,128)(2,1)S(1)}, bf16[160,192]{1,0:T(8,128)(2,1)S(1)}, f32[2,32,768]{2,1,0:T(8,128)S(1)}) custom-call(bf16[2,128,768]{2,1,0:T(8,128)(2,1)S(1)} %copy-done.2, f32[3,768]{1,0:T(4,128)S(1)} %copy-done.6, bf16[3,192,768]{2,1,0:T(8,128)(2,1)S(1)} %bitcast.3, ...), custom_call_target="tpu_custom_call" | custom-call | tf_op jit(solution)/shard_map/cross_attention/pallas_call | solution.py:200
  33.4 0.4 %collective-permute-start.11 = (bf16[160,192]{1,0:T(8,128)(2,1)S(1)}, bf16[160,192]{1,0:T(8,128)(2,1)S(1)}, u32[]{:S(2)}, u32[]{:S(2)}) collective-permute-start(bf16[160,192]{1,0:T(8,128)(2,1)S(1)} %get-tuple-element.22), channel_id=1, source_target_pairs={{0,1},{1,0},{2,3},{3,2},{4,5},{5,4},{6,7},{7,6},{8,9},{9,8},{10,11... | collective-permute-start | bytes 184328 | tf_op jit(solution)/shard_map/ppermute | solution.py:157
  33.8 1.2 %collective-permute-start.12 = (bf16[160,192]{1,0:T(8,128)(2,1)S(1)}, bf16[160,192]{1,0:T(8,128)(2,1)S(1)}, u32[]{:S(2)}, u32[]{:S(2)}) collective-permute-start(bf16[160,192]{1,0:T(8,128)(2,1)S(1)} %get-tuple-element.23), channel_id=1, source_target_pairs={{0,2},{1,3},{2,0},{3,1},{4,6},{5,7},{6,4},{7,5},{8,10},{9,11},{10,... | collective-permute-start | bytes 184328 | tf_op jit(solution)/shard_map/ppermute | solution.py:157
  35.0 0.6 %collective-permute-start.13 = (bf16[160,192]{1,0:T(8,128)(2,1)S(1)}, bf16[160,192]{1,0:T(8,128)(2,1)S(1)}, u32[]{:S(2)}, u32[]{:S(2)}) collective-permute-start(bf16[160,192]{1,0:T(8,128)(2,1)S(1)} %get-tuple-element.24), channel_id=1, source_target_pairs={{0,3},{1,2},{2,1},{3,0},{4,7},{5,6},{6,5},{7,4},{8,11},{9,10},{10,... | collective-permute-start | bytes 184328 | tf_op jit(solution)/shard_map/ppermute | solution.py:157
  35.6 2.1 %collective-permute-done.12.rest_2_ = bf16[160,192]{1,0:T(8,128)(2,1)S(1)} collective-permute-done((bf16[160,192]{1,0:T(8,128)(2,1)S(1)}, bf16[160,192]{1,0:T(8,128)(2,1)S(1)}, u32[]{:S(2)}, u32[]{:S(2)}) %collective-permute-start.12) | collective-permute-done | bytes 61472 | tf_op jit(solution)/shard_map/ppermute | solution.py:157
  37.7 2.1 %collective-permute-done.13.rest_3_ = bf16[160,192]{1,0:T(8,128)(2,1)S(1)} collective-permute-done((bf16[160,192]{1,0:T(8,128)(2,1)S(1)}, bf16[160,192]{1,0:T(8,128)(2,1)S(1)}, u32[]{:S(2)}, u32[]{:S(2)}) %collective-permute-start.13) | collective-permute-done | bytes 61472 | tf_op jit(solution)/shard_map/ppermute | solution.py:157
  39.8 1.9 %pair_output.1 = bf16[2,5,32,768]{3,2,1,0:T(8,128)(2,1)} custom-call(s32[2,5]{1,0:T(2,128)S(1)} %copy-done.7, f32[2,32,768]{2,1,0:T(8,128)S(1)} %get-tuple-element.20.own_rows, bf16[160,192]{1,0:T(8,128)(2,1)S(1)} %get-tuple-element.21.rest_0_, bf16[160,192]{1,0:T(8,128)(2,1)S(1)} %collective-permute-done.11.rest_1_, ...), custom_call_target="tpu_custom_call" | custom-call | tf_op jit(solution)/shard_map/pair_output/pallas_call | solution.py:212
  (22 shorter events, 0.0 us)
Async XLA Ops:
  0.0 1.5 %copy-start.7 = (s32[2,5]{1,0:T(2,128)S(1)}, s32[2,5]{1,0:T(2,128)}, u32[]{:S(2)}) copy-start(s32[2,5]{1,0:T(2,128)} %partners.5) | copy-start | bytes 124
  0.0 24.5 %collective-permute-start.4 = (bf16[192,768]{1,0:T(8,128)(2,1)}, bf16[192,768]{1,0:T(8,128)(2,1)S(1)}, u32[]{:S(2)}, u32[]{:S(2)}) collective-permute-start(bf16[192,768]{1,0:T(8,128)(2,1)} %rest_4_.2), channel_id=1, source_target_pairs={{0,2},{1,3},{2,0},{3,1},{4,6},{5,7},{6,4},{7,5},{8,10},{9,11},{10,... | collective-permute-start | bytes 884744 | tf_op jit(solution)/shard_map/ppermute | solution.py:157
  1.2 23.8 %collective-permute-start.15 = (bf16[192,768]{1,0:T(8,128)(2,1)}, bf16[192,768]{1,0:T(8,128)(2,1)S(1)}, u32[]{:S(2)}, u32[]{:S(2)}) collective-permute-start(bf16[192,768]{1,0:T(8,128)(2,1)} %rest_4_.3), channel_id=1, source_target_pairs={{0,2},{1,3},{2,0},{3,1},{4,6},{5,7},{6,4},{7,5},{8,10},{9,11},{10,... | collective-permute-start | bytes 884744 | tf_op jit(solution)/shard_map/ppermute | solution.py:157
  1.5 1.2 %copy-start = (bf16[3,768,192]{1,2,0:T(8,128)(2,1)S(1)}, bf16[3,768,192]{1,2,0:T(8,128)(2,1)}, u32[]{:S(2)}) copy-start(bf16[3,768,192]{1,2,0:T(8,128)(2,1)} %param.11) | copy-start | bytes 2654212
  2.6 1.0 %copy-start.2 = (bf16[2,128,768]{2,1,0:T(8,128)(2,1)S(1)}, bf16[2,128,768]{2,1,0:T(8,128)(2,1)}, u32[]{:S(2)}) copy-start(bf16[2,128,768]{2,1,0:T(8,128)(2,1)} %states.5) | copy-start | bytes 1179652
  3.6 0.7 %copy-start.6 = (f32[3,768]{1,0:T(4,128)S(1)}, f32[3,768]{1,0:T(4,128)}, u32[]{:S(2)}) copy-start(f32[3,768]{1,0:T(4,128)} %gains.5) | copy-start | bytes 27652
  4.3 15.0 %copy-start.3 = (bf16[3,768,192]{1,2,0:T(8,128)(2,1)S(1)}, bf16[3,768,192]{1,2,0:T(8,128)(2,1)}, u32[]{:S(2)}) copy-start(bf16[3,768,192]{1,2,0:T(8,128)(2,1)} %param.9) | copy-start | bytes 2654212
  4.3 20.3 %copy-start.5 = (bf16[192,768]{1,0:T(8,128)(2,1)S(1)}, bf16[192,768]{1,0:T(8,128)(2,1)}, u32[]{:S(2)}) copy-start(bf16[192,768]{1,0:T(8,128)(2,1)} %rest_4_.3) | copy-start | bytes 884740
  5.5 24.8 %copy-start.1 = (bf16[3,768,192]{1,2,0:T(8,128)(2,1)S(1)}, bf16[3,768,192]{1,2,0:T(8,128)(2,1)}, u32[]{:S(2)}) copy-start(bf16[3,768,192]{1,2,0:T(8,128)(2,1)} %param.11) | copy-start | bytes 2654212
  5.6 8.9 %collective-permute-start.10 = (bf16[384,128]{1,0:T(8,128)(2,1)S(1)}, bf16[384,128]{1,0:T(8,128)(2,1)S(1)}, u32[]{:S(2)}, u32[]{:S(2)}) collective-permute-start(bf16[384,128]{1,0:T(8,128)(2,1)S(1)} %get-tuple-element.19), channel_id=1, source_target_pairs={{0,16},{4,20},{8,24},{12,28},{16,0},{20,4},{24,8},{28,12},{1,17},{... | collective-permute-start | bytes 294920 | tf_op jit(solution)/shard_map/ppermute | solution.py:188
  8.0 6.4 %collective-permute-start.6 = (bf16[384,128]{1,0:T(8,128)(2,1)S(1)}, bf16[384,128]{1,0:T(8,128)(2,1)S(1)}, u32[]{:S(2)}, u32[]{:S(2)}) collective-permute-start(bf16[384,128]{1,0:T(8,128)(2,1)S(1)} %get-tuple-element.15), channel_id=1, source_target_pairs={{0,28},{4,0},{8,4},{12,8},{16,12},{20,16},{24,20},{28,24},{1,29},{... | collective-permute-start | bytes 294920 | tf_op jit(solution)/shard_map/ppermute | solution.py:188
  8.2 12.6 %collective-permute-start.7 = (bf16[384,128]{1,0:T(8,128)(2,1)S(1)}, bf16[384,128]{1,0:T(8,128)(2,1)S(1)}, u32[]{:S(2)}, u32[]{:S(2)}) collective-permute-start(bf16[384,128]{1,0:T(8,128)(2,1)S(1)} %get-tuple-element.16), channel_id=1, source_target_pairs={{0,24},{4,28},{8,0},{12,4},{16,8},{20,12},{24,16},{28,20},{1,25},{... | collective-permute-start | bytes 294920 | tf_op jit(solution)/shard_map/ppermute | solution.py:188
  14.4 7.7 %collective-permute-start.8 = (bf16[384,128]{1,0:T(8,128)(2,1)S(1)}, bf16[384,128]{1,0:T(8,128)(2,1)S(1)}, u32[]{:S(2)}, u32[]{:S(2)}) collective-permute-start(bf16[384,128]{1,0:T(8,128)(2,1)S(1)} %get-tuple-element.17), channel_id=1, source_target_pairs={{0,4},{4,8},{8,12},{12,16},{16,20},{20,24},{24,28},{28,0},{1,5},{5... | collective-permute-start | bytes 294920 | tf_op jit(solution)/shard_map/ppermute | solution.py:188
  14.4 10.2 %collective-permute-start.9 = (bf16[384,128]{1,0:T(8,128)(2,1)S(1)}, bf16[384,128]{1,0:T(8,128)(2,1)S(1)}, u32[]{:S(2)}, u32[]{:S(2)}) collective-permute-start(bf16[384,128]{1,0:T(8,128)(2,1)S(1)} %get-tuple-element.18), channel_id=1, source_target_pairs={{0,8},{4,12},{8,16},{12,20},{16,24},{20,28},{24,0},{28,4},{1,9},{5... | collective-permute-start | bytes 294920 | tf_op jit(solution)/shard_map/ppermute | solution.py:188
  19.3 2.8 %copy-start.4 = (bf16[192,768]{1,0:T(8,128)(2,1)S(1)}, bf16[192,768]{1,0:T(8,128)(2,1)}, u32[]{:S(2)}) copy-start(bf16[192,768]{1,0:T(8,128)(2,1)} %rest_4_.2) | copy-start | bytes 884740
  20.8 4.3 %collective-permute-start.1 = (bf16[256,192]{1,0:T(8,128)(2,1)S(1)}, bf16[256,192]{1,0:T(8,128)(2,1)S(1)}, u32[]{:S(2)}, u32[]{:S(2)}) collective-permute-start(bf16[256,192]{1,0:T(8,128)(2,1)S(1)} %self_attention.1.rest_0_), channel_id=1, source_target_pairs={{0,2},{1,3},{2,0},{3,1},{4,6},{5,7},{6,4},{7,5},{8,10},{9,11},{10,... | collective-permute-start | bytes 294920 | tf_op jit(solution)/shard_map/ppermute | solution.py:157
  22.2 8.2 %collective-permute-start.3 = (bf16[192,768]{1,0:T(8,128)(2,1)S(1)}, bf16[192,768]{1,0:T(8,128)(2,1)S(1)}, u32[]{:S(2)}, u32[]{:S(2)}) collective-permute-start(bf16[192,768]{1,0:T(8,128)(2,1)S(1)} %copy-done.4), channel_id=1, source_target_pairs={{0,1},{1,0},{2,3},{3,2},{4,5},{5,4},{6,7},{7,6},{8,9},{9,8},{10,11... | collective-permute-start | bytes 884744 | tf_op jit(solution)/shard_map/ppermute | solution.py:157
  24.5 5.8 %collective-permute-start.5 = (bf16[192,768]{1,0:T(8,128)(2,1)S(1)}, bf16[192,768]{1,0:T(8,128)(2,1)S(1)}, u32[]{:S(2)}, u32[]{:S(2)}) collective-permute-start(bf16[192,768]{1,0:T(8,128)(2,1)S(1)} %collective-permute-done.4.rest_6_), channel_id=1, source_target_pairs={{0,1},{1,0},{2,3},{3,2},{4,5},{5,4},{6,7},{7,6},{8,9},{9,8},{10,11... | collective-permute-start | bytes 884744 | tf_op jit(solution)/shard_map/ppermute | solution.py:157
  24.6 11.0 %collective-permute-start.14 = (bf16[192,768]{1,0:T(8,128)(2,1)S(1)}, bf16[192,768]{1,0:T(8,128)(2,1)S(1)}, u32[]{:S(2)}, u32[]{:S(2)}) collective-permute-start(bf16[192,768]{1,0:T(8,128)(2,1)S(1)} %copy-done.5), channel_id=1, source_target_pairs={{0,1},{1,0},{2,3},{3,2},{4,5},{5,4},{6,7},{7,6},{8,9},{9,8},{10,11... | collective-permute-start | bytes 884744 | tf_op jit(solution)/shard_map/ppermute | solution.py:157
  25.1 10.6 %collective-permute-start.16 = (bf16[192,768]{1,0:T(8,128)(2,1)S(1)}, bf16[192,768]{1,0:T(8,128)(2,1)S(1)}, u32[]{:S(2)}, u32[]{:S(2)}) collective-permute-start(bf16[192,768]{1,0:T(8,128)(2,1)S(1)} %collective-permute-done.15.rest_6_), channel_id=1, source_target_pairs={{0,1},{1,0},{2,3},{3,2},{4,5},{5,4},{6,7},{7,6},{8,9},{9,8},{10,11... | collective-permute-start | bytes 884744 | tf_op jit(solution)/shard_map/ppermute | solution.py:157
  25.1 3.8 %collective-permute-start = (bf16[256,192]{1,0:T(8,128)(2,1)S(1)}, bf16[256,192]{1,0:T(8,128)(2,1)S(1)}, u32[]{:S(2)}, u32[]{:S(2)}) collective-permute-start(bf16[256,192]{1,0:T(8,128)(2,1)S(1)} %self_attention.1.rest_0_), channel_id=1, source_target_pairs={{0,1},{1,0},{2,3},{3,2},{4,5},{5,4},{6,7},{7,6},{8,9},{9,8},{10,11... | collective-permute-start | bytes 294920 | tf_op jit(solution)/shard_map/ppermute | solution.py:157
  29.0 1.3 %collective-permute-start.2 = (bf16[256,192]{1,0:T(8,128)(2,1)S(1)}, bf16[256,192]{1,0:T(8,128)(2,1)S(1)}, u32[]{:S(2)}, u32[]{:S(2)}) collective-permute-start(bf16[256,192]{1,0:T(8,128)(2,1)S(1)} %collective-permute-done.1.rest_2_), channel_id=1, source_target_pairs={{0,1},{1,0},{2,3},{3,2},{4,5},{5,4},{6,7},{7,6},{8,9},{9,8},{10,11... | collective-permute-start | bytes 294920 | tf_op jit(solution)/shard_map/ppermute | solution.py:157
  33.4 2.2 %collective-permute-start.11 = (bf16[160,192]{1,0:T(8,128)(2,1)S(1)}, bf16[160,192]{1,0:T(8,128)(2,1)S(1)}, u32[]{:S(2)}, u32[]{:S(2)}) collective-permute-start(bf16[160,192]{1,0:T(8,128)(2,1)S(1)} %get-tuple-element.22), channel_id=1, source_target_pairs={{0,1},{1,0},{2,3},{3,2},{4,5},{5,4},{6,7},{7,6},{8,9},{9,8},{10,11... | collective-permute-start | bytes 184328 | tf_op jit(solution)/shard_map/ppermute | solution.py:157
  33.8 3.9 %collective-permute-start.12 = (bf16[160,192]{1,0:T(8,128)(2,1)S(1)}, bf16[160,192]{1,0:T(8,128)(2,1)S(1)}, u32[]{:S(2)}, u32[]{:S(2)}) collective-permute-start(bf16[160,192]{1,0:T(8,128)(2,1)S(1)} %get-tuple-element.23), channel_id=1, source_target_pairs={{0,2},{1,3},{2,0},{3,1},{4,6},{5,7},{6,4},{7,5},{8,10},{9,11},{10,... | collective-permute-start | bytes 184328 | tf_op jit(solution)/shard_map/ppermute | solution.py:157
  35.0 4.8 %collective-permute-start.13 = (bf16[160,192]{1,0:T(8,128)(2,1)S(1)}, bf16[160,192]{1,0:T(8,128)(2,1)S(1)}, u32[]{:S(2)}, u32[]{:S(2)}) collective-permute-start(bf16[160,192]{1,0:T(8,128)(2,1)S(1)} %get-tuple-element.24), channel_id=1, source_target_pairs={{0,3},{1,2},{2,1},{3,0},{4,7},{5,6},{6,5},{7,4},{8,11},{9,10},{10,... | collective-permute-start | bytes 184328 | tf_op jit(solution)/shard_map/ppermute | solution.py:157

commit v2 on v0

v2 whole, which is shorter than its diff:
```python
import functools

import jax
import jax.numpy as jnp
from jax import lax
from jax.experimental import pallas as pl
from jax.experimental.pallas import tpu as pltpu
from jax.sharding import PartitionSpec as P

HEAD = 64
LANES = 128
F32 = jnp.float32
BF16 = jnp.bfloat16
VMEM_BYTES = 24 * 1024 * 1024
EARLY_WEIGHT = 3 * 10**9
LATE_WEIGHT = 10**11

VMEM = pl.BlockSpec(memory_space=pltpu.VMEM)
HBM = pl.BlockSpec(memory_space=pltpu.HBM)
ANY = pl.BlockSpec(memory_space=pl.ANY)


def owner_swaps(slot_count, owner_count):
    near = (slot_count - 1) // 2
    swaps = [(owner_count // 2, 0)]
    for k in range(near, 1, -1):
        swaps += [(k, 1), (k, 0)]
    return swaps + [(1, 0), (1, 1)]


def swap_target(owner, swap, owner_count):
    distance, colour = swap
    step = distance & -distance
    if isinstance(owner, int):
        up = (owner // step) % 2 == colour
        return (owner + (distance if up else owner_count - distance)) % owner_count
    up = jnp.bitwise_and(lax.shift_right_logical(owner, step.bit_length() - 1), 1) == colour
    return lax.rem(owner + jnp.where(up, distance, owner_count - distance), owner_count)


def nn(left, right):
    return lax.dot_general(left, right, (((1,), (0,)), ((), ())), preferred_element_type=F32)


def nt(left, right):
    return lax.dot_general(left, right, (((1,), (1,)), ((), ())), preferred_element_type=F32)


def norm_core(values):
    row_mean = jnp.mean(values, -1, keepdims=True)
    centred = values - row_mean
    row_var = jnp.mean(centred * centred, -1, keepdims=True)
    return centred * lax.rsqrt(row_var + 1e-05)


def head_stack(queries):
    head_of = lax.broadcasted_iota(jnp.int32, queries.shape, 1) // HEAD
    zero = jnp.zeros((), queries.dtype)
    return jnp.concatenate(
        [jnp.where(head_of == h, queries, zero) for h in range(queries.shape[1] // HEAD)], 0
    ).astype(BF16)


def attend(stacked, keys_t, values_t):
    column_n = keys_t.shape[0]
    head_n = column_n // HEAD
    row_n = stacked.shape[0] // head_n
    scores = nn(stacked, keys_t)
    powers = jnp.exp(scores - jnp.max(scores, -1, keepdims=True))
    weights = (powers * (1.0 / jnp.sum(powers, -1, keepdims=True))).astype(BF16)
    spread = nt(weights, values_t)
    head_of = lax.broadcasted_iota(jnp.int32, (row_n, column_n), 1) // HEAD
    context = spread[(head_n - 1) * row_n :]
    for h in range(head_n - 1):
        context = jnp.where(head_of == h, spread[h * row_n : (h + 1) * row_n], context)
    return context


def pack(block):
    row_n = block.shape[0]
    tail = block[:, LANES:]
    return jnp.concatenate(
        [block[:, :LANES], jnp.concatenate([tail[: row_n // 2], tail[row_n // 2 :]], 1)], 0
    ).astype(BF16)


def joined_image(partners, owner, image_n):
    low = owner * image_n
    found = jnp.int32(0)
    for image in range(1, image_n):
        for slot in range(partners.shape[1]):
            gap = partners[image, slot] - low
            found = jnp.where(jnp.logical_and(gap >= 0, gap < image_n), jnp.int32(image), found)
    return found


def own_images_kernel(swaps, owner_n, states, gains, self_t, cross_t, partners, weight, *rest):
    outs, rest = rest[: len(swaps)], rest[len(swaps) :]
    context_out, table, weight_out, states_v, gains_v, self_v, cross_v, partners_s, held, sems = rest
    image_n, patch_n, width = states.shape
    columns = self_t.shape[1]
    copies = [
        pltpu.make_async_copy(states, states_v, sems.at[0]),
        pltpu.make_async_copy(gains, gains_v, sems.at[1]),
        pltpu.make_async_copy(cross_t.at[pl.ds(1, 2)], cross_v, sems.at[2]),
        pltpu.make_async_copy(partners, partners_s, sems.at[3]),
        pltpu.make_async_copy(self_t, self_v, sems.at[4]),
        pltpu.make_async_copy(weight, weight_out, sems.at[5]),
    ]
    for copy in copies:
        copy.start()
    copies[0].wait()
    rows = norm_core(states_v[...].reshape(image_n * patch_n, width).astype(F32))
    copies[1].wait()
    normed = (rows * gains_v[2:3, :]).astype(BF16)
    copies[2].wait()
    projected = nt(cross_v[...].reshape(2 * columns, width), normed).astype(BF16)
    for image in range(image_n):
        held[image] = projected[:, image * patch_n : (image + 1) * patch_n]
    copies[3].wait()
    me = lax.axis_index("owner")
    for at, (out, swap) in enumerate(zip(outs, swaps)):
        image = joined_image(partners_s, swap_target(me, swap, owner_n), image_n)
        out[...] = held[image]
        table[at : at + 1, :] = jnp.full((1, LANES), image, jnp.int32)
    normed = (rows * gains_v[0:1, :]).astype(BF16)
    copies[4].wait()
    queries = nt(normed, self_v[0]).astype(BF16).astype(F32) * HEAD ** (-0.5)
    key_value = nt(self_v[1:3].reshape(2 * columns, width), normed).astype(BF16)
    contexts = []
    for image in range(image_n):
        span = slice(image * patch_n, (image + 1) * patch_n)
        contexts.append(
            attend(head_stack(queries[span]), key_value[:columns, span], key_value[columns:, span])
        )
    context_out[...] = pack(jnp.concatenate(contexts, 0))
    copies[5].wait()


def unpack(block):
    row_n = block.shape[0] * 2 // 3
    tail = block[row_n:, :]
    return jnp.concatenate(
        [block[:row_n, :], jnp.concatenate([tail[:, :HEAD], tail[:, HEAD:]], 0)], 1
    )


def partial_kernel(states, own, got, own_weight, got_weight, cross_out, base, sent, weight_v, sems):
    row_all = base.shape[0]
    copies = [
        pltpu.make_async_copy(got_weight, weight_v, sems.at[0]),
        pltpu.make_async_copy(cross_out, sent.at[pl.ds(row_all, cross_out.shape[0])], sems.at[1]),
    ]
    for copy in copies:
        copy.start()
    part = nn(unpack(own[...]), own_weight[...])
    base[...] = states[...].reshape(part.shape).astype(F32)
    copies[0].wait()
    part = part + nn(unpack(got[...]), weight_v[...])
    sent[:row_all, :] = part.astype(BF16)
    base[...] += part
    copies[1].wait()


def query_kernel(helper_n, base, got, gains, proj_t, own_rows, queries_out, mixed_ref):
    mixed = base[...] + got[: base.shape[0], :].astype(F32)
    image_n, row_n, width = own_rows.shape
    patch_n = row_n * helper_n
    mixed_ref[...] = mixed.reshape(image_n, patch_n, width)
    normed = (norm_core(mixed) * gains[1:2, :]).astype(BF16)
    queries = nt(normed, proj_t[0]).astype(BF16).astype(F32) * HEAD ** (-0.5)
    queries_out[...] = queries.reshape(queries_out.shape)
    start = pl.multiple_of(lax.axis_index("helper") * row_n, row_n)
    own_rows[...] = mixed_ref[:, pl.ds(start, row_n), :]


def hand_on_kernel(weight, waited, out, sem):
    del waited
    copy = pltpu.make_async_copy(weight, out, sem)
    copy.start()
    copy.wait()


def cross_pairs(places, helper_n, queries, table, arrived, put):
    for at, (place, block) in enumerate(zip(places, arrived)):
        chosen = queries[0]
        for image in range(1, queries.shape[0]):
            chosen = jnp.where(table[place : place + 1, 0:1] == image, queries[image], chosen)
        columns = block.shape[0] // 2
        context = attend(head_stack(chosen), block[:columns, :], block[columns:, :])
        row_n = context.shape[0] // helper_n
        for helper in range(helper_n):
            put(at, helper, pack(context[helper * row_n : (helper + 1) * row_n]))


def cross_kernel(places, helper_n, queries, table, *rest):
    *arrived, out = rest

    def put(at, helper, rows):
        out[helper, at] = rows

    cross_pairs(places, helper_n, queries, table, arrived, put)


def last_cross_kernel(places, helper_n, queries, table, before, *rest):
    arrived, (*outs, held) = rest[: len(places)], rest[len(places) :]
    first = before.shape[1]
    helper = lax.axis_index("helper")
    for k, out in enumerate(outs):
        out[:first] = before[jnp.bitwise_xor(helper, k)]

    def put(at, helper, rows):
        held[helper, at] = rows

    cross_pairs(places, helper_n, queries, table, arrived, put)
    for k, out in enumerate(outs):
        out[first:] = held[jnp.bitwise_xor(helper, k)]


def side_rows(block):
    row_n = block.shape[1] * 2 // 3
    main, tail = block[:, :row_n, :], block[:, row_n:, :]
    tail = jnp.concatenate([tail[:, :, :HEAD], tail[:, :, HEAD:]], 1)
    return jnp.concatenate([main.reshape(-1, LANES), tail.reshape(-1, HEAD)], 1)


def out_kernel(swaps, owner_n, helper_n, partners, own_rows, *rest):
    sides, rest = rest[:helper_n], rest[helper_n:]
    weights, rest = rest[:helper_n], rest[helper_n:]
    out, term_ref, partners_s, sem = rest
    copy = pltpu.make_async_copy(partners, partners_s, sem)
    copy.start()
    image_n, row_n, width = own_rows.shape
    columns = HEAD + LANES
    terms = None
    for side, weight in zip(sides, weights):
        part = nn(side_rows(side[...]), weight[weight.shape[0] - columns :, :])
        terms = part if terms is None else terms + part
    term_ref[...] = terms.reshape(len(swaps), row_n, width)
    copy.wait()
    me = lax.axis_index("owner")
    lows = [swap_target(me, swap, owner_n) * image_n for swap in swaps]
    for image in range(image_n):
        for slot in range(partners.shape[1]):
            partner = partners_s[image, slot]
            which = jnp.int32(0)
            for at, low in enumerate(lows):
                gap = partner - low
                which = jnp.where(jnp.logical_and(gap >= 0, gap < image_n), jnp.int32(at), which)
            value = (own_rows[image] + term_ref[which]).astype(BF16)
            out[image, slot] = jnp.where(partner >= 0, value, jnp.zeros_like(value))


def local(owner_n, helper_n, states, partners, self_proj, self_out, cross_proj, cross_out, gains):
    image_n, patch_n, width = states.shape
    slot_n = partners.shape[1]
    columns = self_proj.shape[2]
    row_n = patch_n // helper_n
    row_all = image_n * patch_n
    swaps = owner_swaps(slot_n, owner_n)
    pair_n = len(swaps)
    self_proj_t = jnp.swapaxes(self_proj, 1, 2)
    cross_proj_t = jnp.swapaxes(cross_proj, 1, 2)
    chip_hop, core_hop = helper_n // 2, 1

    def across(value, k):
        return lax.ppermute(value, "helper", [(j, j ^ k) for j in range(helper_n)])

    def exchange(value, swap):
        return lax.ppermute(value, "owner", [(o, swap_target(o, swap, owner_n)) for o in range(owner_n)])

    def call(name, kernel, out_shape, in_specs, scratch, *operands, flops=1):
        with jax.named_scope(name):
            return pl.pallas_call(
                kernel,
                out_shape=out_shape,
                in_specs=in_specs,
                out_specs=jax.tree.map(lambda _: VMEM, out_shape),
                scratch_shapes=scratch,
                compiler_params=pltpu.CompilerParams(vmem_limit_bytes=VMEM_BYTES),
                cost_estimate=pl.CostEstimate(flops=flops, bytes_accessed=1, transcendentals=0),
            )(*operands)

    shape = jax.ShapeDtypeStruct
    dma = pltpu.SemaphoreType.DMA
    index_table = pltpu.SMEM(partners.shape, jnp.int32)
    block = shape((2 * columns, patch_n), BF16)

    partners_h = pltpu.with_memory_space_constraint(partners, pltpu.HBM)
    self_out_got = across(self_out, chip_hop)
    *outgoing, context, table, cross_out_own = call(
        "own_images",
        functools.partial(own_images_kernel, swaps, owner_n),
        [block] * pair_n
        + [
            shape((row_all * columns // LANES, LANES), BF16),
            shape((pair_n, LANES), jnp.int32),
            shape(cross_out.shape, BF16),
        ],
        [HBM] * 6,
        [
            pltpu.VMEM(states.shape, BF16),
            pltpu.VMEM(gains.shape, F32),
            pltpu.VMEM((3, columns, width), BF16),
            pltpu.VMEM((2, columns, width), BF16),
            index_table,
            pltpu.VMEM((image_n, 2 * columns, patch_n), BF16),
            dma((6,)),
        ],
        *[pltpu.with_memory_space_constraint(x, pltpu.HBM) for x in (states, gains, self_proj_t, cross_proj_t)],
        partners_h,
        pltpu.with_memory_space_constraint(cross_out, pltpu.HBM),
    )
    context_got = across(context, chip_hop)
    arrived = [exchange(value, swap) for value, swap in zip(outgoing, swaps)]
    near = (slot_n - 1) // 2
    late = list(range(2, 2 * near))
    early = [at for at in range(pair_n) if at not in late]
    cross_out_sent = call(
        "cross_output_rows",
        hand_on_kernel,
        shape(cross_out.shape, BF16),
        [ANY, ANY],
        [dma],
        cross_out_own, context_got,
    )
    cross_out_got = across(cross_out_sent, chip_hop)

    sent_shape = shape((row_all + columns, width), BF16)
    own_shape = shape((image_n, row_n, width), F32)
    query_shape = shape((image_n, patch_n, columns), F32)

    def mixing(states, gains, cross_proj_t, context, context_got, self_out, self_out_got, cross_out):
        base, sent = call(
            "self_output_share",
            partial_kernel,
            [shape((row_all, width), F32), sent_shape],
            [VMEM] * 4 + [ANY, ANY],
            [pltpu.VMEM(self_out.shape, BF16), dma((2,))],
            states, context, context_got, self_out, self_out_got, cross_out,
        )
        got = across(sent, core_hop)
        own_rows, queries = call(
            "mixed_and_queries",
            functools.partial(query_kernel, helper_n),
            [own_shape, query_shape],
            [VMEM] * 4,
            [pltpu.VMEM((image_n, patch_n, width), F32)],
            base, got, gains, cross_proj_t,
        )
        return own_rows, queries, got

    def no_pairs(*operands):
        return tuple(jnp.zeros(made.shape, made.dtype) for made in (own_shape, query_shape, sent_shape))

    own_rows, queries, got = lax.cond(
        lax.axis_index("owner") < owner_n, mixing, no_pairs,
        states, gains, cross_proj_t, context, context_got, self_out, self_out_got, cross_out_own,
    )
    packed = columns * row_n // LANES
    early_sides = call(
        "early_cross_attention",
        functools.partial(cross_kernel, early, helper_n),
        shape((helper_n, len(early), packed, LANES), BF16),
        [VMEM] * (2 + len(early)),
        [],
        queries, table, *[arrived[at] for at in early],
        flops=EARLY_WEIGHT,
    )
    sides = call(
        "late_cross_attention",
        functools.partial(last_cross_kernel, late, helper_n),
        [shape((pair_n, packed, LANES), BF16)] * helper_n,
        [VMEM] * (3 + len(late)),
        [pltpu.VMEM((helper_n, len(late), packed, LANES), BF16)],
        queries, table, early_sides, *[arrived[at] for at in late],
        flops=LATE_WEIGHT,
    )
    sides = [sides[0]] + [across(sides[k], k) for k in range(1, helper_n)]
    weights = {0: cross_out_own, core_hop: got, chip_hop: cross_out_got}
    weights[chip_hop ^ core_hop] = across(cross_out_got, core_hop)
    return call(
        "pair_output",
        functools.partial(out_kernel, [swaps[at] for at in early + late], owner_n, helper_n),
        shape((image_n, slot_n, row_n, width), BF16),
        [HBM] + [VMEM] * (1 + 2 * helper_n),
        [pltpu.VMEM((pair_n, row_n, width), F32), index_table, dma],
        partners_h, own_rows, *sides, *[weights[k] for k in range(helper_n)],
    )


def solution(mesh):
    return jax.shard_map(
        functools.partial(local, mesh.shape["owner"], mesh.shape["helper"]),
        mesh=mesh,
        in_specs=(
            P("owner", None, None),
            P("owner", None),
            P(None, None, "helper"),
            P("helper", None),
            P(None, None, "helper"),
            P("helper", None),
            P(),
        ),
        out_specs=P("owner", None, "helper", None),
        check_vma=False,
    )
```

time: 102 us -> 35.7 us (0.35)
  waiting for transfers between devices: 54.4 us -> 7.86 us
  between operations: 13.6 us -> 0.11 us
  Pallas kernels: 0 us -> 11.4 us
  matrix products: 10.8 us -> 0 us
  starting transfers between devices: 7.29 us -> 16 us
  local copies, waits for them, and re-layouts: 7.93 us -> 0.02 us
  other arithmetic: 7.86 us -> 0 us
    reduce_scatter x1 -> x0, waiting for transfers between devices: 29.2 us -> none  [local(): lax.psum_scatter(jnp.einsum('spf,fd->psd', side_context, cross_out, prefe...]
    psum x1 -> x0, waiting for transfers between devices: 25.2 us -> none  [local(): lax.psum(own_heads.astype(jnp.bfloat16), 'helper').astype(jnp.float32)]
    ppermute x0 -> x13, starting transfers between devices: none -> 16 us  [the longest x5 9.05 us: exchange(): lax.ppermute(value, 'owner', [(o, swap_target(o, swap, owner_n)) for o in...]
    pallas_call x0 -> x7, Pallas kernels: none -> 11.4 us  [call(): pl.pallas_call(kernel, out_shape=out_shape, in_specs=in_specs, out_specs=...]
    dot_general x9 -> x0, matrix products: 8.33 us -> none  [the longest x2 2.22 us: attend(): jnp.einsum('nhqk,nkhe->nqhe', weights, v_heads, preferred_element_type=jn...]
    ppermute x0 -> x13, waiting for transfers between devices: none -> 7.86 us  [the longest x8 5.23 us: across(): return lax.ppermute(value, 'helper', [(j, j ^ k) for j in range(helper_n)])]
    all_to_all x1 -> x0, starting transfers between devices: 7.25 us -> none  [local(): lax.all_to_all(outgoing, 'owner', split_axis=0, concat_axis=0, tiled=True)]
    reduce_sum x4 -> x0, other arithmetic: 5.72 us -> none  [the longest x2 3.27 us: norm_rows(): row_var = jnp.mean(centred * centred, -1, keepdims=True)]
  transfers between devices with their start and end apart: 3 -> 13, of which waited for: 2 -> 5; matrix products, arithmetic and copies ran while one was open for 9% -> 0% of each run, Pallas kernels for 0% -> 24%
where the time goes in v2:
time: 35.7 us; the launch traced here: 35.5 us
  starting transfers between devices  16 us (45%)
  Pallas kernels  11.4 us (32%)
  waiting for transfers between devices  7.86 us (22%)
    pallas_call x7, Pallas kernels, call(): pl.pallas_call(kernel, out_shape=out_shape, in_specs=in_specs, out_specs=...  11.4 us
    ppermute x5, starting transfers between devices, exchange(): lax.ppermute(value, 'owner', [(o, swap_target(o, swap, owner_n)) for o in...  9.05 us
    ppermute x8, starting transfers between devices, across(): return lax.ppermute(value, 'helper', [(j, j ^ k) for j in range(helper_n)])  6.95 us
    ppermute x8, waiting for transfers between devices, across(): return lax.ppermute(value, 'helper', [(j, j ^ k) for j in range(helper_n)])  5.23 us
    ppermute x5, waiting for transfers between devices, exchange(): lax.ppermute(value, 'owner', [(o, swap_target(o, swap, owner_n)) for o in...  2.63 us
  transfers between devices with their start and end apart: 13, of which 5 were waited for; matrix products, arithmetic and copies ran while one was open for 0% of the time, Pallas kernels for 24%

profile of v2, /device:TPU:0, one launch (start us, length us, event | category | flops | bytes accessed | tf_op | source)
XLA Modules:
  0.0 35.5 jit_solution(9233503015704484858)
XLA Ops:
  0.0 3.0 %collective-permute-start.2 = (bf16[192,768]{1,0:T(8,128)(2,1)}, bf16[192,768]{1,0:T(8,128)(2,1)}, u32[]{:S(2)}, u32[]{:S(2)}) collective-permute-start(bf16[192,768]{1,0:T(8,128)(2,1)} %param.12), channel_id=1, source_target_pairs={{0,2},{1,3},{2,0},{3,1},{4,6},{5,7},{6,4},{7,5},{8,10},{9,11},{10,... | collective-permute-start | bytes 884744 | tf_op jit(solution)/shard_map/ppermute | solution.py:267
  3.0 3.5 %own_images.1 = (bf16[384,128]{1,0:T(8,128)(2,1)S(1)}, bf16[384,128]{1,0:T(8,128)(2,1)S(1)}, bf16[384,128]{1,0:T(8,128)(2,1)S(1)}, bf16[384,128]{1,0:T(8,128)(2,...) custom-call(bf16[2,128,768]{2,1,0:T(8,128)(2,1)} %states.1, ...), custom_call_target="tpu_custom_call" | custom-call | flops 1 | bytes 1 | tf_op jit(solution)/shard_map/own_images/pallas_call | solution.py:274
  6.5 0.0 copy-start.1
  6.5 0.1 collective-permute-start.1
  6.6 3.1 %collective-permute-start.3 = (bf16[384,128]{1,0:T(8,128)(2,1)S(1)}, bf16[384,128]{1,0:T(8,128)(2,1)S(1)}, u32[]{:S(2)}, u32[]{:S(2)}) collective-permute-start(bf16[384,128]{1,0:T(8,128)(2,1)S(1)} %get-tuple-element.53), channel_id=1, source_target_pairs={{0,16},{4,20},{8,24},{12,28},{16,0},{20,4},{24,8},{28,12},{1,17},{... | collective-permute-start | bytes 294920 | tf_op jit(solution)/shard_map/ppermute | solution.py:270
  9.6 1.3 %collective-permute-start.4 = (bf16[384,128]{1,0:T(8,128)(2,1)S(1)}, bf16[384,128]{1,0:T(8,128)(2,1)S(1)}, u32[]{:S(2)}, u32[]{:S(2)}) collective-permute-start(bf16[384,128]{1,0:T(8,128)(2,1)S(1)} %get-tuple-element.54), channel_id=1, source_target_pairs={{0,24},{4,28},{8,16},{12,20},{16,8},{20,12},{24,0},{28,4},{1,25},{... | collective-permute-start | bytes 294920 | tf_op jit(solution)/shard_map/ppermute | solution.py:270
  11.0 3.4 %collective-permute-start.5 = (bf16[384,128]{1,0:T(8,128)(2,1)S(1)}, bf16[384,128]{1,0:T(8,128)(2,1)S(1)}, u32[]{:S(2)}, u32[]{:S(2)}) collective-permute-start(bf16[384,128]{1,0:T(8,128)(2,1)S(1)} %get-tuple-element.55), channel_id=1, source_target_pairs={{0,28},{4,8},{8,4},{12,16},{16,12},{20,24},{24,20},{28,0},{1,29},{... | collective-permute-start | bytes 294920 | tf_op jit(solution)/shard_map/ppermute | solution.py:270
  14.4 0.1 cross_output_rows.1
  14.5 0.0 copy-start.3
  14.5 1.6 %collective-permute-start.11 = (bf16[192,768]{1,0:T(8,128)(2,1)S(1)}, bf16[192,768]{1,0:T(8,128)(2,1)S(1)}, u32[]{:S(2)}, u32[]{:S(2)}) collective-permute-start(bf16[192,768]{1,0:T(8,128)(2,1)S(1)} %cross_output_rows.1), channel_id=1, source_target_pairs={{0,2},{1,3},{2,0},{3,1},{4,6},{5,7},{6,4},{7,5},{8,10},{9,11},{10,... | collective-permute-start | bytes 884744 | tf_op jit(solution)/shard_map/ppermute | solution.py:267
  16.1 0.0 collective-permute-done.2
  16.1 5.3 %conditional.1 = (f32[2,32,768]{2,1,0:T(8,128)S(1)}, f32[2,128,192]{2,1,0:T(8,128)S(1)}, bf16[448,768]{1,0:T(8,128)(2,1)}) conditional(s32[]{:T(128)} %convert_element_type.3, () %tuple.13, (bf16[2,128,768]{2,1,0:T(8,128)(2,1)S(1)}, bf16[384,128]{1,0:T(8,128)(2,1)S(1)}, bf16[384,128]{1,0:T(8,128)(2,1)S(1)}, bf16[192,768]{1,0:T(8,128)(2,1)S(1)}, ...), branch_computations={%region_0.0_spmd, %region_1.0_spmd} | conditional | flops 2 | bytes 2752578 | solution.py:356
  16.1 1.3 %self_output_share.1 = (f32[256,768]{1,0:T(8,128)S(1)}, bf16[448,768]{1,0:T(8,128)(2,1)S(1)}) custom-call(bf16[2,128,768]{2,1,0:T(8,128)(2,1)S(1)} %get-tuple-element.21.states, bf16[384,128]{1,0:T(8,128)(2,1)S(1)} %get-tuple-element.22.own, bf16[384,128]{1,0:T(8,128)(2,1)S(1)} %get-tuple-element.23.got, bf16[192,768]{1,0:T(8,128)(2,1)S(1)} %get-tuple-element.24.own_weight, ...), custom_call_target="tpu_custom_call" | custom-call | flops 1 | bytes 1 | tf_op jit(solution)/shard_map/cond/branch_1_fun/self_output_share/pallas_call | solution.py:274
  17.5 0.1 collective-permute-start
  17.6 2.3 %collective-permute-done.got = bf16[448,768]{1,0:T(8,128)(2,1)} collective-permute-done((bf16[448,768]{1,0:T(8,128)(2,1)S(1)}, bf16[448,768]{1,0:T(8,128)(2,1)}, u32[]{:S(2)}, u32[]{:S(2)}) %collective-permute-start) | collective-permute-done | bytes 688160 | tf_op jit(solution)/shard_map/cond/branch_1_fun/ppermute | solution.py:267
  19.8 1.6 %mixed_and_queries.1 = (f32[2,32,768]{2,1,0:T(8,128)S(1)}, f32[2,128,192]{2,1,0:T(8,128)S(1)}) custom-call(f32[256,768]{1,0:T(8,128)S(1)} %get-tuple-element.27.base, bf16[448,768]{1,0:T(8,128)(2,1)} %collective-permute-done.got, f32[3,768]{1,0:T(4,128)S(1)} %get-tuple-element.29.gains, bf16[3,192,768]{2,1,0:T(8,128)(2,1)S(1)} %get-tuple-element.30.proj_t), custom_call_target="tpu_custom_call" | custom-call | flops 1 | bytes 1 | tf_op jit(solution)/shard_map/cond/branch_1_fun/mixed_and_queries/pallas_call | solution.py:274
  21.4 0.1 collective-permute-start.6
  21.5 0.0 collective-permute-done.3.rest_0_
  21.5 1.2 %collective-permute-start.7 = (bf16[384,128]{1,0:T(8,128)(2,1)S(1)}, bf16[384,128]{1,0:T(8,128)(2,1)S(1)}, u32[]{:S(2)}, u32[]{:S(2)}) collective-permute-start(bf16[384,128]{1,0:T(8,128)(2,1)S(1)} %get-tuple-element.57), channel_id=1, source_target_pairs={{0,4},{4,0},{8,12},{12,8},{16,20},{20,16},{24,28},{28,24},{1,5},{5... | collective-permute-start | bytes 294920 | tf_op jit(solution)/shard_map/ppermute | solution.py:270
  22.7 0.0 collective-permute-done.4.rest_1_
  22.7 0.0 collective-permute-done.5.rest_2_
  22.7 1.0 %early_cross_attention.1.before = bf16[4,3,48,128]{3,2,1,0:T(8,128)(2,1)S(1)} custom-call(f32[2,128,192]{2,1,0:T(8,128)S(1)} %get-tuple-element.51.queries, s32[5,128]{1,0:T(8,128)S(1)} %get-tuple-element.52.table, bf16[384,128]{1,0:T(8,128)(2,1)S(1)} %collective-permute-done.3.rest_0_, bf16[384,128]{1,0:T(8,128)(2,1)S(1)} %collective-permute-done.4.rest_1_, ...), custom_call_target="tpu_custom_call" | custom-call | flops 3000000000 | bytes 1 | tf_op jit(solution)/shard_map/early_cross_attention/pallas_call | solution.py:274
  23.7 0.1 collective-permute-start.12
  23.8 2.5 %collective-permute-done.6.rest_0_ = bf16[384,128]{1,0:T(8,128)(2,1)S(1)} collective-permute-done((bf16[384,128]{1,0:T(8,128)(2,1)S(1)}, bf16[384,128]{1,0:T(8,128)(2,1)S(1)}, u32[]{:S(2)}, u32[]{:S(2)}) %collective-permute-start.6) | collective-permute-done | bytes 98336 | tf_op jit(solution)/shard_map/ppermute | solution.py:270
  26.3 0.1 collective-permute-done.7.rest_1_
  26.4 0.9 %late_cross_attention.1 = (bf16[5,48,128]{2,1,0:T(8,128)(2,1)S(1)}, bf16[5,48,128]{2,1,0:T(8,128)(2,1)S(1)}, bf16[5,48,128]{2,1,0:T(8,128)(2,1)S(1)}, bf16[5,48,128]{2,1,0:T(8,128)(2,1)S(1)}) custom-call(f32[2,128,192]{2,1,0:T(8,128)S(1)} %get-tuple-element.51.queries, s32[5,128]{1,0:T(8,128)S(1)} %get-tuple-element.52.table, ...), custom_call_target="tpu_custom_call" | custom-call | flops 99999997952 | bytes 1 | tf_op jit(solution)/shard_map/late_cross_attention/pallas_call | solution.py:274
  27.3 0.1 collective-permute-start.10
  27.3 0.9 %collective-permute-start.8 = (bf16[5,48,128]{2,1,0:T(8,128)(2,1)S(1)}, bf16[5,48,128]{2,1,0:T(8,128)(2,1)S(1)}, u32[]{:S(2)}, u32[]{:S(2)}) collective-permute-start(bf16[5,48,128]{2,1,0:T(8,128)(2,1)S(1)} %get-tuple-element.59), channel_id=1, source_target_pairs={{0,1},{1,0},{2,3},{3,2},{4,5},{5,4},{6,7},{7,6},{8,9},{9,8},{10,11... | collective-permute-start | bytes 184328 | tf_op jit(solution)/shard_map/ppermute | solution.py:267
  28.2 1.3 %collective-permute-start.9 = (bf16[5,48,128]{2,1,0:T(8,128)(2,1)S(1)}, bf16[5,48,128]{2,1,0:T(8,128)(2,1)S(1)}, u32[]{:S(2)}, u32[]{:S(2)}) collective-permute-start(bf16[5,48,128]{2,1,0:T(8,128)(2,1)S(1)} %get-tuple-element.60), channel_id=1, source_target_pairs={{0,2},{1,3},{2,0},{3,1},{4,6},{5,7},{6,4},{7,5},{8,10},{9,11},{10,... | collective-permute-start | bytes 184328 | tf_op jit(solution)/shard_map/ppermute | solution.py:267
  29.5 1.6 %collective-permute-done.10.rest_3_ = bf16[5,48,128]{2,1,0:T(8,128)(2,1)S(1)} collective-permute-done((bf16[5,48,128]{2,1,0:T(8,128)(2,1)S(1)}, bf16[5,48,128]{2,1,0:T(8,128)(2,1)S(1)}, u32[]{:S(2)}, u32[]{:S(2)}) %collective-permute-start.10) | collective-permute-done | bytes 61472 | tf_op jit(solution)/shard_map/ppermute | solution.py:267
  31.1 1.3 %collective-permute-done.9.rest_2_ = bf16[5,48,128]{2,1,0:T(8,128)(2,1)S(1)} collective-permute-done((bf16[5,48,128]{2,1,0:T(8,128)(2,1)S(1)}, bf16[5,48,128]{2,1,0:T(8,128)(2,1)S(1)}, u32[]{:S(2)}, u32[]{:S(2)}) %collective-permute-start.9) | collective-permute-done | bytes 61472 | tf_op jit(solution)/shard_map/ppermute | solution.py:267
  32.4 3.0 %pair_output.1 = bf16[2,5,32,768]{3,2,1,0:T(8,128)(2,1)} custom-call(s32[2,5]{1,0:T(2,128)} %partners.3, f32[2,32,768]{2,1,0:T(8,128)S(1)} %get-tuple-element.50.own_rows, bf16[5,48,128]{2,1,0:T(8,128)(2,1)S(1)} %get-tuple-element.58.rest_0_, bf16[5,48,128]{2,1,0:T(8,128)(2,1)S(1)} %collective-permute-done.8.rest_1_, ...), custom_call_target="tpu_custom_call" | custom-call | flops 1 | bytes 1 | tf_op jit(solution)/shard_map/pair_output/pallas_call | solution.py:274
  (10 shorter events, 0.0 us)
Async XLA Ops:
  0.0 16.1 %collective-permute-start.2 = (bf16[192,768]{1,0:T(8,128)(2,1)}, bf16[192,768]{1,0:T(8,128)(2,1)}, u32[]{:S(2)}, u32[]{:S(2)}) collective-permute-start(bf16[192,768]{1,0:T(8,128)(2,1)} %param.12), channel_id=1, source_target_pairs={{0,2},{1,3},{2,0},{3,1},{4,6},{5,7},{6,4},{7,5},{8,10},{9,11},{10,... | collective-permute-start | bytes 884744 | tf_op jit(solution)/shard_map/ppermute | solution.py:267
  3.0 13.1 %copy-start = (bf16[3,768,192]{1,2,0:T(8,128)(2,1)S(1)}, bf16[3,768,192]{1,2,0:T(8,128)(2,1)}, u32[]{:S(2)}) copy-start(bf16[3,768,192]{1,2,0:T(8,128)(2,1)} %param.13) | copy-start | bytes 2654212
  6.5 9.6 %copy-start.1 = (bf16[2,128,768]{2,1,0:T(8,128)(2,1)S(1)}, bf16[2,128,768]{2,1,0:T(8,128)(2,1)}, u32[]{:S(2)}) copy-start(bf16[2,128,768]{2,1,0:T(8,128)(2,1)} %states.1) | copy-start | bytes 1179652
  6.5 7.9 %collective-permute-start.1 = (bf16[384,128]{1,0:T(8,128)(2,1)S(1)}, bf16[384,128]{1,0:T(8,128)(2,1)S(1)}, u32[]{:S(2)}, u32[]{:S(2)}) collective-permute-start(bf16[384,128]{1,0:T(8,128)(2,1)S(1)} %get-tuple-element.48), channel_id=1, source_target_pairs={{0,2},{1,3},{2,0},{3,1},{4,6},{5,7},{6,4},{7,5},{8,10},{9,11},{10,... | collective-permute-start | bytes 294920 | tf_op jit(solution)/shard_map/ppermute | solution.py:267
  6.6 14.9 %collective-permute-start.3 = (bf16[384,128]{1,0:T(8,128)(2,1)S(1)}, bf16[384,128]{1,0:T(8,128)(2,1)S(1)}, u32[]{:S(2)}, u32[]{:S(2)}) collective-permute-start(bf16[384,128]{1,0:T(8,128)(2,1)S(1)} %get-tuple-element.53), channel_id=1, source_target_pairs={{0,16},{4,20},{8,24},{12,28},{16,0},{20,4},{24,8},{28,12},{1,17},{... | collective-permute-start | bytes 294920 | tf_op jit(solution)/shard_map/ppermute | solution.py:270
  9.6 13.0 %collective-permute-start.4 = (bf16[384,128]{1,0:T(8,128)(2,1)S(1)}, bf16[384,128]{1,0:T(8,128)(2,1)S(1)}, u32[]{:S(2)}, u32[]{:S(2)}) collective-permute-start(bf16[384,128]{1,0:T(8,128)(2,1)S(1)} %get-tuple-element.54), channel_id=1, source_target_pairs={{0,24},{4,28},{8,16},{12,20},{16,8},{20,12},{24,0},{28,4},{1,25},{... | collective-permute-start | bytes 294920 | tf_op jit(solution)/shard_map/ppermute | solution.py:270
  11.0 11.7 %collective-permute-start.5 = (bf16[384,128]{1,0:T(8,128)(2,1)S(1)}, bf16[384,128]{1,0:T(8,128)(2,1)S(1)}, u32[]{:S(2)}, u32[]{:S(2)}) collective-permute-start(bf16[384,128]{1,0:T(8,128)(2,1)S(1)} %get-tuple-element.55), channel_id=1, source_target_pairs={{0,28},{4,8},{8,4},{12,16},{16,12},{20,24},{24,20},{28,0},{1,29},{... | collective-permute-start | bytes 294920 | tf_op jit(solution)/shard_map/ppermute | solution.py:270
  14.4 1.7 %copy-start.2 = (bf16[192,768]{1,0:T(8,128)(2,1)S(1)}, bf16[192,768]{1,0:T(8,128)(2,1)}, u32[]{:S(2)}) copy-start(bf16[192,768]{1,0:T(8,128)(2,1)} %param.12) | copy-start | bytes 884740
  14.5 1.6 %copy-start.3 = (f32[3,768]{1,0:T(4,128)S(1)}, f32[3,768]{1,0:T(4,128)}, u32[]{:S(2)}) copy-start(f32[3,768]{1,0:T(4,128)} %gains.1) | copy-start | bytes 27652
  14.5 9.2 %collective-permute-start.11 = (bf16[192,768]{1,0:T(8,128)(2,1)S(1)}, bf16[192,768]{1,0:T(8,128)(2,1)S(1)}, u32[]{:S(2)}, u32[]{:S(2)}) collective-permute-start(bf16[192,768]{1,0:T(8,128)(2,1)S(1)} %cross_output_rows.1), channel_id=1, source_target_pairs={{0,2},{1,3},{2,0},{3,1},{4,6},{5,7},{6,4},{7,5},{8,10},{9,11},{10,... | collective-permute-start | bytes 884744 | tf_op jit(solution)/shard_map/ppermute | solution.py:267
  17.5 2.3 %collective-permute-start = (bf16[448,768]{1,0:T(8,128)(2,1)S(1)}, bf16[448,768]{1,0:T(8,128)(2,1)}, u32[]{:S(2)}, u32[]{:S(2)}) collective-permute-start(bf16[448,768]{1,0:T(8,128)(2,1)S(1)} %get-tuple-element.28), channel_id=1, source_target_pairs={{0,1},{1,0},{2,3},{3,2},{4,5},{5,4},{6,7},{7,6},{8,9},{9,8},{10,11... | collective-permute-start | bytes 2064392 | tf_op jit(solution)/shard_map/cond/branch_1_fun/ppermute | solution.py:267
  21.4 4.9 %collective-permute-start.6 = (bf16[384,128]{1,0:T(8,128)(2,1)S(1)}, bf16[384,128]{1,0:T(8,128)(2,1)S(1)}, u32[]{:S(2)}, u32[]{:S(2)}) collective-permute-start(bf16[384,128]{1,0:T(8,128)(2,1)S(1)} %get-tuple-element.56), channel_id=1, source_target_pairs={{0,8},{4,12},{8,0},{12,4},{16,24},{20,28},{24,16},{28,20},{1,9},{5... | collective-permute-start | bytes 294920 | tf_op jit(solution)/shard_map/ppermute | solution.py:270
  21.5 4.9 %collective-permute-start.7 = (bf16[384,128]{1,0:T(8,128)(2,1)S(1)}, bf16[384,128]{1,0:T(8,128)(2,1)S(1)}, u32[]{:S(2)}, u32[]{:S(2)}) collective-permute-start(bf16[384,128]{1,0:T(8,128)(2,1)S(1)} %get-tuple-element.57), channel_id=1, source_target_pairs={{0,4},{4,0},{8,12},{12,8},{16,20},{20,16},{24,28},{28,24},{1,5},{5... | collective-permute-start | bytes 294920 | tf_op jit(solution)/shard_map/ppermute | solution.py:270
  23.7 8.7 %collective-permute-start.12 = (bf16[192,768]{1,0:T(8,128)(2,1)S(1)}, bf16[192,768]{1,0:T(8,128)(2,1)S(1)}, u32[]{:S(2)}, u32[]{:S(2)}) collective-permute-start(bf16[192,768]{1,0:T(8,128)(2,1)S(1)} %collective-permute-done.11.rest_6_), channel_id=1, source_target_pairs={{0,1},{1,0},{2,3},{3,2},{4,5},{5,4},{6,7},{7,6},{8,9},{9,8},{10,11... | collective-permute-start | bytes 884744 | tf_op jit(solution)/shard_map/ppermute | solution.py:267
  27.3 3.8 %collective-permute-start.10 = (bf16[5,48,128]{2,1,0:T(8,128)(2,1)S(1)}, bf16[5,48,128]{2,1,0:T(8,128)(2,1)S(1)}, u32[]{:S(2)}, u32[]{:S(2)}) collective-permute-start(bf16[5,48,128]{2,1,0:T(8,128)(2,1)S(1)} %get-tuple-element.61), channel_id=1, source_target_pairs={{0,3},{1,2},{2,1},{3,0},{4,7},{5,6},{6,5},{7,4},{8,11},{9,10},{10,... | collective-permute-start | bytes 184328 | tf_op jit(solution)/shard_map/ppermute | solution.py:267
  27.3 3.8 %collective-permute-start.8 = (bf16[5,48,128]{2,1,0:T(8,128)(2,1)S(1)}, bf16[5,48,128]{2,1,0:T(8,128)(2,1)S(1)}, u32[]{:S(2)}, u32[]{:S(2)}) collective-permute-start(bf16[5,48,128]{2,1,0:T(8,128)(2,1)S(1)} %get-tuple-element.59), channel_id=1, source_target_pairs={{0,1},{1,0},{2,3},{3,2},{4,5},{5,4},{6,7},{7,6},{8,9},{9,8},{10,11... | collective-permute-start | bytes 184328 | tf_op jit(solution)/shard_map/ppermute | solution.py:267
  28.2 4.2 %collective-permute-start.9 = (bf16[5,48,128]{2,1,0:T(8,128)(2,1)S(1)}, bf16[5,48,128]{2,1,0:T(8,128)(2,1)S(1)}, u32[]{:S(2)}, u32[]{:S(2)}) collective-permute-start(bf16[5,48,128]{2,1,0:T(8,128)(2,1)S(1)} %get-tuple-element.60), channel_id=1, source_target_pairs={{0,2},{1,3},{2,0},{3,1},{4,6},{5,7},{6,4},{7,5},{8,10},{9,11},{10,... | collective-permute-start | bytes 184328 | tf_op jit(solution)/shard_map/ppermute | solution.py:267

commit v3 on v2

--- a/solution.py
+++ b/solution.py
@@ -162,7 +162,10 @@
     copies[1].wait()
 
 
-def query_kernel(helper_n, base, got, gains, proj_t, own_rows, queries_out, mixed_ref):
+def query_kernel(helper_n, base, got, gains, proj_t, *rest):
+    own_rows, queries_out, weight_out, mixed_ref, sem = rest[-5:]
+    copy = pltpu.make_async_copy(got.at[pl.ds(base.shape[0], weight_out.shape[0])], weight_out, sem)
+    copy.start()
     mixed = base[...] + got[: base.shape[0], :].astype(F32)
     image_n, row_n, width = own_rows.shape
     patch_n = row_n * helper_n
@@ -172,6 +175,7 @@
     queries_out[...] = queries.reshape(queries_out.shape)
     start = pl.multiple_of(lax.axis_index("helper") * row_n, row_n)
     own_rows[...] = mixed_ref[:, pl.ds(start, row_n), :]
+    copy.wait()
 
 
 def hand_on_kernel(weight, waited, out, sem):
@@ -231,10 +235,9 @@
     copy = pltpu.make_async_copy(partners, partners_s, sem)
     copy.start()
     image_n, row_n, width = own_rows.shape
-    columns = HEAD + LANES
     terms = None
     for side, weight in zip(sides, weights):
-        part = nn(side_rows(side[...]), weight[weight.shape[0] - columns :, :])
+        part = nn(side_rows(side[...]), weight[...])
         terms = part if terms is None else terms + part
     term_ref[...] = terms.reshape(len(swaps), row_n, width)
     copy.wait()
@@ -313,8 +316,7 @@
     )
     context_got = across(context, chip_hop)
     arrived = [exchange(value, swap) for value, swap in zip(outgoing, swaps)]
-    near = (slot_n - 1) // 2
-    late = list(range(2, 2 * near))
+    late = [at for at, (_, colour) in enumerate(swaps) if colour]
     early = [at for at in range(pair_n) if at not in late]
     cross_out_sent = call(
         "cross_output_rows",
@@ -326,36 +328,37 @@
     )
     cross_out_got = across(cross_out_sent, chip_hop)
 
-    sent_shape = shape((row_all + columns, width), BF16)
-    own_shape = shape((image_n, row_n, width), F32)
-    query_shape = shape((image_n, patch_n, columns), F32)
-
-    def mixing(states, gains, cross_proj_t, context, context_got, self_out, self_out_got, cross_out):
-        base, sent = call(
-            "self_output_share",
-            partial_kernel,
-            [shape((row_all, width), F32), sent_shape],
-            [VMEM] * 4 + [ANY, ANY],
-            [pltpu.VMEM(self_out.shape, BF16), dma((2,))],
-            states, context, context_got, self_out, self_out_got, cross_out,
-        )
-        got = across(sent, core_hop)
-        own_rows, queries = call(
+    base, sent = call(
+        "self_output_share",
+        partial_kernel,
+        [shape((row_all, width), F32), shape((row_all + columns, width), BF16)],
+        [VMEM] * 4 + [ANY, ANY],
+        [pltpu.VMEM(self_out.shape, BF16), dma((2,))],
+        states, context, context_got, self_out, self_out_got, cross_out_own,
+    )
+    made_shapes = [
+        shape((image_n, row_n, width), F32),
+        shape((image_n, patch_n, columns), F32),
+        shape(cross_out.shape, BF16),
+    ]
+
+    def mixing(base, sent, gains, cross_proj_t, *waited):
+        made = call(
             "mixed_and_queries",
             functools.partial(query_kernel, helper_n),
-            [own_shape, query_shape],
-            [VMEM] * 4,
-            [pltpu.VMEM((image_n, patch_n, width), F32)],
-            base, got, gains, cross_proj_t,
+            made_shapes,
+            [VMEM] * 4 + [ANY] * len(waited),
+            [pltpu.VMEM((image_n, patch_n, width), F32), dma],
+            base, across(sent, core_hop), gains, cross_proj_t, *waited,
         )
-        return own_rows, queries, got
-
-    def no_pairs(*operands):
-        return tuple(jnp.zeros(made.shape, made.dtype) for made in (own_shape, query_shape, sent_shape))
-
-    own_rows, queries, got = lax.cond(
-        lax.axis_index("owner") < owner_n, mixing, no_pairs,
-        states, gains, cross_proj_t, context, context_got, self_out, self_out_got, cross_out_own,
+        return tuple(made)
+
+    def no_images(*operands):
+        return tuple(jnp.zeros(made.shape, made.dtype) for made in made_shapes)
+
+    own_rows, queries, cross_out_core = lax.cond(
+        lax.axis_index("owner") < owner_n, mixing, no_images,
+        base, sent, gains, cross_proj_t, *[arrived[at] for at in early],
     )
     packed = columns * row_n // LANES
     early_sides = call(
@@ -377,7 +380,7 @@
         flops=LATE_WEIGHT,
     )
     sides = [sides[0]] + [across(sides[k], k) for k in range(1, helper_n)]
-    weights = {0: cross_out_own, core_hop: got, chip_hop: cross_out_got}
+    weights = {0: cross_out_own, core_hop: cross_out_core, chip_hop: cross_out_got}
     weights[chip_hop ^ core_hop] = across(cross_out_got, core_hop)
     return call(
         "pair_output",

time: 35.7 us -> 35.9 us (level)
  waiting for transfers between devices: 7.86 us -> 5.84 us
  starting transfers between devices: 16 us -> 17.9 us
    ppermute x5, waiting for transfers between devices: 2.63 us -> 0.01 us  [exchange(): lax.ppermute(value, 'owner', [(o, swap_target(o, swap, owner_n)) for o in...]
    ppermute x5, starting transfers between devices: 9.05 us -> 10.8 us  [exchange(): lax.ppermute(value, 'owner', [(o, swap_target(o, swap, owner_n)) for o in...]
    ppermute x8, waiting for transfers between devices: 5.23 us -> 5.83 us  [across(): return lax.ppermute(value, 'helper', [(j, j ^ k) for j in range(helper_n)])]
  transfers between devices with their start and end apart: 13 -> 13, of which waited for: 5 -> 3; matrix products, arithmetic and copies ran while one was open for 0% -> 0% of each run, Pallas kernels for 24% -> 28%
where the time goes in v3:
time: 35.9 us; the launch traced here: 35.6 us
  starting transfers between devices  17.9 us (50%)
  Pallas kernels  11.7 us (33%)
  waiting for transfers between devices  5.84 us (16%)
    pallas_call x7, Pallas kernels, call(): pl.pallas_call(kernel, out_shape=out_shape, in_specs=in_specs, out_specs=...  11.7 us
    ppermute x5, starting transfers between devices, exchange(): lax.ppermute(value, 'owner', [(o, swap_target(o, swap, owner_n)) for o in...  10.8 us
    ppermute x8, starting transfers between devices, across(): return lax.ppermute(value, 'helper', [(j, j ^ k) for j in range(helper_n)])  7.1 us
    ppermute x8, waiting for transfers between devices, across(): return lax.ppermute(value, 'helper', [(j, j ^ k) for j in range(helper_n)])  5.83 us
  transfers between devices with their start and end apart: 13, of which 3 were waited for; matrix products, arithmetic and copies ran while one was open for 0% of the time, Pallas kernels for 28%

profile of v3, /device:TPU:0, one launch (start us, length us, event | category | flops | bytes accessed | tf_op | source)
XLA Modules:
  0.0 35.6 jit_solution(12092540162018622467)
XLA Ops:
  0.0 3.0 %collective-permute-start.2 = (bf16[192,768]{1,0:T(8,128)(2,1)}, bf16[192,768]{1,0:T(8,128)(2,1)S(1)}, u32[]{:S(2)}, u32[]{:S(2)}) collective-permute-start(bf16[192,768]{1,0:T(8,128)(2,1)} %own_weight.1), channel_id=1, source_target_pairs={{0,2},{1,3},{2,0},{3,1},{4,6},{5,7},{6,4},{7,5},{8,10},{9,11},{10,... | collective-permute-start | bytes 884744 | tf_op jit(solution)/shard_map/ppermute | solution.py:270
  3.0 3.4 %own_images.1 = (bf16[384,128]{1,0:T(8,128)(2,1)S(1)}, bf16[384,128]{1,0:T(8,128)(2,1)S(1)}, bf16[384,128]{1,0:T(8,128)(2,1)S(1)}, bf16[384,128]{1,0:T(8,128)(2,...) custom-call(bf16[2,128,768]{2,1,0:T(8,128)(2,1)} %states.3, ...), custom_call_target="tpu_custom_call" | custom-call | flops 1 | bytes 1 | tf_op jit(solution)/shard_map/own_images/pallas_call | solution.py:277
  6.4 0.0 copy-start
  6.4 0.1 collective-permute-start.1
  6.5 3.1 %collective-permute-start.3 = (bf16[384,128]{1,0:T(8,128)(2,1)S(1)}, bf16[384,128]{1,0:T(8,128)(2,1)}, u32[]{:S(2)}, u32[]{:S(2)}) collective-permute-start(bf16[384,128]{1,0:T(8,128)(2,1)S(1)} %get-tuple-element.47), channel_id=1, source_target_pairs={{0,16},{4,20},{8,24},{12,28},{16,0},{20,4},{24,8},{28,12},{1,17},{... | collective-permute-start | bytes 294920 | tf_op jit(solution)/shard_map/ppermute | solution.py:273
  9.6 1.6 %collective-permute-start.4 = (bf16[384,128]{1,0:T(8,128)(2,1)S(1)}, bf16[384,128]{1,0:T(8,128)(2,1)}, u32[]{:S(2)}, u32[]{:S(2)}) collective-permute-start(bf16[384,128]{1,0:T(8,128)(2,1)S(1)} %get-tuple-element.48), channel_id=1, source_target_pairs={{0,8},{4,12},{8,0},{12,4},{16,24},{20,28},{24,16},{28,20},{1,9},{5... | collective-permute-start | bytes 294920 | tf_op jit(solution)/shard_map/ppermute | solution.py:273
  11.1 1.5 %collective-permute-start.5 = (bf16[384,128]{1,0:T(8,128)(2,1)S(1)}, bf16[384,128]{1,0:T(8,128)(2,1)}, u32[]{:S(2)}, u32[]{:S(2)}) collective-permute-start(bf16[384,128]{1,0:T(8,128)(2,1)S(1)} %get-tuple-element.49), channel_id=1, source_target_pairs={{0,4},{4,0},{8,12},{12,8},{16,20},{20,16},{24,28},{28,24},{1,5},{5... | collective-permute-start | bytes 294920 | tf_op jit(solution)/shard_map/ppermute | solution.py:273
  12.6 0.1 cross_output_rows.1
  12.7 0.0 copy-start.2
  12.7 1.6 %collective-permute-start.11 = (bf16[192,768]{1,0:T(8,128)(2,1)S(1)}, bf16[192,768]{1,0:T(8,128)(2,1)S(1)}, u32[]{:S(2)}, u32[]{:S(2)}) collective-permute-start(bf16[192,768]{1,0:T(8,128)(2,1)S(1)} %cross_output_rows.1), channel_id=1, source_target_pairs={{0,2},{1,3},{2,0},{3,1},{4,6},{5,7},{6,4},{7,5},{8,10},{9,11},{10,... | collective-permute-start | bytes 884744 | tf_op jit(solution)/shard_map/ppermute | solution.py:270
  14.3 0.0 collective-permute-done.2.got_weight
  14.3 3.5 %collective-permute-start.6 = (bf16[384,128]{1,0:T(8,128)(2,1)S(1)}, bf16[384,128]{1,0:T(8,128)(2,1)S(1)}, u32[]{:S(2)}, u32[]{:S(2)}) collective-permute-start(bf16[384,128]{1,0:T(8,128)(2,1)S(1)} %get-tuple-element.53), channel_id=1, source_target_pairs={{0,24},{4,28},{8,16},{12,20},{16,8},{20,12},{24,0},{28,4},{1,25},{... | collective-permute-start | bytes 294920 | tf_op jit(solution)/shard_map/ppermute | solution.py:273
  17.8 1.7 %self_output_share.1 = (f32[256,768]{1,0:T(8,128)}, bf16[448,768]{1,0:T(8,128)(2,1)}) custom-call(bf16[2,128,768]{2,1,0:T(8,128)(2,1)S(1)} %copy-done, bf16[384,128]{1,0:T(8,128)(2,1)S(1)} %get-tuple-element.43.own, bf16[384,128]{1,0:T(8,128)(2,1)S(1)} %collective-permute-done.1.got.waited, bf16[192,768]{1,0:T(8,128)(2,1)S(1)} %copy-done.1, ...), custom_call_target="tpu_custom_call" | custom-call | flops 1 | bytes 1 | tf_op jit(solution)/shard_map/self_output_share/pallas_call | solution.py:277
  19.5 0.0 collective-permute-done.3.rest_0_
  19.5 1.2 %collective-permute-start.7 = (bf16[384,128]{1,0:T(8,128)(2,1)S(1)}, bf16[384,128]{1,0:T(8,128)(2,1)S(1)}, u32[]{:S(2)}, u32[]{:S(2)}) collective-permute-start(bf16[384,128]{1,0:T(8,128)(2,1)S(1)} %get-tuple-element.54), channel_id=1, source_target_pairs={{0,28},{4,8},{8,4},{12,16},{16,12},{20,24},{24,20},{28,0},{1,29},{... | collective-permute-start | bytes 294920 | tf_op jit(solution)/shard_map/ppermute | solution.py:273
  20.8 0.0 collective-permute-done.4.rest_1_
  20.8 4.1 %conditional.1 = ((f32[2,32,768]{2,1,0:T(8,128)S(1)}, f32[2,128,192]{2,1,0:T(8,128)S(1)}, bf16[192,768]{1,0:T(8,128)(2,1)S(1)})) conditional(s32[]{:T(128)} %convert_element_type.3, () %tuple.12, (bf16[448,768]{1,0:T(8,128)(2,1)}, f32[256,768]{1,0:T(8,128)}, f32[3,768]{1,0:T(4,128)S(1)}, bf16[3,192,768]{2,1,0:T(8,128)(2,1)S(1)}, ...), branch_computations={%region_0.0_spmd, %region_1.0_spmd} | conditional | flops 1 | bytes 2752561 | solution.py:359
  20.8 0.1 collective-permute-start
  20.9 2.3 %collective-permute-done.got = bf16[448,768]{1,0:T(8,128)(2,1)S(1)} collective-permute-done((bf16[448,768]{1,0:T(8,128)(2,1)}, bf16[448,768]{1,0:T(8,128)(2,1)S(1)}, u32[]{:S(2)}, u32[]{:S(2)}) %collective-permute-start) | collective-permute-done | bytes 688160 | tf_op jit(solution)/shard_map/cond/branch_1_fun/ppermute | solution.py:270
  23.2 1.7 %mixed_and_queries.1 = (f32[2,32,768]{2,1,0:T(8,128)S(1)}, f32[2,128,192]{2,1,0:T(8,128)S(1)}, bf16[192,768]{1,0:T(8,128)(2,1)S(1)}) custom-call(f32[256,768]{1,0:T(8,128)} %get-tuple-element.19.base, bf16[448,768]{1,0:T(8,128)(2,1)S(1)} %collective-permute-done.got, f32[3,768]{1,0:T(4,128)S(1)} %get-tuple-element.21.gains, ...), custom_call_target="tpu_custom_call" | custom-call | flops 1 | bytes 1 | tf_op jit(solution)/shard_map/cond/branch_1_fun/mixed_and_queries/pallas_call | solution.py:277
  24.9 2.0 %early_cross_attention.1.before = bf16[4,3,48,128]{3,2,1,0:T(8,128)(2,1)S(1)} custom-call(f32[2,128,192]{2,1,0:T(8,128)S(1)} %get-tuple-element.51.queries, s32[5,128]{1,0:T(8,128)S(1)} %get-tuple-element.52.table, bf16[384,128]{1,0:T(8,128)(2,1)} %collective-permute-done.3.rest_0_, bf16[384,128]{1,0:T(8,128)(2,1)} %collective-permute-done.4.rest_1_, ...), custom_call_target="tpu_custom_call" | custom-call | flops 3000000000 | bytes 1 | tf_op jit(solution)/shard_map/early_cross_attention/pallas_call | solution.py:277
  27.0 0.0 collective-permute-done.11.rest_6_
  27.0 0.2 collective-permute-start.12
  27.2 0.9 %late_cross_attention.1 = (bf16[5,48,128]{2,1,0:T(8,128)(2,1)S(1)}, bf16[5,48,128]{2,1,0:T(8,128)(2,1)S(1)}, bf16[5,48,128]{2,1,0:T(8,128)(2,1)S(1)}, bf16[5,48,128]{2,1,0:T(8,128)(2,1)S(1)}) custom-call(f32[2,128,192]{2,1,0:T(8,128)S(1)} %get-tuple-element.51.queries, s32[5,128]{1,0:T(8,128)S(1)} %get-tuple-element.52.table, ...), custom_call_target="tpu_custom_call" | custom-call | flops 99999997952 | bytes 1 | tf_op jit(solution)/shard_map/late_cross_attention/pallas_call | solution.py:277
  28.0 0.6 %collective-permute-start.10 = (bf16[5,48,128]{2,1,0:T(8,128)(2,1)S(1)}, bf16[5,48,128]{2,1,0:T(8,128)(2,1)S(1)}, u32[]{:S(2)}, u32[]{:S(2)}) collective-permute-start(bf16[5,48,128]{2,1,0:T(8,128)(2,1)S(1)} %get-tuple-element.58), channel_id=1, source_target_pairs={{0,3},{1,2},{2,1},{3,0},{4,7},{5,6},{6,5},{7,4},{8,11},{9,10},{10,... | collective-permute-start | bytes 184328 | tf_op jit(solution)/shard_map/ppermute | solution.py:270
  28.6 0.2 collective-permute-start.8
  28.8 1.5 %collective-permute-start.9 = (bf16[5,48,128]{2,1,0:T(8,128)(2,1)S(1)}, bf16[5,48,128]{2,1,0:T(8,128)(2,1)S(1)}, u32[]{:S(2)}, u32[]{:S(2)}) collective-permute-start(bf16[5,48,128]{2,1,0:T(8,128)(2,1)S(1)} %get-tuple-element.57), channel_id=1, source_target_pairs={{0,2},{1,3},{2,0},{3,1},{4,6},{5,7},{6,4},{7,5},{8,10},{9,11},{10,... | collective-permute-start | bytes 184328 | tf_op jit(solution)/shard_map/ppermute | solution.py:270
  30.2 1.7 %collective-permute-done.10.rest_3_ = bf16[5,48,128]{2,1,0:T(8,128)(2,1)S(1)} collective-permute-done((bf16[5,48,128]{2,1,0:T(8,128)(2,1)S(1)}, bf16[5,48,128]{2,1,0:T(8,128)(2,1)S(1)}, u32[]{:S(2)}, u32[]{:S(2)}) %collective-permute-start.10) | collective-permute-done | bytes 61472 | tf_op jit(solution)/shard_map/ppermute | solution.py:270
  31.9 0.0 collective-permute-done.8.rest_1_
  31.9 1.8 %collective-permute-done.9.rest_2_ = bf16[5,48,128]{2,1,0:T(8,128)(2,1)S(1)} collective-permute-done((bf16[5,48,128]{2,1,0:T(8,128)(2,1)S(1)}, bf16[5,48,128]{2,1,0:T(8,128)(2,1)S(1)}, u32[]{:S(2)}, u32[]{:S(2)}) %collective-permute-start.9) | collective-permute-done | bytes 61472 | tf_op jit(solution)/shard_map/ppermute | solution.py:270
  33.7 0.0 collective-permute-done.12.rest_7_
  33.7 1.9 %pair_output.1 = bf16[2,5,32,768]{3,2,1,0:T(8,128)(2,1)} custom-call(s32[2,5]{1,0:T(2,128)} %partners.3, f32[2,32,768]{2,1,0:T(8,128)S(1)} %get-tuple-element.50.own_rows, bf16[5,48,128]{2,1,0:T(8,128)(2,1)S(1)} %get-tuple-element.55.rest_0_, bf16[5,48,128]{2,1,0:T(8,128)(2,1)S(1)} %collective-permute-done.8.rest_1_, ...), custom_call_target="tpu_custom_call" | custom-call | flops 1 | bytes 1 | tf_op jit(solution)/shard_map/pair_output/pallas_call | solution.py:277
  (10 shorter events, 0.0 us)
Async XLA Ops:
  0.0 14.3 %collective-permute-start.2 = (bf16[192,768]{1,0:T(8,128)(2,1)}, bf16[192,768]{1,0:T(8,128)(2,1)S(1)}, u32[]{:S(2)}, u32[]{:S(2)}) collective-permute-start(bf16[192,768]{1,0:T(8,128)(2,1)} %own_weight.1), channel_id=1, source_target_pairs={{0,2},{1,3},{2,0},{3,1},{4,6},{5,7},{6,4},{7,5},{8,10},{9,11},{10,... | collective-permute-start | bytes 884744 | tf_op jit(solution)/shard_map/ppermute | solution.py:270
  6.4 11.4 %copy-start = (bf16[2,128,768]{2,1,0:T(8,128)(2,1)S(1)}, bf16[2,128,768]{2,1,0:T(8,128)(2,1)}, u32[]{:S(2)}) copy-start(bf16[2,128,768]{2,1,0:T(8,128)(2,1)} %states.3) | copy-start | bytes 1179652
  6.4 6.2 %collective-permute-start.1 = (bf16[384,128]{1,0:T(8,128)(2,1)S(1)}, bf16[384,128]{1,0:T(8,128)(2,1)S(1)}, u32[]{:S(2)}, u32[]{:S(2)}) collective-permute-start(bf16[384,128]{1,0:T(8,128)(2,1)S(1)} %get-tuple-element.43.own), channel_id=1, source_target_pairs={{0,2},{1,3},{2,0},{3,1},{4,6},{5,7},{6,4},{7,5},{8,10},{9,11},{10,... | collective-permute-start | bytes 294920 | tf_op jit(solution)/shard_map/ppermute | solution.py:270
  6.5 13.0 %collective-permute-start.3 = (bf16[384,128]{1,0:T(8,128)(2,1)S(1)}, bf16[384,128]{1,0:T(8,128)(2,1)}, u32[]{:S(2)}, u32[]{:S(2)}) collective-permute-start(bf16[384,128]{1,0:T(8,128)(2,1)S(1)} %get-tuple-element.47), channel_id=1, source_target_pairs={{0,16},{4,20},{8,24},{12,28},{16,0},{20,4},{24,8},{28,12},{1,17},{... | collective-permute-start | bytes 294920 | tf_op jit(solution)/shard_map/ppermute | solution.py:273
  9.6 11.2 %collective-permute-start.4 = (bf16[384,128]{1,0:T(8,128)(2,1)S(1)}, bf16[384,128]{1,0:T(8,128)(2,1)}, u32[]{:S(2)}, u32[]{:S(2)}) collective-permute-start(bf16[384,128]{1,0:T(8,128)(2,1)S(1)} %get-tuple-element.48), channel_id=1, source_target_pairs={{0,8},{4,12},{8,0},{12,4},{16,24},{20,28},{24,16},{28,20},{1,9},{5... | collective-permute-start | bytes 294920 | tf_op jit(solution)/shard_map/ppermute | solution.py:273
  11.1 9.6 %collective-permute-start.5 = (bf16[384,128]{1,0:T(8,128)(2,1)S(1)}, bf16[384,128]{1,0:T(8,128)(2,1)}, u32[]{:S(2)}, u32[]{:S(2)}) collective-permute-start(bf16[384,128]{1,0:T(8,128)(2,1)S(1)} %get-tuple-element.49), channel_id=1, source_target_pairs={{0,4},{4,0},{8,12},{12,8},{16,20},{20,16},{24,28},{28,24},{1,5},{5... | collective-permute-start | bytes 294920 | tf_op jit(solution)/shard_map/ppermute | solution.py:273
  12.6 5.2 %copy-start.1 = (bf16[192,768]{1,0:T(8,128)(2,1)S(1)}, bf16[192,768]{1,0:T(8,128)(2,1)}, u32[]{:S(2)}) copy-start(bf16[192,768]{1,0:T(8,128)(2,1)} %own_weight.1) | copy-start | bytes 884740
  12.7 8.0 %copy-start.2 = (bf16[3,768,192]{1,2,0:T(8,128)(2,1)S(1)}, bf16[3,768,192]{1,2,0:T(8,128)(2,1)}, u32[]{:S(2)}) copy-start(bf16[3,768,192]{1,2,0:T(8,128)(2,1)} %param.13) | copy-start | bytes 2654212
  12.7 14.2 %collective-permute-start.11 = (bf16[192,768]{1,0:T(8,128)(2,1)S(1)}, bf16[192,768]{1,0:T(8,128)(2,1)S(1)}, u32[]{:S(2)}, u32[]{:S(2)}) collective-permute-start(bf16[192,768]{1,0:T(8,128)(2,1)S(1)} %cross_output_rows.1), channel_id=1, source_target_pairs={{0,2},{1,3},{2,0},{3,1},{4,6},{5,7},{6,4},{7,5},{8,10},{9,11},{10,... | collective-permute-start | bytes 884744 | tf_op jit(solution)/shard_map/ppermute | solution.py:270
  14.3 6.5 %copy-start.3 = (f32[3,768]{1,0:T(4,128)S(1)}, f32[3,768]{1,0:T(4,128)}, u32[]{:S(2)}) copy-start(f32[3,768]{1,0:T(4,128)} %gains.1) | copy-start | bytes 27652
  14.3 12.8 %collective-permute-start.6 = (bf16[384,128]{1,0:T(8,128)(2,1)S(1)}, bf16[384,128]{1,0:T(8,128)(2,1)S(1)}, u32[]{:S(2)}, u32[]{:S(2)}) collective-permute-start(bf16[384,128]{1,0:T(8,128)(2,1)S(1)} %get-tuple-element.53), channel_id=1, source_target_pairs={{0,24},{4,28},{8,16},{12,20},{16,8},{20,12},{24,0},{28,4},{1,25},{... | collective-permute-start | bytes 294920 | tf_op jit(solution)/shard_map/ppermute | solution.py:273
  19.5 7.6 %collective-permute-start.7 = (bf16[384,128]{1,0:T(8,128)(2,1)S(1)}, bf16[384,128]{1,0:T(8,128)(2,1)S(1)}, u32[]{:S(2)}, u32[]{:S(2)}) collective-permute-start(bf16[384,128]{1,0:T(8,128)(2,1)S(1)} %get-tuple-element.54), channel_id=1, source_target_pairs={{0,28},{4,8},{8,4},{12,16},{16,12},{20,24},{24,20},{28,0},{1,29},{... | collective-permute-start | bytes 294920 | tf_op jit(solution)/shard_map/ppermute | solution.py:273
  20.8 2.4 %collective-permute-start = (bf16[448,768]{1,0:T(8,128)(2,1)}, bf16[448,768]{1,0:T(8,128)(2,1)S(1)}, u32[]{:S(2)}, u32[]{:S(2)}) collective-permute-start(bf16[448,768]{1,0:T(8,128)(2,1)} %get-tuple-element.20), channel_id=1, source_target_pairs={{0,1},{1,0},{2,3},{3,2},{4,5},{5,4},{6,7},{7,6},{8,9},{9,8},{10,11... | collective-permute-start | bytes 2064392 | tf_op jit(solution)/shard_map/cond/branch_1_fun/ppermute | solution.py:270
  27.0 6.8 %collective-permute-start.12 = (bf16[192,768]{1,0:T(8,128)(2,1)S(1)}, bf16[192,768]{1,0:T(8,128)(2,1)S(1)}, u32[]{:S(2)}, u32[]{:S(2)}) collective-permute-start(bf16[192,768]{1,0:T(8,128)(2,1)S(1)} %collective-permute-done.11.rest_6_), channel_id=1, source_target_pairs={{0,1},{1,0},{2,3},{3,2},{4,5},{5,4},{6,7},{7,6},{8,9},{9,8},{10,11... | collective-permute-start | bytes 884744 | tf_op jit(solution)/shard_map/ppermute | solution.py:270
  28.0 3.9 %collective-permute-start.10 = (bf16[5,48,128]{2,1,0:T(8,128)(2,1)S(1)}, bf16[5,48,128]{2,1,0:T(8,128)(2,1)S(1)}, u32[]{:S(2)}, u32[]{:S(2)}) collective-permute-start(bf16[5,48,128]{2,1,0:T(8,128)(2,1)S(1)} %get-tuple-element.58), channel_id=1, source_target_pairs={{0,3},{1,2},{2,1},{3,0},{4,7},{5,6},{6,5},{7,4},{8,11},{9,10},{10,... | collective-permute-start | bytes 184328 | tf_op jit(solution)/shard_map/ppermute | solution.py:270
  28.6 3.3 %collective-permute-start.8 = (bf16[5,48,128]{2,1,0:T(8,128)(2,1)S(1)}, bf16[5,48,128]{2,1,0:T(8,128)(2,1)S(1)}, u32[]{:S(2)}, u32[]{:S(2)}) collective-permute-start(bf16[5,48,128]{2,1,0:T(8,128)(2,1)S(1)} %get-tuple-element.56), channel_id=1, source_target_pairs={{0,1},{1,0},{2,3},{3,2},{4,5},{5,4},{6,7},{7,6},{8,9},{9,8},{10,11... | collective-permute-start | bytes 184328 | tf_op jit(solution)/shard_map/ppermute | solution.py:270
  28.8 4.9 %collective-permute-start.9 = (bf16[5,48,128]{2,1,0:T(8,128)(2,1)S(1)}, bf16[5,48,128]{2,1,0:T(8,128)(2,1)S(1)}, u32[]{:S(2)}, u32[]{:S(2)}) collective-permute-start(bf16[5,48,128]{2,1,0:T(8,128)(2,1)S(1)} %get-tuple-element.57), channel_id=1, source_target_pairs={{0,2},{1,3},{2,0},{3,1},{4,6},{5,7},{6,4},{7,5},{8,10},{9,11},{10,... | collective-permute-start | bytes 184328 | tf_op jit(solution)/shard_map/ppermute | solution.py:270

commit v4 on v3

--- a/solution.py
+++ b/solution.py
@@ -12,7 +12,7 @@
 F32 = jnp.float32
 BF16 = jnp.bfloat16
 VMEM_BYTES = 24 * 1024 * 1024
-EARLY_WEIGHT = 3 * 10**9
+EARLY_WEIGHT = 1
 LATE_WEIGHT = 10**11
 
 VMEM = pl.BlockSpec(memory_space=pltpu.VMEM)
@@ -145,27 +145,19 @@
     )
 
 
-def partial_kernel(states, own, got, own_weight, got_weight, cross_out, base, sent, weight_v, sems):
+def partial_kernel(states, own, got, own_weight, got_weight, cross_out, *rest):
+    base, sent, sem = rest[-3:]
     row_all = base.shape[0]
-    copies = [
-        pltpu.make_async_copy(got_weight, weight_v, sems.at[0]),
-        pltpu.make_async_copy(cross_out, sent.at[pl.ds(row_all, cross_out.shape[0])], sems.at[1]),
-    ]
-    for copy in copies:
-        copy.start()
-    part = nn(unpack(own[...]), own_weight[...])
-    base[...] = states[...].reshape(part.shape).astype(F32)
-    copies[0].wait()
-    part = part + nn(unpack(got[...]), weight_v[...])
+    copy = pltpu.make_async_copy(cross_out, sent.at[pl.ds(row_all, cross_out.shape[0])], sem)
+    copy.start()
+    rows = jnp.concatenate([unpack(own[...]), unpack(got[...])], 1)
+    part = nn(rows, jnp.concatenate([own_weight[...], got_weight[...]], 0))
     sent[:row_all, :] = part.astype(BF16)
-    base[...] += part
-    copies[1].wait()
-
-
-def query_kernel(helper_n, base, got, gains, proj_t, *rest):
-    own_rows, queries_out, weight_out, mixed_ref, sem = rest[-5:]
-    copy = pltpu.make_async_copy(got.at[pl.ds(base.shape[0], weight_out.shape[0])], weight_out, sem)
-    copy.start()
+    base[...] = states[...].reshape(part.shape).astype(F32) + part
+    copy.wait()
+
+
+def query_kernel(helper_n, base, got, gains, proj_t, own_rows, queries_out, mixed_ref):
     mixed = base[...] + got[: base.shape[0], :].astype(F32)
     image_n, row_n, width = own_rows.shape
     patch_n = row_n * helper_n
@@ -175,7 +167,6 @@
     queries_out[...] = queries.reshape(queries_out.shape)
     start = pl.multiple_of(lax.axis_index("helper") * row_n, row_n)
     own_rows[...] = mixed_ref[:, pl.ds(start, row_n), :]
-    copy.wait()
 
 
 def hand_on_kernel(weight, waited, out, sem):
@@ -235,9 +226,10 @@
     copy = pltpu.make_async_copy(partners, partners_s, sem)
     copy.start()
     image_n, row_n, width = own_rows.shape
+    columns = HEAD + LANES
     terms = None
     for side, weight in zip(sides, weights):
-        part = nn(side_rows(side[...]), weight[...])
+        part = nn(side_rows(side[...]), weight[weight.shape[0] - columns :, :])
         terms = part if terms is None else terms + part
     term_ref[...] = terms.reshape(len(swaps), row_n, width)
     copy.wait()
@@ -332,33 +324,18 @@
         "self_output_share",
         partial_kernel,
         [shape((row_all, width), F32), shape((row_all + columns, width), BF16)],
-        [VMEM] * 4 + [ANY, ANY],
-        [pltpu.VMEM(self_out.shape, BF16), dma((2,))],
-        states, context, context_got, self_out, self_out_got, cross_out_own,
-    )
-    made_shapes = [
-        shape((image_n, row_n, width), F32),
-        shape((image_n, patch_n, columns), F32),
-        shape(cross_out.shape, BF16),
-    ]
-
-    def mixing(base, sent, gains, cross_proj_t, *waited):
-        made = call(
-            "mixed_and_queries",
-            functools.partial(query_kernel, helper_n),
-            made_shapes,
-            [VMEM] * 4 + [ANY] * len(waited),
-            [pltpu.VMEM((image_n, patch_n, width), F32), dma],
-            base, across(sent, core_hop), gains, cross_proj_t, *waited,
-        )
-        return tuple(made)
-
-    def no_images(*operands):
-        return tuple(jnp.zeros(made.shape, made.dtype) for made in made_shapes)
-
-    own_rows, queries, cross_out_core = lax.cond(
-        lax.axis_index("owner") < owner_n, mixing, no_images,
-        base, sent, gains, cross_proj_t, *[arrived[at] for at in early],
+        [VMEM] * 5 + [ANY] * (1 + len(early)),
+        [dma],
+        states, context, context_got, self_out, self_out_got, cross_out_own, *[arrived[at] for at in early],
+    )
+    got = across(sent, core_hop)
+    own_rows, queries = call(
+        "mixed_and_queries",
+        functools.partial(query_kernel, helper_n),
+        [shape((image_n, row_n, width), F32), shape((image_n, patch_n, columns), F32)],
+        [VMEM] * 4,
+        [pltpu.VMEM((image_n, patch_n, width), F32)],
+        base, got, gains, cross_proj_t,
     )
     packed = columns * row_n // LANES
     early_sides = call(
@@ -380,8 +357,16 @@
         flops=LATE_WEIGHT,
     )
     sides = [sides[0]] + [across(sides[k], k) for k in range(1, helper_n)]
-    weights = {0: cross_out_own, core_hop: cross_out_core, chip_hop: cross_out_got}
-    weights[chip_hop ^ core_hop] = across(cross_out_got, core_hop)
+    weights = {0: cross_out_own, core_hop: got, chip_hop: cross_out_got}
+    cross_out_far = call(
+        "cross_output_far_rows",
+        hand_on_kernel,
+        shape(cross_out.shape, BF16),
+        [ANY, ANY],
+        [dma],
+        cross_out_got, early_sides,
+    )
+    weights[chip_hop ^ core_hop] = across(cross_out_far, core_hop)
     return call(
         "pair_output",
         functools.partial(out_kernel, [swaps[at] for at in early + late], owner_n, helper_n),

time: 35.9 us -> 36.3 us (1.011)
  waiting for transfers between devices: 5.84 us -> 9.9 us
  Pallas kernels: 11.7 us -> 8.48 us
    ppermute x5, waiting for transfers between devices: 0.01 us -> 4.93 us  [exchange(): lax.ppermute(value, 'owner', [(o, swap_target(o, swap, owner_n)) for o in...]
    pallas_call x7 -> x8, Pallas kernels: 11.7 us -> 8.48 us  [call(): pl.pallas_call(kernel, out_shape=out_shape, in_specs=in_specs, out_specs=...]
    ppermute x8, waiting for transfers between devices: 5.83 us -> 4.97 us  [across(): return lax.ppermute(value, 'helper', [(j, j ^ k) for j in range(helper_n)])]
    ppermute x8, starting transfers between devices: 7.1 us -> 6.69 us  [across(): return lax.ppermute(value, 'helper', [(j, j ^ k) for j in range(helper_n)])]
  transfers between devices with their start and end apart: 13 -> 13, of which waited for: 3 -> 7; matrix products, arithmetic and copies ran while one was open for 0% -> 0% of each run, Pallas kernels for 28% -> 17%
where the time goes in v4:
time: 36.3 us; the launch traced here: 36.1 us
  starting transfers between devices  17.6 us (48%)
  waiting for transfers between devices  9.9 us (27%)
  Pallas kernels  8.48 us (23%)
    ppermute x5, starting transfers between devices, exchange(): lax.ppermute(value, 'owner', [(o, swap_target(o, swap, owner_n)) for o in...  10.9 us
    pallas_call x8, Pallas kernels, call(): pl.pallas_call(kernel, out_shape=out_shape, in_specs=in_specs, out_specs=...  8.48 us
    ppermute x8, starting transfers between devices, across(): return lax.ppermute(value, 'helper', [(j, j ^ k) for j in range(helper_n)])  6.69 us
    ppermute x8, waiting for transfers between devices, across(): return lax.ppermute(value, 'helper', [(j, j ^ k) for j in range(helper_n)])  4.97 us
    ppermute x5, waiting for transfers between devices, exchange(): lax.ppermute(value, 'owner', [(o, swap_target(o, swap, owner_n)) for o in...  4.93 us
  transfers between devices with their start and end apart: 13, of which 7 were waited for; matrix products, arithmetic and copies ran while one was open for 0% of the time, Pallas kernels for 17%

profile of v4, /device:TPU:0, one launch (start us, length us, event | category | flops | bytes accessed | tf_op | source)
XLA Modules:
  0.0 36.1 jit_solution(9602702616717132105)
XLA Ops:
  0.0 3.0 %collective-permute-start.1 = (bf16[192,768]{1,0:T(8,128)(2,1)}, bf16[192,768]{1,0:T(8,128)(2,1)S(1)}, u32[]{:S(2)}, u32[]{:S(2)}) collective-permute-start(bf16[192,768]{1,0:T(8,128)(2,1)} %own_weight.1), channel_id=1, source_target_pairs={{0,2},{1,3},{2,0},{3,1},{4,6},{5,7},{6,4},{7,5},{8,10},{9,11},{10,... | collective-permute-start | bytes 884744 | tf_op jit(solution)/shard_map/ppermute | solution.py:262
  3.0 3.5 %own_images.1 = (bf16[384,128]{1,0:T(8,128)(2,1)S(1)}, bf16[384,128]{1,0:T(8,128)(2,1)S(1)}, bf16[384,128]{1,0:T(8,128)(2,1)S(1)}, bf16[384,128]{1,0:T(8,128)(2,...) custom-call(bf16[2,128,768]{2,1,0:T(8,128)(2,1)} %states.3, ...), custom_call_target="tpu_custom_call" | custom-call | flops 1 | bytes 1 | tf_op jit(solution)/shard_map/own_images/pallas_call | solution.py:269
  6.5 0.1 collective-permute-start
  6.5 3.1 %collective-permute-start.2 = (bf16[384,128]{1,0:T(8,128)(2,1)S(1)}, bf16[384,128]{1,0:T(8,128)(2,1)S(1)}, u32[]{:S(2)}, u32[]{:S(2)}) collective-permute-start(bf16[384,128]{1,0:T(8,128)(2,1)S(1)} %get-tuple-element.23), channel_id=1, source_target_pairs={{0,16},{4,20},{8,24},{12,28},{16,0},{20,4},{24,8},{28,12},{1,17},{... | collective-permute-start | bytes 294920 | tf_op jit(solution)/shard_map/ppermute | solution.py:265
  9.6 1.6 %collective-permute-start.3 = (bf16[384,128]{1,0:T(8,128)(2,1)S(1)}, bf16[384,128]{1,0:T(8,128)(2,1)S(1)}, u32[]{:S(2)}, u32[]{:S(2)}) collective-permute-start(bf16[384,128]{1,0:T(8,128)(2,1)S(1)} %get-tuple-element.24), channel_id=1, source_target_pairs={{0,8},{4,12},{8,0},{12,4},{16,24},{20,28},{24,16},{28,20},{1,9},{5... | collective-permute-start | bytes 294920 | tf_op jit(solution)/shard_map/ppermute | solution.py:265
  11.2 1.5 %collective-permute-start.4 = (bf16[384,128]{1,0:T(8,128)(2,1)S(1)}, bf16[384,128]{1,0:T(8,128)(2,1)S(1)}, u32[]{:S(2)}, u32[]{:S(2)}) collective-permute-start(bf16[384,128]{1,0:T(8,128)(2,1)S(1)} %get-tuple-element.25), channel_id=1, source_target_pairs={{0,4},{4,0},{8,12},{12,8},{16,20},{20,16},{24,28},{28,24},{1,5},{5... | collective-permute-start | bytes 294920 | tf_op jit(solution)/shard_map/ppermute | solution.py:265
  12.7 0.0 collective-permute-done.got.waited
  12.7 0.6 %collective-permute-done.2.rest_0_ = bf16[384,128]{1,0:T(8,128)(2,1)S(1)} collective-permute-done((bf16[384,128]{1,0:T(8,128)(2,1)S(1)}, bf16[384,128]{1,0:T(8,128)(2,1)S(1)}, u32[]{:S(2)}, u32[]{:S(2)}) %collective-permute-start.2) | collective-permute-done | bytes 98336 | tf_op jit(solution)/shard_map/ppermute | solution.py:265
  13.3 1.1 %collective-permute-done.3.rest_1_ = bf16[384,128]{1,0:T(8,128)(2,1)S(1)} collective-permute-done((bf16[384,128]{1,0:T(8,128)(2,1)S(1)}, bf16[384,128]{1,0:T(8,128)(2,1)S(1)}, u32[]{:S(2)}, u32[]{:S(2)}) %collective-permute-start.3) | collective-permute-done | bytes 98336 | tf_op jit(solution)/shard_map/ppermute | solution.py:265
  14.4 1.4 %collective-permute-done.4.rest_2_ = bf16[384,128]{1,0:T(8,128)(2,1)S(1)} collective-permute-done((bf16[384,128]{1,0:T(8,128)(2,1)S(1)}, bf16[384,128]{1,0:T(8,128)(2,1)S(1)}, u32[]{:S(2)}, u32[]{:S(2)}) %collective-permute-start.4) | collective-permute-done | bytes 98336 | tf_op jit(solution)/shard_map/ppermute | solution.py:265
  15.8 0.0 copy-start
  15.8 0.5 %self_output_share.1 = (f32[256,768]{1,0:T(8,128)S(1)}, bf16[448,768]{1,0:T(8,128)(2,1)S(1)}) custom-call(bf16[2,128,768]{2,1,0:T(8,128)(2,1)S(1)} %copy-done.1, bf16[384,128]{1,0:T(8,128)(2,1)S(1)} %get-tuple-element.21.own, bf16[384,128]{1,0:T(8,128)(2,1)S(1)} %collective-permute-done.got.waited, bf16[192,768]{1,0:T(8,128)(2,1)S(1)} %copy-done.2, ...), custom_call_target="tpu_custom_call" | custom-call | flops 1 | bytes 1 | tf_op jit(solution)/shard_map/self_output_share/pallas_call | solution.py:269
  16.4 0.1 collective-permute-start.5
  16.4 0.0 copy-start.3
  16.5 0.1 cross_output_rows.1
  16.5 1.6 %collective-permute-start.11 = (bf16[192,768]{1,0:T(8,128)(2,1)S(1)}, bf16[192,768]{1,0:T(8,128)(2,1)S(1)}, u32[]{:S(2)}, u32[]{:S(2)}) collective-permute-start(bf16[192,768]{1,0:T(8,128)(2,1)S(1)} %cross_output_rows.1), channel_id=1, source_target_pairs={{0,2},{1,3},{2,0},{3,1},{4,6},{5,7},{6,4},{7,5},{8,10},{9,11},{10,... | collective-permute-start | bytes 884744 | tf_op jit(solution)/shard_map/ppermute | solution.py:262
  18.1 1.7 %collective-permute-start.6 = (bf16[384,128]{1,0:T(8,128)(2,1)S(1)}, bf16[384,128]{1,0:T(8,128)(2,1)S(1)}, u32[]{:S(2)}, u32[]{:S(2)}) collective-permute-start(bf16[384,128]{1,0:T(8,128)(2,1)S(1)} %get-tuple-element.31), channel_id=1, source_target_pairs={{0,24},{4,28},{8,16},{12,20},{16,8},{20,12},{24,0},{28,4},{1,25},{... | collective-permute-start | bytes 294920 | tf_op jit(solution)/shard_map/ppermute | solution.py:265
  19.8 3.0 %collective-permute-start.7 = (bf16[384,128]{1,0:T(8,128)(2,1)S(1)}, bf16[384,128]{1,0:T(8,128)(2,1)S(1)}, u32[]{:S(2)}, u32[]{:S(2)}) collective-permute-start(bf16[384,128]{1,0:T(8,128)(2,1)S(1)} %get-tuple-element.32), channel_id=1, source_target_pairs={{0,28},{4,8},{8,4},{12,16},{16,12},{20,24},{24,20},{28,0},{1,29},{... | collective-permute-start | bytes 294920 | tf_op jit(solution)/shard_map/ppermute | solution.py:265
  22.9 0.0 collective-permute-done.5.got.rest_5_
  22.9 0.5 %mixed_and_queries.1 = (f32[2,32,768]{2,1,0:T(8,128)S(1)}, f32[2,128,192]{2,1,0:T(8,128)S(1)}) custom-call(f32[256,768]{1,0:T(8,128)S(1)} %get-tuple-element.26.base, bf16[448,768]{1,0:T(8,128)(2,1)S(1)} %collective-permute-done.5.got.rest_5_, f32[3,768]{1,0:T(4,128)S(1)} %copy-done.3, bf16[3,192,768]{2,1,0:T(8,128)(2,1)S(1)} %bitcast.3), custom_call_target="tpu_custom_call" | custom-call | flops 1 | bytes 1 | tf_op jit(solution)/shard_map/mixed_and_queries/pallas_call | solution.py:269
  23.4 1.0 %early_cross_attention.1.before.waited = bf16[4,3,48,128]{3,2,1,0:T(8,128)(2,1)S(1)} custom-call(f32[2,128,192]{2,1,0:T(8,128)S(1)} %get-tuple-element.29.queries, s32[5,128]{1,0:T(8,128)S(1)} %get-tuple-element.30.table, bf16[384,128]{1,0:T(8,128)(2,1)S(1)} %collective-permute-done.2.rest_0_, bf16[384,128]{1,0:T(8,128)(2,1)S(1)} %collective-permute-done.3.rest_1_, ...), custom_call_target="tpu_custom_call" | custom-call | flops 1 | bytes 1 | tf_op jit(solution)/shard_map/early_cross_attention/pallas_call | solution.py:269
  24.5 1.5 %collective-permute-done.11.weight.rest_6_ = bf16[192,768]{1,0:T(8,128)(2,1)S(1)} collective-permute-done((bf16[192,768]{1,0:T(8,128)(2,1)S(1)}, bf16[192,768]{1,0:T(8,128)(2,1)S(1)}, u32[]{:S(2)}, u32[]{:S(2)}) %collective-permute-start.11) | collective-permute-done | bytes 294944 | tf_op jit(solution)/shard_map/ppermute | solution.py:262
  26.0 0.1 cross_output_far_rows.1
  26.1 0.1 collective-permute-start.12
  26.2 1.8 %collective-permute-done.7.rest_1_ = bf16[384,128]{1,0:T(8,128)(2,1)S(1)} collective-permute-done((bf16[384,128]{1,0:T(8,128)(2,1)S(1)}, bf16[384,128]{1,0:T(8,128)(2,1)S(1)}, u32[]{:S(2)}, u32[]{:S(2)}) %collective-permute-start.7) | collective-permute-done | bytes 98336 | tf_op jit(solution)/shard_map/ppermute | solution.py:265
  28.0 0.9 %late_cross_attention.1 = (bf16[5,48,128]{2,1,0:T(8,128)(2,1)S(1)}, bf16[5,48,128]{2,1,0:T(8,128)(2,1)S(1)}, bf16[5,48,128]{2,1,0:T(8,128)(2,1)S(1)}, bf16[5,48,128]{2,1,0:T(8,128)(2,1)S(1)}) custom-call(f32[2,128,192]{2,1,0:T(8,128)S(1)} %get-tuple-element.29.queries, s32[5,128]{1,0:T(8,128)S(1)} %get-tuple-element.30.table, ...), custom_call_target="tpu_custom_call" | custom-call | flops 99999997952 | bytes 1 | tf_op jit(solution)/shard_map/late_cross_attention/pallas_call | solution.py:269
  28.8 0.1 collective-permute-start.8
  28.9 0.6 %collective-permute-start.9 = (bf16[5,48,128]{2,1,0:T(8,128)(2,1)S(1)}, bf16[5,48,128]{2,1,0:T(8,128)(2,1)S(1)}, u32[]{:S(2)}, u32[]{:S(2)}) collective-permute-start(bf16[5,48,128]{2,1,0:T(8,128)(2,1)S(1)} %get-tuple-element.35), channel_id=1, source_target_pairs={{0,2},{1,3},{2,0},{3,1},{4,6},{5,7},{6,4},{7,5},{8,10},{9,11},{10,... | collective-permute-start | bytes 184328 | tf_op jit(solution)/shard_map/ppermute | solution.py:262
  29.5 1.3 %collective-permute-start.10 = (bf16[5,48,128]{2,1,0:T(8,128)(2,1)S(1)}, bf16[5,48,128]{2,1,0:T(8,128)(2,1)S(1)}, u32[]{:S(2)}, u32[]{:S(2)}) collective-permute-start(bf16[5,48,128]{2,1,0:T(8,128)(2,1)S(1)} %get-tuple-element.36), channel_id=1, source_target_pairs={{0,3},{1,2},{2,1},{3,0},{4,7},{5,6},{6,5},{7,4},{8,11},{9,10},{10,... | collective-permute-start | bytes 184328 | tf_op jit(solution)/shard_map/ppermute | solution.py:262
  30.8 3.0 %collective-permute-done.9.rest_2_ = bf16[5,48,128]{2,1,0:T(8,128)(2,1)S(1)} collective-permute-done((bf16[5,48,128]{2,1,0:T(8,128)(2,1)S(1)}, bf16[5,48,128]{2,1,0:T(8,128)(2,1)S(1)}, u32[]{:S(2)}, u32[]{:S(2)}) %collective-permute-start.9) | collective-permute-done | bytes 61472 | tf_op jit(solution)/shard_map/ppermute | solution.py:262
  33.8 0.4 %collective-permute-done.10.rest_3_ = bf16[5,48,128]{2,1,0:T(8,128)(2,1)S(1)} collective-permute-done((bf16[5,48,128]{2,1,0:T(8,128)(2,1)S(1)}, bf16[5,48,128]{2,1,0:T(8,128)(2,1)S(1)}, u32[]{:S(2)}, u32[]{:S(2)}) %collective-permute-start.10) | collective-permute-done | bytes 61472 | tf_op jit(solution)/shard_map/ppermute | solution.py:262
  34.2 1.9 %pair_output.1 = bf16[2,5,32,768]{3,2,1,0:T(8,128)(2,1)} custom-call(s32[2,5]{1,0:T(2,128)} %partners.3, f32[2,32,768]{2,1,0:T(8,128)S(1)} %get-tuple-element.28.own_rows, bf16[5,48,128]{2,1,0:T(8,128)(2,1)S(1)} %get-tuple-element.33.rest_0_, bf16[5,48,128]{2,1,0:T(8,128)(2,1)S(1)} %collective-permute-done.8.rest_1_, ...), custom_call_target="tpu_custom_call" | custom-call | flops 1 | bytes 1 | tf_op jit(solution)/shard_map/pair_output/pallas_call | solution.py:269
  (10 shorter events, 0.0 us)
Async XLA Ops:
  0.0 15.8 %collective-permute-start.1 = (bf16[192,768]{1,0:T(8,128)(2,1)}, bf16[192,768]{1,0:T(8,128)(2,1)S(1)}, u32[]{:S(2)}, u32[]{:S(2)}) collective-permute-start(bf16[192,768]{1,0:T(8,128)(2,1)} %own_weight.1), channel_id=1, source_target_pairs={{0,2},{1,3},{2,0},{3,1},{4,6},{5,7},{6,4},{7,5},{8,10},{9,11},{10,... | collective-permute-start | bytes 884744 | tf_op jit(solution)/shard_map/ppermute | solution.py:262
  3.0 12.9 %copy-start.1 = (bf16[2,128,768]{2,1,0:T(8,128)(2,1)S(1)}, bf16[2,128,768]{2,1,0:T(8,128)(2,1)}, u32[]{:S(2)}) copy-start(bf16[2,128,768]{2,1,0:T(8,128)(2,1)} %states.3) | copy-start | bytes 1179652
  3.0 12.9 %copy-start.2 = (bf16[192,768]{1,0:T(8,128)(2,1)S(1)}, bf16[192,768]{1,0:T(8,128)(2,1)}, u32[]{:S(2)}) copy-start(bf16[192,768]{1,0:T(8,128)(2,1)} %own_weight.1) | copy-start | bytes 884740
  6.5 6.2 %collective-permute-start = (bf16[384,128]{1,0:T(8,128)(2,1)S(1)}, bf16[384,128]{1,0:T(8,128)(2,1)S(1)}, u32[]{:S(2)}, u32[]{:S(2)}) collective-permute-start(bf16[384,128]{1,0:T(8,128)(2,1)S(1)} %get-tuple-element.21.own), channel_id=1, source_target_pairs={{0,2},{1,3},{2,0},{3,1},{4,6},{5,7},{6,4},{7,5},{8,10},{9,11},{10,... | collective-permute-start | bytes 294920 | tf_op jit(solution)/shard_map/ppermute | solution.py:262
  6.5 6.7 %collective-permute-start.2 = (bf16[384,128]{1,0:T(8,128)(2,1)S(1)}, bf16[384,128]{1,0:T(8,128)(2,1)S(1)}, u32[]{:S(2)}, u32[]{:S(2)}) collective-permute-start(bf16[384,128]{1,0:T(8,128)(2,1)S(1)} %get-tuple-element.23), channel_id=1, source_target_pairs={{0,16},{4,20},{8,24},{12,28},{16,0},{20,4},{24,8},{28,12},{1,17},{... | collective-permute-start | bytes 294920 | tf_op jit(solution)/shard_map/ppermute | solution.py:265
  9.6 4.8 %collective-permute-start.3 = (bf16[384,128]{1,0:T(8,128)(2,1)S(1)}, bf16[384,128]{1,0:T(8,128)(2,1)S(1)}, u32[]{:S(2)}, u32[]{:S(2)}) collective-permute-start(bf16[384,128]{1,0:T(8,128)(2,1)S(1)} %get-tuple-element.24), channel_id=1, source_target_pairs={{0,8},{4,12},{8,0},{12,4},{16,24},{20,28},{24,16},{28,20},{1,9},{5... | collective-permute-start | bytes 294920 | tf_op jit(solution)/shard_map/ppermute | solution.py:265
  11.2 4.6 %collective-permute-start.4 = (bf16[384,128]{1,0:T(8,128)(2,1)S(1)}, bf16[384,128]{1,0:T(8,128)(2,1)S(1)}, u32[]{:S(2)}, u32[]{:S(2)}) collective-permute-start(bf16[384,128]{1,0:T(8,128)(2,1)S(1)} %get-tuple-element.25), channel_id=1, source_target_pairs={{0,4},{4,0},{8,12},{12,8},{16,20},{20,16},{24,28},{28,24},{1,5},{5... | collective-permute-start | bytes 294920 | tf_op jit(solution)/shard_map/ppermute | solution.py:265
  15.8 7.1 %copy-start = (bf16[3,768,192]{1,2,0:T(8,128)(2,1)S(1)}, bf16[3,768,192]{1,2,0:T(8,128)(2,1)}, u32[]{:S(2)}) copy-start(bf16[3,768,192]{1,2,0:T(8,128)(2,1)} %param.11) | copy-start | bytes 2654212
  16.4 6.5 %collective-permute-start.5 = (bf16[448,768]{1,0:T(8,128)(2,1)S(1)}, bf16[448,768]{1,0:T(8,128)(2,1)S(1)}, u32[]{:S(2)}, u32[]{:S(2)}) collective-permute-start(bf16[448,768]{1,0:T(8,128)(2,1)S(1)} %get-tuple-element.27), channel_id=1, source_target_pairs={{0,1},{1,0},{2,3},{3,2},{4,5},{5,4},{6,7},{7,6},{8,9},{9,8},{10,11... | collective-permute-start | bytes 2064392 | tf_op jit(solution)/shard_map/ppermute | solution.py:262
  16.4 6.4 %copy-start.3 = (f32[3,768]{1,0:T(4,128)S(1)}, f32[3,768]{1,0:T(4,128)}, u32[]{:S(2)}) copy-start(f32[3,768]{1,0:T(4,128)} %gains.3) | copy-start | bytes 27652
  16.5 9.5 %collective-permute-start.11 = (bf16[192,768]{1,0:T(8,128)(2,1)S(1)}, bf16[192,768]{1,0:T(8,128)(2,1)S(1)}, u32[]{:S(2)}, u32[]{:S(2)}) collective-permute-start(bf16[192,768]{1,0:T(8,128)(2,1)S(1)} %cross_output_rows.1), channel_id=1, source_target_pairs={{0,2},{1,3},{2,0},{3,1},{4,6},{5,7},{6,4},{7,5},{8,10},{9,11},{10,... | collective-permute-start | bytes 884744 | tf_op jit(solution)/shard_map/ppermute | solution.py:262
  18.1 8.0 %collective-permute-start.6 = (bf16[384,128]{1,0:T(8,128)(2,1)S(1)}, bf16[384,128]{1,0:T(8,128)(2,1)S(1)}, u32[]{:S(2)}, u32[]{:S(2)}) collective-permute-start(bf16[384,128]{1,0:T(8,128)(2,1)S(1)} %get-tuple-element.31), channel_id=1, source_target_pairs={{0,24},{4,28},{8,16},{12,20},{16,8},{20,12},{24,0},{28,4},{1,25},{... | collective-permute-start | bytes 294920 | tf_op jit(solution)/shard_map/ppermute | solution.py:265
  19.8 8.1 %collective-permute-start.7 = (bf16[384,128]{1,0:T(8,128)(2,1)S(1)}, bf16[384,128]{1,0:T(8,128)(2,1)S(1)}, u32[]{:S(2)}, u32[]{:S(2)}) collective-permute-start(bf16[384,128]{1,0:T(8,128)(2,1)S(1)} %get-tuple-element.32), channel_id=1, source_target_pairs={{0,28},{4,8},{8,4},{12,16},{16,12},{20,24},{24,20},{28,0},{1,29},{... | collective-permute-start | bytes 294920 | tf_op jit(solution)/shard_map/ppermute | solution.py:265
  26.1 8.1 %collective-permute-start.12 = (bf16[192,768]{1,0:T(8,128)(2,1)S(1)}, bf16[192,768]{1,0:T(8,128)(2,1)S(1)}, u32[]{:S(2)}, u32[]{:S(2)}) collective-permute-start(bf16[192,768]{1,0:T(8,128)(2,1)S(1)} %cross_output_far_rows.1), channel_id=1, source_target_pairs={{0,1},{1,0},{2,3},{3,2},{4,5},{5,4},{6,7},{7,6},{8,9},{9,8},{10,11... | collective-permute-start | bytes 884744 | tf_op jit(solution)/shard_map/ppermute | solution.py:262
  28.8 1.9 %collective-permute-start.8 = (bf16[5,48,128]{2,1,0:T(8,128)(2,1)S(1)}, bf16[5,48,128]{2,1,0:T(8,128)(2,1)S(1)}, u32[]{:S(2)}, u32[]{:S(2)}) collective-permute-start(bf16[5,48,128]{2,1,0:T(8,128)(2,1)S(1)} %get-tuple-element.34), channel_id=1, source_target_pairs={{0,1},{1,0},{2,3},{3,2},{4,5},{5,4},{6,7},{7,6},{8,9},{9,8},{10,11... | collective-permute-start | bytes 184328 | tf_op jit(solution)/shard_map/ppermute | solution.py:262
  28.9 4.9 %collective-permute-start.9 = (bf16[5,48,128]{2,1,0:T(8,128)(2,1)S(1)}, bf16[5,48,128]{2,1,0:T(8,128)(2,1)S(1)}, u32[]{:S(2)}, u32[]{:S(2)}) collective-permute-start(bf16[5,48,128]{2,1,0:T(8,128)(2,1)S(1)} %get-tuple-element.35), channel_id=1, source_target_pairs={{0,2},{1,3},{2,0},{3,1},{4,6},{5,7},{6,4},{7,5},{8,10},{9,11},{10,... | collective-permute-start | bytes 184328 | tf_op jit(solution)/shard_map/ppermute | solution.py:262
  29.5 4.7 %collective-permute-start.10 = (bf16[5,48,128]{2,1,0:T(8,128)(2,1)S(1)}, bf16[5,48,128]{2,1,0:T(8,128)(2,1)S(1)}, u32[]{:S(2)}, u32[]{:S(2)}) collective-permute-start(bf16[5,48,128]{2,1,0:T(8,128)(2,1)S(1)} %get-tuple-element.36), channel_id=1, source_target_pairs={{0,3},{1,2},{2,1},{3,0},{4,7},{5,6},{6,5},{7,4},{8,11},{9,10},{10,... | collective-permute-start | bytes 184328 | tf_op jit(solution)/shard_map/ppermute | solution.py:262

commit v5 on v3

--- a/solution.py
+++ b/solution.py
@@ -12,7 +12,7 @@
 F32 = jnp.float32
 BF16 = jnp.bfloat16
 VMEM_BYTES = 24 * 1024 * 1024
-EARLY_WEIGHT = 3 * 10**9
+EARLY_WEIGHT = 10**11
 LATE_WEIGHT = 10**11
 
 VMEM = pl.BlockSpec(memory_space=pltpu.VMEM)
@@ -145,25 +145,18 @@
     )
 
 
-def partial_kernel(states, own, got, own_weight, got_weight, cross_out, base, sent, weight_v, sems):
+def partial_kernel(states, own, got, own_weight, got_weight, cross_out, base, sent, sem):
     row_all = base.shape[0]
-    copies = [
-        pltpu.make_async_copy(got_weight, weight_v, sems.at[0]),
-        pltpu.make_async_copy(cross_out, sent.at[pl.ds(row_all, cross_out.shape[0])], sems.at[1]),
-    ]
-    for copy in copies:
-        copy.start()
-    part = nn(unpack(own[...]), own_weight[...])
-    base[...] = states[...].reshape(part.shape).astype(F32)
-    copies[0].wait()
-    part = part + nn(unpack(got[...]), weight_v[...])
+    copy = pltpu.make_async_copy(cross_out, sent.at[pl.ds(row_all, cross_out.shape[0])], sem)
+    copy.start()
+    rows = jnp.concatenate([unpack(own[...]), unpack(got[...])], 1)
+    part = nn(rows, jnp.concatenate([own_weight[...], got_weight[...]], 0))
     sent[:row_all, :] = part.astype(BF16)
-    base[...] += part
-    copies[1].wait()
-
-
-def query_kernel(helper_n, base, got, gains, proj_t, *rest):
-    own_rows, queries_out, weight_out, mixed_ref, sem = rest[-5:]
+    base[...] = states[...].reshape(part.shape).astype(F32) + part
+    copy.wait()
+
+
+def query_kernel(helper_n, base, got, gains, proj_t, own_rows, queries_out, weight_out, mixed_ref, sem):
     copy = pltpu.make_async_copy(got.at[pl.ds(base.shape[0], weight_out.shape[0])], weight_out, sem)
     copy.start()
     mixed = base[...] + got[: base.shape[0], :].astype(F32)
@@ -178,8 +171,8 @@
     copy.wait()
 
 
-def hand_on_kernel(weight, waited, out, sem):
-    del waited
+def hand_on_kernel(weight, *rest):
+    out, sem = rest[-2:]
     copy = pltpu.make_async_copy(weight, out, sem)
     copy.start()
     copy.wait()
@@ -316,40 +309,43 @@
     )
     context_got = across(context, chip_hop)
     arrived = [exchange(value, swap) for value, swap in zip(outgoing, swaps)]
+    near = (slot_n - 1) // 2
     late = [at for at, (_, colour) in enumerate(swaps) if colour]
     early = [at for at in range(pair_n) if at not in late]
+    short = [2 * near - 2, 2 * near - 1]
+    before = [context_got, self_out_got] + [arrived[at] for at in short]
     cross_out_sent = call(
         "cross_output_rows",
         hand_on_kernel,
         shape(cross_out.shape, BF16),
-        [ANY, ANY],
+        [ANY] * (1 + len(before)),
         [dma],
-        cross_out_own, context_got,
+        cross_out_own, *before,
     )
     cross_out_got = across(cross_out_sent, chip_hop)
 
-    base, sent = call(
-        "self_output_share",
-        partial_kernel,
-        [shape((row_all, width), F32), shape((row_all + columns, width), BF16)],
-        [VMEM] * 4 + [ANY, ANY],
-        [pltpu.VMEM(self_out.shape, BF16), dma((2,))],
-        states, context, context_got, self_out, self_out_got, cross_out_own,
-    )
     made_shapes = [
         shape((image_n, row_n, width), F32),
         shape((image_n, patch_n, columns), F32),
         shape(cross_out.shape, BF16),
     ]
 
-    def mixing(base, sent, gains, cross_proj_t, *waited):
+    def mixing(states, gains, cross_proj_t, context, context_got, self_out, self_out_got, cross_out):
+        base, sent = call(
+            "self_output_share",
+            partial_kernel,
+            [shape((row_all, width), F32), shape((row_all + columns, width), BF16)],
+            [VMEM] * 5 + [ANY],
+            [dma],
+            states, context, context_got, self_out, self_out_got, cross_out,
+        )
         made = call(
             "mixed_and_queries",
             functools.partial(query_kernel, helper_n),
             made_shapes,
-            [VMEM] * 4 + [ANY] * len(waited),
+            [VMEM] * 4,
             [pltpu.VMEM((image_n, patch_n, width), F32), dma],
-            base, across(sent, core_hop), gains, cross_proj_t, *waited,
+            base, across(sent, core_hop), gains, cross_proj_t,
         )
         return tuple(made)
 
@@ -358,7 +354,7 @@
 
     own_rows, queries, cross_out_core = lax.cond(
         lax.axis_index("owner") < owner_n, mixing, no_images,
-        base, sent, gains, cross_proj_t, *[arrived[at] for at in early],
+        states, gains, cross_proj_t, context, context_got, self_out, self_out_got, cross_out_own,
     )
     packed = columns * row_n // LANES
     early_sides = call(

time: 35.9 us -> 35.1 us (0.978)
  Pallas kernels: 11.7 us -> 11.3 us
    pallas_call x7, Pallas kernels: 11.7 us -> 11.3 us  [call(): pl.pallas_call(kernel, out_shape=out_shape, in_specs=in_specs, out_specs=...]
  transfers between devices with their start and end apart: 13 -> 13, of which waited for: 3 -> 3; matrix products, arithmetic and copies ran while one was open for 0% -> 0% of each run, Pallas kernels for 28% -> 27%
where the time goes in v5:
time: 35.1 us; the launch traced here: 34.9 us
  starting transfers between devices  17.8 us (51%)
  Pallas kernels  11.3 us (32%)
  waiting for transfers between devices  5.62 us (16%)
    pallas_call x7, Pallas kernels, call(): pl.pallas_call(kernel, out_shape=out_shape, in_specs=in_specs, out_specs=...  11.3 us
    ppermute x5, starting transfers between devices, exchange(): lax.ppermute(value, 'owner', [(o, swap_target(o, swap, owner_n)) for o in...  10.7 us
    ppermute x8, starting transfers between devices, across(): return lax.ppermute(value, 'helper', [(j, j ^ k) for j in range(helper_n)])  7.12 us
    ppermute x8, waiting for transfers between devices, across(): return lax.ppermute(value, 'helper', [(j, j ^ k) for j in range(helper_n)])  5.61 us
  transfers between devices with their start and end apart: 13, of which 3 were waited for; matrix products, arithmetic and copies ran while one was open for 0% of the time, Pallas kernels for 27%

profile of v5, /device:TPU:0, one launch (start us, length us, event | category | flops | bytes accessed | tf_op | source)
XLA Modules:
  0.0 34.9 jit_solution(10861635609377450357)
XLA Ops:
  0.0 3.0 %collective-permute-start.2 = (bf16[192,768]{1,0:T(8,128)(2,1)}, bf16[192,768]{1,0:T(8,128)(2,1)S(1)}, u32[]{:S(2)}, u32[]{:S(2)}) collective-permute-start(bf16[192,768]{1,0:T(8,128)(2,1)} %param.12), channel_id=1, source_target_pairs={{0,2},{1,3},{2,0},{3,1},{4,6},{5,7},{6,4},{7,5},{8,10},{9,11},{10,... | collective-permute-start | bytes 884744 | tf_op jit(solution)/shard_map/ppermute | solution.py:263
  3.0 3.5 %own_images.1 = (bf16[384,128]{1,0:T(8,128)(2,1)S(1)}, bf16[384,128]{1,0:T(8,128)(2,1)S(1)}, bf16[384,128]{1,0:T(8,128)(2,1)S(1)}, bf16[384,128]{1,0:T(8,128)(2,...) custom-call(bf16[2,128,768]{2,1,0:T(8,128)(2,1)} %states.1, ...), custom_call_target="tpu_custom_call" | custom-call | flops 1 | bytes 1 | tf_op jit(solution)/shard_map/own_images/pallas_call | solution.py:270
  6.5 0.0 copy-start
  6.5 0.1 collective-permute-start.1
  6.6 2.1 %collective-permute-start.4 = (bf16[384,128]{1,0:T(8,128)(2,1)S(1)}, bf16[384,128]{1,0:T(8,128)(2,1)S(1)}, u32[]{:S(2)}, u32[]{:S(2)}) collective-permute-start(bf16[384,128]{1,0:T(8,128)(2,1)S(1)} %get-tuple-element.52), channel_id=1, source_target_pairs={{0,8},{4,12},{8,0},{12,4},{16,24},{20,28},{24,16},{28,20},{1,9},{5... | collective-permute-start | bytes 294920 | tf_op jit(solution)/shard_map/ppermute | solution.py:266
  8.6 1.5 %collective-permute-start.5 = (bf16[384,128]{1,0:T(8,128)(2,1)S(1)}, bf16[384,128]{1,0:T(8,128)(2,1)S(1)}, u32[]{:S(2)}, u32[]{:S(2)}) collective-permute-start(bf16[384,128]{1,0:T(8,128)(2,1)S(1)} %get-tuple-element.53), channel_id=1, source_target_pairs={{0,4},{4,0},{8,12},{12,8},{16,20},{20,16},{24,28},{28,24},{1,5},{5... | collective-permute-start | bytes 294920 | tf_op jit(solution)/shard_map/ppermute | solution.py:266
  10.1 2.6 %collective-permute-start.3 = (bf16[384,128]{1,0:T(8,128)(2,1)S(1)}, bf16[384,128]{1,0:T(8,128)(2,1)S(1)}, u32[]{:S(2)}, u32[]{:S(2)}) collective-permute-start(bf16[384,128]{1,0:T(8,128)(2,1)S(1)} %get-tuple-element.51), channel_id=1, source_target_pairs={{0,16},{4,20},{8,24},{12,28},{16,0},{20,4},{24,8},{28,12},{1,17},{... | collective-permute-start | bytes 294920 | tf_op jit(solution)/shard_map/ppermute | solution.py:266
  12.7 0.0 collective-permute-done.1.rest_0_
  12.7 3.4 %collective-permute-start.6 = (bf16[384,128]{1,0:T(8,128)(2,1)S(1)}, bf16[384,128]{1,0:T(8,128)(2,1)S(1)}, u32[]{:S(2)}, u32[]{:S(2)}) collective-permute-start(bf16[384,128]{1,0:T(8,128)(2,1)S(1)} %get-tuple-element.54), channel_id=1, source_target_pairs={{0,24},{4,28},{8,16},{12,20},{16,8},{20,12},{24,0},{28,4},{1,25},{... | collective-permute-start | bytes 294920 | tf_op jit(solution)/shard_map/ppermute | solution.py:266
  16.1 0.0 collective-permute-done.4.rest_1_.rest_2_
  16.1 1.1 %collective-permute-start.7 = (bf16[384,128]{1,0:T(8,128)(2,1)S(1)}, bf16[384,128]{1,0:T(8,128)(2,1)S(1)}, u32[]{:S(2)}, u32[]{:S(2)}) collective-permute-start(bf16[384,128]{1,0:T(8,128)(2,1)S(1)} %get-tuple-element.55), channel_id=1, source_target_pairs={{0,28},{4,8},{8,4},{12,16},{16,12},{20,24},{24,20},{28,0},{1,29},{... | collective-permute-start | bytes 294920 | tf_op jit(solution)/shard_map/ppermute | solution.py:266
  17.3 0.0 collective-permute-done.5.rest_2_.rest_3_
  17.3 0.0 collective-permute-done.2.rest_1_
  17.3 0.1 cross_output_rows.1
  17.4 1.6 %collective-permute-start.11 = (bf16[192,768]{1,0:T(8,128)(2,1)S(1)}, bf16[192,768]{1,0:T(8,128)(2,1)S(1)}, u32[]{:S(2)}, u32[]{:S(2)}) collective-permute-start(bf16[192,768]{1,0:T(8,128)(2,1)S(1)} %cross_output_rows.1), channel_id=1, source_target_pairs={{0,2},{1,3},{2,0},{3,1},{4,6},{5,7},{6,4},{7,5},{8,10},{9,11},{10,... | collective-permute-start | bytes 884744 | tf_op jit(solution)/shard_map/ppermute | solution.py:263
  19.0 5.1 %conditional.1 = ((f32[2,32,768]{2,1,0:T(8,128)}, f32[2,128,192]{2,1,0:T(8,128)}, bf16[192,768]{1,0:T(8,128)(2,1)})) conditional(s32[]{:T(128)} %convert_element_type.3, () %tuple.12, (bf16[2,128,768]{2,1,0:T(8,128)(2,1)S(1)}, bf16[384,128]{1,0:T(8,128)(2,1)S(1)}, bf16[384,128]{1,0:T(8,128)(2,1)S(1)}, bf16[192,768]{1,0:T(8,128)(2,1)}, ...), branch_computations={%region_0.0_spmd, %region_1.0_spmd} | conditional | flops 2 | bytes 2752562 | solution.py:355
  19.0 1.5 %self_output_share.1 = (f32[256,768]{1,0:T(8,128)S(1)}, bf16[448,768]{1,0:T(8,128)(2,1)S(1)}) custom-call(bf16[2,128,768]{2,1,0:T(8,128)(2,1)S(1)} %get-tuple-element.21.states, bf16[384,128]{1,0:T(8,128)(2,1)S(1)} %get-tuple-element.22.own, bf16[384,128]{1,0:T(8,128)(2,1)S(1)} %get-tuple-element.23.got, bf16[192,768]{1,0:T(8,128)(2,1)} %get-tuple-element.24.own_weight, ...), custom_call_target="tpu_custom_call" | custom-call | flops 1 | bytes 1 | tf_op jit(solution)/shard_map/cond/branch_1_fun/self_output_share/pallas_call | solution.py:270
  20.5 0.1 collective-permute-start
  20.5 2.1 %collective-permute-done.got = bf16[448,768]{1,0:T(8,128)(2,1)S(1)} collective-permute-done((bf16[448,768]{1,0:T(8,128)(2,1)S(1)}, bf16[448,768]{1,0:T(8,128)(2,1)S(1)}, u32[]{:S(2)}, u32[]{:S(2)}) %collective-permute-start) | collective-permute-done | bytes 688160 | tf_op jit(solution)/shard_map/cond/branch_1_fun/ppermute | solution.py:263
  22.7 1.4 %mixed_and_queries.1 = (f32[2,32,768]{2,1,0:T(8,128)}, f32[2,128,192]{2,1,0:T(8,128)}, bf16[192,768]{1,0:T(8,128)(2,1)}) custom-call(f32[256,768]{1,0:T(8,128)S(1)} %get-tuple-element.27.base, bf16[448,768]{1,0:T(8,128)(2,1)S(1)} %collective-permute-done.got, f32[3,768]{1,0:T(4,128)S(1)} %get-tuple-element.29.gains, ...), custom_call_target="tpu_custom_call" | custom-call | flops 1 | bytes 1 | tf_op jit(solution)/shard_map/cond/branch_1_fun/mixed_and_queries/pallas_call | solution.py:270
  24.1 2.1 %early_cross_attention.1.before = bf16[4,3,48,128]{3,2,1,0:T(8,128)(2,1)S(1)} custom-call(f32[2,128,192]{2,1,0:T(8,128)} %get-tuple-element.49.queries, s32[5,128]{1,0:T(8,128)S(1)} %get-tuple-element.50.table, bf16[384,128]{1,0:T(8,128)(2,1)S(1)} %collective-permute-done.3.rest_0_, bf16[384,128]{1,0:T(8,128)(2,1)S(1)} %collective-permute-done.4.rest_1_.rest_2_, ...), custom_call_target="tpu_custom_call" | custom-call | flops 99999997952 | bytes 1 | tf_op jit(solution)/shard_map/early_cross_attention/pallas_call | solution.py:270
  26.2 0.0 collective-permute-done.11.rest_6_
  26.2 0.2 collective-permute-start.12
  26.4 0.0 collective-permute-done.6.rest_0_
  26.4 0.0 collective-permute-done.7.rest_1_
  26.4 0.9 %late_cross_attention.1 = (bf16[5,48,128]{2,1,0:T(8,128)(2,1)S(1)}, bf16[5,48,128]{2,1,0:T(8,128)(2,1)S(1)}, bf16[5,48,128]{2,1,0:T(8,128)(2,1)S(1)}, bf16[5,48,128]{2,1,0:T(8,128)(2,1)S(1)}) custom-call(f32[2,128,192]{2,1,0:T(8,128)S(1)} %copy-done.6, s32[5,128]{1,0:T(8,128)S(1)} %get-tuple-element.50.table, ...), custom_call_target="tpu_custom_call" | custom-call | flops 99999997952 | bytes 1 | tf_op jit(solution)/shard_map/late_cross_attention/pallas_call | solution.py:270
  27.3 0.6 %collective-permute-start.10 = (bf16[5,48,128]{2,1,0:T(8,128)(2,1)S(1)}, bf16[5,48,128]{2,1,0:T(8,128)(2,1)S(1)}, u32[]{:S(2)}, u32[]{:S(2)}) collective-permute-start(bf16[5,48,128]{2,1,0:T(8,128)(2,1)S(1)} %get-tuple-element.59), channel_id=1, source_target_pairs={{0,3},{1,2},{2,1},{3,0},{4,7},{5,6},{6,5},{7,4},{8,11},{9,10},{10,... | collective-permute-start | bytes 184328 | tf_op jit(solution)/shard_map/ppermute | solution.py:263
  27.9 0.2 collective-permute-start.8
  28.0 1.5 %collective-permute-start.9 = (bf16[5,48,128]{2,1,0:T(8,128)(2,1)S(1)}, bf16[5,48,128]{2,1,0:T(8,128)(2,1)S(1)}, u32[]{:S(2)}, u32[]{:S(2)}) collective-permute-start(bf16[5,48,128]{2,1,0:T(8,128)(2,1)S(1)} %get-tuple-element.58), channel_id=1, source_target_pairs={{0,2},{1,3},{2,0},{3,1},{4,6},{5,7},{6,4},{7,5},{8,10},{9,11},{10,... | collective-permute-start | bytes 184328 | tf_op jit(solution)/shard_map/ppermute | solution.py:263
  29.5 1.7 %collective-permute-done.10.rest_3_ = bf16[5,48,128]{2,1,0:T(8,128)(2,1)S(1)} collective-permute-done((bf16[5,48,128]{2,1,0:T(8,128)(2,1)S(1)}, bf16[5,48,128]{2,1,0:T(8,128)(2,1)S(1)}, u32[]{:S(2)}, u32[]{:S(2)}) %collective-permute-start.10) | collective-permute-done | bytes 61472 | tf_op jit(solution)/shard_map/ppermute | solution.py:263
  31.2 1.8 %collective-permute-done.9.rest_2_ = bf16[5,48,128]{2,1,0:T(8,128)(2,1)S(1)} collective-permute-done((bf16[5,48,128]{2,1,0:T(8,128)(2,1)S(1)}, bf16[5,48,128]{2,1,0:T(8,128)(2,1)S(1)}, u32[]{:S(2)}, u32[]{:S(2)}) %collective-permute-start.9) | collective-permute-done | bytes 61472 | tf_op jit(solution)/shard_map/ppermute | solution.py:263
  33.0 1.9 %pair_output.1 = bf16[2,5,32,768]{3,2,1,0:T(8,128)(2,1)} custom-call(s32[2,5]{1,0:T(2,128)} %partners.3, f32[2,32,768]{2,1,0:T(8,128)S(1)} %copy-done.5, bf16[5,48,128]{2,1,0:T(8,128)(2,1)S(1)} %get-tuple-element.56.rest_0_, bf16[5,48,128]{2,1,0:T(8,128)(2,1)S(1)} %collective-permute-done.8.rest_1_, bf16[5,48,128]{2,1,0:T(8,128)(2,1)S(1)} %collective-permute-done.9.rest_2_, ...), custom_call_target="tpu_custom_call" | custom-call | flops 1 | bytes 1 | tf_op jit(solution)/shard_map/pair_output/pallas_call | solution.py:270
  (18 shorter events, 0.0 us)
Async XLA Ops:
  0.0 17.3 %collective-permute-start.2 = (bf16[192,768]{1,0:T(8,128)(2,1)}, bf16[192,768]{1,0:T(8,128)(2,1)S(1)}, u32[]{:S(2)}, u32[]{:S(2)}) collective-permute-start(bf16[192,768]{1,0:T(8,128)(2,1)} %param.12), channel_id=1, source_target_pairs={{0,2},{1,3},{2,0},{3,1},{4,6},{5,7},{6,4},{7,5},{8,10},{9,11},{10,... | collective-permute-start | bytes 884744 | tf_op jit(solution)/shard_map/ppermute | solution.py:263
  3.0 16.0 %copy-start.3 = (bf16[2,128,768]{2,1,0:T(8,128)(2,1)S(1)}, bf16[2,128,768]{2,1,0:T(8,128)(2,1)}, u32[]{:S(2)}) copy-start(bf16[2,128,768]{2,1,0:T(8,128)(2,1)} %states.1) | copy-start | bytes 1179652
  6.5 12.5 %copy-start.1 = (bf16[192,768]{1,0:T(8,128)(2,1)}, bf16[192,768]{1,0:T(8,128)(2,1)S(1)}, u32[]{:S(2)}) copy-start(bf16[192,768]{1,0:T(8,128)(2,1)S(1)} %get-tuple-element.47.weight.rest_4_) | copy-start | bytes 884740
  6.5 12.5 %copy-start = (bf16[3,768,192]{1,2,0:T(8,128)(2,1)S(1)}, bf16[3,768,192]{1,2,0:T(8,128)(2,1)}, u32[]{:S(2)}) copy-start(bf16[3,768,192]{1,2,0:T(8,128)(2,1)} %param.13) | copy-start | bytes 2654212
  6.5 6.2 %collective-permute-start.1 = (bf16[384,128]{1,0:T(8,128)(2,1)S(1)}, bf16[384,128]{1,0:T(8,128)(2,1)S(1)}, u32[]{:S(2)}, u32[]{:S(2)}) collective-permute-start(bf16[384,128]{1,0:T(8,128)(2,1)S(1)} %get-tuple-element.46), channel_id=1, source_target_pairs={{0,2},{1,3},{2,0},{3,1},{4,6},{5,7},{6,4},{7,5},{8,10},{9,11},{10,... | collective-permute-start | bytes 294920 | tf_op jit(solution)/shard_map/ppermute | solution.py:263
  6.6 9.5 %collective-permute-start.4 = (bf16[384,128]{1,0:T(8,128)(2,1)S(1)}, bf16[384,128]{1,0:T(8,128)(2,1)S(1)}, u32[]{:S(2)}, u32[]{:S(2)}) collective-permute-start(bf16[384,128]{1,0:T(8,128)(2,1)S(1)} %get-tuple-element.52), channel_id=1, source_target_pairs={{0,8},{4,12},{8,0},{12,4},{16,24},{20,28},{24,16},{28,20},{1,9},{5... | collective-permute-start | bytes 294920 | tf_op jit(solution)/shard_map/ppermute | solution.py:266
  8.6 8.6 %collective-permute-start.5 = (bf16[384,128]{1,0:T(8,128)(2,1)S(1)}, bf16[384,128]{1,0:T(8,128)(2,1)S(1)}, u32[]{:S(2)}, u32[]{:S(2)}) collective-permute-start(bf16[384,128]{1,0:T(8,128)(2,1)S(1)} %get-tuple-element.53), channel_id=1, source_target_pairs={{0,4},{4,0},{8,12},{12,8},{16,20},{20,16},{24,28},{28,24},{1,5},{5... | collective-permute-start | bytes 294920 | tf_op jit(solution)/shard_map/ppermute | solution.py:266
  10.1 14.0 %collective-permute-start.3 = (bf16[384,128]{1,0:T(8,128)(2,1)S(1)}, bf16[384,128]{1,0:T(8,128)(2,1)S(1)}, u32[]{:S(2)}, u32[]{:S(2)}) collective-permute-start(bf16[384,128]{1,0:T(8,128)(2,1)S(1)} %get-tuple-element.51), channel_id=1, source_target_pairs={{0,16},{4,20},{8,24},{12,28},{16,0},{20,4},{24,8},{28,12},{1,17},{... | collective-permute-start | bytes 294920 | tf_op jit(solution)/shard_map/ppermute | solution.py:266
  12.7 13.7 %collective-permute-start.6 = (bf16[384,128]{1,0:T(8,128)(2,1)S(1)}, bf16[384,128]{1,0:T(8,128)(2,1)S(1)}, u32[]{:S(2)}, u32[]{:S(2)}) collective-permute-start(bf16[384,128]{1,0:T(8,128)(2,1)S(1)} %get-tuple-element.54), channel_id=1, source_target_pairs={{0,24},{4,28},{8,16},{12,20},{16,8},{20,12},{24,0},{28,4},{1,25},{... | collective-permute-start | bytes 294920 | tf_op jit(solution)/shard_map/ppermute | solution.py:266
  16.1 10.3 %collective-permute-start.7 = (bf16[384,128]{1,0:T(8,128)(2,1)S(1)}, bf16[384,128]{1,0:T(8,128)(2,1)S(1)}, u32[]{:S(2)}, u32[]{:S(2)}) collective-permute-start(bf16[384,128]{1,0:T(8,128)(2,1)S(1)} %get-tuple-element.55), channel_id=1, source_target_pairs={{0,28},{4,8},{8,4},{12,16},{16,12},{20,24},{24,20},{28,0},{1,29},{... | collective-permute-start | bytes 294920 | tf_op jit(solution)/shard_map/ppermute | solution.py:266
  17.3 1.7 %copy-start.7 = (f32[3,768]{1,0:T(4,128)S(1)}, f32[3,768]{1,0:T(4,128)}, u32[]{:S(2)}) copy-start(f32[3,768]{1,0:T(4,128)} %gains.1) | copy-start | bytes 27652
  17.4 8.9 %collective-permute-start.11 = (bf16[192,768]{1,0:T(8,128)(2,1)S(1)}, bf16[192,768]{1,0:T(8,128)(2,1)S(1)}, u32[]{:S(2)}, u32[]{:S(2)}) collective-permute-start(bf16[192,768]{1,0:T(8,128)(2,1)S(1)} %cross_output_rows.1), channel_id=1, source_target_pairs={{0,2},{1,3},{2,0},{3,1},{4,6},{5,7},{6,4},{7,5},{8,10},{9,11},{10,... | collective-permute-start | bytes 884744 | tf_op jit(solution)/shard_map/ppermute | solution.py:263
  20.5 2.2 %collective-permute-start = (bf16[448,768]{1,0:T(8,128)(2,1)S(1)}, bf16[448,768]{1,0:T(8,128)(2,1)S(1)}, u32[]{:S(2)}, u32[]{:S(2)}) collective-permute-start(bf16[448,768]{1,0:T(8,128)(2,1)S(1)} %get-tuple-element.28), channel_id=1, source_target_pairs={{0,1},{1,0},{2,3},{3,2},{4,5},{5,4},{6,7},{7,6},{8,9},{9,8},{10,11... | collective-permute-start | bytes 2064392 | tf_op jit(solution)/shard_map/cond/branch_1_fun/ppermute | solution.py:263
  24.1 2.3 %copy-start.6 = (f32[2,128,192]{2,1,0:T(8,128)S(1)}, f32[2,128,192]{2,1,0:T(8,128)}, u32[]{:S(2)}) copy-start(f32[2,128,192]{2,1,0:T(8,128)} %get-tuple-element.49.queries) | copy-start | bytes 589828
  26.2 6.8 %copy-start.2 = (bf16[192,768]{1,0:T(8,128)(2,1)S(1)}, bf16[192,768]{1,0:T(8,128)(2,1)}, u32[]{:S(2)}) copy-start(bf16[192,768]{1,0:T(8,128)(2,1)} %copy-done.1) | copy-start | bytes 884740
  26.2 6.8 %copy-start.4 = (bf16[192,768]{1,0:T(8,128)(2,1)S(1)}, bf16[192,768]{1,0:T(8,128)(2,1)}, u32[]{:S(2)}) copy-start(bf16[192,768]{1,0:T(8,128)(2,1)} %get-tuple-element.60.rest_5_) | copy-start | bytes 884740
  26.2 6.8 %copy-start.5 = (f32[2,32,768]{2,1,0:T(8,128)S(1)}, f32[2,32,768]{2,1,0:T(8,128)}, u32[]{:S(2)}) copy-start(f32[2,32,768]{2,1,0:T(8,128)} %get-tuple-element.48.own_rows) | copy-start | bytes 589828
  26.2 6.8 %collective-permute-start.12 = (bf16[192,768]{1,0:T(8,128)(2,1)S(1)}, bf16[192,768]{1,0:T(8,128)(2,1)S(1)}, u32[]{:S(2)}, u32[]{:S(2)}) collective-permute-start(bf16[192,768]{1,0:T(8,128)(2,1)S(1)} %collective-permute-done.11.rest_6_), channel_id=1, source_target_pairs={{0,1},{1,0},{2,3},{3,2},{4,5},{5,4},{6,7},{7,6},{8,9},{9,8},{10,11... | collective-permute-start | bytes 884744 | tf_op jit(solution)/shard_map/ppermute | solution.py:263
  27.3 3.9 %collective-permute-start.10 = (bf16[5,48,128]{2,1,0:T(8,128)(2,1)S(1)}, bf16[5,48,128]{2,1,0:T(8,128)(2,1)S(1)}, u32[]{:S(2)}, u32[]{:S(2)}) collective-permute-start(bf16[5,48,128]{2,1,0:T(8,128)(2,1)S(1)} %get-tuple-element.59), channel_id=1, source_target_pairs={{0,3},{1,2},{2,1},{3,0},{4,7},{5,6},{6,5},{7,4},{8,11},{9,10},{10,... | collective-permute-start | bytes 184328 | tf_op jit(solution)/shard_map/ppermute | solution.py:263
  27.9 3.3 %collective-permute-start.8 = (bf16[5,48,128]{2,1,0:T(8,128)(2,1)S(1)}, bf16[5,48,128]{2,1,0:T(8,128)(2,1)S(1)}, u32[]{:S(2)}, u32[]{:S(2)}) collective-permute-start(bf16[5,48,128]{2,1,0:T(8,128)(2,1)S(1)} %get-tuple-element.57), channel_id=1, source_target_pairs={{0,1},{1,0},{2,3},{3,2},{4,5},{5,4},{6,7},{7,6},{8,9},{9,8},{10,11... | collective-permute-start | bytes 184328 | tf_op jit(solution)/shard_map/ppermute | solution.py:263
  28.0 5.0 %collective-permute-start.9 = (bf16[5,48,128]{2,1,0:T(8,128)(2,1)S(1)}, bf16[5,48,128]{2,1,0:T(8,128)(2,1)S(1)}, u32[]{:S(2)}, u32[]{:S(2)}) collective-permute-start(bf16[5,48,128]{2,1,0:T(8,128)(2,1)S(1)} %get-tuple-element.58), channel_id=1, source_target_pairs={{0,2},{1,3},{2,0},{3,1},{4,6},{5,7},{6,4},{7,5},{8,10},{9,11},{10,... | collective-permute-start | bytes 184328 | tf_op jit(solution)/shard_map/ppermute | solution.py:263

commit v6 on v5

--- a/solution.py
+++ b/solution.py
@@ -96,7 +96,7 @@
 
 def own_images_kernel(swaps, owner_n, states, gains, self_t, cross_t, partners, weight, *rest):
     outs, rest = rest[: len(swaps)], rest[len(swaps) :]
-    context_out, table, weight_out, states_v, gains_v, self_v, cross_v, partners_s, held, sems = rest
+    context_out, table, weight_out, query_weight_out, states_v, gains_v, self_v, cross_v, partners_s, held, sems = rest
     image_n, patch_n, width = states.shape
     columns = self_t.shape[1]
     copies = [
@@ -106,6 +106,7 @@
         pltpu.make_async_copy(partners, partners_s, sems.at[3]),
         pltpu.make_async_copy(self_t, self_v, sems.at[4]),
         pltpu.make_async_copy(weight, weight_out, sems.at[5]),
+        pltpu.make_async_copy(cross_t.at[0], query_weight_out, sems.at[6]),
     ]
     for copy in copies:
         copy.start()
@@ -135,6 +136,7 @@
         )
     context_out[...] = pack(jnp.concatenate(contexts, 0))
     copies[5].wait()
+    copies[6].wait()
 
 
 def unpack(block):
@@ -145,44 +147,47 @@
     )
 
 
-def partial_kernel(states, own, got, own_weight, got_weight, cross_out, base, sent, sem):
-    row_all = base.shape[0]
-    copy = pltpu.make_async_copy(cross_out, sent.at[pl.ds(row_all, cross_out.shape[0])], sem)
-    copy.start()
+def partial_kernel(states, own, got, own_weight, got_weight, base, sent):
     rows = jnp.concatenate([unpack(own[...]), unpack(got[...])], 1)
     part = nn(rows, jnp.concatenate([own_weight[...], got_weight[...]], 0))
-    sent[:row_all, :] = part.astype(BF16)
+    sent[...] = part.astype(BF16)
     base[...] = states[...].reshape(part.shape).astype(F32) + part
-    copy.wait()
-
-
-def query_kernel(helper_n, base, got, gains, proj_t, own_rows, queries_out, weight_out, mixed_ref, sem):
-    copy = pltpu.make_async_copy(got.at[pl.ds(base.shape[0], weight_out.shape[0])], weight_out, sem)
-    copy.start()
-    mixed = base[...] + got[: base.shape[0], :].astype(F32)
+
+
+def query_kernel(helper_n, base, got, gains, weight, own_rows, queries_out, mixed_ref):
+    mixed = base[...] + got[...].astype(F32)
     image_n, row_n, width = own_rows.shape
     patch_n = row_n * helper_n
     mixed_ref[...] = mixed.reshape(image_n, patch_n, width)
     normed = (norm_core(mixed) * gains[1:2, :]).astype(BF16)
-    queries = nt(normed, proj_t[0]).astype(BF16).astype(F32) * HEAD ** (-0.5)
-    queries_out[...] = queries.reshape(queries_out.shape)
+    queries = nt(normed, weight[...]).astype(BF16).astype(F32) * HEAD ** (-0.5)
+    queries_out[...] = queries.reshape(queries_out.shape).astype(BF16)
     start = pl.multiple_of(lax.axis_index("helper") * row_n, row_n)
     own_rows[...] = mixed_ref[:, pl.ds(start, row_n), :]
-    copy.wait()
-
-
-def hand_on_kernel(weight, *rest):
-    out, sem = rest[-2:]
-    copy = pltpu.make_async_copy(weight, out, sem)
-    copy.start()
-    copy.wait()
+
+
+def hand_on_kernel(*refs):
+    del refs
+
+
+def both_kernel(own, got, waited, out, sems):
+    del waited
+    row_n = own.shape[0]
+    copies = [
+        pltpu.make_async_copy(own, out.at[pl.ds(0, row_n)], sems.at[0]),
+        pltpu.make_async_copy(got, out.at[pl.ds(row_n, row_n)], sems.at[1]),
+    ]
+    for copy in copies:
+        copy.start()
+    for copy in copies:
+        copy.wait()
 
 
 def cross_pairs(places, helper_n, queries, table, arrived, put):
     for at, (place, block) in enumerate(zip(places, arrived)):
-        chosen = queries[0]
+        chosen = queries[0].astype(F32)
         for image in range(1, queries.shape[0]):
-            chosen = jnp.where(table[place : place + 1, 0:1] == image, queries[image], chosen)
+            chosen = jnp.where(table[place : place + 1, 0:1] == image, queries[image].astype(F32), chosen)
         columns = block.shape[0] // 2
         context = attend(head_stack(chosen), block[:columns, :], block[columns:, :])
         row_n = context.shape[0] // helper_n
@@ -221,17 +226,15 @@
     return jnp.concatenate([main.reshape(-1, LANES), tail.reshape(-1, HEAD)], 1)
 
 
-def out_kernel(swaps, owner_n, helper_n, partners, own_rows, *rest):
-    sides, rest = rest[:helper_n], rest[helper_n:]
-    weights, rest = rest[:helper_n], rest[helper_n:]
-    out, term_ref, partners_s, sem = rest
+def out_kernel(swaps, owner_n, partners, own_rows, own_weights, core_weights, *rest):
+    *sides, out, term_ref, partners_s, sem = rest
     copy = pltpu.make_async_copy(partners, partners_s, sem)
     copy.start()
     image_n, row_n, width = own_rows.shape
-    terms = None
-    for side, weight in zip(sides, weights):
-        part = nn(side_rows(side[...]), weight[...])
-        terms = part if terms is None else terms + part
+    half = len(sides) // 2
+    rows = [side_rows(side[...]) for side in sides]
+    terms = nn(jnp.concatenate(rows[:half], 1), own_weights[...])
+    terms = terms + nn(jnp.concatenate(rows[half:], 1), core_weights[...])
     term_ref[...] = terms.reshape(len(swaps), row_n, width)
     copy.wait()
     me = lax.axis_index("owner")
@@ -284,7 +287,7 @@
 
     partners_h = pltpu.with_memory_space_constraint(partners, pltpu.HBM)
     self_out_got = across(self_out, chip_hop)
-    *outgoing, context, table, cross_out_own = call(
+    *outgoing, context, table, cross_out_own, query_weight = call(
         "own_images",
         functools.partial(own_images_kernel, swaps, owner_n),
         [block] * pair_n
@@ -292,6 +295,7 @@
             shape((row_all * columns // LANES, LANES), BF16),
             shape((pair_n, LANES), jnp.int32),
             shape(cross_out.shape, BF16),
+            shape((columns, width), BF16),
         ],
         [HBM] * 6,
         [
@@ -301,7 +305,7 @@
             pltpu.VMEM((2, columns, width), BF16),
             index_table,
             pltpu.VMEM((image_n, 2 * columns, patch_n), BF16),
-            dma((6,)),
+            dma((7,)),
         ],
         *[pltpu.with_memory_space_constraint(x, pltpu.HBM) for x in (states, gains, self_proj_t, cross_proj_t)],
         partners_h,
@@ -314,47 +318,46 @@
     early = [at for at in range(pair_n) if at not in late]
     short = [2 * near - 2, 2 * near - 1]
     before = [context_got, self_out_got] + [arrived[at] for at in short]
-    cross_out_sent = call(
-        "cross_output_rows",
+    cross_out_own = pl.pallas_call(
         hand_on_kernel,
-        shape(cross_out.shape, BF16),
-        [ANY] * (1 + len(before)),
-        [dma],
-        cross_out_own, *before,
-    )
-    cross_out_got = across(cross_out_sent, chip_hop)
+        out_shape=shape(cross_out.shape, BF16),
+        in_specs=[ANY] * (1 + len(before)),
+        out_specs=ANY,
+        input_output_aliases={0: 0},
+        name="cross_output_rows",
+    )(cross_out_own, *before)
+    cross_out_got = across(cross_out_own, chip_hop)
 
     made_shapes = [
         shape((image_n, row_n, width), F32),
-        shape((image_n, patch_n, columns), F32),
-        shape(cross_out.shape, BF16),
+        shape((image_n, patch_n, columns), BF16),
     ]
 
-    def mixing(states, gains, cross_proj_t, context, context_got, self_out, self_out_got, cross_out):
+    def mixing(states, gains, query_weight, context, context_got, self_out, self_out_got):
         base, sent = call(
             "self_output_share",
             partial_kernel,
-            [shape((row_all, width), F32), shape((row_all + columns, width), BF16)],
-            [VMEM] * 5 + [ANY],
-            [dma],
-            states, context, context_got, self_out, self_out_got, cross_out,
+            [shape((row_all, width), F32), shape((row_all, width), BF16)],
+            [VMEM] * 5,
+            [],
+            states, context, context_got, self_out, self_out_got,
         )
         made = call(
             "mixed_and_queries",
             functools.partial(query_kernel, helper_n),
             made_shapes,
             [VMEM] * 4,
-            [pltpu.VMEM((image_n, patch_n, width), F32), dma],
-            base, across(sent, core_hop), gains, cross_proj_t,
+            [pltpu.VMEM((image_n, patch_n, width), F32)],
+            base, across(sent, core_hop), gains, query_weight,
         )
         return tuple(made)
 
     def no_images(*operands):
         return tuple(jnp.zeros(made.shape, made.dtype) for made in made_shapes)
 
-    own_rows, queries, cross_out_core = lax.cond(
+    own_rows, queries = lax.cond(
         lax.axis_index("owner") < owner_n, mixing, no_images,
-        states, gains, cross_proj_t, context, context_got, self_out, self_out_got, cross_out_own,
+        states, gains, query_weight, context, context_got, self_out, self_out_got,
     )
     packed = columns * row_n // LANES
     early_sides = call(
@@ -376,15 +379,23 @@
         flops=LATE_WEIGHT,
     )
     sides = [sides[0]] + [across(sides[k], k) for k in range(1, helper_n)]
-    weights = {0: cross_out_own, core_hop: cross_out_core, chip_hop: cross_out_got}
-    weights[chip_hop ^ core_hop] = across(cross_out_got, core_hop)
+    cross_out_both = call(
+        "cross_output_both_rows",
+        both_kernel,
+        shape((2 * columns, width), BF16),
+        [ANY] * 3,
+        [dma((2,))],
+        cross_out_own, cross_out_got, early_sides,
+    )
+    cross_out_core = across(cross_out_both, core_hop)
     return call(
         "pair_output",
-        functools.partial(out_kernel, [swaps[at] for at in early + late], owner_n, helper_n),
+        functools.partial(out_kernel, [swaps[at] for at in early + late], owner_n),
         shape((image_n, slot_n, row_n, width), BF16),
-        [HBM] + [VMEM] * (1 + 2 * helper_n),
+        [HBM] + [VMEM] * (3 + helper_n),
         [pltpu.VMEM((pair_n, row_n, width), F32), index_table, dma],
-        partners_h, own_rows, *sides, *[weights[k] for k in range(helper_n)],
+        partners_h, own_rows, cross_out_both, cross_out_core,
+        *[sides[k] for k in (0, chip_hop, core_hop, chip_hop ^ core_hop)],
     )
 
 

time: 35.1 us -> 33.1 us (0.943)
  Pallas kernels: 11.3 us -> 8.85 us
  starting transfers between devices: 17.8 us -> 16.8 us
  waiting for transfers between devices: 5.62 us -> 6.36 us
  local copies, waits for them, and re-layouts: 0.03 us -> 0.75 us
    pallas_call x7, Pallas kernels: 11.3 us -> 8.84 us  [call(): pl.pallas_call(kernel, out_shape=out_shape, in_specs=in_specs, out_specs=...]
    ppermute x5, starting transfers between devices: 10.7 us -> 9.77 us  [exchange(): lax.ppermute(value, 'owner', [(o, swap_target(o, swap, owner_n)) for o in...]
    ppermute x8, waiting for transfers between devices: 5.61 us -> 6.35 us  [across(): return lax.ppermute(value, 'helper', [(j, j ^ k) for j in range(helper_n)])]
    unnamed x16 -> x20, local copies, waits for them, and re-layouts: 0.03 us -> 0.75 us
  transfers between devices with their start and end apart: 13 -> 13, of which waited for: 3 -> 4; matrix products, arithmetic and copies ran while one was open for 0% -> 0% of each run, Pallas kernels for 27% -> 21%
where the time goes in v6:
time: 33.1 us; the launch traced here: 33 us
  starting transfers between devices  16.8 us (51%)
  Pallas kernels  8.85 us (27%)
  waiting for transfers between devices  6.36 us (19%)
  local copies, waits for them, and re-layouts  0.75 us (2%)
    ppermute x5, starting transfers between devices, exchange(): lax.ppermute(value, 'owner', [(o, swap_target(o, swap, owner_n)) for o in...  9.77 us
    pallas_call x7, Pallas kernels, call(): pl.pallas_call(kernel, out_shape=out_shape, in_specs=in_specs, out_specs=...  8.84 us
    ppermute x8, starting transfers between devices, across(): return lax.ppermute(value, 'helper', [(j, j ^ k) for j in range(helper_n)])  7.08 us
    ppermute x8, waiting for transfers between devices, across(): return lax.ppermute(value, 'helper', [(j, j ^ k) for j in range(helper_n)])  6.35 us
    unnamed x20, local copies, waits for them, and re-layouts  0.75 us
  transfers between devices with their start and end apart: 13, of which 4 were waited for; matrix products, arithmetic and copies ran while one was open for 0% of the time, Pallas kernels for 21%

profile of v6, /device:TPU:0, one launch (start us, length us, event | category | flops | bytes accessed | tf_op | source)
XLA Modules:
  0.0 33.0 jit_solution(4930397915317613437)
XLA Ops:
  0.0 3.0 %collective-permute-start.2 = (bf16[192,768]{1,0:T(8,128)(2,1)}, bf16[192,768]{1,0:T(8,128)(2,1)S(1)}, u32[]{:S(2)}, u32[]{:S(2)}) collective-permute-start(bf16[192,768]{1,0:T(8,128)(2,1)} %param.12), channel_id=1, source_target_pairs={{0,2},{1,3},{2,0},{3,1},{4,6},{5,7},{6,4},{7,5},{8,10},{9,11},{10,... | collective-permute-start | bytes 884744 | tf_op jit(solution)/shard_map/ppermute | solution.py:266
  3.0 3.4 %own_images.1 = (bf16[384,128]{1,0:T(8,128)(2,1)S(1)}, bf16[384,128]{1,0:T(8,128)(2,1)S(1)}, bf16[384,128]{1,0:T(8,128)(2,1)S(1)}, bf16[384,128]{1,0:T(8,128)(2,...) custom-call(bf16[2,128,768]{2,1,0:T(8,128)(2,1)} %states.1, ...), custom_call_target="tpu_custom_call" | custom-call | flops 1 | bytes 1 | tf_op jit(solution)/shard_map/own_images/pallas_call | solution.py:273
  6.4 0.0 copy-start
  6.4 0.7 %copy-done = bf16[192,768]{1,0:T(8,128)(2,1)} copy-done((bf16[192,768]{1,0:T(8,128)(2,1)}, bf16[192,768]{1,0:T(8,128)(2,1)S(1)}, u32[]{:S(2)}) %copy-start) | copy-done | bytes 294936
  7.1 1.6 %collective-permute-start.3 = (bf16[384,128]{1,0:T(8,128)(2,1)S(1)}, bf16[384,128]{1,0:T(8,128)(2,1)S(1)}, u32[]{:S(2)}, u32[]{:S(2)}) collective-permute-start(bf16[384,128]{1,0:T(8,128)(2,1)S(1)} %get-tuple-element.47), channel_id=1, source_target_pairs={{0,8},{4,12},{8,0},{12,4},{16,24},{20,28},{24,16},{28,20},{1,9},{5... | collective-permute-start | bytes 294920 | tf_op jit(solution)/shard_map/ppermute | solution.py:269
  8.7 1.5 %collective-permute-start.4 = (bf16[384,128]{1,0:T(8,128)(2,1)S(1)}, bf16[384,128]{1,0:T(8,128)(2,1)S(1)}, u32[]{:S(2)}, u32[]{:S(2)}) collective-permute-start(bf16[384,128]{1,0:T(8,128)(2,1)S(1)} %get-tuple-element.48), channel_id=1, source_target_pairs={{0,4},{4,0},{8,12},{12,8},{16,20},{20,16},{24,28},{28,24},{1,5},{5... | collective-permute-start | bytes 294920 | tf_op jit(solution)/shard_map/ppermute | solution.py:269
  10.2 0.5 %collective-permute-start.1 = (bf16[384,128]{1,0:T(8,128)(2,1)S(1)}, bf16[384,128]{1,0:T(8,128)(2,1)S(1)}, u32[]{:S(2)}, u32[]{:S(2)}) collective-permute-start(bf16[384,128]{1,0:T(8,128)(2,1)S(1)} %get-tuple-element.43), channel_id=1, source_target_pairs={{0,2},{1,3},{2,0},{3,1},{4,6},{5,7},{6,4},{7,5},{8,10},{9,11},{10,... | collective-permute-start | bytes 294920 | tf_op jit(solution)/shard_map/ppermute | solution.py:266
  10.7 2.6 %collective-permute-start.6 = (bf16[384,128]{1,0:T(8,128)(2,1)S(1)}, bf16[384,128]{1,0:T(8,128)(2,1)S(1)}, u32[]{:S(2)}, u32[]{:S(2)}) collective-permute-start(bf16[384,128]{1,0:T(8,128)(2,1)S(1)} %get-tuple-element.51), channel_id=1, source_target_pairs={{0,16},{4,20},{8,24},{12,28},{16,0},{20,4},{24,8},{28,12},{1,17},{... | collective-permute-start | bytes 294920 | tf_op jit(solution)/shard_map/ppermute | solution.py:269
  13.3 0.0 collective-permute-done.3.refs_3_.rest_1_
  13.3 2.1 %collective-permute-start.8 = (bf16[384,128]{1,0:T(8,128)(2,1)S(1)}, bf16[384,128]{1,0:T(8,128)(2,1)S(1)}, u32[]{:S(2)}, u32[]{:S(2)}) collective-permute-start(bf16[384,128]{1,0:T(8,128)(2,1)S(1)} %get-tuple-element.52), channel_id=1, source_target_pairs={{0,24},{4,28},{8,16},{12,20},{16,8},{20,12},{24,0},{28,4},{1,25},{... | collective-permute-start | bytes 294920 | tf_op jit(solution)/shard_map/ppermute | solution.py:269
  15.3 2.1 %collective-permute-start.9 = (bf16[384,128]{1,0:T(8,128)(2,1)S(1)}, bf16[384,128]{1,0:T(8,128)(2,1)S(1)}, u32[]{:S(2)}, u32[]{:S(2)}) collective-permute-start(bf16[384,128]{1,0:T(8,128)(2,1)S(1)} %get-tuple-element.53), channel_id=1, source_target_pairs={{0,28},{4,8},{8,4},{12,16},{16,12},{20,24},{24,20},{28,0},{1,29},{... | collective-permute-start | bytes 294920 | tf_op jit(solution)/shard_map/ppermute | solution.py:269
  17.4 0.0 copy-start.6
  17.4 0.0 copy-start.8
  17.5 0.0 copy-start.9
  17.5 1.3 %collective-permute-start.5 = (bf16[192,768]{1,0:T(8,128)(2,1)}, bf16[192,768]{1,0:T(8,128)(2,1)S(1)}, u32[]{:S(2)}, u32[]{:S(2)}) collective-permute-start(bf16[192,768]{1,0:T(8,128)(2,1)} %cross_output_rows.1.own), channel_id=1, source_target_pairs={{0,2},{1,3},{2,0},{3,1},{4,6},{5,7},{6,4},{7,5},{8,10},{9,11},{10,... | collective-permute-start | bytes 884744 | tf_op jit(solution)/shard_map/ppermute | solution.py:266
  18.8 3.2 %conditional.1 = ((f32[2,32,768]{2,1,0:T(8,128)}, bf16[2,128,192]{2,1,0:T(8,128)(2,1)S(1)})) conditional(s32[]{:T(128)} %convert_element_type.3, () %tuple.12, (bf16[2,128,768]{2,1,0:T(8,128)(2,1)S(1)}, bf16[384,128]{1,0:T(8,128)(2,1)S(1)}, bf16[384,128]{1,0:T(8,128)(2,1)S(1)}, bf16[192,768]{1,0:T(8,128)(2,1)S(1)}, bf16[192,768]{1,0:T(8,128)(2,1)S(1)}, ...), branch_computations={%region_0.0_spmd, %region_1.0_spmd} | conditional | flops 2 | bytes 1572914 | solution.py:358
  18.8 0.4 %self_output_share.1 = (f32[256,768]{1,0:T(8,128)S(1)}, bf16[256,768]{1,0:T(8,128)(2,1)S(1)}) custom-call(bf16[2,128,768]{2,1,0:T(8,128)(2,1)S(1)} %get-tuple-element.19.states, bf16[384,128]{1,0:T(8,128)(2,1)S(1)} %get-tuple-element.20.own, bf16[384,128]{1,0:T(8,128)(2,1)S(1)} %get-tuple-element.21.got, bf16[192,768]{1,0:T(8,128)(2,1)S(1)} %get-tuple-element.22.own_weight, ...), custom_call_target="tpu_custom_call" | custom-call | flops 1 | bytes 1 | tf_op jit(solution)/shard_map/cond/branch_1_fun/self_output_share/pallas_call | solution.py:273
  19.2 0.1 collective-permute-start
  19.3 1.7 %collective-permute-done.got = bf16[256,768]{1,0:T(8,128)(2,1)S(1)} collective-permute-done((bf16[256,768]{1,0:T(8,128)(2,1)S(1)}, bf16[256,768]{1,0:T(8,128)(2,1)S(1)}, u32[]{:S(2)}, u32[]{:S(2)}) %collective-permute-start) | collective-permute-done | bytes 393248 | tf_op jit(solution)/shard_map/cond/branch_1_fun/ppermute | solution.py:266
  21.0 1.0 %mixed_and_queries.1 = (f32[2,32,768]{2,1,0:T(8,128)}, bf16[2,128,192]{2,1,0:T(8,128)(2,1)S(1)}) custom-call(f32[256,768]{1,0:T(8,128)S(1)} %get-tuple-element.24.base, bf16[256,768]{1,0:T(8,128)(2,1)S(1)} %collective-permute-done.got, f32[3,768]{1,0:T(4,128)S(1)} %get-tuple-element.26.gains, bf16[192,768]{1,0:T(8,128)(2,1)S(1)} %get-tuple-element.27.weight), custom_call_target="tpu_custom_call" | custom-call | flops 1 | bytes 1 | tf_op jit(solution)/shard_map/cond/branch_1_fun/mixed_and_queries/pallas_call | solution.py:273
  22.0 0.0 copy-start.1
  22.0 1.0 %early_cross_attention.1.waited.before = bf16[4,3,48,128]{3,2,1,0:T(8,128)(2,1)S(1)} custom-call(bf16[2,128,192]{2,1,0:T(8,128)(2,1)S(1)} %get-tuple-element.49.queries, s32[5,128]{1,0:T(8,128)S(1)} %get-tuple-element.50.table, bf16[384,128]{1,0:T(8,128)(2,1)S(1)} %collective-permute-done.6.rest_0_, bf16[384,128]{1,0:T(8,128)(2,1)S(1)} %copy-done.3, ...), custom_call_target="tpu_custom_call" | custom-call | flops 99999997952 | bytes 1 | tf_op jit(solution)/shard_map/early_cross_attention/pallas_call | solution.py:273
  23.1 1.4 %collective-permute-done.5.got = bf16[192,768]{1,0:T(8,128)(2,1)S(1)} collective-permute-done((bf16[192,768]{1,0:T(8,128)(2,1)}, bf16[192,768]{1,0:T(8,128)(2,1)S(1)}, u32[]{:S(2)}, u32[]{:S(2)}) %collective-permute-start.5) | collective-permute-done | bytes 294944 | tf_op jit(solution)/shard_map/ppermute | solution.py:266
  24.5 0.1 cross_output_both_rows.1.own_weights
  24.6 0.1 collective-permute-start.7
  24.7 0.9 %late_cross_attention.1 = (bf16[5,48,128]{2,1,0:T(8,128)(2,1)S(1)}, bf16[5,48,128]{2,1,0:T(8,128)(2,1)S(1)}, bf16[5,48,128]{2,1,0:T(8,128)(2,1)S(1)}, bf16[5,48,128]{2,1,0:T(8,128)(2,1)S(1)}) custom-call(bf16[2,128,192]{2,1,0:T(8,128)(2,1)S(1)} %get-tuple-element.49.queries, s32[5,128]{1,0:T(8,128)S(1)} %get-tuple-element.50.table, ...), custom_call_target="tpu_custom_call" | custom-call | flops 99999997952 | bytes 1 | tf_op jit(solution)/shard_map/late_cross_attention/pallas_call | solution.py:273
  25.6 1.3 %collective-permute-start.10 = (bf16[5,48,128]{2,1,0:T(8,128)(2,1)S(1)}, bf16[5,48,128]{2,1,0:T(8,128)(2,1)S(1)}, u32[]{:S(2)}, u32[]{:S(2)}) collective-permute-start(bf16[5,48,128]{2,1,0:T(8,128)(2,1)S(1)} %get-tuple-element.55), channel_id=1, source_target_pairs={{0,2},{1,3},{2,0},{3,1},{4,6},{5,7},{6,4},{7,5},{8,10},{9,11},{10,... | collective-permute-start | bytes 184328 | tf_op jit(solution)/shard_map/ppermute | solution.py:266
  26.9 0.2 collective-permute-start.11
  27.1 0.7 %collective-permute-start.12 = (bf16[5,48,128]{2,1,0:T(8,128)(2,1)S(1)}, bf16[5,48,128]{2,1,0:T(8,128)(2,1)S(1)}, u32[]{:S(2)}, u32[]{:S(2)}) collective-permute-start(bf16[5,48,128]{2,1,0:T(8,128)(2,1)S(1)} %get-tuple-element.57), channel_id=1, source_target_pairs={{0,3},{1,2},{2,1},{3,0},{4,7},{5,6},{6,5},{7,4},{8,11},{9,10},{10,... | collective-permute-start | bytes 184328 | tf_op jit(solution)/shard_map/ppermute | solution.py:266
  27.8 2.2 %collective-permute-done.10.rest_1_ = bf16[5,48,128]{2,1,0:T(8,128)(2,1)S(1)} collective-permute-done((bf16[5,48,128]{2,1,0:T(8,128)(2,1)S(1)}, bf16[5,48,128]{2,1,0:T(8,128)(2,1)S(1)}, u32[]{:S(2)}, u32[]{:S(2)}) %collective-permute-start.10) | collective-permute-done | bytes 61472 | tf_op jit(solution)/shard_map/ppermute | solution.py:266
  30.0 1.0 %collective-permute-done.12.rest_3_ = bf16[5,48,128]{2,1,0:T(8,128)(2,1)S(1)} collective-permute-done((bf16[5,48,128]{2,1,0:T(8,128)(2,1)S(1)}, bf16[5,48,128]{2,1,0:T(8,128)(2,1)S(1)}, u32[]{:S(2)}, u32[]{:S(2)}) %collective-permute-start.12) | collective-permute-done | bytes 61472 | tf_op jit(solution)/shard_map/ppermute | solution.py:266
  31.0 2.0 %pair_output.1 = bf16[2,5,32,768]{3,2,1,0:T(8,128)(2,1)} custom-call(s32[2,5]{1,0:T(2,128)} %partners.3, f32[2,32,768]{2,1,0:T(8,128)S(1)} %copy-done.7, bf16[384,768]{1,0:T(8,128)(2,1)S(1)} %cross_output_both_rows.1.own_weights, bf16[384,768]{1,0:T(8,128)(2,1)S(1)} %collective-permute-done.7.core_weights, ...), custom_call_target="tpu_custom_call" | custom-call | flops 1 | bytes 1 | tf_op jit(solution)/shard_map/pair_output/pallas_call | solution.py:273
  (23 shorter events, 0.1 us)
Async XLA Ops:
  0.0 17.4 %collective-permute-start.2 = (bf16[192,768]{1,0:T(8,128)(2,1)}, bf16[192,768]{1,0:T(8,128)(2,1)S(1)}, u32[]{:S(2)}, u32[]{:S(2)}) collective-permute-start(bf16[192,768]{1,0:T(8,128)(2,1)} %param.12), channel_id=1, source_target_pairs={{0,2},{1,3},{2,0},{3,1},{4,6},{5,7},{6,4},{7,5},{8,10},{9,11},{10,... | collective-permute-start | bytes 884744 | tf_op jit(solution)/shard_map/ppermute | solution.py:266
  6.4 0.7 %copy-start = (bf16[192,768]{1,0:T(8,128)(2,1)}, bf16[192,768]{1,0:T(8,128)(2,1)S(1)}, u32[]{:S(2)}) copy-start(bf16[192,768]{1,0:T(8,128)(2,1)S(1)} %get-tuple-element.46.refs_0_) | copy-start | bytes 884740
  7.1 6.2 %collective-permute-start.3 = (bf16[384,128]{1,0:T(8,128)(2,1)S(1)}, bf16[384,128]{1,0:T(8,128)(2,1)S(1)}, u32[]{:S(2)}, u32[]{:S(2)}) collective-permute-start(bf16[384,128]{1,0:T(8,128)(2,1)S(1)} %get-tuple-element.47), channel_id=1, source_target_pairs={{0,8},{4,12},{8,0},{12,4},{16,24},{20,28},{24,16},{28,20},{1,9},{5... | collective-permute-start | bytes 294920 | tf_op jit(solution)/shard_map/ppermute | solution.py:269
  8.7 6.6 %collective-permute-start.4 = (bf16[384,128]{1,0:T(8,128)(2,1)S(1)}, bf16[384,128]{1,0:T(8,128)(2,1)S(1)}, u32[]{:S(2)}, u32[]{:S(2)}) collective-permute-start(bf16[384,128]{1,0:T(8,128)(2,1)S(1)} %get-tuple-element.48), channel_id=1, source_target_pairs={{0,4},{4,0},{8,12},{12,8},{16,20},{20,16},{24,28},{28,24},{1,5},{5... | collective-permute-start | bytes 294920 | tf_op jit(solution)/shard_map/ppermute | solution.py:269
  10.2 7.2 %collective-permute-start.1 = (bf16[384,128]{1,0:T(8,128)(2,1)S(1)}, bf16[384,128]{1,0:T(8,128)(2,1)S(1)}, u32[]{:S(2)}, u32[]{:S(2)}) collective-permute-start(bf16[384,128]{1,0:T(8,128)(2,1)S(1)} %get-tuple-element.43), channel_id=1, source_target_pairs={{0,2},{1,3},{2,0},{3,1},{4,6},{5,7},{6,4},{7,5},{8,10},{9,11},{10,... | collective-permute-start | bytes 294920 | tf_op jit(solution)/shard_map/ppermute | solution.py:266
  10.7 11.3 %collective-permute-start.6 = (bf16[384,128]{1,0:T(8,128)(2,1)S(1)}, bf16[384,128]{1,0:T(8,128)(2,1)S(1)}, u32[]{:S(2)}, u32[]{:S(2)}) collective-permute-start(bf16[384,128]{1,0:T(8,128)(2,1)S(1)} %get-tuple-element.51), channel_id=1, source_target_pairs={{0,16},{4,20},{8,24},{12,28},{16,0},{20,4},{24,8},{28,12},{1,17},{... | collective-permute-start | bytes 294920 | tf_op jit(solution)/shard_map/ppermute | solution.py:269
  13.3 4.1 %copy-start.2 = (bf16[384,128]{1,0:T(8,128)(2,1)}, bf16[384,128]{1,0:T(8,128)(2,1)S(1)}, u32[]{:S(2)}) copy-start(bf16[384,128]{1,0:T(8,128)(2,1)S(1)} %collective-permute-done.3.refs_3_.rest_1_) | copy-start | bytes 294916
  13.3 11.4 %collective-permute-start.8 = (bf16[384,128]{1,0:T(8,128)(2,1)S(1)}, bf16[384,128]{1,0:T(8,128)(2,1)S(1)}, u32[]{:S(2)}, u32[]{:S(2)}) collective-permute-start(bf16[384,128]{1,0:T(8,128)(2,1)S(1)} %get-tuple-element.52), channel_id=1, source_target_pairs={{0,24},{4,28},{8,16},{12,20},{16,8},{20,12},{24,0},{28,4},{1,25},{... | collective-permute-start | bytes 294920 | tf_op jit(solution)/shard_map/ppermute | solution.py:269
  15.3 2.1 %copy-start.4 = (bf16[384,128]{1,0:T(8,128)(2,1)}, bf16[384,128]{1,0:T(8,128)(2,1)S(1)}, u32[]{:S(2)}) copy-start(bf16[384,128]{1,0:T(8,128)(2,1)S(1)} %collective-permute-done.4.refs_4_.rest_2_) | copy-start | bytes 294916
  15.3 9.4 %collective-permute-start.9 = (bf16[384,128]{1,0:T(8,128)(2,1)S(1)}, bf16[384,128]{1,0:T(8,128)(2,1)S(1)}, u32[]{:S(2)}, u32[]{:S(2)}) collective-permute-start(bf16[384,128]{1,0:T(8,128)(2,1)S(1)} %get-tuple-element.53), channel_id=1, source_target_pairs={{0,28},{4,8},{8,4},{12,16},{16,12},{20,24},{24,20},{28,0},{1,29},{... | collective-permute-start | bytes 294920 | tf_op jit(solution)/shard_map/ppermute | solution.py:269
  17.4 1.3 %copy-start.6 = (bf16[2,128,768]{2,1,0:T(8,128)(2,1)S(1)}, bf16[2,128,768]{2,1,0:T(8,128)(2,1)}, u32[]{:S(2)}) copy-start(bf16[2,128,768]{2,1,0:T(8,128)(2,1)} %states.1) | copy-start | bytes 1179652
  17.4 1.3 %copy-start.8 = (bf16[192,768]{1,0:T(8,128)(2,1)S(1)}, bf16[192,768]{1,0:T(8,128)(2,1)}, u32[]{:S(2)}) copy-start(bf16[192,768]{1,0:T(8,128)(2,1)} %param.12) | copy-start | bytes 884740
  17.5 1.3 %copy-start.9 = (f32[3,768]{1,0:T(4,128)S(1)}, f32[3,768]{1,0:T(4,128)}, u32[]{:S(2)}) copy-start(f32[3,768]{1,0:T(4,128)} %gains.1) | copy-start | bytes 27652
  17.5 7.0 %collective-permute-start.5 = (bf16[192,768]{1,0:T(8,128)(2,1)}, bf16[192,768]{1,0:T(8,128)(2,1)S(1)}, u32[]{:S(2)}, u32[]{:S(2)}) collective-permute-start(bf16[192,768]{1,0:T(8,128)(2,1)} %cross_output_rows.1.own), channel_id=1, source_target_pairs={{0,2},{1,3},{2,0},{3,1},{4,6},{5,7},{6,4},{7,5},{8,10},{9,11},{10,... | collective-permute-start | bytes 884744 | tf_op jit(solution)/shard_map/ppermute | solution.py:266
  18.8 3.2 %copy-start.3 = (bf16[384,128]{1,0:T(8,128)(2,1)S(1)}, bf16[384,128]{1,0:T(8,128)(2,1)}, u32[]{:S(2)}) copy-start(bf16[384,128]{1,0:T(8,128)(2,1)} %copy-done.2) | copy-start | bytes 294916
  18.8 3.2 %copy-start.5 = (bf16[384,128]{1,0:T(8,128)(2,1)S(1)}, bf16[384,128]{1,0:T(8,128)(2,1)}, u32[]{:S(2)}) copy-start(bf16[384,128]{1,0:T(8,128)(2,1)} %copy-done.4) | copy-start | bytes 294916
  19.2 1.8 %collective-permute-start = (bf16[256,768]{1,0:T(8,128)(2,1)S(1)}, bf16[256,768]{1,0:T(8,128)(2,1)S(1)}, u32[]{:S(2)}, u32[]{:S(2)}) collective-permute-start(bf16[256,768]{1,0:T(8,128)(2,1)S(1)} %get-tuple-element.25), channel_id=1, source_target_pairs={{0,1},{1,0},{2,3},{3,2},{4,5},{5,4},{6,7},{7,6},{8,9},{9,8},{10,11... | collective-permute-start | bytes 1179656 | tf_op jit(solution)/shard_map/cond/branch_1_fun/ppermute | solution.py:266
  22.0 2.5 %copy-start.1 = (bf16[192,768]{1,0:T(8,128)(2,1)S(1)}, bf16[192,768]{1,0:T(8,128)(2,1)}, u32[]{:S(2)}) copy-start(bf16[192,768]{1,0:T(8,128)(2,1)} %cross_output_rows.1.own) | copy-start | bytes 884740
  24.6 6.4 %copy-start.7 = (f32[2,32,768]{2,1,0:T(8,128)S(1)}, f32[2,32,768]{2,1,0:T(8,128)}, u32[]{:S(2)}) copy-start(f32[2,32,768]{2,1,0:T(8,128)} %get-tuple-element.45.own_rows) | copy-start | bytes 589828
  24.6 6.4 %collective-permute-start.7 = (bf16[384,768]{1,0:T(8,128)(2,1)S(1)}, bf16[384,768]{1,0:T(8,128)(2,1)S(1)}, u32[]{:S(2)}, u32[]{:S(2)}) collective-permute-start(bf16[384,768]{1,0:T(8,128)(2,1)S(1)} %cross_output_both_rows.1.own_weights), channel_id=1, source_target_pairs={{0,1},{1,0},{2,3},{3,2},{4,5},{5,4},{6,7},{7,6},{8,9},{9,8},{10,11... | collective-permute-start | bytes 1769480 | tf_op jit(solution)/shard_map/ppermute | solution.py:266
  25.6 4.4 %collective-permute-start.10 = (bf16[5,48,128]{2,1,0:T(8,128)(2,1)S(1)}, bf16[5,48,128]{2,1,0:T(8,128)(2,1)S(1)}, u32[]{:S(2)}, u32[]{:S(2)}) collective-permute-start(bf16[5,48,128]{2,1,0:T(8,128)(2,1)S(1)} %get-tuple-element.55), channel_id=1, source_target_pairs={{0,2},{1,3},{2,0},{3,1},{4,6},{5,7},{6,4},{7,5},{8,10},{9,11},{10,... | collective-permute-start | bytes 184328 | tf_op jit(solution)/shard_map/ppermute | solution.py:266
  26.9 3.1 %collective-permute-start.11 = (bf16[5,48,128]{2,1,0:T(8,128)(2,1)S(1)}, bf16[5,48,128]{2,1,0:T(8,128)(2,1)S(1)}, u32[]{:S(2)}, u32[]{:S(2)}) collective-permute-start(bf16[5,48,128]{2,1,0:T(8,128)(2,1)S(1)} %get-tuple-element.56), channel_id=1, source_target_pairs={{0,1},{1,0},{2,3},{3,2},{4,5},{5,4},{6,7},{7,6},{8,9},{9,8},{10,11... | collective-permute-start | bytes 184328 | tf_op jit(solution)/shard_map/ppermute | solution.py:266
  27.1 3.9 %collective-permute-start.12 = (bf16[5,48,128]{2,1,0:T(8,128)(2,1)S(1)}, bf16[5,48,128]{2,1,0:T(8,128)(2,1)S(1)}, u32[]{:S(2)}, u32[]{:S(2)}) collective-permute-start(bf16[5,48,128]{2,1,0:T(8,128)(2,1)S(1)} %get-tuple-element.57), channel_id=1, source_target_pairs={{0,3},{1,2},{2,1},{3,0},{4,7},{5,6},{6,5},{7,4},{8,11},{9,10},{10,... | collective-permute-start | bytes 184328 | tf_op jit(solution)/shard_map/ppermute | solution.py:266

commit v7 on v6

--- a/solution.py
+++ b/solution.py
@@ -12,7 +12,7 @@
 F32 = jnp.float32
 BF16 = jnp.bfloat16
 VMEM_BYTES = 24 * 1024 * 1024
-EARLY_WEIGHT = 10**11
+EARLY_WEIGHT = 1
 LATE_WEIGHT = 10**11
 
 VMEM = pl.BlockSpec(memory_space=pltpu.VMEM)
@@ -94,9 +94,9 @@
     return found
 
 
-def own_images_kernel(swaps, owner_n, states, gains, self_t, cross_t, partners, weight, *rest):
+def own_images_kernel(swaps, owner_n, states, gains, self_t, cross_t, partners, *rest):
     outs, rest = rest[: len(swaps)], rest[len(swaps) :]
-    context_out, table, weight_out, query_weight_out, states_v, gains_v, self_v, cross_v, partners_s, held, sems = rest
+    context_out, table, query_weight_out, states_v, gains_v, self_v, cross_v, partners_s, held, sems = rest
     image_n, patch_n, width = states.shape
     columns = self_t.shape[1]
     copies = [
@@ -105,8 +105,7 @@
         pltpu.make_async_copy(cross_t.at[pl.ds(1, 2)], cross_v, sems.at[2]),
         pltpu.make_async_copy(partners, partners_s, sems.at[3]),
         pltpu.make_async_copy(self_t, self_v, sems.at[4]),
-        pltpu.make_async_copy(weight, weight_out, sems.at[5]),
-        pltpu.make_async_copy(cross_t.at[0], query_weight_out, sems.at[6]),
+        pltpu.make_async_copy(cross_t.at[0], query_weight_out, sems.at[5]),
     ]
     for copy in copies:
         copy.start()
@@ -136,7 +135,6 @@
         )
     context_out[...] = pack(jnp.concatenate(contexts, 0))
     copies[5].wait()
-    copies[6].wait()
 
 
 def unpack(block):
@@ -166,8 +164,9 @@
     own_rows[...] = mixed_ref[:, pl.ds(start, row_n), :]
 
 
-def hand_on_kernel(*refs):
-    del refs
+def hand_on_kernel(value, *rest):
+    out = rest[-1]
+    out[...] = value[...]
 
 
 def both_kernel(own, got, waited, out, sems):
@@ -287,17 +286,17 @@
 
     partners_h = pltpu.with_memory_space_constraint(partners, pltpu.HBM)
     self_out_got = across(self_out, chip_hop)
-    *outgoing, context, table, cross_out_own, query_weight = call(
+    cross_out_got = across(cross_out, chip_hop)
+    *outgoing, context, table, query_weight = call(
         "own_images",
         functools.partial(own_images_kernel, swaps, owner_n),
         [block] * pair_n
         + [
             shape((row_all * columns // LANES, LANES), BF16),
             shape((pair_n, LANES), jnp.int32),
-            shape(cross_out.shape, BF16),
             shape((columns, width), BF16),
         ],
-        [HBM] * 6,
+        [HBM] * 5,
         [
             pltpu.VMEM(states.shape, BF16),
             pltpu.VMEM(gains.shape, F32),
@@ -305,28 +304,26 @@
             pltpu.VMEM((2, columns, width), BF16),
             index_table,
             pltpu.VMEM((image_n, 2 * columns, patch_n), BF16),
-            dma((7,)),
+            dma((6,)),
         ],
         *[pltpu.with_memory_space_constraint(x, pltpu.HBM) for x in (states, gains, self_proj_t, cross_proj_t)],
         partners_h,
-        pltpu.with_memory_space_constraint(cross_out, pltpu.HBM),
-    )
+    )
+    arrived = [exchange(value, swap) for value, swap in zip(outgoing, swaps)]
     context_got = across(context, chip_hop)
-    arrived = [exchange(value, swap) for value, swap in zip(outgoing, swaps)]
     near = (slot_n - 1) // 2
     late = [at for at, (_, colour) in enumerate(swaps) if colour]
     early = [at for at in range(pair_n) if at not in late]
     short = [2 * near - 2, 2 * near - 1]
-    before = [context_got, self_out_got] + [arrived[at] for at in short]
-    cross_out_own = pl.pallas_call(
+    before = [arrived[at] for at in short] + [self_out_got]
+    gains_then = call(
+        "gains",
         hand_on_kernel,
-        out_shape=shape(cross_out.shape, BF16),
-        in_specs=[ANY] * (1 + len(before)),
-        out_specs=ANY,
-        input_output_aliases={0: 0},
-        name="cross_output_rows",
-    )(cross_out_own, *before)
-    cross_out_got = across(cross_out_own, chip_hop)
+        shape(gains.shape, F32),
+        [VMEM] + [ANY] * len(before),
+        [],
+        gains, *before,
+    )
 
     made_shapes = [
         shape((image_n, row_n, width), F32),
@@ -357,7 +354,7 @@
 
     own_rows, queries = lax.cond(
         lax.axis_index("owner") < owner_n, mixing, no_images,
-        states, gains, query_weight, context, context_got, self_out, self_out_got,
+        states, gains_then, query_weight, context, context_got, self_out, self_out_got,
     )
     packed = columns * row_n // LANES
     early_sides = call(
@@ -383,9 +380,9 @@
         "cross_output_both_rows",
         both_kernel,
         shape((2 * columns, width), BF16),
-        [ANY] * 3,
+        [VMEM, ANY, ANY],
         [dma((2,))],
-        cross_out_own, cross_out_got, early_sides,
+        cross_out, cross_out_got, early_sides,
     )
     cross_out_core = across(cross_out_both, core_hop)
     return call(

time: 33.1 us -> 32.4 us (0.979)
  the two profiles are of different devices: /device:TPU:0 before, /device:TPU:17 now
where the time goes in v7:
time: 32.4 us; the launch traced here: 32.3 us
  starting transfers between devices  12.4 us (38%)
  waiting for transfers between devices  11.3 us (35%)
  Pallas kernels  8.43 us (26%)
    ppermute x8, waiting for transfers between devices, across(): return lax.ppermute(value, 'helper', [(j, j ^ k) for j in range(helper_n)])  8.91 us
    pallas_call x8, Pallas kernels, call(): pl.pallas_call(kernel, out_shape=out_shape, in_specs=in_specs, out_specs=...  8.43 us
    ppermute x8, starting transfers between devices, across(): return lax.ppermute(value, 'helper', [(j, j ^ k) for j in range(helper_n)])  7.43 us
    ppermute x5, starting transfers between devices, exchange(): lax.ppermute(value, 'owner', [(o, swap_target(o, swap, owner_n)) for o in...  5.01 us
    ppermute x5, waiting for transfers between devices, exchange(): lax.ppermute(value, 'owner', [(o, swap_target(o, swap, owner_n)) for o in...  2.41 us
  transfers between devices with their start and end apart: 13, of which 8 were waited for; matrix products, arithmetic and copies ran while one was open for 0% of the time, Pallas kernels for 20%

profile of v7, /device:TPU:17, one launch (start us, length us, event | category | flops | bytes accessed | tf_op | source)
XLA Modules:
  0.0 32.3 jit_solution(17760443219133811406)
XLA Ops:
  0.0 1.2 %collective-permute-start.2 = (bf16[192,768]{1,0:T(8,128)(2,1)}, bf16[192,768]{1,0:T(8,128)(2,1)S(1)}, u32[]{:S(2)}, u32[]{:S(2)}) collective-permute-start(bf16[192,768]{1,0:T(8,128)(2,1)} %param.12), channel_id=1, source_target_pairs={{0,2},{1,3},{2,0},{3,1},{4,6},{5,7},{6,4},{7,5},{8,10},{9,11},{10,... | collective-permute-start | bytes 884744 | tf_op jit(solution)/shard_map/ppermute | solution.py:265
  1.2 0.2 collective-permute-start.5
  1.5 3.5 %own_images.1 = (bf16[384,128]{1,0:T(8,128)(2,1)S(1)}, bf16[384,128]{1,0:T(8,128)(2,1)S(1)}, bf16[384,128]{1,0:T(8,128)(2,1)S(1)}, bf16[384,128]{1,0:T(8,128)(2,...) custom-call(bf16[2,128,768]{2,1,0:T(8,128)(2,1)} %states.1, ...), custom_call_target="tpu_custom_call" | custom-call | flops 1 | bytes 1 | tf_op jit(solution)/shard_map/own_images/pallas_call | solution.py:272
  4.9 0.0 copy-start.1
  5.0 0.0 copy-start.2
  5.0 1.4 %collective-permute-start.3 = (bf16[384,128]{1,0:T(8,128)(2,1)S(1)}, bf16[384,128]{1,0:T(8,128)(2,1)S(1)}, u32[]{:S(2)}, u32[]{:S(2)}) collective-permute-start(bf16[384,128]{1,0:T(8,128)(2,1)S(1)} %get-tuple-element.43), channel_id=1, source_target_pairs={{0,8},{4,12},{8,0},{12,4},{16,24},{20,28},{24,16},{28,20},{1,9},{5... | collective-permute-start | bytes 294920 | tf_op jit(solution)/shard_map/ppermute | solution.py:268
  6.3 1.2 %collective-permute-start.4 = (bf16[384,128]{1,0:T(8,128)(2,1)S(1)}, bf16[384,128]{1,0:T(8,128)(2,1)S(1)}, u32[]{:S(2)}, u32[]{:S(2)}) collective-permute-start(bf16[384,128]{1,0:T(8,128)(2,1)S(1)} %get-tuple-element.44), channel_id=1, source_target_pairs={{0,4},{4,0},{8,12},{12,8},{16,20},{20,16},{24,28},{28,24},{1,5},{5... | collective-permute-start | bytes 294920 | tf_op jit(solution)/shard_map/ppermute | solution.py:268
  7.5 1.2 %collective-permute-start.1 = (bf16[384,128]{1,0:T(8,128)(2,1)S(1)}, bf16[384,128]{1,0:T(8,128)(2,1)S(1)}, u32[]{:S(2)}, u32[]{:S(2)}) collective-permute-start(bf16[384,128]{1,0:T(8,128)(2,1)S(1)} %get-tuple-element.42), channel_id=1, source_target_pairs={{0,2},{1,3},{2,0},{3,1},{4,6},{5,7},{6,4},{7,5},{8,10},{9,11},{10,... | collective-permute-start | bytes 294920 | tf_op jit(solution)/shard_map/ppermute | solution.py:265
  8.8 0.0 collective-permute-done.3.rest_0_.rest_1_
  8.8 0.0 collective-permute-start.6
  8.8 1.3 %collective-permute-done.4.rest_1_.rest_2_ = bf16[384,128]{1,0:T(8,128)(2,1)S(1)} collective-permute-done((bf16[384,128]{1,0:T(8,128)(2,1)S(1)}, bf16[384,128]{1,0:T(8,128)(2,1)S(1)}, u32[]{:S(2)}, u32[]{:S(2)}) %collective-permute-start.4) | collective-permute-done | bytes 98336 | tf_op jit(solution)/shard_map/ppermute | solution.py:268
  10.1 1.2 %collective-permute-start.8 = (bf16[384,128]{1,0:T(8,128)(2,1)S(1)}, bf16[384,128]{1,0:T(8,128)(2,1)S(1)}, u32[]{:S(2)}, u32[]{:S(2)}) collective-permute-start(bf16[384,128]{1,0:T(8,128)(2,1)S(1)} %get-tuple-element.50), channel_id=1, source_target_pairs={{0,24},{4,28},{8,16},{12,20},{16,8},{20,12},{24,0},{28,4},{1,25},{... | collective-permute-start | bytes 294920 | tf_op jit(solution)/shard_map/ppermute | solution.py:268
  11.3 1.2 %collective-permute-start.9 = (bf16[384,128]{1,0:T(8,128)(2,1)S(1)}, bf16[384,128]{1,0:T(8,128)(2,1)S(1)}, u32[]{:S(2)}, u32[]{:S(2)}) collective-permute-start(bf16[384,128]{1,0:T(8,128)(2,1)S(1)} %get-tuple-element.51), channel_id=1, source_target_pairs={{0,28},{4,8},{8,4},{12,16},{16,12},{20,24},{24,20},{28,0},{1,29},{... | collective-permute-start | bytes 294920 | tf_op jit(solution)/shard_map/ppermute | solution.py:268
  12.5 4.0 %collective-permute-done.1 = bf16[384,128]{1,0:T(8,128)(2,1)S(1)} collective-permute-done((bf16[384,128]{1,0:T(8,128)(2,1)S(1)}, bf16[384,128]{1,0:T(8,128)(2,1)S(1)}, u32[]{:S(2)}, u32[]{:S(2)}) %collective-permute-start.1) | collective-permute-done | bytes 98336 | tf_op jit(solution)/shard_map/ppermute | solution.py:265
  16.5 3.9 %conditional.1 = ((f32[2,32,768]{2,1,0:T(8,128)S(1)}, bf16[2,128,192]{2,1,0:T(8,128)(2,1)S(1)})) conditional(s32[]{:T(128)} %convert_element_type.3, () %tuple.12, (bf16[2,128,768]{2,1,0:T(8,128)(2,1)S(1)}, bf16[384,128]{1,0:T(8,128)(2,1)S(1)}, bf16[384,128]{1,0:T(8,128)(2,1)S(1)}, bf16[192,768]{1,0:T(8,128)(2,1)S(1)}, ...), branch_computations={%region_0.0_spmd, %region_1.0_spmd} | conditional | flops 2 | bytes 1572914 | solution.py:355
  16.5 0.4 %self_output_share.1 = (f32[256,768]{1,0:T(8,128)S(1)}, bf16[256,768]{1,0:T(8,128)(2,1)S(1)}) custom-call(bf16[2,128,768]{2,1,0:T(8,128)(2,1)S(1)} %get-tuple-element.19.states, bf16[384,128]{1,0:T(8,128)(2,1)S(1)} %get-tuple-element.20.own, bf16[384,128]{1,0:T(8,128)(2,1)S(1)} %get-tuple-element.21.got, bf16[192,768]{1,0:T(8,128)(2,1)S(1)} %get-tuple-element.22.own_weight, ...), custom_call_target="tpu_custom_call" | custom-call | flops 1 | bytes 1 | tf_op jit(solution)/shard_map/cond/branch_1_fun/self_output_share/pallas_call | solution.py:272
  17.0 1.6 %collective-permute-start = (bf16[256,768]{1,0:T(8,128)(2,1)S(1)}, bf16[256,768]{1,0:T(8,128)(2,1)S(1)}, u32[]{:S(2)}, u32[]{:S(2)}) collective-permute-start(bf16[256,768]{1,0:T(8,128)(2,1)S(1)} %get-tuple-element.25), channel_id=1, source_target_pairs={{0,1},{1,0},{2,3},{3,2},{4,5},{5,4},{6,7},{7,6},{8,9},{9,8},{10,11... | collective-permute-start | bytes 1179656 | tf_op jit(solution)/shard_map/cond/branch_1_fun/ppermute | solution.py:265
  18.6 1.3 %collective-permute-done.got = bf16[256,768]{1,0:T(8,128)(2,1)S(1)} collective-permute-done((bf16[256,768]{1,0:T(8,128)(2,1)S(1)}, bf16[256,768]{1,0:T(8,128)(2,1)S(1)}, u32[]{:S(2)}, u32[]{:S(2)}) %collective-permute-start) | collective-permute-done | bytes 393248 | tf_op jit(solution)/shard_map/cond/branch_1_fun/ppermute | solution.py:265
  19.9 0.5 %mixed_and_queries.1 = (f32[2,32,768]{2,1,0:T(8,128)S(1)}, bf16[2,128,192]{2,1,0:T(8,128)(2,1)S(1)}) custom-call(f32[256,768]{1,0:T(8,128)S(1)} %get-tuple-element.24.base, bf16[256,768]{1,0:T(8,128)(2,1)S(1)} %collective-permute-done.got, f32[3,768]{1,0:T(4,128)S(1)} %get-tuple-element.26.gains, bf16[192,768]{1,0:T(8,128)(2,1)S(1)} %get-tuple-element.27.weight), custom_call_target="tpu_custom_call" | custom-call | flops 1 | bytes 1 | tf_op jit(solution)/shard_map/cond/branch_1_fun/mixed_and_queries/pallas_call | solution.py:272
  20.5 1.0 %early_cross_attention.1.waited.before = bf16[4,3,48,128]{3,2,1,0:T(8,128)(2,1)S(1)} custom-call(bf16[2,128,192]{2,1,0:T(8,128)(2,1)S(1)} %get-tuple-element.47.queries, s32[5,128]{1,0:T(8,128)S(1)} %get-tuple-element.48.table, bf16[384,128]{1,0:T(8,128)(2,1)S(1)} %collective-permute-done.6.rest_0_, ...), custom_call_target="tpu_custom_call" | custom-call | flops 1 | bytes 1 | tf_op jit(solution)/shard_map/early_cross_attention/pallas_call | solution.py:272
  21.5 0.1 cross_output_both_rows.1.own_weights
  21.7 0.4 %collective-permute-start.7 = (bf16[384,768]{1,0:T(8,128)(2,1)S(1)}, bf16[384,768]{1,0:T(8,128)(2,1)S(1)}, u32[]{:S(2)}, u32[]{:S(2)}) collective-permute-start(bf16[384,768]{1,0:T(8,128)(2,1)S(1)} %cross_output_both_rows.1.own_weights), channel_id=1, source_target_pairs={{0,1},{1,0},{2,3},{3,2},{4,5},{5,4},{6,7},{7,6},{8,9},{9,8},{10,11... | collective-permute-start | bytes 1769480 | tf_op jit(solution)/shard_map/ppermute | solution.py:265
  22.1 0.3 collective-permute-done.8.rest_0_
  22.4 0.8 %collective-permute-done.9.rest_1_ = bf16[384,128]{1,0:T(8,128)(2,1)S(1)} collective-permute-done((bf16[384,128]{1,0:T(8,128)(2,1)S(1)}, bf16[384,128]{1,0:T(8,128)(2,1)S(1)}, u32[]{:S(2)}, u32[]{:S(2)}) %collective-permute-start.9) | collective-permute-done | bytes 98336 | tf_op jit(solution)/shard_map/ppermute | solution.py:268
  23.3 0.9 %late_cross_attention.1 = (bf16[5,48,128]{2,1,0:T(8,128)(2,1)S(1)}, bf16[5,48,128]{2,1,0:T(8,128)(2,1)S(1)}, bf16[5,48,128]{2,1,0:T(8,128)(2,1)S(1)}, bf16[5,48,128]{2,1,0:T(8,128)(2,1)S(1)}) custom-call(bf16[2,128,192]{2,1,0:T(8,128)(2,1)S(1)} %get-tuple-element.47.queries, s32[5,128]{1,0:T(8,128)S(1)} %get-tuple-element.48.table, ...), custom_call_target="tpu_custom_call" | custom-call | flops 99999997952 | bytes 1 | tf_op jit(solution)/shard_map/late_cross_attention/pallas_call | solution.py:272
  24.1 1.3 %collective-permute-start.10 = (bf16[5,48,128]{2,1,0:T(8,128)(2,1)S(1)}, bf16[5,48,128]{2,1,0:T(8,128)(2,1)S(1)}, u32[]{:S(2)}, u32[]{:S(2)}) collective-permute-start(bf16[5,48,128]{2,1,0:T(8,128)(2,1)S(1)} %get-tuple-element.53), channel_id=1, source_target_pairs={{0,2},{1,3},{2,0},{3,1},{4,6},{5,7},{6,4},{7,5},{8,10},{9,11},{10,... | collective-permute-start | bytes 184328 | tf_op jit(solution)/shard_map/ppermute | solution.py:265
  25.4 1.3 %collective-permute-start.11 = (bf16[5,48,128]{2,1,0:T(8,128)(2,1)S(1)}, bf16[5,48,128]{2,1,0:T(8,128)(2,1)S(1)}, u32[]{:S(2)}, u32[]{:S(2)}) collective-permute-start(bf16[5,48,128]{2,1,0:T(8,128)(2,1)S(1)} %get-tuple-element.54), channel_id=1, source_target_pairs={{0,1},{1,0},{2,3},{3,2},{4,5},{5,4},{6,7},{7,6},{8,9},{9,8},{10,11... | collective-permute-start | bytes 184328 | tf_op jit(solution)/shard_map/ppermute | solution.py:265
  26.7 0.1 collective-permute-start.12
  26.8 0.4 %collective-permute-done.10.rest_1_ = bf16[5,48,128]{2,1,0:T(8,128)(2,1)S(1)} collective-permute-done((bf16[5,48,128]{2,1,0:T(8,128)(2,1)S(1)}, bf16[5,48,128]{2,1,0:T(8,128)(2,1)S(1)}, u32[]{:S(2)}, u32[]{:S(2)}) %collective-permute-start.10) | collective-permute-done | bytes 61472 | tf_op jit(solution)/shard_map/ppermute | solution.py:265
  27.2 0.3 %collective-permute-done.11.rest_2_ = bf16[5,48,128]{2,1,0:T(8,128)(2,1)S(1)} collective-permute-done((bf16[5,48,128]{2,1,0:T(8,128)(2,1)S(1)}, bf16[5,48,128]{2,1,0:T(8,128)(2,1)S(1)}, u32[]{:S(2)}, u32[]{:S(2)}) %collective-permute-start.11) | collective-permute-done | bytes 61472 | tf_op jit(solution)/shard_map/ppermute | solution.py:265
  27.6 2.7 %collective-permute-done.12.rest_3_ = bf16[5,48,128]{2,1,0:T(8,128)(2,1)S(1)} collective-permute-done((bf16[5,48,128]{2,1,0:T(8,128)(2,1)S(1)}, bf16[5,48,128]{2,1,0:T(8,128)(2,1)S(1)}, u32[]{:S(2)}, u32[]{:S(2)}) %collective-permute-start.12) | collective-permute-done | bytes 61472 | tf_op jit(solution)/shard_map/ppermute | solution.py:265
  30.3 2.0 %pair_output.1 = bf16[2,5,32,768]{3,2,1,0:T(8,128)(2,1)} custom-call(s32[2,5]{1,0:T(2,128)} %partners.3, f32[2,32,768]{2,1,0:T(8,128)S(1)} %get-tuple-element.46.own_rows, bf16[384,768]{1,0:T(8,128)(2,1)S(1)} %cross_output_both_rows.1.own_weights, bf16[384,768]{1,0:T(8,128)(2,1)S(1)} %collective-permute-done.7.core_weights, ...), custom_call_target="tpu_custom_call" | custom-call | flops 1 | bytes 1 | tf_op jit(solution)/shard_map/pair_output/pallas_call | solution.py:272
  (11 shorter events, 0.0 us)
Async XLA Ops:
  0.0 11.3 %collective-permute-start.2 = (bf16[192,768]{1,0:T(8,128)(2,1)}, bf16[192,768]{1,0:T(8,128)(2,1)S(1)}, u32[]{:S(2)}, u32[]{:S(2)}) collective-permute-start(bf16[192,768]{1,0:T(8,128)(2,1)} %param.12), channel_id=1, source_target_pairs={{0,2},{1,3},{2,0},{3,1},{4,6},{5,7},{6,4},{7,5},{8,10},{9,11},{10,... | collective-permute-start | bytes 884744 | tf_op jit(solution)/shard_map/ppermute | solution.py:265
  1.2 20.3 %collective-permute-start.5 = (bf16[192,768]{1,0:T(8,128)(2,1)}, bf16[192,768]{1,0:T(8,128)(2,1)S(1)}, u32[]{:S(2)}, u32[]{:S(2)}) collective-permute-start(bf16[192,768]{1,0:T(8,128)(2,1)} %own.1), channel_id=1, source_target_pairs={{0,2},{1,3},{2,0},{3,1},{4,6},{5,7},{6,4},{7,5},{8,10},{9,11},{10,... | collective-permute-start | bytes 884744 | tf_op jit(solution)/shard_map/ppermute | solution.py:265
  1.5 15.0 %copy-start.3 = (bf16[192,768]{1,0:T(8,128)(2,1)S(1)}, bf16[192,768]{1,0:T(8,128)(2,1)}, u32[]{:S(2)}) copy-start(bf16[192,768]{1,0:T(8,128)(2,1)} %param.12) | copy-start | bytes 884740
  4.9 7.5 %copy-start.1 = (f32[3,768]{1,0:T(4,128)S(1)}, f32[3,768]{1,0:T(4,128)}, u32[]{:S(2)}) copy-start(f32[3,768]{1,0:T(4,128)} %value.1) | copy-start | bytes 27652
  5.0 11.6 %copy-start.2 = (bf16[2,128,768]{2,1,0:T(8,128)(2,1)S(1)}, bf16[2,128,768]{2,1,0:T(8,128)(2,1)}, u32[]{:S(2)}) copy-start(bf16[2,128,768]{2,1,0:T(8,128)(2,1)} %states.1) | copy-start | bytes 1179652
  5.0 3.8 %collective-permute-start.3 = (bf16[384,128]{1,0:T(8,128)(2,1)S(1)}, bf16[384,128]{1,0:T(8,128)(2,1)S(1)}, u32[]{:S(2)}, u32[]{:S(2)}) collective-permute-start(bf16[384,128]{1,0:T(8,128)(2,1)S(1)} %get-tuple-element.43), channel_id=1, source_target_pairs={{0,8},{4,12},{8,0},{12,4},{16,24},{20,28},{24,16},{28,20},{1,9},{5... | collective-permute-start | bytes 294920 | tf_op jit(solution)/shard_map/ppermute | solution.py:268
  6.3 3.8 %collective-permute-start.4 = (bf16[384,128]{1,0:T(8,128)(2,1)S(1)}, bf16[384,128]{1,0:T(8,128)(2,1)S(1)}, u32[]{:S(2)}, u32[]{:S(2)}) collective-permute-start(bf16[384,128]{1,0:T(8,128)(2,1)S(1)} %get-tuple-element.44), channel_id=1, source_target_pairs={{0,4},{4,0},{8,12},{12,8},{16,20},{20,16},{24,28},{28,24},{1,5},{5... | collective-permute-start | bytes 294920 | tf_op jit(solution)/shard_map/ppermute | solution.py:268
  7.5 9.0 %collective-permute-start.1 = (bf16[384,128]{1,0:T(8,128)(2,1)S(1)}, bf16[384,128]{1,0:T(8,128)(2,1)S(1)}, u32[]{:S(2)}, u32[]{:S(2)}) collective-permute-start(bf16[384,128]{1,0:T(8,128)(2,1)S(1)} %get-tuple-element.42), channel_id=1, source_target_pairs={{0,2},{1,3},{2,0},{3,1},{4,6},{5,7},{6,4},{7,5},{8,10},{9,11},{10,... | collective-permute-start | bytes 294920 | tf_op jit(solution)/shard_map/ppermute | solution.py:265
  8.8 11.7 %collective-permute-start.6 = (bf16[384,128]{1,0:T(8,128)(2,1)S(1)}, bf16[384,128]{1,0:T(8,128)(2,1)S(1)}, u32[]{:S(2)}, u32[]{:S(2)}) collective-permute-start(bf16[384,128]{1,0:T(8,128)(2,1)S(1)} %get-tuple-element.49), channel_id=1, source_target_pairs={{0,16},{4,20},{8,24},{12,28},{16,0},{20,4},{24,8},{28,12},{1,17},{... | collective-permute-start | bytes 294920 | tf_op jit(solution)/shard_map/ppermute | solution.py:268
  10.1 12.3 %collective-permute-start.8 = (bf16[384,128]{1,0:T(8,128)(2,1)S(1)}, bf16[384,128]{1,0:T(8,128)(2,1)S(1)}, u32[]{:S(2)}, u32[]{:S(2)}) collective-permute-start(bf16[384,128]{1,0:T(8,128)(2,1)S(1)} %get-tuple-element.50), channel_id=1, source_target_pairs={{0,24},{4,28},{8,16},{12,20},{16,8},{20,12},{24,0},{28,4},{1,25},{... | collective-permute-start | bytes 294920 | tf_op jit(solution)/shard_map/ppermute | solution.py:268
  11.3 12.0 %collective-permute-start.9 = (bf16[384,128]{1,0:T(8,128)(2,1)S(1)}, bf16[384,128]{1,0:T(8,128)(2,1)S(1)}, u32[]{:S(2)}, u32[]{:S(2)}) collective-permute-start(bf16[384,128]{1,0:T(8,128)(2,1)S(1)} %get-tuple-element.51), channel_id=1, source_target_pairs={{0,28},{4,8},{8,4},{12,16},{16,12},{20,24},{24,20},{28,0},{1,29},{... | collective-permute-start | bytes 294920 | tf_op jit(solution)/shard_map/ppermute | solution.py:268
  17.0 3.0 %collective-permute-start = (bf16[256,768]{1,0:T(8,128)(2,1)S(1)}, bf16[256,768]{1,0:T(8,128)(2,1)S(1)}, u32[]{:S(2)}, u32[]{:S(2)}) collective-permute-start(bf16[256,768]{1,0:T(8,128)(2,1)S(1)} %get-tuple-element.25), channel_id=1, source_target_pairs={{0,1},{1,0},{2,3},{3,2},{4,5},{5,4},{6,7},{7,6},{8,9},{9,8},{10,11... | collective-permute-start | bytes 1179656 | tf_op jit(solution)/shard_map/cond/branch_1_fun/ppermute | solution.py:265
  20.5 1.1 %copy-start = (bf16[192,768]{1,0:T(8,128)(2,1)S(1)}, bf16[192,768]{1,0:T(8,128)(2,1)}, u32[]{:S(2)}) copy-start(bf16[192,768]{1,0:T(8,128)(2,1)} %own.1) | copy-start | bytes 884740
  21.7 8.7 %collective-permute-start.7 = (bf16[384,768]{1,0:T(8,128)(2,1)S(1)}, bf16[384,768]{1,0:T(8,128)(2,1)S(1)}, u32[]{:S(2)}, u32[]{:S(2)}) collective-permute-start(bf16[384,768]{1,0:T(8,128)(2,1)S(1)} %cross_output_both_rows.1.own_weights), channel_id=1, source_target_pairs={{0,1},{1,0},{2,3},{3,2},{4,5},{5,4},{6,7},{7,6},{8,9},{9,8},{10,11... | collective-permute-start | bytes 1769480 | tf_op jit(solution)/shard_map/ppermute | solution.py:265
  24.1 3.1 %collective-permute-start.10 = (bf16[5,48,128]{2,1,0:T(8,128)(2,1)S(1)}, bf16[5,48,128]{2,1,0:T(8,128)(2,1)S(1)}, u32[]{:S(2)}, u32[]{:S(2)}) collective-permute-start(bf16[5,48,128]{2,1,0:T(8,128)(2,1)S(1)} %get-tuple-element.53), channel_id=1, source_target_pairs={{0,2},{1,3},{2,0},{3,1},{4,6},{5,7},{6,4},{7,5},{8,10},{9,11},{10,... | collective-permute-start | bytes 184328 | tf_op jit(solution)/shard_map/ppermute | solution.py:265
  25.4 2.2 %collective-permute-start.11 = (bf16[5,48,128]{2,1,0:T(8,128)(2,1)S(1)}, bf16[5,48,128]{2,1,0:T(8,128)(2,1)S(1)}, u32[]{:S(2)}, u32[]{:S(2)}) collective-permute-start(bf16[5,48,128]{2,1,0:T(8,128)(2,1)S(1)} %get-tuple-element.54), channel_id=1, source_target_pairs={{0,1},{1,0},{2,3},{3,2},{4,5},{5,4},{6,7},{7,6},{8,9},{9,8},{10,11... | collective-permute-start | bytes 184328 | tf_op jit(solution)/shard_map/ppermute | solution.py:265
  26.7 3.6 %collective-permute-start.12 = (bf16[5,48,128]{2,1,0:T(8,128)(2,1)S(1)}, bf16[5,48,128]{2,1,0:T(8,128)(2,1)S(1)}, u32[]{:S(2)}, u32[]{:S(2)}) collective-permute-start(bf16[5,48,128]{2,1,0:T(8,128)(2,1)S(1)} %get-tuple-element.55), channel_id=1, source_target_pairs={{0,3},{1,2},{2,1},{3,0},{4,7},{5,6},{6,5},{7,4},{8,11},{9,10},{10,... | collective-permute-start | bytes 184328 | tf_op jit(solution)/shard_map/ppermute | solution.py:265

commit v8 on v7

--- a/solution.py
+++ b/solution.py
@@ -94,9 +94,9 @@
     return found
 
 
-def own_images_kernel(swaps, owner_n, states, gains, self_t, cross_t, partners, *rest):
+def own_images_kernel(swaps, owner_n, states, gains, self_t, cross_t, partners, weight, *rest):
     outs, rest = rest[: len(swaps)], rest[len(swaps) :]
-    context_out, table, query_weight_out, states_v, gains_v, self_v, cross_v, partners_s, held, sems = rest
+    context_out, table, query_weight_out, weight_out, states_v, gains_v, self_v, cross_v, partners_s, held, sems = rest
     image_n, patch_n, width = states.shape
     columns = self_t.shape[1]
     copies = [
@@ -106,6 +106,7 @@
         pltpu.make_async_copy(partners, partners_s, sems.at[3]),
         pltpu.make_async_copy(self_t, self_v, sems.at[4]),
         pltpu.make_async_copy(cross_t.at[0], query_weight_out, sems.at[5]),
+        pltpu.make_async_copy(weight, weight_out, sems.at[6]),
     ]
     for copy in copies:
         copy.start()
@@ -135,6 +136,7 @@
         )
     context_out[...] = pack(jnp.concatenate(contexts, 0))
     copies[5].wait()
+    copies[6].wait()
 
 
 def unpack(block):
@@ -226,18 +228,17 @@
 
 
 def out_kernel(swaps, owner_n, partners, own_rows, own_weights, core_weights, *rest):
-    *sides, out, term_ref, partners_s, sem = rest
-    copy = pltpu.make_async_copy(partners, partners_s, sem)
+    *sides, out, term_ref, out_v, partners_s, sems = rest
+    copy = pltpu.make_async_copy(partners, partners_s, sems.at[0])
     copy.start()
     image_n, row_n, width = own_rows.shape
-    half = len(sides) // 2
-    rows = [side_rows(side[...]) for side in sides]
-    terms = nn(jnp.concatenate(rows[:half], 1), own_weights[...])
-    terms = terms + nn(jnp.concatenate(rows[half:], 1), core_weights[...])
+    rows = jnp.concatenate([side_rows(side[...]) for side in sides], 1)
+    terms = nn(rows, jnp.concatenate([own_weights[...], core_weights[...]], 0))
     term_ref[...] = terms.reshape(len(swaps), row_n, width)
     copy.wait()
     me = lax.axis_index("owner")
     lows = [swap_target(me, swap, owner_n) * image_n for swap in swaps]
+    sent = []
     for image in range(image_n):
         for slot in range(partners.shape[1]):
             partner = partners_s[image, slot]
@@ -246,7 +247,11 @@
                 gap = partner - low
                 which = jnp.where(jnp.logical_and(gap >= 0, gap < image_n), jnp.int32(at), which)
             value = (own_rows[image] + term_ref[which]).astype(BF16)
-            out[image, slot] = jnp.where(partner >= 0, value, jnp.zeros_like(value))
+            out_v[image, slot] = jnp.where(partner >= 0, value, jnp.zeros_like(value))
+        sent.append(pltpu.make_async_copy(out_v.at[image], out.at[image], sems.at[1 + image]))
+        sent[-1].start()
+    for copy in sent:
+        copy.wait()
 
 
 def local(owner_n, helper_n, states, partners, self_proj, self_out, cross_proj, cross_out, gains):
@@ -267,13 +272,13 @@
     def exchange(value, swap):
         return lax.ppermute(value, "owner", [(o, swap_target(o, swap, owner_n)) for o in range(owner_n)])
 
-    def call(name, kernel, out_shape, in_specs, scratch, *operands, flops=1):
+    def call(name, kernel, out_shape, in_specs, scratch, *operands, out_specs=None, flops=1):
         with jax.named_scope(name):
             return pl.pallas_call(
                 kernel,
                 out_shape=out_shape,
                 in_specs=in_specs,
-                out_specs=jax.tree.map(lambda _: VMEM, out_shape),
+                out_specs=out_specs or jax.tree.map(lambda _: VMEM, out_shape),
                 scratch_shapes=scratch,
                 compiler_params=pltpu.CompilerParams(vmem_limit_bytes=VMEM_BYTES),
                 cost_estimate=pl.CostEstimate(flops=flops, bytes_accessed=1, transcendentals=0),
@@ -286,8 +291,7 @@
 
     partners_h = pltpu.with_memory_space_constraint(partners, pltpu.HBM)
     self_out_got = across(self_out, chip_hop)
-    cross_out_got = across(cross_out, chip_hop)
-    *outgoing, context, table, query_weight = call(
+    *outgoing, context, table, query_weight, cross_out_own = call(
         "own_images",
         functools.partial(own_images_kernel, swaps, owner_n),
         [block] * pair_n
@@ -295,8 +299,9 @@
             shape((row_all * columns // LANES, LANES), BF16),
             shape((pair_n, LANES), jnp.int32),
             shape((columns, width), BF16),
+            shape(cross_out.shape, BF16),
         ],
-        [HBM] * 5,
+        [HBM] * 6,
         [
             pltpu.VMEM(states.shape, BF16),
             pltpu.VMEM(gains.shape, F32),
@@ -304,11 +309,13 @@
             pltpu.VMEM((2, columns, width), BF16),
             index_table,
             pltpu.VMEM((image_n, 2 * columns, patch_n), BF16),
-            dma((6,)),
+            dma((7,)),
         ],
         *[pltpu.with_memory_space_constraint(x, pltpu.HBM) for x in (states, gains, self_proj_t, cross_proj_t)],
         partners_h,
-    )
+        pltpu.with_memory_space_constraint(cross_out, pltpu.HBM),
+    )
+    cross_out_got = across(cross_out_own, chip_hop)
     arrived = [exchange(value, swap) for value, swap in zip(outgoing, swaps)]
     context_got = across(context, chip_hop)
     near = (slot_n - 1) // 2
@@ -390,9 +397,15 @@
         functools.partial(out_kernel, [swaps[at] for at in early + late], owner_n),
         shape((image_n, slot_n, row_n, width), BF16),
         [HBM] + [VMEM] * (3 + helper_n),
-        [pltpu.VMEM((pair_n, row_n, width), F32), index_table, dma],
+        [
+            pltpu.VMEM((pair_n, row_n, width), F32),
+            pltpu.VMEM((image_n, slot_n, row_n, width), BF16),
+            index_table,
+            dma((1 + image_n,)),
+        ],
         partners_h, own_rows, cross_out_both, cross_out_core,
         *[sides[k] for k in (0, chip_hop, core_hop, chip_hop ^ core_hop)],
+        out_specs=HBM,
     )
 
 

time: 32.4 us -> 32.4 us (level)
  no operation moved by 1% of the time
where the time goes in v8:
time: 32.4 us; the launch traced here: 32.3 us
  starting transfers between devices  12.4 us (38%)
  waiting for transfers between devices  11.3 us (35%)
  Pallas kernels  8.39 us (26%)
    ppermute x8, waiting for transfers between devices, across(): return lax.ppermute(value, 'helper', [(j, j ^ k) for j in range(helper_n)])  8.9 us
    pallas_call x8, Pallas kernels, call(): pl.pallas_call(kernel, out_shape=out_shape, in_specs=in_specs, out_specs=...  8.39 us
    ppermute x8, starting transfers between devices, across(): return lax.ppermute(value, 'helper', [(j, j ^ k) for j in range(helper_n)])  7.49 us
    ppermute x5, starting transfers between devices, exchange(): lax.ppermute(value, 'owner', [(o, swap_target(o, swap, owner_n)) for o in...  4.94 us
    ppermute x5, waiting for transfers between devices, exchange(): lax.ppermute(value, 'owner', [(o, swap_target(o, swap, owner_n)) for o in...  2.43 us
  transfers between devices with their start and end apart: 13, of which 8 were waited for; matrix products, arithmetic and copies ran while one was open for 0% of the time, Pallas kernels for 20%

profile of v8, /device:TPU:17, one launch (start us, length us, event | category | flops | bytes accessed | tf_op | source)
XLA Modules:
  0.0 32.3 jit_solution(13374988276196720465)
XLA Ops:
  0.0 1.2 %collective-permute-start.2 = (bf16[192,768]{1,0:T(8,128)(2,1)}, bf16[192,768]{1,0:T(8,128)(2,1)S(1)}, u32[]{:S(2)}, u32[]{:S(2)}) collective-permute-start(bf16[192,768]{1,0:T(8,128)(2,1)} %param.12), channel_id=1, source_target_pairs={{0,2},{1,3},{2,0},{3,1},{4,6},{5,7},{6,4},{7,5},{8,10},{9,11},{10,... | collective-permute-start | bytes 884744 | tf_op jit(solution)/shard_map/ppermute | solution.py:270
  1.2 3.5 %own_images.1 = (bf16[384,128]{1,0:T(8,128)(2,1)S(1)}, bf16[384,128]{1,0:T(8,128)(2,1)S(1)}, bf16[384,128]{1,0:T(8,128)(2,1)S(1)}, bf16[384,128]{1,0:T(8,128)(2,...) custom-call(bf16[2,128,768]{2,1,0:T(8,128)(2,1)} %states.1, ...), custom_call_target="tpu_custom_call" | custom-call | flops 1 | bytes 1 | tf_op jit(solution)/shard_map/own_images/pallas_call | solution.py:277
  4.7 0.0 copy-start.1
  4.7 0.0 copy-start.2
  4.7 0.3 collective-permute-start.5
  5.0 1.3 %collective-permute-start.3 = (bf16[384,128]{1,0:T(8,128)(2,1)S(1)}, bf16[384,128]{1,0:T(8,128)(2,1)S(1)}, u32[]{:S(2)}, u32[]{:S(2)}) collective-permute-start(bf16[384,128]{1,0:T(8,128)(2,1)S(1)} %get-tuple-element.44), channel_id=1, source_target_pairs={{0,8},{4,12},{8,0},{12,4},{16,24},{20,28},{24,16},{28,20},{1,9},{5... | collective-permute-start | bytes 294920 | tf_op jit(solution)/shard_map/ppermute | solution.py:273
  6.3 1.2 %collective-permute-start.4 = (bf16[384,128]{1,0:T(8,128)(2,1)S(1)}, bf16[384,128]{1,0:T(8,128)(2,1)S(1)}, u32[]{:S(2)}, u32[]{:S(2)}) collective-permute-start(bf16[384,128]{1,0:T(8,128)(2,1)S(1)} %get-tuple-element.45), channel_id=1, source_target_pairs={{0,4},{4,0},{8,12},{12,8},{16,20},{20,16},{24,28},{28,24},{1,5},{5... | collective-permute-start | bytes 294920 | tf_op jit(solution)/shard_map/ppermute | solution.py:273
  7.5 1.2 %collective-permute-start.1 = (bf16[384,128]{1,0:T(8,128)(2,1)S(1)}, bf16[384,128]{1,0:T(8,128)(2,1)S(1)}, u32[]{:S(2)}, u32[]{:S(2)}) collective-permute-start(bf16[384,128]{1,0:T(8,128)(2,1)S(1)} %get-tuple-element.43), channel_id=1, source_target_pairs={{0,2},{1,3},{2,0},{3,1},{4,6},{5,7},{6,4},{7,5},{8,10},{9,11},{10,... | collective-permute-start | bytes 294920 | tf_op jit(solution)/shard_map/ppermute | solution.py:270
  8.8 0.0 collective-permute-done.3.rest_0_.rest_1_
  8.8 0.0 collective-permute-start.6
  8.8 1.3 %collective-permute-done.4.rest_1_.rest_2_ = bf16[384,128]{1,0:T(8,128)(2,1)S(1)} collective-permute-done((bf16[384,128]{1,0:T(8,128)(2,1)S(1)}, bf16[384,128]{1,0:T(8,128)(2,1)S(1)}, u32[]{:S(2)}, u32[]{:S(2)}) %collective-permute-start.4) | collective-permute-done | bytes 98336 | tf_op jit(solution)/shard_map/ppermute | solution.py:273
  10.1 1.2 %collective-permute-start.8 = (bf16[384,128]{1,0:T(8,128)(2,1)S(1)}, bf16[384,128]{1,0:T(8,128)(2,1)S(1)}, u32[]{:S(2)}, u32[]{:S(2)}) collective-permute-start(bf16[384,128]{1,0:T(8,128)(2,1)S(1)} %get-tuple-element.52), channel_id=1, source_target_pairs={{0,24},{4,28},{8,16},{12,20},{16,8},{20,12},{24,0},{28,4},{1,25},{... | collective-permute-start | bytes 294920 | tf_op jit(solution)/shard_map/ppermute | solution.py:273
  11.3 1.2 %collective-permute-start.9 = (bf16[384,128]{1,0:T(8,128)(2,1)S(1)}, bf16[384,128]{1,0:T(8,128)(2,1)S(1)}, u32[]{:S(2)}, u32[]{:S(2)}) collective-permute-start(bf16[384,128]{1,0:T(8,128)(2,1)S(1)} %get-tuple-element.53), channel_id=1, source_target_pairs={{0,28},{4,8},{8,4},{12,16},{16,12},{20,24},{24,20},{28,0},{1,29},{... | collective-permute-start | bytes 294920 | tf_op jit(solution)/shard_map/ppermute | solution.py:273
  12.5 4.0 %collective-permute-done.1 = bf16[384,128]{1,0:T(8,128)(2,1)S(1)} collective-permute-done((bf16[384,128]{1,0:T(8,128)(2,1)S(1)}, bf16[384,128]{1,0:T(8,128)(2,1)S(1)}, u32[]{:S(2)}, u32[]{:S(2)}) %collective-permute-start.1) | collective-permute-done | bytes 98336 | tf_op jit(solution)/shard_map/ppermute | solution.py:270
  16.5 3.9 %conditional.1 = ((f32[2,32,768]{2,1,0:T(8,128)S(1)}, bf16[2,128,192]{2,1,0:T(8,128)(2,1)S(1)})) conditional(s32[]{:T(128)} %convert_element_type.3, () %tuple.12, (bf16[2,128,768]{2,1,0:T(8,128)(2,1)S(1)}, bf16[384,128]{1,0:T(8,128)(2,1)S(1)}, bf16[384,128]{1,0:T(8,128)(2,1)S(1)}, bf16[192,768]{1,0:T(8,128)(2,1)S(1)}, ...), branch_computations={%region_0.0_spmd, %region_1.0_spmd} | conditional | flops 2 | bytes 1572914 | solution.py:362
  16.5 0.4 %self_output_share.1 = (f32[256,768]{1,0:T(8,128)S(1)}, bf16[256,768]{1,0:T(8,128)(2,1)S(1)}) custom-call(bf16[2,128,768]{2,1,0:T(8,128)(2,1)S(1)} %get-tuple-element.19.states, bf16[384,128]{1,0:T(8,128)(2,1)S(1)} %get-tuple-element.20.own, bf16[384,128]{1,0:T(8,128)(2,1)S(1)} %get-tuple-element.21.got, bf16[192,768]{1,0:T(8,128)(2,1)S(1)} %get-tuple-element.22.own_weight, ...), custom_call_target="tpu_custom_call" | custom-call | flops 1 | bytes 1 | tf_op jit(solution)/shard_map/cond/branch_1_fun/self_output_share/pallas_call | solution.py:277
  17.0 1.6 %collective-permute-start = (bf16[256,768]{1,0:T(8,128)(2,1)S(1)}, bf16[256,768]{1,0:T(8,128)(2,1)S(1)}, u32[]{:S(2)}, u32[]{:S(2)}) collective-permute-start(bf16[256,768]{1,0:T(8,128)(2,1)S(1)} %get-tuple-element.25), channel_id=1, source_target_pairs={{0,1},{1,0},{2,3},{3,2},{4,5},{5,4},{6,7},{7,6},{8,9},{9,8},{10,11... | collective-permute-start | bytes 1179656 | tf_op jit(solution)/shard_map/cond/branch_1_fun/ppermute | solution.py:270
  18.6 1.3 %collective-permute-done.got = bf16[256,768]{1,0:T(8,128)(2,1)S(1)} collective-permute-done((bf16[256,768]{1,0:T(8,128)(2,1)S(1)}, bf16[256,768]{1,0:T(8,128)(2,1)S(1)}, u32[]{:S(2)}, u32[]{:S(2)}) %collective-permute-start) | collective-permute-done | bytes 393248 | tf_op jit(solution)/shard_map/cond/branch_1_fun/ppermute | solution.py:270
  19.9 0.5 %mixed_and_queries.1 = (f32[2,32,768]{2,1,0:T(8,128)S(1)}, bf16[2,128,192]{2,1,0:T(8,128)(2,1)S(1)}) custom-call(f32[256,768]{1,0:T(8,128)S(1)} %get-tuple-element.24.base, bf16[256,768]{1,0:T(8,128)(2,1)S(1)} %collective-permute-done.got, f32[3,768]{1,0:T(4,128)S(1)} %get-tuple-element.26.gains, bf16[192,768]{1,0:T(8,128)(2,1)S(1)} %get-tuple-element.27.weight), custom_call_target="tpu_custom_call" | custom-call | flops 1 | bytes 1 | tf_op jit(solution)/shard_map/cond/branch_1_fun/mixed_and_queries/pallas_call | solution.py:277
  20.5 1.0 %early_cross_attention.1.waited.before = bf16[4,3,48,128]{3,2,1,0:T(8,128)(2,1)S(1)} custom-call(bf16[2,128,192]{2,1,0:T(8,128)(2,1)S(1)} %get-tuple-element.49.queries, s32[5,128]{1,0:T(8,128)S(1)} %get-tuple-element.50.table, bf16[384,128]{1,0:T(8,128)(2,1)S(1)} %collective-permute-done.6.rest_0_, ...), custom_call_target="tpu_custom_call" | custom-call | flops 1 | bytes 1 | tf_op jit(solution)/shard_map/early_cross_attention/pallas_call | solution.py:277
  21.5 0.1 cross_output_both_rows.1.own_weights
  21.7 0.4 %collective-permute-start.7 = (bf16[384,768]{1,0:T(8,128)(2,1)S(1)}, bf16[384,768]{1,0:T(8,128)(2,1)S(1)}, u32[]{:S(2)}, u32[]{:S(2)}) collective-permute-start(bf16[384,768]{1,0:T(8,128)(2,1)S(1)} %cross_output_both_rows.1.own_weights), channel_id=1, source_target_pairs={{0,1},{1,0},{2,3},{3,2},{4,5},{5,4},{6,7},{7,6},{8,9},{9,8},{10,11... | collective-permute-start | bytes 1769480 | tf_op jit(solution)/shard_map/ppermute | solution.py:270
  22.1 0.3 collective-permute-done.8.rest_0_
  22.4 0.8 %collective-permute-done.9.rest_1_ = bf16[384,128]{1,0:T(8,128)(2,1)S(1)} collective-permute-done((bf16[384,128]{1,0:T(8,128)(2,1)S(1)}, bf16[384,128]{1,0:T(8,128)(2,1)S(1)}, u32[]{:S(2)}, u32[]{:S(2)}) %collective-permute-start.9) | collective-permute-done | bytes 98336 | tf_op jit(solution)/shard_map/ppermute | solution.py:273
  23.3 0.9 %late_cross_attention.1 = (bf16[5,48,128]{2,1,0:T(8,128)(2,1)S(1)}, bf16[5,48,128]{2,1,0:T(8,128)(2,1)S(1)}, bf16[5,48,128]{2,1,0:T(8,128)(2,1)S(1)}, bf16[5,48,128]{2,1,0:T(8,128)(2,1)S(1)}) custom-call(bf16[2,128,192]{2,1,0:T(8,128)(2,1)S(1)} %get-tuple-element.49.queries, s32[5,128]{1,0:T(8,128)S(1)} %get-tuple-element.50.table, ...), custom_call_target="tpu_custom_call" | custom-call | flops 99999997952 | bytes 1 | tf_op jit(solution)/shard_map/late_cross_attention/pallas_call | solution.py:277
  24.1 1.3 %collective-permute-start.10 = (bf16[5,48,128]{2,1,0:T(8,128)(2,1)S(1)}, bf16[5,48,128]{2,1,0:T(8,128)(2,1)S(1)}, u32[]{:S(2)}, u32[]{:S(2)}) collective-permute-start(bf16[5,48,128]{2,1,0:T(8,128)(2,1)S(1)} %get-tuple-element.55), channel_id=1, source_target_pairs={{0,2},{1,3},{2,0},{3,1},{4,6},{5,7},{6,4},{7,5},{8,10},{9,11},{10,... | collective-permute-start | bytes 184328 | tf_op jit(solution)/shard_map/ppermute | solution.py:270
  25.4 1.3 %collective-permute-start.11 = (bf16[5,48,128]{2,1,0:T(8,128)(2,1)S(1)}, bf16[5,48,128]{2,1,0:T(8,128)(2,1)S(1)}, u32[]{:S(2)}, u32[]{:S(2)}) collective-permute-start(bf16[5,48,128]{2,1,0:T(8,128)(2,1)S(1)} %get-tuple-element.56), channel_id=1, source_target_pairs={{0,1},{1,0},{2,3},{3,2},{4,5},{5,4},{6,7},{7,6},{8,9},{9,8},{10,11... | collective-permute-start | bytes 184328 | tf_op jit(solution)/shard_map/ppermute | solution.py:270
  26.7 0.1 collective-permute-start.12
  26.8 0.4 %collective-permute-done.10.rest_1_ = bf16[5,48,128]{2,1,0:T(8,128)(2,1)S(1)} collective-permute-done((bf16[5,48,128]{2,1,0:T(8,128)(2,1)S(1)}, bf16[5,48,128]{2,1,0:T(8,128)(2,1)S(1)}, u32[]{:S(2)}, u32[]{:S(2)}) %collective-permute-start.10) | collective-permute-done | bytes 61472 | tf_op jit(solution)/shard_map/ppermute | solution.py:270
  27.3 0.3 %collective-permute-done.11.rest_2_ = bf16[5,48,128]{2,1,0:T(8,128)(2,1)S(1)} collective-permute-done((bf16[5,48,128]{2,1,0:T(8,128)(2,1)S(1)}, bf16[5,48,128]{2,1,0:T(8,128)(2,1)S(1)}, u32[]{:S(2)}, u32[]{:S(2)}) %collective-permute-start.11) | collective-permute-done | bytes 61472 | tf_op jit(solution)/shard_map/ppermute | solution.py:270
  27.6 2.7 %collective-permute-done.12.rest_3_ = bf16[5,48,128]{2,1,0:T(8,128)(2,1)S(1)} collective-permute-done((bf16[5,48,128]{2,1,0:T(8,128)(2,1)S(1)}, bf16[5,48,128]{2,1,0:T(8,128)(2,1)S(1)}, u32[]{:S(2)}, u32[]{:S(2)}) %collective-permute-start.12) | collective-permute-done | bytes 61472 | tf_op jit(solution)/shard_map/ppermute | solution.py:270
  30.3 1.9 %pair_output.1 = bf16[2,5,32,768]{3,2,1,0:T(8,128)(2,1)} custom-call(s32[2,5]{1,0:T(2,128)} %partners.3, f32[2,32,768]{2,1,0:T(8,128)S(1)} %get-tuple-element.47.own_rows, bf16[384,768]{1,0:T(8,128)(2,1)S(1)} %cross_output_both_rows.1.own_weights, bf16[384,768]{1,0:T(8,128)(2,1)S(1)} %collective-permute-done.7.core_weights, ...), custom_call_target="tpu_custom_call" | custom-call | flops 1 | bytes 1 | tf_op jit(solution)/shard_map/pair_output/pallas_call | solution.py:277
  (11 shorter events, 0.0 us)
Async XLA Ops:
  0.0 11.3 %collective-permute-start.2 = (bf16[192,768]{1,0:T(8,128)(2,1)}, bf16[192,768]{1,0:T(8,128)(2,1)S(1)}, u32[]{:S(2)}, u32[]{:S(2)}) collective-permute-start(bf16[192,768]{1,0:T(8,128)(2,1)} %param.12), channel_id=1, source_target_pairs={{0,2},{1,3},{2,0},{3,1},{4,6},{5,7},{6,4},{7,5},{8,10},{9,11},{10,... | collective-permute-start | bytes 884744 | tf_op jit(solution)/shard_map/ppermute | solution.py:270
  1.2 15.3 %copy-start.3 = (bf16[192,768]{1,0:T(8,128)(2,1)S(1)}, bf16[192,768]{1,0:T(8,128)(2,1)}, u32[]{:S(2)}) copy-start(bf16[192,768]{1,0:T(8,128)(2,1)} %param.12) | copy-start | bytes 884740
  4.7 7.8 %copy-start.1 = (f32[3,768]{1,0:T(4,128)S(1)}, f32[3,768]{1,0:T(4,128)}, u32[]{:S(2)}) copy-start(f32[3,768]{1,0:T(4,128)} %value.1) | copy-start | bytes 27652
  4.7 11.8 %copy-start.2 = (bf16[2,128,768]{2,1,0:T(8,128)(2,1)S(1)}, bf16[2,128,768]{2,1,0:T(8,128)(2,1)}, u32[]{:S(2)}) copy-start(bf16[2,128,768]{2,1,0:T(8,128)(2,1)} %states.1) | copy-start | bytes 1179652
  4.7 16.8 %collective-permute-start.5 = (bf16[192,768]{1,0:T(8,128)(2,1)S(1)}, bf16[192,768]{1,0:T(8,128)(2,1)S(1)}, u32[]{:S(2)}, u32[]{:S(2)}) collective-permute-start(bf16[192,768]{1,0:T(8,128)(2,1)S(1)} %get-tuple-element.48), channel_id=1, source_target_pairs={{0,2},{1,3},{2,0},{3,1},{4,6},{5,7},{6,4},{7,5},{8,10},{9,11},{10,... | collective-permute-start | bytes 884744 | tf_op jit(solution)/shard_map/ppermute | solution.py:270
  5.0 3.8 %collective-permute-start.3 = (bf16[384,128]{1,0:T(8,128)(2,1)S(1)}, bf16[384,128]{1,0:T(8,128)(2,1)S(1)}, u32[]{:S(2)}, u32[]{:S(2)}) collective-permute-start(bf16[384,128]{1,0:T(8,128)(2,1)S(1)} %get-tuple-element.44), channel_id=1, source_target_pairs={{0,8},{4,12},{8,0},{12,4},{16,24},{20,28},{24,16},{28,20},{1,9},{5... | collective-permute-start | bytes 294920 | tf_op jit(solution)/shard_map/ppermute | solution.py:273
  6.3 3.8 %collective-permute-start.4 = (bf16[384,128]{1,0:T(8,128)(2,1)S(1)}, bf16[384,128]{1,0:T(8,128)(2,1)S(1)}, u32[]{:S(2)}, u32[]{:S(2)}) collective-permute-start(bf16[384,128]{1,0:T(8,128)(2,1)S(1)} %get-tuple-element.45), channel_id=1, source_target_pairs={{0,4},{4,0},{8,12},{12,8},{16,20},{20,16},{24,28},{28,24},{1,5},{5... | collective-permute-start | bytes 294920 | tf_op jit(solution)/shard_map/ppermute | solution.py:273
  7.5 9.0 %collective-permute-start.1 = (bf16[384,128]{1,0:T(8,128)(2,1)S(1)}, bf16[384,128]{1,0:T(8,128)(2,1)S(1)}, u32[]{:S(2)}, u32[]{:S(2)}) collective-permute-start(bf16[384,128]{1,0:T(8,128)(2,1)S(1)} %get-tuple-element.43), channel_id=1, source_target_pairs={{0,2},{1,3},{2,0},{3,1},{4,6},{5,7},{6,4},{7,5},{8,10},{9,11},{10,... | collective-permute-start | bytes 294920 | tf_op jit(solution)/shard_map/ppermute | solution.py:270
  8.8 11.7 %collective-permute-start.6 = (bf16[384,128]{1,0:T(8,128)(2,1)S(1)}, bf16[384,128]{1,0:T(8,128)(2,1)S(1)}, u32[]{:S(2)}, u32[]{:S(2)}) collective-permute-start(bf16[384,128]{1,0:T(8,128)(2,1)S(1)} %get-tuple-element.51), channel_id=1, source_target_pairs={{0,16},{4,20},{8,24},{12,28},{16,0},{20,4},{24,8},{28,12},{1,17},{... | collective-permute-start | bytes 294920 | tf_op jit(solution)/shard_map/ppermute | solution.py:273
  10.1 12.3 %collective-permute-start.8 = (bf16[384,128]{1,0:T(8,128)(2,1)S(1)}, bf16[384,128]{1,0:T(8,128)(2,1)S(1)}, u32[]{:S(2)}, u32[]{:S(2)}) collective-permute-start(bf16[384,128]{1,0:T(8,128)(2,1)S(1)} %get-tuple-element.52), channel_id=1, source_target_pairs={{0,24},{4,28},{8,16},{12,20},{16,8},{20,12},{24,0},{28,4},{1,25},{... | collective-permute-start | bytes 294920 | tf_op jit(solution)/shard_map/ppermute | solution.py:273
  11.3 12.0 %collective-permute-start.9 = (bf16[384,128]{1,0:T(8,128)(2,1)S(1)}, bf16[384,128]{1,0:T(8,128)(2,1)S(1)}, u32[]{:S(2)}, u32[]{:S(2)}) collective-permute-start(bf16[384,128]{1,0:T(8,128)(2,1)S(1)} %get-tuple-element.53), channel_id=1, source_target_pairs={{0,28},{4,8},{8,4},{12,16},{16,12},{20,24},{24,20},{28,0},{1,29},{... | collective-permute-start | bytes 294920 | tf_op jit(solution)/shard_map/ppermute | solution.py:273
  17.0 3.0 %collective-permute-start = (bf16[256,768]{1,0:T(8,128)(2,1)S(1)}, bf16[256,768]{1,0:T(8,128)(2,1)S(1)}, u32[]{:S(2)}, u32[]{:S(2)}) collective-permute-start(bf16[256,768]{1,0:T(8,128)(2,1)S(1)} %get-tuple-element.25), channel_id=1, source_target_pairs={{0,1},{1,0},{2,3},{3,2},{4,5},{5,4},{6,7},{7,6},{8,9},{9,8},{10,11... | collective-permute-start | bytes 1179656 | tf_op jit(solution)/shard_map/cond/branch_1_fun/ppermute | solution.py:270
  20.5 1.1 %copy-start = (bf16[192,768]{1,0:T(8,128)(2,1)S(1)}, bf16[192,768]{1,0:T(8,128)(2,1)}, u32[]{:S(2)}) copy-start(bf16[192,768]{1,0:T(8,128)(2,1)} %own.1) | copy-start | bytes 884740
  21.7 8.7 %collective-permute-start.7 = (bf16[384,768]{1,0:T(8,128)(2,1)S(1)}, bf16[384,768]{1,0:T(8,128)(2,1)S(1)}, u32[]{:S(2)}, u32[]{:S(2)}) collective-permute-start(bf16[384,768]{1,0:T(8,128)(2,1)S(1)} %cross_output_both_rows.1.own_weights), channel_id=1, source_target_pairs={{0,1},{1,0},{2,3},{3,2},{4,5},{5,4},{6,7},{7,6},{8,9},{9,8},{10,11... | collective-permute-start | bytes 1769480 | tf_op jit(solution)/shard_map/ppermute | solution.py:270
  24.1 3.1 %collective-permute-start.10 = (bf16[5,48,128]{2,1,0:T(8,128)(2,1)S(1)}, bf16[5,48,128]{2,1,0:T(8,128)(2,1)S(1)}, u32[]{:S(2)}, u32[]{:S(2)}) collective-permute-start(bf16[5,48,128]{2,1,0:T(8,128)(2,1)S(1)} %get-tuple-element.55), channel_id=1, source_target_pairs={{0,2},{1,3},{2,0},{3,1},{4,6},{5,7},{6,4},{7,5},{8,10},{9,11},{10,... | collective-permute-start | bytes 184328 | tf_op jit(solution)/shard_map/ppermute | solution.py:270
  25.4 2.2 %collective-permute-start.11 = (bf16[5,48,128]{2,1,0:T(8,128)(2,1)S(1)}, bf16[5,48,128]{2,1,0:T(8,128)(2,1)S(1)}, u32[]{:S(2)}, u32[]{:S(2)}) collective-permute-start(bf16[5,48,128]{2,1,0:T(8,128)(2,1)S(1)} %get-tuple-element.56), channel_id=1, source_target_pairs={{0,1},{1,0},{2,3},{3,2},{4,5},{5,4},{6,7},{7,6},{8,9},{9,8},{10,11... | collective-permute-start | bytes 184328 | tf_op jit(solution)/shard_map/ppermute | solution.py:270
  26.7 3.6 %collective-permute-start.12 = (bf16[5,48,128]{2,1,0:T(8,128)(2,1)S(1)}, bf16[5,48,128]{2,1,0:T(8,128)(2,1)S(1)}, u32[]{:S(2)}, u32[]{:S(2)}) collective-permute-start(bf16[5,48,128]{2,1,0:T(8,128)(2,1)S(1)} %get-tuple-element.57), channel_id=1, source_target_pairs={{0,3},{1,2},{2,1},{3,0},{4,7},{5,6},{6,5},{7,4},{8,11},{9,10},{10,... | collective-permute-start | bytes 184328 | tf_op jit(solution)/shard_map/ppermute | solution.py:270

commit v9 on v8

--- a/solution.py
+++ b/solution.py
@@ -12,7 +12,7 @@
 F32 = jnp.float32
 BF16 = jnp.bfloat16
 VMEM_BYTES = 24 * 1024 * 1024
-EARLY_WEIGHT = 1
+EARLY_WEIGHT = 3*10**9
 LATE_WEIGHT = 10**11
 
 VMEM = pl.BlockSpec(memory_space=pltpu.VMEM)
@@ -84,14 +84,23 @@
     ).astype(BF16)
 
 
-def joined_image(partners, owner, image_n):
+def pair_place(partners, owner, image_n):
     low = owner * image_n
-    found = jnp.int32(0)
-    for image in range(1, image_n):
+    found_image, found_slot = jnp.int32(0), jnp.int32(0)
+    for image in range(image_n):
         for slot in range(partners.shape[1]):
             gap = partners[image, slot] - low
-            found = jnp.where(jnp.logical_and(gap >= 0, gap < image_n), jnp.int32(image), found)
-    return found
+            hit = jnp.logical_and(gap >= 0, gap < image_n)
+            found_image = jnp.where(hit, jnp.int32(image), found_image)
+            found_slot = jnp.where(hit, jnp.int32(slot), found_slot)
+    return found_image, found_slot
+
+
+def live_count(partners, image):
+    count = jnp.int32(0)
+    for slot in range(partners.shape[1]):
+        count = count + jnp.where(partners[image, slot] >= 0, jnp.int32(1), jnp.int32(0))
+    return count
 
 
 def own_images_kernel(swaps, owner_n, states, gains, self_t, cross_t, partners, weight, *rest):
@@ -120,10 +129,14 @@
         held[image] = projected[:, image * patch_n : (image + 1) * patch_n]
     copies[3].wait()
     me = lax.axis_index("owner")
+    pair_n = len(swaps)
     for at, (out, swap) in enumerate(zip(outs, swaps)):
-        image = joined_image(partners_s, swap_target(me, swap, owner_n), image_n)
+        image, slot = pair_place(partners_s, swap_target(me, swap, owner_n), image_n)
         out[...] = held[image]
+        position = jnp.where(image == 0, slot, pair_n - 1 - slot)
         table[at : at + 1, :] = jnp.full((1, LANES), image, jnp.int32)
+        table[pair_n + at : pair_n + at + 1, :] = jnp.full((1, LANES), position, jnp.int32)
+    table[2 * pair_n :, :] = jnp.full((1, LANES), live_count(partners_s, 0), jnp.int32)
     normed = (rows * gains_v[0:1, :]).astype(BF16)
     copies[4].wait()
     queries = nt(normed, self_v[0]).astype(BF16).astype(F32) * HEAD ** (-0.5)
@@ -227,30 +240,36 @@
     return jnp.concatenate([main.reshape(-1, LANES), tail.reshape(-1, HEAD)], 1)
 
 
-def out_kernel(swaps, owner_n, partners, own_rows, own_weights, core_weights, *rest):
-    *sides, out, term_ref, out_v, partners_s, sems = rest
-    copy = pltpu.make_async_copy(partners, partners_s, sems.at[0])
-    copy.start()
-    image_n, row_n, width = own_rows.shape
-    rows = jnp.concatenate([side_rows(side[...]) for side in sides], 1)
-    terms = nn(rows, jnp.concatenate([own_weights[...], core_weights[...]], 0))
-    term_ref[...] = terms.reshape(len(swaps), row_n, width)
-    copy.wait()
-    me = lax.axis_index("owner")
-    lows = [swap_target(me, swap, owner_n) * image_n for swap in swaps]
-    sent = []
-    for image in range(image_n):
-        for slot in range(partners.shape[1]):
-            partner = partners_s[image, slot]
-            which = jnp.int32(0)
-            for at, low in enumerate(lows):
-                gap = partner - low
-                which = jnp.where(jnp.logical_and(gap >= 0, gap < image_n), jnp.int32(at), which)
-            value = (own_rows[image] + term_ref[which]).astype(BF16)
-            out_v[image, slot] = jnp.where(partner >= 0, value, jnp.zeros_like(value))
-        sent.append(pltpu.make_async_copy(out_v.at[image], out.at[image], sems.at[1 + image]))
-        sent[-1].start()
-    for copy in sent:
+def out_kernel(order, own_rows, table, own_weights, core_weights, *rest):
+    *sides, out, out_v, sems = rest
+    row_n, width = own_rows.shape[1:]
+    pair_n = len(order)
+    placed = []
+    for side in sides:
+        pairs = [side[at].astype(F32) for at in range(pair_n)]
+        for position in range(pair_n):
+            block = pairs[0]
+            for at in range(1, pair_n):
+                row = pair_n + order[at]
+                block = jnp.where(table[row : row + 1, 0:1] == position, pairs[at], block)
+            placed.append(block.astype(BF16)[None])
+    rows = [
+        side_rows(jnp.concatenate(placed[at * pair_n : (at + 1) * pair_n], 0)) for at in range(len(sides))
+    ]
+    half = len(sides) // 2
+    terms = nn(jnp.concatenate(rows[:half], 1), own_weights[...])
+    terms = terms + nn(jnp.concatenate(rows[half:], 1), core_weights[...])
+    first_n = table[2 * pair_n :, 0:1]
+    zero = jnp.zeros((row_n, width), F32)
+    for position in range(pair_n):
+        term = terms[position * row_n : (position + 1) * row_n]
+        is_first = first_n > position
+        out_v[0, position] = jnp.where(is_first, own_rows[0] + term, zero).astype(BF16)
+        out_v[1, pair_n - 1 - position] = jnp.where(is_first, zero, own_rows[1] + term).astype(BF16)
+    copies = [pltpu.make_async_copy(out_v.at[image], out.at[image], sems.at[image]) for image in range(2)]
+    for copy in copies:
+        copy.start()
+    for copy in copies:
         copy.wait()
 
 
@@ -297,7 +316,7 @@
         [block] * pair_n
         + [
             shape((row_all * columns // LANES, LANES), BF16),
-            shape((pair_n, LANES), jnp.int32),
+            shape((2 * pair_n + 1, LANES), jnp.int32),
             shape((columns, width), BF16),
             shape(cross_out.shape, BF16),
         ],
@@ -315,13 +334,21 @@
         partners_h,
         pltpu.with_memory_space_constraint(cross_out, pltpu.HBM),
     )
-    cross_out_got = across(cross_out_own, chip_hop)
     arrived = [exchange(value, swap) for value, swap in zip(outgoing, swaps)]
     context_got = across(context, chip_hop)
     near = (slot_n - 1) // 2
     late = [at for at, (_, colour) in enumerate(swaps) if colour]
     early = [at for at in range(pair_n) if at not in late]
     short = [2 * near - 2, 2 * near - 1]
+    cross_out_sent = call(
+        "cross_output_rows",
+        hand_on_kernel,
+        shape(cross_out.shape, BF16),
+        [VMEM] + [ANY] * len([arrived[short[0]]]),
+        [],
+        cross_out_own, *[arrived[short[0]]],
+    )
+    cross_out_got = across(cross_out_sent, chip_hop)
     before = [arrived[at] for at in short] + [self_out_got]
     gains_then = call(
         "gains",
@@ -394,16 +421,11 @@
     cross_out_core = across(cross_out_both, core_hop)
     return call(
         "pair_output",
-        functools.partial(out_kernel, [swaps[at] for at in early + late], owner_n),
+        functools.partial(out_kernel, early + late),
         shape((image_n, slot_n, row_n, width), BF16),
-        [HBM] + [VMEM] * (3 + helper_n),
-        [
-            pltpu.VMEM((pair_n, row_n, width), F32),
-            pltpu.VMEM((image_n, slot_n, row_n, width), BF16),
-            index_table,
-            dma((1 + image_n,)),
-        ],
-        partners_h, own_rows, cross_out_both, cross_out_core,
+        [VMEM] * (4 + helper_n),
+        [pltpu.VMEM((image_n, slot_n, row_n, width), BF16), dma((image_n,))],
+        own_rows, table, cross_out_both, cross_out_core,
         *[sides[k] for k in (0, chip_hop, core_hop, chip_hop ^ core_hop)],
         out_specs=HBM,
     )

time: 32.4 us -> 30.4 us (0.938)
  the two profiles are of different devices: /device:TPU:17 before, /device:TPU:0 now
where the time goes in v9:
time: 30.4 us; the launch traced here: 30.2 us
  starting transfers between devices  17 us (56%)
  Pallas kernels  7.87 us (26%)
  waiting for transfers between devices  5.19 us (17%)
    ppermute x5, starting transfers between devices, exchange(): lax.ppermute(value, 'owner', [(o, swap_target(o, swap, owner_n)) for o in...  9.5 us
    pallas_call x9, Pallas kernels, call(): pl.pallas_call(kernel, out_shape=out_shape, in_specs=in_specs, out_specs=...  7.87 us
    ppermute x8, starting transfers between devices, across(): return lax.ppermute(value, 'helper', [(j, j ^ k) for j in range(helper_n)])  7.54 us
    ppermute x8, waiting for transfers between devices, across(): return lax.ppermute(value, 'helper', [(j, j ^ k) for j in range(helper_n)])  4.75 us
  transfers between devices with their start and end apart: 13, of which 4 were waited for; matrix products, arithmetic and copies ran while one was open for 0% of the time, Pallas kernels for 22%

profile of v9, /device:TPU:0, one launch (start us, length us, event | category | flops | bytes accessed | tf_op | source)
XLA Modules:
  0.0 30.2 jit_solution(13210687598718579944)
XLA Ops:
  0.0 3.0 %collective-permute-start.2 = (bf16[192,768]{1,0:T(8,128)(2,1)}, bf16[192,768]{1,0:T(8,128)(2,1)S(1)}, u32[]{:S(2)}, u32[]{:S(2)}) collective-permute-start(bf16[192,768]{1,0:T(8,128)(2,1)} %param.12), channel_id=1, source_target_pairs={{0,2},{1,3},{2,0},{3,1},{4,6},{5,7},{6,4},{7,5},{8,10},{9,11},{10,... | collective-permute-start | bytes 884744 | tf_op jit(solution)/shard_map/ppermute | solution.py:289
  3.0 3.5 %own_images.1 = (bf16[384,128]{1,0:T(8,128)(2,1)S(1)}, bf16[384,128]{1,0:T(8,128)(2,1)S(1)}, bf16[384,128]{1,0:T(8,128)(2,1)S(1)}, bf16[384,128]{1,0:T(8,128)(2,...) custom-call(bf16[2,128,768]{2,1,0:T(8,128)(2,1)} %states.1, ...), custom_call_target="tpu_custom_call" | custom-call | flops 1 | bytes 1 | tf_op jit(solution)/shard_map/own_images/pallas_call | solution.py:296
  6.4 1.6 %collective-permute-start.3 = (bf16[384,128]{1,0:T(8,128)(2,1)S(1)}, bf16[384,128]{1,0:T(8,128)(2,1)S(1)}, u32[]{:S(2)}, u32[]{:S(2)}) collective-permute-start(bf16[384,128]{1,0:T(8,128)(2,1)S(1)} %get-tuple-element.44), channel_id=1, source_target_pairs={{0,8},{4,12},{8,0},{12,4},{16,24},{20,28},{24,16},{28,20},{1,9},{5... | collective-permute-start | bytes 294920 | tf_op jit(solution)/shard_map/ppermute | solution.py:292
  8.1 1.5 %collective-permute-start.4 = (bf16[384,128]{1,0:T(8,128)(2,1)S(1)}, bf16[384,128]{1,0:T(8,128)(2,1)S(1)}, u32[]{:S(2)}, u32[]{:S(2)}) collective-permute-start(bf16[384,128]{1,0:T(8,128)(2,1)S(1)} %get-tuple-element.45), channel_id=1, source_target_pairs={{0,4},{4,0},{8,12},{12,8},{16,20},{20,16},{24,28},{28,24},{1,5},{5... | collective-permute-start | bytes 294920 | tf_op jit(solution)/shard_map/ppermute | solution.py:292
  9.6 0.5 %collective-permute-start.1 = (bf16[384,128]{1,0:T(8,128)(2,1)S(1)}, bf16[384,128]{1,0:T(8,128)(2,1)S(1)}, u32[]{:S(2)}, u32[]{:S(2)}) collective-permute-start(bf16[384,128]{1,0:T(8,128)(2,1)S(1)} %get-tuple-element.43), channel_id=1, source_target_pairs={{0,2},{1,3},{2,0},{3,1},{4,6},{5,7},{6,4},{7,5},{8,10},{9,11},{10,... | collective-permute-start | bytes 294920 | tf_op jit(solution)/shard_map/ppermute | solution.py:289
  10.1 2.6 %collective-permute-start.6 = (bf16[384,128]{1,0:T(8,128)(2,1)S(1)}, bf16[384,128]{1,0:T(8,128)(2,1)S(1)}, u32[]{:S(2)}, u32[]{:S(2)}) collective-permute-start(bf16[384,128]{1,0:T(8,128)(2,1)S(1)} %get-tuple-element.51), channel_id=1, source_target_pairs={{0,16},{4,20},{8,24},{12,28},{16,0},{20,4},{24,8},{28,12},{1,17},{... | collective-permute-start | bytes 294920 | tf_op jit(solution)/shard_map/ppermute | solution.py:292
  12.7 0.0 copy-start.1
  12.7 0.0 copy-start.2
  12.7 1.6 %collective-permute-start.5 = (bf16[192,768]{1,0:T(8,128)(2,1)S(1)}, bf16[192,768]{1,0:T(8,128)(2,1)S(1)}, u32[]{:S(2)}, u32[]{:S(2)}) collective-permute-start(bf16[192,768]{1,0:T(8,128)(2,1)S(1)} %cross_output_rows.1), channel_id=1, source_target_pairs={{0,2},{1,3},{2,0},{3,1},{4,6},{5,7},{6,4},{7,5},{8,10},{9,11},{10,... | collective-permute-start | bytes 884744 | tf_op jit(solution)/shard_map/ppermute | solution.py:289
  14.3 1.0 %collective-permute-start.8 = (bf16[384,128]{1,0:T(8,128)(2,1)S(1)}, bf16[384,128]{1,0:T(8,128)(2,1)S(1)}, u32[]{:S(2)}, u32[]{:S(2)}) collective-permute-start(bf16[384,128]{1,0:T(8,128)(2,1)S(1)} %get-tuple-element.52), channel_id=1, source_target_pairs={{0,24},{4,28},{8,16},{12,20},{16,8},{20,12},{24,0},{28,4},{1,25},{... | collective-permute-start | bytes 294920 | tf_op jit(solution)/shard_map/ppermute | solution.py:292
  15.4 0.0 collective-permute-done.2.rest_2_
  15.4 2.8 %collective-permute-start.9 = (bf16[384,128]{1,0:T(8,128)(2,1)S(1)}, bf16[384,128]{1,0:T(8,128)(2,1)S(1)}, u32[]{:S(2)}, u32[]{:S(2)}) collective-permute-start(bf16[384,128]{1,0:T(8,128)(2,1)S(1)} %get-tuple-element.53), channel_id=1, source_target_pairs={{0,28},{4,8},{8,4},{12,16},{16,12},{20,24},{24,20},{28,0},{1,29},{... | collective-permute-start | bytes 294920 | tf_op jit(solution)/shard_map/ppermute | solution.py:292
  18.1 0.0 collective-permute-done.1
  18.1 2.8 %conditional.1 = ((f32[2,32,768]{2,1,0:T(8,128)S(1)}, bf16[2,128,192]{2,1,0:T(8,128)(2,1)S(1)})) conditional(s32[]{:T(128)} %convert_element_type.3, () %tuple.12, (bf16[2,128,768]{2,1,0:T(8,128)(2,1)S(1)}, bf16[384,128]{1,0:T(8,128)(2,1)S(1)}, bf16[384,128]{1,0:T(8,128)(2,1)S(1)}, bf16[192,768]{1,0:T(8,128)(2,1)S(1)}, ...), branch_computations={%region_0.0_spmd, %region_1.0_spmd} | conditional | flops 2 | bytes 1572914 | solution.py:389
  18.2 0.4 %self_output_share.1 = (f32[256,768]{1,0:T(8,128)S(1)}, bf16[256,768]{1,0:T(8,128)(2,1)S(1)}) custom-call(bf16[2,128,768]{2,1,0:T(8,128)(2,1)S(1)} %get-tuple-element.19.states, bf16[384,128]{1,0:T(8,128)(2,1)S(1)} %get-tuple-element.20.own, bf16[384,128]{1,0:T(8,128)(2,1)S(1)} %get-tuple-element.21.got, bf16[192,768]{1,0:T(8,128)(2,1)S(1)} %get-tuple-element.22.own_weight, ...), custom_call_target="tpu_custom_call" | custom-call | flops 1 | bytes 1 | tf_op jit(solution)/shard_map/cond/branch_1_fun/self_output_share/pallas_call | solution.py:296
  18.6 0.1 collective-permute-start
  18.7 1.7 %collective-permute-done.got = bf16[256,768]{1,0:T(8,128)(2,1)S(1)} collective-permute-done((bf16[256,768]{1,0:T(8,128)(2,1)S(1)}, bf16[256,768]{1,0:T(8,128)(2,1)S(1)}, u32[]{:S(2)}, u32[]{:S(2)}) %collective-permute-start) | collective-permute-done | bytes 393248 | tf_op jit(solution)/shard_map/cond/branch_1_fun/ppermute | solution.py:289
  20.4 0.5 %mixed_and_queries.1 = (f32[2,32,768]{2,1,0:T(8,128)S(1)}, bf16[2,128,192]{2,1,0:T(8,128)(2,1)S(1)}) custom-call(f32[256,768]{1,0:T(8,128)S(1)} %get-tuple-element.24.base, bf16[256,768]{1,0:T(8,128)(2,1)S(1)} %collective-permute-done.got, f32[3,768]{1,0:T(4,128)S(1)} %get-tuple-element.26.gains, bf16[192,768]{1,0:T(8,128)(2,1)S(1)} %get-tuple-element.27.weight), custom_call_target="tpu_custom_call" | custom-call | flops 1 | bytes 1 | tf_op jit(solution)/shard_map/cond/branch_1_fun/mixed_and_queries/pallas_call | solution.py:296
  20.9 0.0 collective-permute-done.6.rest_0_
  20.9 0.0 copy-start
  20.9 1.0 %early_cross_attention.1.waited.before = bf16[4,3,48,128]{3,2,1,0:T(8,128)(2,1)S(1)} custom-call(bf16[2,128,192]{2,1,0:T(8,128)(2,1)S(1)} %get-tuple-element.50.queries, s32[11,128]{1,0:T(8,128)S(1)} %get-tuple-element.48.table, bf16[384,128]{1,0:T(8,128)(2,1)S(1)} %collective-permute-done.6.rest_0_, ...), custom_call_target="tpu_custom_call" | custom-call | flops 3000000000 | bytes 1 | tf_op jit(solution)/shard_map/early_cross_attention/pallas_call | solution.py:296
  22.0 0.1 cross_output_both_rows.1.own_weights
  22.1 0.2 collective-permute-start.7
  22.4 0.4 %collective-permute-done.9.rest_1_ = bf16[384,128]{1,0:T(8,128)(2,1)S(1)} collective-permute-done((bf16[384,128]{1,0:T(8,128)(2,1)S(1)}, bf16[384,128]{1,0:T(8,128)(2,1)S(1)}, u32[]{:S(2)}, u32[]{:S(2)}) %collective-permute-start.9) | collective-permute-done | bytes 98336 | tf_op jit(solution)/shard_map/ppermute | solution.py:292
  22.8 0.9 %late_cross_attention.1 = (bf16[5,48,128]{2,1,0:T(8,128)(2,1)S(1)}, bf16[5,48,128]{2,1,0:T(8,128)(2,1)S(1)}, bf16[5,48,128]{2,1,0:T(8,128)(2,1)S(1)}, bf16[5,48,128]{2,1,0:T(8,128)(2,1)S(1)}) custom-call(bf16[2,128,192]{2,1,0:T(8,128)(2,1)S(1)} %get-tuple-element.50.queries, s32[11,128]{1,0:T(8,128)S(1)} %get-tuple-element.48.table, ...), custom_call_target="tpu_custom_call" | custom-call | flops 99999997952 | bytes 1 | tf_op jit(solution)/shard_map/late_cross_attention/pallas_call | solution.py:296
  23.6 1.6 %collective-permute-start.10 = (bf16[5,48,128]{2,1,0:T(8,128)(2,1)S(1)}, bf16[5,48,128]{2,1,0:T(8,128)(2,1)S(1)}, u32[]{:S(2)}, u32[]{:S(2)}) collective-permute-start(bf16[5,48,128]{2,1,0:T(8,128)(2,1)S(1)} %get-tuple-element.55), channel_id=1, source_target_pairs={{0,2},{1,3},{2,0},{3,1},{4,6},{5,7},{6,4},{7,5},{8,10},{9,11},{10,... | collective-permute-start | bytes 184328 | tf_op jit(solution)/shard_map/ppermute | solution.py:289
  25.2 0.0 collective-permute-start.11
  25.2 0.6 %collective-permute-start.12 = (bf16[5,48,128]{2,1,0:T(8,128)(2,1)S(1)}, bf16[5,48,128]{2,1,0:T(8,128)(2,1)S(1)}, u32[]{:S(2)}, u32[]{:S(2)}) collective-permute-start(bf16[5,48,128]{2,1,0:T(8,128)(2,1)S(1)} %get-tuple-element.57), channel_id=1, source_target_pairs={{0,3},{1,2},{2,1},{3,0},{4,7},{5,6},{6,5},{7,4},{8,11},{9,10},{10,... | collective-permute-start | bytes 184328 | tf_op jit(solution)/shard_map/ppermute | solution.py:289
  25.8 2.1 %collective-permute-done.10.rest_1_ = bf16[5,48,128]{2,1,0:T(8,128)(2,1)S(1)} collective-permute-done((bf16[5,48,128]{2,1,0:T(8,128)(2,1)S(1)}, bf16[5,48,128]{2,1,0:T(8,128)(2,1)S(1)}, u32[]{:S(2)}, u32[]{:S(2)}) %collective-permute-start.10) | collective-permute-done | bytes 61472 | tf_op jit(solution)/shard_map/ppermute | solution.py:289
  27.9 0.0 collective-permute-done.11.rest_2_
  27.9 0.9 %collective-permute-done.12.rest_3_ = bf16[5,48,128]{2,1,0:T(8,128)(2,1)S(1)} collective-permute-done((bf16[5,48,128]{2,1,0:T(8,128)(2,1)S(1)}, bf16[5,48,128]{2,1,0:T(8,128)(2,1)S(1)}, u32[]{:S(2)}, u32[]{:S(2)}) %collective-permute-start.12) | collective-permute-done | bytes 61472 | tf_op jit(solution)/shard_map/ppermute | solution.py:289
  28.9 1.4 %pair_output.1 = bf16[2,5,32,768]{3,2,1,0:T(8,128)(2,1)} custom-call(f32[2,32,768]{2,1,0:T(8,128)S(1)} %get-tuple-element.47.own_rows, s32[11,128]{1,0:T(8,128)S(1)} %get-tuple-element.48.table, bf16[384,768]{1,0:T(8,128)(2,1)S(1)} %cross_output_both_rows.1.own_weights, bf16[384,768]{1,0:T(8,128)(2,1)S(1)} %collective-permute-done.7.core_weights, ...), custom_call_target="tpu_custom_call" | custom-call | flops 1 | bytes 1 | tf_op jit(solution)/shard_map/pair_output/pallas_call | solution.py:296
  (12 shorter events, 0.0 us)
Async XLA Ops:
  0.0 15.4 %collective-permute-start.2 = (bf16[192,768]{1,0:T(8,128)(2,1)}, bf16[192,768]{1,0:T(8,128)(2,1)S(1)}, u32[]{:S(2)}, u32[]{:S(2)}) collective-permute-start(bf16[192,768]{1,0:T(8,128)(2,1)} %param.12), channel_id=1, source_target_pairs={{0,2},{1,3},{2,0},{3,1},{4,6},{5,7},{6,4},{7,5},{8,10},{9,11},{10,... | collective-permute-start | bytes 884744 | tf_op jit(solution)/shard_map/ppermute | solution.py:289
  6.4 6.2 %collective-permute-start.3 = (bf16[384,128]{1,0:T(8,128)(2,1)S(1)}, bf16[384,128]{1,0:T(8,128)(2,1)S(1)}, u32[]{:S(2)}, u32[]{:S(2)}) collective-permute-start(bf16[384,128]{1,0:T(8,128)(2,1)S(1)} %get-tuple-element.44), channel_id=1, source_target_pairs={{0,8},{4,12},{8,0},{12,4},{16,24},{20,28},{24,16},{28,20},{1,9},{5... | collective-permute-start | bytes 294920 | tf_op jit(solution)/shard_map/ppermute | solution.py:292
  8.1 6.2 %collective-permute-start.4 = (bf16[384,128]{1,0:T(8,128)(2,1)S(1)}, bf16[384,128]{1,0:T(8,128)(2,1)S(1)}, u32[]{:S(2)}, u32[]{:S(2)}) collective-permute-start(bf16[384,128]{1,0:T(8,128)(2,1)S(1)} %get-tuple-element.45), channel_id=1, source_target_pairs={{0,4},{4,0},{8,12},{12,8},{16,20},{20,16},{24,28},{28,24},{1,5},{5... | collective-permute-start | bytes 294920 | tf_op jit(solution)/shard_map/ppermute | solution.py:292
  9.6 8.5 %collective-permute-start.1 = (bf16[384,128]{1,0:T(8,128)(2,1)S(1)}, bf16[384,128]{1,0:T(8,128)(2,1)S(1)}, u32[]{:S(2)}, u32[]{:S(2)}) collective-permute-start(bf16[384,128]{1,0:T(8,128)(2,1)S(1)} %get-tuple-element.43), channel_id=1, source_target_pairs={{0,2},{1,3},{2,0},{3,1},{4,6},{5,7},{6,4},{7,5},{8,10},{9,11},{10,... | collective-permute-start | bytes 294920 | tf_op jit(solution)/shard_map/ppermute | solution.py:289
  10.1 10.8 %collective-permute-start.6 = (bf16[384,128]{1,0:T(8,128)(2,1)S(1)}, bf16[384,128]{1,0:T(8,128)(2,1)S(1)}, u32[]{:S(2)}, u32[]{:S(2)}) collective-permute-start(bf16[384,128]{1,0:T(8,128)(2,1)S(1)} %get-tuple-element.51), channel_id=1, source_target_pairs={{0,16},{4,20},{8,24},{12,28},{16,0},{20,4},{24,8},{28,12},{1,17},{... | collective-permute-start | bytes 294920 | tf_op jit(solution)/shard_map/ppermute | solution.py:292
  12.7 5.5 %copy-start.3 = (bf16[192,768]{1,0:T(8,128)(2,1)S(1)}, bf16[192,768]{1,0:T(8,128)(2,1)}, u32[]{:S(2)}) copy-start(bf16[192,768]{1,0:T(8,128)(2,1)} %param.12) | copy-start | bytes 884740
  12.7 5.4 %copy-start.1 = (f32[3,768]{1,0:T(4,128)S(1)}, f32[3,768]{1,0:T(4,128)}, u32[]{:S(2)}) copy-start(f32[3,768]{1,0:T(4,128)} %value.1) | copy-start | bytes 27652
  12.7 5.4 %copy-start.2 = (bf16[2,128,768]{2,1,0:T(8,128)(2,1)S(1)}, bf16[2,128,768]{2,1,0:T(8,128)(2,1)}, u32[]{:S(2)}) copy-start(bf16[2,128,768]{2,1,0:T(8,128)(2,1)} %states.1) | copy-start | bytes 1179652
  12.7 9.3 %collective-permute-start.5 = (bf16[192,768]{1,0:T(8,128)(2,1)S(1)}, bf16[192,768]{1,0:T(8,128)(2,1)S(1)}, u32[]{:S(2)}, u32[]{:S(2)}) collective-permute-start(bf16[192,768]{1,0:T(8,128)(2,1)S(1)} %cross_output_rows.1), channel_id=1, source_target_pairs={{0,2},{1,3},{2,0},{3,1},{4,6},{5,7},{6,4},{7,5},{8,10},{9,11},{10,... | collective-permute-start | bytes 884744 | tf_op jit(solution)/shard_map/ppermute | solution.py:289
  14.3 8.0 %collective-permute-start.8 = (bf16[384,128]{1,0:T(8,128)(2,1)S(1)}, bf16[384,128]{1,0:T(8,128)(2,1)S(1)}, u32[]{:S(2)}, u32[]{:S(2)}) collective-permute-start(bf16[384,128]{1,0:T(8,128)(2,1)S(1)} %get-tuple-element.52), channel_id=1, source_target_pairs={{0,24},{4,28},{8,16},{12,20},{16,8},{20,12},{24,0},{28,4},{1,25},{... | collective-permute-start | bytes 294920 | tf_op jit(solution)/shard_map/ppermute | solution.py:292
  15.4 7.4 %collective-permute-start.9 = (bf16[384,128]{1,0:T(8,128)(2,1)S(1)}, bf16[384,128]{1,0:T(8,128)(2,1)S(1)}, u32[]{:S(2)}, u32[]{:S(2)}) collective-permute-start(bf16[384,128]{1,0:T(8,128)(2,1)S(1)} %get-tuple-element.53), channel_id=1, source_target_pairs={{0,28},{4,8},{8,4},{12,16},{16,12},{20,24},{24,20},{28,0},{1,29},{... | collective-permute-start | bytes 294920 | tf_op jit(solution)/shard_map/ppermute | solution.py:292
  18.6 1.8 %collective-permute-start = (bf16[256,768]{1,0:T(8,128)(2,1)S(1)}, bf16[256,768]{1,0:T(8,128)(2,1)S(1)}, u32[]{:S(2)}, u32[]{:S(2)}) collective-permute-start(bf16[256,768]{1,0:T(8,128)(2,1)S(1)} %get-tuple-element.25), channel_id=1, source_target_pairs={{0,1},{1,0},{2,3},{3,2},{4,5},{5,4},{6,7},{7,6},{8,9},{9,8},{10,11... | collective-permute-start | bytes 1179656 | tf_op jit(solution)/shard_map/cond/branch_1_fun/ppermute | solution.py:289
  20.9 1.1 %copy-start = (bf16[192,768]{1,0:T(8,128)(2,1)S(1)}, bf16[192,768]{1,0:T(8,128)(2,1)}, u32[]{:S(2)}) copy-start(bf16[192,768]{1,0:T(8,128)(2,1)} %own.1) | copy-start | bytes 884740
  22.1 6.7 %collective-permute-start.7 = (bf16[384,768]{1,0:T(8,128)(2,1)S(1)}, bf16[384,768]{1,0:T(8,128)(2,1)S(1)}, u32[]{:S(2)}, u32[]{:S(2)}) collective-permute-start(bf16[384,768]{1,0:T(8,128)(2,1)S(1)} %cross_output_both_rows.1.own_weights), channel_id=1, source_target_pairs={{0,1},{1,0},{2,3},{3,2},{4,5},{5,4},{6,7},{7,6},{8,9},{9,8},{10,11... | collective-permute-start | bytes 1769480 | tf_op jit(solution)/shard_map/ppermute | solution.py:289
  23.6 4.3 %collective-permute-start.10 = (bf16[5,48,128]{2,1,0:T(8,128)(2,1)S(1)}, bf16[5,48,128]{2,1,0:T(8,128)(2,1)S(1)}, u32[]{:S(2)}, u32[]{:S(2)}) collective-permute-start(bf16[5,48,128]{2,1,0:T(8,128)(2,1)S(1)} %get-tuple-element.55), channel_id=1, source_target_pairs={{0,2},{1,3},{2,0},{3,1},{4,6},{5,7},{6,4},{7,5},{8,10},{9,11},{10,... | collective-permute-start | bytes 184328 | tf_op jit(solution)/shard_map/ppermute | solution.py:289
  25.2 2.7 %collective-permute-start.11 = (bf16[5,48,128]{2,1,0:T(8,128)(2,1)S(1)}, bf16[5,48,128]{2,1,0:T(8,128)(2,1)S(1)}, u32[]{:S(2)}, u32[]{:S(2)}) collective-permute-start(bf16[5,48,128]{2,1,0:T(8,128)(2,1)S(1)} %get-tuple-element.56), channel_id=1, source_target_pairs={{0,1},{1,0},{2,3},{3,2},{4,5},{5,4},{6,7},{7,6},{8,9},{9,8},{10,11... | collective-permute-start | bytes 184328 | tf_op jit(solution)/shard_map/ppermute | solution.py:289
  25.2 3.6 %collective-permute-start.12 = (bf16[5,48,128]{2,1,0:T(8,128)(2,1)S(1)}, bf16[5,48,128]{2,1,0:T(8,128)(2,1)S(1)}, u32[]{:S(2)}, u32[]{:S(2)}) collective-permute-start(bf16[5,48,128]{2,1,0:T(8,128)(2,1)S(1)} %get-tuple-element.57), channel_id=1, source_target_pairs={{0,3},{1,2},{2,1},{3,0},{4,7},{5,6},{6,5},{7,4},{8,11},{9,10},{10,... | collective-permute-start | bytes 184328 | tf_op jit(solution)/shard_map/ppermute | solution.py:289

commit v10 on v9

--- a/solution.py
+++ b/solution.py
@@ -12,7 +12,7 @@
 F32 = jnp.float32
 BF16 = jnp.bfloat16
 VMEM_BYTES = 24 * 1024 * 1024
-EARLY_WEIGHT = 3*10**9
+EARLY_WEIGHT = 3 * 10**9
 LATE_WEIGHT = 10**11
 
 VMEM = pl.BlockSpec(memory_space=pltpu.VMEM)
@@ -121,13 +121,21 @@
         copy.start()
     copies[0].wait()
     rows = norm_core(states_v[...].reshape(image_n * patch_n, width).astype(F32))
-    copies[1].wait()
+    for copy in copies[1:5]:
+        copy.wait()
     normed = (rows * gains_v[2:3, :]).astype(BF16)
-    copies[2].wait()
     projected = nt(cross_v[...].reshape(2 * columns, width), normed).astype(BF16)
     for image in range(image_n):
         held[image] = projected[:, image * patch_n : (image + 1) * patch_n]
-    copies[3].wait()
+    normed = (rows * gains_v[0:1, :]).astype(BF16)
+    queries = nt(normed, self_v[0]).astype(BF16).astype(F32) * HEAD ** (-0.5)
+    key_value = nt(self_v[1:3].reshape(2 * columns, width), normed).astype(BF16)
+    contexts = []
+    for image in range(image_n):
+        span = slice(image * patch_n, (image + 1) * patch_n)
+        contexts.append(
+            attend(head_stack(queries[span]), key_value[:columns, span], key_value[columns:, span])
+        )
     me = lax.axis_index("owner")
     pair_n = len(swaps)
     for at, (out, swap) in enumerate(zip(outs, swaps)):
@@ -137,16 +145,6 @@
         table[at : at + 1, :] = jnp.full((1, LANES), image, jnp.int32)
         table[pair_n + at : pair_n + at + 1, :] = jnp.full((1, LANES), position, jnp.int32)
     table[2 * pair_n :, :] = jnp.full((1, LANES), live_count(partners_s, 0), jnp.int32)
-    normed = (rows * gains_v[0:1, :]).astype(BF16)
-    copies[4].wait()
-    queries = nt(normed, self_v[0]).astype(BF16).astype(F32) * HEAD ** (-0.5)
-    key_value = nt(self_v[1:3].reshape(2 * columns, width), normed).astype(BF16)
-    contexts = []
-    for image in range(image_n):
-        span = slice(image * patch_n, (image + 1) * patch_n)
-        contexts.append(
-            attend(head_stack(queries[span]), key_value[:columns, span], key_value[columns:, span])
-        )
     context_out[...] = pack(jnp.concatenate(contexts, 0))
     copies[5].wait()
     copies[6].wait()
@@ -241,7 +239,8 @@
 
 
 def out_kernel(order, own_rows, table, own_weights, core_weights, *rest):
-    *sides, out, out_v, sems = rest
+    own, across_chip, across_both, across_core, out, out_v, sems = rest
+    sides = [own, across_chip, across_core, across_both]
     row_n, width = own_rows.shape[1:]
     pair_n = len(order)
     placed = []
@@ -349,7 +348,7 @@
         cross_out_own, *[arrived[short[0]]],
     )
     cross_out_got = across(cross_out_sent, chip_hop)
-    before = [arrived[at] for at in short] + [self_out_got]
+    before = [arrived[at] for at in short] + [self_out_got, arrived[0]]
     gains_then = call(
         "gains",
         hand_on_kernel,
@@ -426,7 +425,7 @@
         [VMEM] * (4 + helper_n),
         [pltpu.VMEM((image_n, slot_n, row_n, width), BF16), dma((image_n,))],
         own_rows, table, cross_out_both, cross_out_core,
-        *[sides[k] for k in (0, chip_hop, core_hop, chip_hop ^ core_hop)],
+        *[sides[k] for k in (0, chip_hop, chip_hop ^ core_hop, core_hop)],
         out_specs=HBM,
     )
 

time: 30.4 us -> 32.5 us (1.069)
  waiting for transfers between devices: 5.19 us -> 8.83 us
  starting transfers between devices: 17 us -> 15.8 us
  Pallas kernels: 7.87 us -> 7.46 us
    ppermute x5, waiting for transfers between devices: 0.43 us -> 4.44 us  [exchange(): lax.ppermute(value, 'owner', [(o, swap_target(o, swap, owner_n)) for o in...]
    ppermute x5, starting transfers between devices: 9.5 us -> 8.32 us  [exchange(): lax.ppermute(value, 'owner', [(o, swap_target(o, swap, owner_n)) for o in...]
    pallas_call x9, Pallas kernels: 7.87 us -> 7.46 us  [call(): pl.pallas_call(kernel, out_shape=out_shape, in_specs=in_specs, out_specs=...]
    ppermute x8, waiting for transfers between devices: 4.75 us -> 4.4 us  [across(): return lax.ppermute(value, 'helper', [(j, j ^ k) for j in range(helper_n)])]
  transfers between devices with their start and end apart: 13 -> 13, of which waited for: 4 -> 4; matrix products, arithmetic and copies ran while one was open for 0% -> 0% of each run, Pallas kernels for 22% -> 19%
where the time goes in v10:
time: 32.5 us; the launch traced here: 32.3 us
  starting transfers between devices  15.8 us (49%)
  waiting for transfers between devices  8.83 us (27%)
  Pallas kernels  7.46 us (23%)
    ppermute x5, starting transfers between devices, exchange(): lax.ppermute(value, 'owner', [(o, swap_target(o, swap, owner_n)) for o in...  8.32 us
    ppermute x8, starting transfers between devices, across(): return lax.ppermute(value, 'helper', [(j, j ^ k) for j in range(helper_n)])  7.53 us
    pallas_call x9, Pallas kernels, call(): pl.pallas_call(kernel, out_shape=out_shape, in_specs=in_specs, out_specs=...  7.46 us
    ppermute x5, waiting for transfers between devices, exchange(): lax.ppermute(value, 'owner', [(o, swap_target(o, swap, owner_n)) for o in...  4.44 us
    ppermute x8, waiting for transfers between devices, across(): return lax.ppermute(value, 'helper', [(j, j ^ k) for j in range(helper_n)])  4.4 us
  transfers between devices with their start and end apart: 13, of which 4 were waited for; matrix products, arithmetic and copies ran while one was open for 0% of the time, Pallas kernels for 19%

profile of v10, /device:TPU:0, one launch (start us, length us, event | category | flops | bytes accessed | tf_op | source)
XLA Modules:
  0.0 32.3 jit_solution(16075161687601758833)
XLA Ops:
  0.0 3.0 %collective-permute-start.2 = (bf16[192,768]{1,0:T(8,128)(2,1)}, bf16[192,768]{1,0:T(8,128)(2,1)S(1)}, u32[]{:S(2)}, u32[]{:S(2)}) collective-permute-start(bf16[192,768]{1,0:T(8,128)(2,1)} %param.12), channel_id=1, source_target_pairs={{0,2},{1,3},{2,0},{3,1},{4,6},{5,7},{6,4},{7,5},{8,10},{9,11},{10,... | collective-permute-start | bytes 884744 | tf_op jit(solution)/shard_map/ppermute | solution.py:288
  3.0 3.1 %own_images.1 = (bf16[384,128]{1,0:T(8,128)(2,1)S(1)}, bf16[384,128]{1,0:T(8,128)(2,1)S(1)}, bf16[384,128]{1,0:T(8,128)(2,1)S(1)}, bf16[384,128]{1,0:T(8,128)(2,...) custom-call(bf16[2,128,768]{2,1,0:T(8,128)(2,1)} %states.1, ...), custom_call_target="tpu_custom_call" | custom-call | flops 1 | bytes 1 | tf_op jit(solution)/shard_map/own_images/pallas_call | solution.py:295
  6.0 1.6 %collective-permute-start.3 = (bf16[384,128]{1,0:T(8,128)(2,1)S(1)}, bf16[384,128]{1,0:T(8,128)(2,1)S(1)}, u32[]{:S(2)}, u32[]{:S(2)}) collective-permute-start(bf16[384,128]{1,0:T(8,128)(2,1)S(1)} %get-tuple-element.44), channel_id=1, source_target_pairs={{0,8},{4,12},{8,0},{12,4},{16,24},{20,28},{24,16},{28,20},{1,9},{5... | collective-permute-start | bytes 294920 | tf_op jit(solution)/shard_map/ppermute | solution.py:291
  7.7 1.5 %collective-permute-start.4 = (bf16[384,128]{1,0:T(8,128)(2,1)S(1)}, bf16[384,128]{1,0:T(8,128)(2,1)S(1)}, u32[]{:S(2)}, u32[]{:S(2)}) collective-permute-start(bf16[384,128]{1,0:T(8,128)(2,1)S(1)} %get-tuple-element.45), channel_id=1, source_target_pairs={{0,4},{4,0},{8,12},{12,8},{16,20},{20,16},{24,28},{28,24},{1,5},{5... | collective-permute-start | bytes 294920 | tf_op jit(solution)/shard_map/ppermute | solution.py:291
  9.2 2.6 %collective-permute-start.5 = (bf16[384,128]{1,0:T(8,128)(2,1)S(1)}, bf16[384,128]{1,0:T(8,128)(2,1)S(1)}, u32[]{:S(2)}, u32[]{:S(2)}) collective-permute-start(bf16[384,128]{1,0:T(8,128)(2,1)S(1)} %get-tuple-element.46), channel_id=1, source_target_pairs={{0,16},{4,20},{8,24},{12,28},{16,0},{20,4},{24,8},{28,12},{1,17},{... | collective-permute-start | bytes 294920 | tf_op jit(solution)/shard_map/ppermute | solution.py:291
  11.8 0.5 %collective-permute-start.1 = (bf16[384,128]{1,0:T(8,128)(2,1)S(1)}, bf16[384,128]{1,0:T(8,128)(2,1)S(1)}, u32[]{:S(2)}, u32[]{:S(2)}) collective-permute-start(bf16[384,128]{1,0:T(8,128)(2,1)S(1)} %get-tuple-element.43), channel_id=1, source_target_pairs={{0,2},{1,3},{2,0},{3,1},{4,6},{5,7},{6,4},{7,5},{8,10},{9,11},{10,... | collective-permute-start | bytes 294920 | tf_op jit(solution)/shard_map/ppermute | solution.py:288
  12.3 0.0 collective-permute-done.3.rest_0_.rest_1_
  12.3 0.0 copy-start.1
  12.3 0.0 copy-start.2
  12.3 1.6 %collective-permute-start.6 = (bf16[192,768]{1,0:T(8,128)(2,1)S(1)}, bf16[192,768]{1,0:T(8,128)(2,1)S(1)}, u32[]{:S(2)}, u32[]{:S(2)}) collective-permute-start(bf16[192,768]{1,0:T(8,128)(2,1)S(1)} %cross_output_rows.1), channel_id=1, source_target_pairs={{0,2},{1,3},{2,0},{3,1},{4,6},{5,7},{6,4},{7,5},{8,10},{9,11},{10,... | collective-permute-start | bytes 884744 | tf_op jit(solution)/shard_map/ppermute | solution.py:288
  13.9 0.0 collective-permute-done.4.rest_1_.rest_2_
  13.9 2.1 %collective-permute-start.8 = (bf16[384,128]{1,0:T(8,128)(2,1)S(1)}, bf16[384,128]{1,0:T(8,128)(2,1)S(1)}, u32[]{:S(2)}, u32[]{:S(2)}) collective-permute-start(bf16[384,128]{1,0:T(8,128)(2,1)S(1)} %get-tuple-element.52), channel_id=1, source_target_pairs={{0,24},{4,28},{8,16},{12,20},{16,8},{20,12},{24,0},{28,4},{1,25},{... | collective-permute-start | bytes 294920 | tf_op jit(solution)/shard_map/ppermute | solution.py:291
  16.0 1.8 %collective-permute-done.5.rest_3_.rest_0_ = bf16[384,128]{1,0:T(8,128)(2,1)S(1)} collective-permute-done((bf16[384,128]{1,0:T(8,128)(2,1)S(1)}, bf16[384,128]{1,0:T(8,128)(2,1)S(1)}, u32[]{:S(2)}, u32[]{:S(2)}) %collective-permute-start.5) | collective-permute-done | bytes 98336 | tf_op jit(solution)/shard_map/ppermute | solution.py:291
  17.9 0.5 %collective-permute-start.9 = (bf16[384,128]{1,0:T(8,128)(2,1)S(1)}, bf16[384,128]{1,0:T(8,128)(2,1)S(1)}, u32[]{:S(2)}, u32[]{:S(2)}) collective-permute-start(bf16[384,128]{1,0:T(8,128)(2,1)S(1)} %get-tuple-element.53), channel_id=1, source_target_pairs={{0,28},{4,8},{8,4},{12,16},{16,12},{20,24},{24,20},{28,0},{1,29},{... | collective-permute-start | bytes 294920 | tf_op jit(solution)/shard_map/ppermute | solution.py:291
  18.3 0.0 collective-permute-done.1
  18.4 2.8 %conditional.1 = ((f32[2,32,768]{2,1,0:T(8,128)S(1)}, bf16[2,128,192]{2,1,0:T(8,128)(2,1)S(1)})) conditional(s32[]{:T(128)} %convert_element_type.3, () %tuple.12, (bf16[2,128,768]{2,1,0:T(8,128)(2,1)S(1)}, bf16[384,128]{1,0:T(8,128)(2,1)S(1)}, bf16[384,128]{1,0:T(8,128)(2,1)S(1)}, bf16[192,768]{1,0:T(8,128)(2,1)S(1)}, ...), branch_computations={%region_0.0_spmd, %region_1.0_spmd} | conditional | flops 2 | bytes 1572914 | solution.py:388
  18.4 0.4 %self_output_share.1 = (f32[256,768]{1,0:T(8,128)S(1)}, bf16[256,768]{1,0:T(8,128)(2,1)S(1)}) custom-call(bf16[2,128,768]{2,1,0:T(8,128)(2,1)S(1)} %get-tuple-element.19.states, bf16[384,128]{1,0:T(8,128)(2,1)S(1)} %get-tuple-element.20.own, bf16[384,128]{1,0:T(8,128)(2,1)S(1)} %get-tuple-element.21.got, bf16[192,768]{1,0:T(8,128)(2,1)S(1)} %get-tuple-element.22.own_weight, ...), custom_call_target="tpu_custom_call" | custom-call | flops 1 | bytes 1 | tf_op jit(solution)/shard_map/cond/branch_1_fun/self_output_share/pallas_call | solution.py:295
  18.8 0.1 collective-permute-start
  18.9 1.7 %collective-permute-done.got = bf16[256,768]{1,0:T(8,128)(2,1)S(1)} collective-permute-done((bf16[256,768]{1,0:T(8,128)(2,1)S(1)}, bf16[256,768]{1,0:T(8,128)(2,1)S(1)}, u32[]{:S(2)}, u32[]{:S(2)}) %collective-permute-start) | collective-permute-done | bytes 393248 | tf_op jit(solution)/shard_map/cond/branch_1_fun/ppermute | solution.py:288
  20.6 0.5 %mixed_and_queries.1 = (f32[2,32,768]{2,1,0:T(8,128)S(1)}, bf16[2,128,192]{2,1,0:T(8,128)(2,1)S(1)}) custom-call(f32[256,768]{1,0:T(8,128)S(1)} %get-tuple-element.24.base, bf16[256,768]{1,0:T(8,128)(2,1)S(1)} %collective-permute-done.got, f32[3,768]{1,0:T(4,128)S(1)} %get-tuple-element.26.gains, bf16[192,768]{1,0:T(8,128)(2,1)S(1)} %get-tuple-element.27.weight), custom_call_target="tpu_custom_call" | custom-call | flops 1 | bytes 1 | tf_op jit(solution)/shard_map/cond/branch_1_fun/mixed_and_queries/pallas_call | solution.py:295
  21.2 0.0 copy-start
  21.2 1.0 %early_cross_attention.1.waited.before = bf16[4,3,48,128]{3,2,1,0:T(8,128)(2,1)S(1)} custom-call(bf16[2,128,192]{2,1,0:T(8,128)(2,1)S(1)} %get-tuple-element.51.queries, s32[11,128]{1,0:T(8,128)S(1)} %get-tuple-element.49.table, bf16[384,128]{1,0:T(8,128)(2,1)S(1)} %collective-permute-done.5.rest_3_.rest_0_, ...), custom_call_target="tpu_custom_call" | custom-call | flops 3000000000 | bytes 1 | tf_op jit(solution)/shard_map/early_cross_attention/pallas_call | solution.py:295
  22.2 0.0 collective-permute-done.6.got
  22.2 0.1 cross_output_both_rows.1.own_weights
  22.4 0.2 collective-permute-start.7
  22.6 2.6 %collective-permute-done.9.rest_1_ = bf16[384,128]{1,0:T(8,128)(2,1)S(1)} collective-permute-done((bf16[384,128]{1,0:T(8,128)(2,1)S(1)}, bf16[384,128]{1,0:T(8,128)(2,1)S(1)}, u32[]{:S(2)}, u32[]{:S(2)}) %collective-permute-start.9) | collective-permute-done | bytes 98336 | tf_op jit(solution)/shard_map/ppermute | solution.py:291
  25.2 0.9 %late_cross_attention.1 = (bf16[5,48,128]{2,1,0:T(8,128)(2,1)S(1)}, bf16[5,48,128]{2,1,0:T(8,128)(2,1)S(1)}, bf16[5,48,128]{2,1,0:T(8,128)(2,1)S(1)}, bf16[5,48,128]{2,1,0:T(8,128)(2,1)S(1)}) custom-call(bf16[2,128,192]{2,1,0:T(8,128)(2,1)S(1)} %get-tuple-element.51.queries, s32[11,128]{1,0:T(8,128)S(1)} %get-tuple-element.49.table, ...), custom_call_target="tpu_custom_call" | custom-call | flops 99999997952 | bytes 1 | tf_op jit(solution)/shard_map/late_cross_attention/pallas_call | solution.py:295
  26.0 0.6 %collective-permute-start.10 = (bf16[5,48,128]{2,1,0:T(8,128)(2,1)S(1)}, bf16[5,48,128]{2,1,0:T(8,128)(2,1)S(1)}, u32[]{:S(2)}, u32[]{:S(2)}) collective-permute-start(bf16[5,48,128]{2,1,0:T(8,128)(2,1)S(1)} %get-tuple-element.55), channel_id=1, source_target_pairs={{0,2},{1,3},{2,0},{3,1},{4,6},{5,7},{6,4},{7,5},{8,10},{9,11},{10,... | collective-permute-start | bytes 184328 | tf_op jit(solution)/shard_map/ppermute | solution.py:288
  26.6 1.6 %collective-permute-start.12 = (bf16[5,48,128]{2,1,0:T(8,128)(2,1)S(1)}, bf16[5,48,128]{2,1,0:T(8,128)(2,1)S(1)}, u32[]{:S(2)}, u32[]{:S(2)}) collective-permute-start(bf16[5,48,128]{2,1,0:T(8,128)(2,1)S(1)} %get-tuple-element.57), channel_id=1, source_target_pairs={{0,1},{1,0},{2,3},{3,2},{4,5},{5,4},{6,7},{7,6},{8,9},{9,8},{10,11... | collective-permute-start | bytes 184328 | tf_op jit(solution)/shard_map/ppermute | solution.py:288
  28.2 2.7 %collective-permute-done.10.rest_1_ = bf16[5,48,128]{2,1,0:T(8,128)(2,1)S(1)} collective-permute-done((bf16[5,48,128]{2,1,0:T(8,128)(2,1)S(1)}, bf16[5,48,128]{2,1,0:T(8,128)(2,1)S(1)}, u32[]{:S(2)}, u32[]{:S(2)}) %collective-permute-start.10) | collective-permute-done | bytes 61472 | tf_op jit(solution)/shard_map/ppermute | solution.py:288
  30.9 0.0 collective-permute-done.11.rest_2_
  30.9 1.4 %pair_output.1 = bf16[2,5,32,768]{3,2,1,0:T(8,128)(2,1)} custom-call(f32[2,32,768]{2,1,0:T(8,128)S(1)} %get-tuple-element.48.own_rows, s32[11,128]{1,0:T(8,128)S(1)} %get-tuple-element.49.table, bf16[384,768]{1,0:T(8,128)(2,1)S(1)} %cross_output_both_rows.1.own_weights, bf16[384,768]{1,0:T(8,128)(2,1)S(1)} %collective-permute-done.7.core_weights, ...), custom_call_target="tpu_custom_call" | custom-call | flops 1 | bytes 1 | tf_op jit(solution)/shard_map/pair_output/pallas_call | solution.py:295
  (12 shorter events, 0.0 us)
Async XLA Ops:
  0.0 18.3 %collective-permute-start.2 = (bf16[192,768]{1,0:T(8,128)(2,1)}, bf16[192,768]{1,0:T(8,128)(2,1)S(1)}, u32[]{:S(2)}, u32[]{:S(2)}) collective-permute-start(bf16[192,768]{1,0:T(8,128)(2,1)} %param.12), channel_id=1, source_target_pairs={{0,2},{1,3},{2,0},{3,1},{4,6},{5,7},{6,4},{7,5},{8,10},{9,11},{10,... | collective-permute-start | bytes 884744 | tf_op jit(solution)/shard_map/ppermute | solution.py:288
  6.0 6.2 %collective-permute-start.3 = (bf16[384,128]{1,0:T(8,128)(2,1)S(1)}, bf16[384,128]{1,0:T(8,128)(2,1)S(1)}, u32[]{:S(2)}, u32[]{:S(2)}) collective-permute-start(bf16[384,128]{1,0:T(8,128)(2,1)S(1)} %get-tuple-element.44), channel_id=1, source_target_pairs={{0,8},{4,12},{8,0},{12,4},{16,24},{20,28},{24,16},{28,20},{1,9},{5... | collective-permute-start | bytes 294920 | tf_op jit(solution)/shard_map/ppermute | solution.py:291
  7.7 6.2 %collective-permute-start.4 = (bf16[384,128]{1,0:T(8,128)(2,1)S(1)}, bf16[384,128]{1,0:T(8,128)(2,1)S(1)}, u32[]{:S(2)}, u32[]{:S(2)}) collective-permute-start(bf16[384,128]{1,0:T(8,128)(2,1)S(1)} %get-tuple-element.45), channel_id=1, source_target_pairs={{0,4},{4,0},{8,12},{12,8},{16,20},{20,16},{24,28},{28,24},{1,5},{5... | collective-permute-start | bytes 294920 | tf_op jit(solution)/shard_map/ppermute | solution.py:291
  9.2 8.7 %collective-permute-start.5 = (bf16[384,128]{1,0:T(8,128)(2,1)S(1)}, bf16[384,128]{1,0:T(8,128)(2,1)S(1)}, u32[]{:S(2)}, u32[]{:S(2)}) collective-permute-start(bf16[384,128]{1,0:T(8,128)(2,1)S(1)} %get-tuple-element.46), channel_id=1, source_target_pairs={{0,16},{4,20},{8,24},{12,28},{16,0},{20,4},{24,8},{28,12},{1,17},{... | collective-permute-start | bytes 294920 | tf_op jit(solution)/shard_map/ppermute | solution.py:291
  11.8 6.6 %collective-permute-start.1 = (bf16[384,128]{1,0:T(8,128)(2,1)S(1)}, bf16[384,128]{1,0:T(8,128)(2,1)S(1)}, u32[]{:S(2)}, u32[]{:S(2)}) collective-permute-start(bf16[384,128]{1,0:T(8,128)(2,1)S(1)} %get-tuple-element.43), channel_id=1, source_target_pairs={{0,2},{1,3},{2,0},{3,1},{4,6},{5,7},{6,4},{7,5},{8,10},{9,11},{10,... | collective-permute-start | bytes 294920 | tf_op jit(solution)/shard_map/ppermute | solution.py:288
  12.3 6.1 %copy-start.3 = (bf16[192,768]{1,0:T(8,128)(2,1)S(1)}, bf16[192,768]{1,0:T(8,128)(2,1)}, u32[]{:S(2)}) copy-start(bf16[192,768]{1,0:T(8,128)(2,1)} %param.12) | copy-start | bytes 884740
  12.3 6.0 %copy-start.1 = (f32[3,768]{1,0:T(4,128)S(1)}, f32[3,768]{1,0:T(4,128)}, u32[]{:S(2)}) copy-start(f32[3,768]{1,0:T(4,128)} %value.1) | copy-start | bytes 27652
  12.3 6.1 %copy-start.2 = (bf16[2,128,768]{2,1,0:T(8,128)(2,1)S(1)}, bf16[2,128,768]{2,1,0:T(8,128)(2,1)}, u32[]{:S(2)}) copy-start(bf16[2,128,768]{2,1,0:T(8,128)(2,1)} %states.1) | copy-start | bytes 1179652
  12.3 9.9 %collective-permute-start.6 = (bf16[192,768]{1,0:T(8,128)(2,1)S(1)}, bf16[192,768]{1,0:T(8,128)(2,1)S(1)}, u32[]{:S(2)}, u32[]{:S(2)}) collective-permute-start(bf16[192,768]{1,0:T(8,128)(2,1)S(1)} %cross_output_rows.1), channel_id=1, source_target_pairs={{0,2},{1,3},{2,0},{3,1},{4,6},{5,7},{6,4},{7,5},{8,10},{9,11},{10,... | collective-permute-start | bytes 884744 | tf_op jit(solution)/shard_map/ppermute | solution.py:288
  13.9 8.7 %collective-permute-start.8 = (bf16[384,128]{1,0:T(8,128)(2,1)S(1)}, bf16[384,128]{1,0:T(8,128)(2,1)S(1)}, u32[]{:S(2)}, u32[]{:S(2)}) collective-permute-start(bf16[384,128]{1,0:T(8,128)(2,1)S(1)} %get-tuple-element.52), channel_id=1, source_target_pairs={{0,24},{4,28},{8,16},{12,20},{16,8},{20,12},{24,0},{28,4},{1,25},{... | collective-permute-start | bytes 294920 | tf_op jit(solution)/shard_map/ppermute | solution.py:291
  17.9 7.3 %collective-permute-start.9 = (bf16[384,128]{1,0:T(8,128)(2,1)S(1)}, bf16[384,128]{1,0:T(8,128)(2,1)S(1)}, u32[]{:S(2)}, u32[]{:S(2)}) collective-permute-start(bf16[384,128]{1,0:T(8,128)(2,1)S(1)} %get-tuple-element.53), channel_id=1, source_target_pairs={{0,28},{4,8},{8,4},{12,16},{16,12},{20,24},{24,20},{28,0},{1,29},{... | collective-permute-start | bytes 294920 | tf_op jit(solution)/shard_map/ppermute | solution.py:291
  18.8 1.8 %collective-permute-start = (bf16[256,768]{1,0:T(8,128)(2,1)S(1)}, bf16[256,768]{1,0:T(8,128)(2,1)S(1)}, u32[]{:S(2)}, u32[]{:S(2)}) collective-permute-start(bf16[256,768]{1,0:T(8,128)(2,1)S(1)} %get-tuple-element.25), channel_id=1, source_target_pairs={{0,1},{1,0},{2,3},{3,2},{4,5},{5,4},{6,7},{7,6},{8,9},{9,8},{10,11... | collective-permute-start | bytes 1179656 | tf_op jit(solution)/shard_map/cond/branch_1_fun/ppermute | solution.py:288
  21.2 1.1 %copy-start = (bf16[192,768]{1,0:T(8,128)(2,1)S(1)}, bf16[192,768]{1,0:T(8,128)(2,1)}, u32[]{:S(2)}) copy-start(bf16[192,768]{1,0:T(8,128)(2,1)} %own.1) | copy-start | bytes 884740
  22.4 8.5 %collective-permute-start.7 = (bf16[384,768]{1,0:T(8,128)(2,1)S(1)}, bf16[384,768]{1,0:T(8,128)(2,1)S(1)}, u32[]{:S(2)}, u32[]{:S(2)}) collective-permute-start(bf16[384,768]{1,0:T(8,128)(2,1)S(1)} %cross_output_both_rows.1.own_weights), channel_id=1, source_target_pairs={{0,1},{1,0},{2,3},{3,2},{4,5},{5,4},{6,7},{7,6},{8,9},{9,8},{10,11... | collective-permute-start | bytes 1769480 | tf_op jit(solution)/shard_map/ppermute | solution.py:288
  26.0 4.9 %collective-permute-start.10 = (bf16[5,48,128]{2,1,0:T(8,128)(2,1)S(1)}, bf16[5,48,128]{2,1,0:T(8,128)(2,1)S(1)}, u32[]{:S(2)}, u32[]{:S(2)}) collective-permute-start(bf16[5,48,128]{2,1,0:T(8,128)(2,1)S(1)} %get-tuple-element.55), channel_id=1, source_target_pairs={{0,2},{1,3},{2,0},{3,1},{4,6},{5,7},{6,4},{7,5},{8,10},{9,11},{10,... | collective-permute-start | bytes 184328 | tf_op jit(solution)/shard_map/ppermute | solution.py:288
  26.6 4.3 %collective-permute-start.11 = (bf16[5,48,128]{2,1,0:T(8,128)(2,1)S(1)}, bf16[5,48,128]{2,1,0:T(8,128)(2,1)S(1)}, u32[]{:S(2)}, u32[]{:S(2)}) collective-permute-start(bf16[5,48,128]{2,1,0:T(8,128)(2,1)S(1)} %get-tuple-element.56), channel_id=1, source_target_pairs={{0,3},{1,2},{2,1},{3,0},{4,7},{5,6},{6,5},{7,4},{8,11},{9,10},{10,... | collective-permute-start | bytes 184328 | tf_op jit(solution)/shard_map/ppermute | solution.py:288
  26.6 4.3 %collective-permute-start.12 = (bf16[5,48,128]{2,1,0:T(8,128)(2,1)S(1)}, bf16[5,48,128]{2,1,0:T(8,128)(2,1)S(1)}, u32[]{:S(2)}, u32[]{:S(2)}) collective-permute-start(bf16[5,48,128]{2,1,0:T(8,128)(2,1)S(1)} %get-tuple-element.57), channel_id=1, source_target_pairs={{0,1},{1,0},{2,3},{3,2},{4,5},{5,4},{6,7},{7,6},{8,9},{9,8},{10,11... | collective-permute-start | bytes 184328 | tf_op jit(solution)/shard_map/ppermute | solution.py:288

commit v11 on v10

--- a/solution.py
+++ b/solution.py
@@ -348,7 +348,7 @@
         cross_out_own, *[arrived[short[0]]],
     )
     cross_out_got = across(cross_out_sent, chip_hop)
-    before = [arrived[at] for at in short] + [self_out_got, arrived[0]]
+    before = [arrived[at] for at in short] + [self_out_got]
     gains_then = call(
         "gains",
         hand_on_kernel,

time: 32.5 us -> 30.4 us (0.935)
  waiting for transfers between devices: 8.83 us -> 5.55 us
  starting transfers between devices: 15.8 us -> 17.1 us
    ppermute x5, waiting for transfers between devices: 4.44 us -> 0.44 us  [exchange(): lax.ppermute(value, 'owner', [(o, swap_target(o, swap, owner_n)) for o in...]
    ppermute x5, starting transfers between devices: 8.32 us -> 9.53 us  [exchange(): lax.ppermute(value, 'owner', [(o, swap_target(o, swap, owner_n)) for o in...]
    ppermute x8, waiting for transfers between devices: 4.4 us -> 5.12 us  [across(): return lax.ppermute(value, 'helper', [(j, j ^ k) for j in range(helper_n)])]
  transfers between devices with their start and end apart: 13 -> 13, of which waited for: 4 -> 4; matrix products, arithmetic and copies ran while one was open for 0% -> 0% of each run, Pallas kernels for 19% -> 20%
where the time goes in v11:
time: 30.4 us; the launch traced here: 30.2 us
  starting transfers between devices  17.1 us (56%)
  Pallas kernels  7.46 us (25%)
  waiting for transfers between devices  5.55 us (18%)
    ppermute x5, starting transfers between devices, exchange(): lax.ppermute(value, 'owner', [(o, swap_target(o, swap, owner_n)) for o in...  9.53 us
    ppermute x8, starting transfers between devices, across(): return lax.ppermute(value, 'helper', [(j, j ^ k) for j in range(helper_n)])  7.54 us
    pallas_call x9, Pallas kernels, call(): pl.pallas_call(kernel, out_shape=out_shape, in_specs=in_specs, out_specs=...  7.46 us
    ppermute x8, waiting for transfers between devices, across(): return lax.ppermute(value, 'helper', [(j, j ^ k) for j in range(helper_n)])  5.12 us
  transfers between devices with their start and end apart: 13, of which 4 were waited for; matrix products, arithmetic and copies ran while one was open for 0% of the time, Pallas kernels for 20%

profile of v11, /device:TPU:0, one launch (start us, length us, event | category | flops | bytes accessed | tf_op | source)
XLA Modules:
  0.0 30.2 jit_solution(8212872267214299525)
XLA Ops:
  0.0 3.0 %collective-permute-start.2 = (bf16[192,768]{1,0:T(8,128)(2,1)}, bf16[192,768]{1,0:T(8,128)(2,1)S(1)}, u32[]{:S(2)}, u32[]{:S(2)}) collective-permute-start(bf16[192,768]{1,0:T(8,128)(2,1)} %param.12), channel_id=1, source_target_pairs={{0,2},{1,3},{2,0},{3,1},{4,6},{5,7},{6,4},{7,5},{8,10},{9,11},{10,... | collective-permute-start | bytes 884744 | tf_op jit(solution)/shard_map/ppermute | solution.py:288
  3.0 3.1 %own_images.1 = (bf16[384,128]{1,0:T(8,128)(2,1)S(1)}, bf16[384,128]{1,0:T(8,128)(2,1)S(1)}, bf16[384,128]{1,0:T(8,128)(2,1)S(1)}, bf16[384,128]{1,0:T(8,128)(2,...) custom-call(bf16[2,128,768]{2,1,0:T(8,128)(2,1)} %states.1, ...), custom_call_target="tpu_custom_call" | custom-call | flops 1 | bytes 1 | tf_op jit(solution)/shard_map/own_images/pallas_call | solution.py:295
  6.0 1.7 %collective-permute-start.3 = (bf16[384,128]{1,0:T(8,128)(2,1)S(1)}, bf16[384,128]{1,0:T(8,128)(2,1)S(1)}, u32[]{:S(2)}, u32[]{:S(2)}) collective-permute-start(bf16[384,128]{1,0:T(8,128)(2,1)S(1)} %get-tuple-element.44), channel_id=1, source_target_pairs={{0,8},{4,12},{8,0},{12,4},{16,24},{20,28},{24,16},{28,20},{1,9},{5... | collective-permute-start | bytes 294920 | tf_op jit(solution)/shard_map/ppermute | solution.py:291
  7.7 1.5 %collective-permute-start.4 = (bf16[384,128]{1,0:T(8,128)(2,1)S(1)}, bf16[384,128]{1,0:T(8,128)(2,1)S(1)}, u32[]{:S(2)}, u32[]{:S(2)}) collective-permute-start(bf16[384,128]{1,0:T(8,128)(2,1)S(1)} %get-tuple-element.45), channel_id=1, source_target_pairs={{0,4},{4,0},{8,12},{12,8},{16,20},{20,16},{24,28},{28,24},{1,5},{5... | collective-permute-start | bytes 294920 | tf_op jit(solution)/shard_map/ppermute | solution.py:291
  9.2 0.5 %collective-permute-start.1 = (bf16[384,128]{1,0:T(8,128)(2,1)S(1)}, bf16[384,128]{1,0:T(8,128)(2,1)S(1)}, u32[]{:S(2)}, u32[]{:S(2)}) collective-permute-start(bf16[384,128]{1,0:T(8,128)(2,1)S(1)} %get-tuple-element.43), channel_id=1, source_target_pairs={{0,2},{1,3},{2,0},{3,1},{4,6},{5,7},{6,4},{7,5},{8,10},{9,11},{10,... | collective-permute-start | bytes 294920 | tf_op jit(solution)/shard_map/ppermute | solution.py:288
  9.7 2.6 %collective-permute-start.6 = (bf16[384,128]{1,0:T(8,128)(2,1)S(1)}, bf16[384,128]{1,0:T(8,128)(2,1)S(1)}, u32[]{:S(2)}, u32[]{:S(2)}) collective-permute-start(bf16[384,128]{1,0:T(8,128)(2,1)S(1)} %get-tuple-element.51), channel_id=1, source_target_pairs={{0,16},{4,20},{8,24},{12,28},{16,0},{20,4},{24,8},{28,12},{1,17},{... | collective-permute-start | bytes 294920 | tf_op jit(solution)/shard_map/ppermute | solution.py:291
  12.3 0.0 collective-permute-done.3.rest_0_.rest_1_
  12.3 0.0 copy-start.1
  12.3 0.0 copy-start.2
  12.3 1.6 %collective-permute-start.5 = (bf16[192,768]{1,0:T(8,128)(2,1)S(1)}, bf16[192,768]{1,0:T(8,128)(2,1)S(1)}, u32[]{:S(2)}, u32[]{:S(2)}) collective-permute-start(bf16[192,768]{1,0:T(8,128)(2,1)S(1)} %cross_output_rows.1), channel_id=1, source_target_pairs={{0,2},{1,3},{2,0},{3,1},{4,6},{5,7},{6,4},{7,5},{8,10},{9,11},{10,... | collective-permute-start | bytes 884744 | tf_op jit(solution)/shard_map/ppermute | solution.py:288
  13.9 1.0 %collective-permute-start.8 = (bf16[384,128]{1,0:T(8,128)(2,1)S(1)}, bf16[384,128]{1,0:T(8,128)(2,1)S(1)}, u32[]{:S(2)}, u32[]{:S(2)}) collective-permute-start(bf16[384,128]{1,0:T(8,128)(2,1)S(1)} %get-tuple-element.52), channel_id=1, source_target_pairs={{0,24},{4,28},{8,16},{12,20},{16,8},{20,12},{24,0},{28,4},{1,25},{... | collective-permute-start | bytes 294920 | tf_op jit(solution)/shard_map/ppermute | solution.py:291
  15.0 0.0 collective-permute-done.2.rest_2_
  15.0 2.8 %collective-permute-start.9 = (bf16[384,128]{1,0:T(8,128)(2,1)S(1)}, bf16[384,128]{1,0:T(8,128)(2,1)S(1)}, u32[]{:S(2)}, u32[]{:S(2)}) collective-permute-start(bf16[384,128]{1,0:T(8,128)(2,1)S(1)} %get-tuple-element.53), channel_id=1, source_target_pairs={{0,28},{4,8},{8,4},{12,16},{16,12},{20,24},{24,20},{28,0},{1,29},{... | collective-permute-start | bytes 294920 | tf_op jit(solution)/shard_map/ppermute | solution.py:291
  17.8 2.8 %conditional.1 = ((f32[2,32,768]{2,1,0:T(8,128)S(1)}, bf16[2,128,192]{2,1,0:T(8,128)(2,1)S(1)})) conditional(s32[]{:T(128)} %convert_element_type.3, () %tuple.12, (bf16[2,128,768]{2,1,0:T(8,128)(2,1)S(1)}, bf16[384,128]{1,0:T(8,128)(2,1)S(1)}, bf16[384,128]{1,0:T(8,128)(2,1)S(1)}, bf16[192,768]{1,0:T(8,128)(2,1)S(1)}, ...), branch_computations={%region_0.0_spmd, %region_1.0_spmd} | conditional | flops 2 | bytes 1572914 | solution.py:388
  17.8 0.4 %self_output_share.1 = (f32[256,768]{1,0:T(8,128)S(1)}, bf16[256,768]{1,0:T(8,128)(2,1)S(1)}) custom-call(bf16[2,128,768]{2,1,0:T(8,128)(2,1)S(1)} %get-tuple-element.19.states, bf16[384,128]{1,0:T(8,128)(2,1)S(1)} %get-tuple-element.20.own, bf16[384,128]{1,0:T(8,128)(2,1)S(1)} %get-tuple-element.21.got, bf16[192,768]{1,0:T(8,128)(2,1)S(1)} %get-tuple-element.22.own_weight, ...), custom_call_target="tpu_custom_call" | custom-call | flops 1 | bytes 1 | tf_op jit(solution)/shard_map/cond/branch_1_fun/self_output_share/pallas_call | solution.py:295
  18.2 0.1 collective-permute-start
  18.3 1.7 %collective-permute-done.got = bf16[256,768]{1,0:T(8,128)(2,1)S(1)} collective-permute-done((bf16[256,768]{1,0:T(8,128)(2,1)S(1)}, bf16[256,768]{1,0:T(8,128)(2,1)S(1)}, u32[]{:S(2)}, u32[]{:S(2)}) %collective-permute-start) | collective-permute-done | bytes 393248 | tf_op jit(solution)/shard_map/cond/branch_1_fun/ppermute | solution.py:288
  20.0 0.5 %mixed_and_queries.1 = (f32[2,32,768]{2,1,0:T(8,128)S(1)}, bf16[2,128,192]{2,1,0:T(8,128)(2,1)S(1)}) custom-call(f32[256,768]{1,0:T(8,128)S(1)} %get-tuple-element.24.base, bf16[256,768]{1,0:T(8,128)(2,1)S(1)} %collective-permute-done.got, f32[3,768]{1,0:T(4,128)S(1)} %get-tuple-element.26.gains, bf16[192,768]{1,0:T(8,128)(2,1)S(1)} %get-tuple-element.27.weight), custom_call_target="tpu_custom_call" | custom-call | flops 1 | bytes 1 | tf_op jit(solution)/shard_map/cond/branch_1_fun/mixed_and_queries/pallas_call | solution.py:295
  20.5 0.0 collective-permute-done.6.rest_0_
  20.5 0.0 copy-start
  20.6 1.0 %early_cross_attention.1.waited.before = bf16[4,3,48,128]{3,2,1,0:T(8,128)(2,1)S(1)} custom-call(bf16[2,128,192]{2,1,0:T(8,128)(2,1)S(1)} %get-tuple-element.50.queries, s32[11,128]{1,0:T(8,128)S(1)} %get-tuple-element.48.table, bf16[384,128]{1,0:T(8,128)(2,1)S(1)} %collective-permute-done.6.rest_0_, ...), custom_call_target="tpu_custom_call" | custom-call | flops 3000000000 | bytes 1 | tf_op jit(solution)/shard_map/early_cross_attention/pallas_call | solution.py:295
  21.6 0.0 collective-permute-done.5.got
  21.6 0.1 cross_output_both_rows.1.own_weights
  21.8 0.2 collective-permute-start.7
  22.0 0.4 %collective-permute-done.9.rest_1_ = bf16[384,128]{1,0:T(8,128)(2,1)S(1)} collective-permute-done((bf16[384,128]{1,0:T(8,128)(2,1)S(1)}, bf16[384,128]{1,0:T(8,128)(2,1)S(1)}, u32[]{:S(2)}, u32[]{:S(2)}) %collective-permute-start.9) | collective-permute-done | bytes 98336 | tf_op jit(solution)/shard_map/ppermute | solution.py:291
  22.4 0.9 %late_cross_attention.1 = (bf16[5,48,128]{2,1,0:T(8,128)(2,1)S(1)}, bf16[5,48,128]{2,1,0:T(8,128)(2,1)S(1)}, bf16[5,48,128]{2,1,0:T(8,128)(2,1)S(1)}, bf16[5,48,128]{2,1,0:T(8,128)(2,1)S(1)}) custom-call(bf16[2,128,192]{2,1,0:T(8,128)(2,1)S(1)} %get-tuple-element.50.queries, s32[11,128]{1,0:T(8,128)S(1)} %get-tuple-element.48.table, ...), custom_call_target="tpu_custom_call" | custom-call | flops 99999997952 | bytes 1 | tf_op jit(solution)/shard_map/late_cross_attention/pallas_call | solution.py:295
  23.2 1.6 %collective-permute-start.10 = (bf16[5,48,128]{2,1,0:T(8,128)(2,1)S(1)}, bf16[5,48,128]{2,1,0:T(8,128)(2,1)S(1)}, u32[]{:S(2)}, u32[]{:S(2)}) collective-permute-start(bf16[5,48,128]{2,1,0:T(8,128)(2,1)S(1)} %get-tuple-element.55), channel_id=1, source_target_pairs={{0,2},{1,3},{2,0},{3,1},{4,6},{5,7},{6,4},{7,5},{8,10},{9,11},{10,... | collective-permute-start | bytes 184328 | tf_op jit(solution)/shard_map/ppermute | solution.py:288
  24.8 0.0 collective-permute-start.11
  24.8 0.6 %collective-permute-start.12 = (bf16[5,48,128]{2,1,0:T(8,128)(2,1)S(1)}, bf16[5,48,128]{2,1,0:T(8,128)(2,1)S(1)}, u32[]{:S(2)}, u32[]{:S(2)}) collective-permute-start(bf16[5,48,128]{2,1,0:T(8,128)(2,1)S(1)} %get-tuple-element.57), channel_id=1, source_target_pairs={{0,1},{1,0},{2,3},{3,2},{4,5},{5,4},{6,7},{7,6},{8,9},{9,8},{10,11... | collective-permute-start | bytes 184328 | tf_op jit(solution)/shard_map/ppermute | solution.py:288
  25.4 2.1 %collective-permute-done.10.rest_1_ = bf16[5,48,128]{2,1,0:T(8,128)(2,1)S(1)} collective-permute-done((bf16[5,48,128]{2,1,0:T(8,128)(2,1)S(1)}, bf16[5,48,128]{2,1,0:T(8,128)(2,1)S(1)}, u32[]{:S(2)}, u32[]{:S(2)}) %collective-permute-start.10) | collective-permute-done | bytes 61472 | tf_op jit(solution)/shard_map/ppermute | solution.py:288
  27.5 1.3 %collective-permute-done.11.rest_2_ = bf16[5,48,128]{2,1,0:T(8,128)(2,1)S(1)} collective-permute-done((bf16[5,48,128]{2,1,0:T(8,128)(2,1)S(1)}, bf16[5,48,128]{2,1,0:T(8,128)(2,1)S(1)}, u32[]{:S(2)}, u32[]{:S(2)}) %collective-permute-start.11) | collective-permute-done | bytes 61472 | tf_op jit(solution)/shard_map/ppermute | solution.py:288
  28.8 1.4 %pair_output.1 = bf16[2,5,32,768]{3,2,1,0:T(8,128)(2,1)} custom-call(f32[2,32,768]{2,1,0:T(8,128)S(1)} %get-tuple-element.47.own_rows, s32[11,128]{1,0:T(8,128)S(1)} %get-tuple-element.48.table, bf16[384,768]{1,0:T(8,128)(2,1)S(1)} %cross_output_both_rows.1.own_weights, bf16[384,768]{1,0:T(8,128)(2,1)S(1)} %collective-permute-done.7.core_weights, ...), custom_call_target="tpu_custom_call" | custom-call | flops 1 | bytes 1 | tf_op jit(solution)/shard_map/pair_output/pallas_call | solution.py:295
  (12 shorter events, 0.0 us)
Async XLA Ops:
  0.0 15.0 %collective-permute-start.2 = (bf16[192,768]{1,0:T(8,128)(2,1)}, bf16[192,768]{1,0:T(8,128)(2,1)S(1)}, u32[]{:S(2)}, u32[]{:S(2)}) collective-permute-start(bf16[192,768]{1,0:T(8,128)(2,1)} %param.12), channel_id=1, source_target_pairs={{0,2},{1,3},{2,0},{3,1},{4,6},{5,7},{6,4},{7,5},{8,10},{9,11},{10,... | collective-permute-start | bytes 884744 | tf_op jit(solution)/shard_map/ppermute | solution.py:288
  6.0 6.2 %collective-permute-start.3 = (bf16[384,128]{1,0:T(8,128)(2,1)S(1)}, bf16[384,128]{1,0:T(8,128)(2,1)S(1)}, u32[]{:S(2)}, u32[]{:S(2)}) collective-permute-start(bf16[384,128]{1,0:T(8,128)(2,1)S(1)} %get-tuple-element.44), channel_id=1, source_target_pairs={{0,8},{4,12},{8,0},{12,4},{16,24},{20,28},{24,16},{28,20},{1,9},{5... | collective-permute-start | bytes 294920 | tf_op jit(solution)/shard_map/ppermute | solution.py:291
  7.7 6.2 %collective-permute-start.4 = (bf16[384,128]{1,0:T(8,128)(2,1)S(1)}, bf16[384,128]{1,0:T(8,128)(2,1)S(1)}, u32[]{:S(2)}, u32[]{:S(2)}) collective-permute-start(bf16[384,128]{1,0:T(8,128)(2,1)S(1)} %get-tuple-element.45), channel_id=1, source_target_pairs={{0,4},{4,0},{8,12},{12,8},{16,20},{20,16},{24,28},{28,24},{1,5},{5... | collective-permute-start | bytes 294920 | tf_op jit(solution)/shard_map/ppermute | solution.py:291
  9.2 8.6 %collective-permute-start.1 = (bf16[384,128]{1,0:T(8,128)(2,1)S(1)}, bf16[384,128]{1,0:T(8,128)(2,1)S(1)}, u32[]{:S(2)}, u32[]{:S(2)}) collective-permute-start(bf16[384,128]{1,0:T(8,128)(2,1)S(1)} %get-tuple-element.43), channel_id=1, source_target_pairs={{0,2},{1,3},{2,0},{3,1},{4,6},{5,7},{6,4},{7,5},{8,10},{9,11},{10,... | collective-permute-start | bytes 294920 | tf_op jit(solution)/shard_map/ppermute | solution.py:288
  9.7 10.9 %collective-permute-start.6 = (bf16[384,128]{1,0:T(8,128)(2,1)S(1)}, bf16[384,128]{1,0:T(8,128)(2,1)S(1)}, u32[]{:S(2)}, u32[]{:S(2)}) collective-permute-start(bf16[384,128]{1,0:T(8,128)(2,1)S(1)} %get-tuple-element.51), channel_id=1, source_target_pairs={{0,16},{4,20},{8,24},{12,28},{16,0},{20,4},{24,8},{28,12},{1,17},{... | collective-permute-start | bytes 294920 | tf_op jit(solution)/shard_map/ppermute | solution.py:291
  12.3 5.5 %copy-start.3 = (bf16[192,768]{1,0:T(8,128)(2,1)S(1)}, bf16[192,768]{1,0:T(8,128)(2,1)}, u32[]{:S(2)}) copy-start(bf16[192,768]{1,0:T(8,128)(2,1)} %param.12) | copy-start | bytes 884740
  12.3 5.4 %copy-start.1 = (f32[3,768]{1,0:T(4,128)S(1)}, f32[3,768]{1,0:T(4,128)}, u32[]{:S(2)}) copy-start(f32[3,768]{1,0:T(4,128)} %value.1) | copy-start | bytes 27652
  12.3 5.4 %copy-start.2 = (bf16[2,128,768]{2,1,0:T(8,128)(2,1)S(1)}, bf16[2,128,768]{2,1,0:T(8,128)(2,1)}, u32[]{:S(2)}) copy-start(bf16[2,128,768]{2,1,0:T(8,128)(2,1)} %states.1) | copy-start | bytes 1179652
  12.3 9.3 %collective-permute-start.5 = (bf16[192,768]{1,0:T(8,128)(2,1)S(1)}, bf16[192,768]{1,0:T(8,128)(2,1)S(1)}, u32[]{:S(2)}, u32[]{:S(2)}) collective-permute-start(bf16[192,768]{1,0:T(8,128)(2,1)S(1)} %cross_output_rows.1), channel_id=1, source_target_pairs={{0,2},{1,3},{2,0},{3,1},{4,6},{5,7},{6,4},{7,5},{8,10},{9,11},{10,... | collective-permute-start | bytes 884744 | tf_op jit(solution)/shard_map/ppermute | solution.py:288
  13.9 8.0 %collective-permute-start.8 = (bf16[384,128]{1,0:T(8,128)(2,1)S(1)}, bf16[384,128]{1,0:T(8,128)(2,1)S(1)}, u32[]{:S(2)}, u32[]{:S(2)}) collective-permute-start(bf16[384,128]{1,0:T(8,128)(2,1)S(1)} %get-tuple-element.52), channel_id=1, source_target_pairs={{0,24},{4,28},{8,16},{12,20},{16,8},{20,12},{24,0},{28,4},{1,25},{... | collective-permute-start | bytes 294920 | tf_op jit(solution)/shard_map/ppermute | solution.py:291
  15.0 7.4 %collective-permute-start.9 = (bf16[384,128]{1,0:T(8,128)(2,1)S(1)}, bf16[384,128]{1,0:T(8,128)(2,1)S(1)}, u32[]{:S(2)}, u32[]{:S(2)}) collective-permute-start(bf16[384,128]{1,0:T(8,128)(2,1)S(1)} %get-tuple-element.53), channel_id=1, source_target_pairs={{0,28},{4,8},{8,4},{12,16},{16,12},{20,24},{24,20},{28,0},{1,29},{... | collective-permute-start | bytes 294920 | tf_op jit(solution)/shard_map/ppermute | solution.py:291
  18.2 1.8 %collective-permute-start = (bf16[256,768]{1,0:T(8,128)(2,1)S(1)}, bf16[256,768]{1,0:T(8,128)(2,1)S(1)}, u32[]{:S(2)}, u32[]{:S(2)}) collective-permute-start(bf16[256,768]{1,0:T(8,128)(2,1)S(1)} %get-tuple-element.25), channel_id=1, source_target_pairs={{0,1},{1,0},{2,3},{3,2},{4,5},{5,4},{6,7},{7,6},{8,9},{9,8},{10,11... | collective-permute-start | bytes 1179656 | tf_op jit(solution)/shard_map/cond/branch_1_fun/ppermute | solution.py:288
  20.5 1.1 %copy-start = (bf16[192,768]{1,0:T(8,128)(2,1)S(1)}, bf16[192,768]{1,0:T(8,128)(2,1)}, u32[]{:S(2)}) copy-start(bf16[192,768]{1,0:T(8,128)(2,1)} %own.1) | copy-start | bytes 884740
  21.8 7.1 %collective-permute-start.7 = (bf16[384,768]{1,0:T(8,128)(2,1)S(1)}, bf16[384,768]{1,0:T(8,128)(2,1)S(1)}, u32[]{:S(2)}, u32[]{:S(2)}) collective-permute-start(bf16[384,768]{1,0:T(8,128)(2,1)S(1)} %cross_output_both_rows.1.own_weights), channel_id=1, source_target_pairs={{0,1},{1,0},{2,3},{3,2},{4,5},{5,4},{6,7},{7,6},{8,9},{9,8},{10,11... | collective-permute-start | bytes 1769480 | tf_op jit(solution)/shard_map/ppermute | solution.py:288
  23.2 4.3 %collective-permute-start.10 = (bf16[5,48,128]{2,1,0:T(8,128)(2,1)S(1)}, bf16[5,48,128]{2,1,0:T(8,128)(2,1)S(1)}, u32[]{:S(2)}, u32[]{:S(2)}) collective-permute-start(bf16[5,48,128]{2,1,0:T(8,128)(2,1)S(1)} %get-tuple-element.55), channel_id=1, source_target_pairs={{0,2},{1,3},{2,0},{3,1},{4,6},{5,7},{6,4},{7,5},{8,10},{9,11},{10,... | collective-permute-start | bytes 184328 | tf_op jit(solution)/shard_map/ppermute | solution.py:288
  24.8 4.0 %collective-permute-start.11 = (bf16[5,48,128]{2,1,0:T(8,128)(2,1)S(1)}, bf16[5,48,128]{2,1,0:T(8,128)(2,1)S(1)}, u32[]{:S(2)}, u32[]{:S(2)}) collective-permute-start(bf16[5,48,128]{2,1,0:T(8,128)(2,1)S(1)} %get-tuple-element.56), channel_id=1, source_target_pairs={{0,3},{1,2},{2,1},{3,0},{4,7},{5,6},{6,5},{7,4},{8,11},{9,10},{10,... | collective-permute-start | bytes 184328 | tf_op jit(solution)/shard_map/ppermute | solution.py:288
  24.8 4.0 %collective-permute-start.12 = (bf16[5,48,128]{2,1,0:T(8,128)(2,1)S(1)}, bf16[5,48,128]{2,1,0:T(8,128)(2,1)S(1)}, u32[]{:S(2)}, u32[]{:S(2)}) collective-permute-start(bf16[5,48,128]{2,1,0:T(8,128)(2,1)S(1)} %get-tuple-element.57), channel_id=1, source_target_pairs={{0,1},{1,0},{2,3},{3,2},{4,5},{5,4},{6,7},{7,6},{8,9},{9,8},{10,11... | collective-permute-start | bytes 184328 | tf_op jit(solution)/shard_map/ppermute | solution.py:288

commit v12 on v11

--- a/solution.py
+++ b/solution.py
@@ -66,14 +66,15 @@
     head_n = column_n // HEAD
     row_n = stacked.shape[0] // head_n
     scores = nn(stacked, keys_t)
-    powers = jnp.exp(scores - jnp.max(scores, -1, keepdims=True))
-    weights = (powers * (1.0 / jnp.sum(powers, -1, keepdims=True))).astype(BF16)
+    weights = jnp.exp(scores - jnp.max(scores, -1, keepdims=True)).astype(BF16)
     spread = nt(weights, values_t)
+    totals = nn(weights, jnp.ones((weights.shape[1], column_n), BF16))
     head_of = lax.broadcasted_iota(jnp.int32, (row_n, column_n), 1) // HEAD
-    context = spread[(head_n - 1) * row_n :]
+    context, total = spread[(head_n - 1) * row_n :], totals[(head_n - 1) * row_n :]
     for h in range(head_n - 1):
         context = jnp.where(head_of == h, spread[h * row_n : (h + 1) * row_n], context)
-    return context
+        total = jnp.where(head_of == h, totals[h * row_n : (h + 1) * row_n], total)
+    return context / total
 
 
 def pack(block):
@@ -343,9 +344,9 @@
         "cross_output_rows",
         hand_on_kernel,
         shape(cross_out.shape, BF16),
-        [VMEM] + [ANY] * len([arrived[short[0]]]),
+        [VMEM] + [ANY] * len([arrived[short[1]]]),
         [],
-        cross_out_own, *[arrived[short[0]]],
+        cross_out_own, *[arrived[short[1]]],
     )
     cross_out_got = across(cross_out_sent, chip_hop)
     before = [arrived[at] for at in short] + [self_out_got]

time: 30.4 us -> 31.5 us (1.036)
  waiting for transfers between devices: 5.55 us -> 6.43 us
    ppermute x5, waiting for transfers between devices: 0.44 us -> 1.63 us  [exchange(): lax.ppermute(value, 'owner', [(o, swap_target(o, swap, owner_n)) for o in...]
    ppermute x8, waiting for transfers between devices: 5.12 us -> 4.8 us  [across(): return lax.ppermute(value, 'helper', [(j, j ^ k) for j in range(helper_n)])]
where the time goes in v12:
time: 31.5 us; the launch traced here: 31.4 us
  starting transfers between devices  17.1 us (54%)
  Pallas kernels  7.74 us (25%)
  waiting for transfers between devices  6.43 us (20%)
    ppermute x5, starting transfers between devices, exchange(): lax.ppermute(value, 'owner', [(o, swap_target(o, swap, owner_n)) for o in...  9.53 us
    pallas_call x9, Pallas kernels, call(): pl.pallas_call(kernel, out_shape=out_shape, in_specs=in_specs, out_specs=...  7.74 us
    ppermute x8, starting transfers between devices, across(): return lax.ppermute(value, 'helper', [(j, j ^ k) for j in range(helper_n)])  7.55 us
    ppermute x8, waiting for transfers between devices, across(): return lax.ppermute(value, 'helper', [(j, j ^ k) for j in range(helper_n)])  4.8 us
    ppermute x5, waiting for transfers between devices, exchange(): lax.ppermute(value, 'owner', [(o, swap_target(o, swap, owner_n)) for o in...  1.63 us
  transfers between devices with their start and end apart: 13, of which 4 were waited for; matrix products, arithmetic and copies ran while one was open for 0% of the time, Pallas kernels for 20%

profile of v12, /device:TPU:0, one launch (start us, length us, event | category | flops | bytes accessed | tf_op | source)
XLA Modules:
  0.0 31.4 jit_solution(5585825412276880657)
XLA Ops:
  0.0 3.0 %collective-permute-start.2 = (bf16[192,768]{1,0:T(8,128)(2,1)}, bf16[192,768]{1,0:T(8,128)(2,1)S(1)}, u32[]{:S(2)}, u32[]{:S(2)}) collective-permute-start(bf16[192,768]{1,0:T(8,128)(2,1)} %param.12), channel_id=1, source_target_pairs={{0,2},{1,3},{2,0},{3,1},{4,6},{5,7},{6,4},{7,5},{8,10},{9,11},{10,... | collective-permute-start | bytes 884744 | tf_op jit(solution)/shard_map/ppermute | solution.py:289
  3.0 3.1 %own_images.1 = (bf16[384,128]{1,0:T(8,128)(2,1)S(1)}, bf16[384,128]{1,0:T(8,128)(2,1)S(1)}, bf16[384,128]{1,0:T(8,128)(2,1)S(1)}, bf16[384,128]{1,0:T(8,128)(2,...) custom-call(bf16[2,128,768]{2,1,0:T(8,128)(2,1)} %states.1, ...), custom_call_target="tpu_custom_call" | custom-call | flops 1 | bytes 1 | tf_op jit(solution)/shard_map/own_images/pallas_call | solution.py:296
  6.1 1.6 %collective-permute-start.4 = (bf16[384,128]{1,0:T(8,128)(2,1)S(1)}, bf16[384,128]{1,0:T(8,128)(2,1)S(1)}, u32[]{:S(2)}, u32[]{:S(2)}) collective-permute-start(bf16[384,128]{1,0:T(8,128)(2,1)S(1)} %get-tuple-element.45), channel_id=1, source_target_pairs={{0,4},{4,0},{8,12},{12,8},{16,20},{20,16},{24,28},{28,24},{1,5},{5... | collective-permute-start | bytes 294920 | tf_op jit(solution)/shard_map/ppermute | solution.py:292
  7.7 1.6 %collective-permute-start.3 = (bf16[384,128]{1,0:T(8,128)(2,1)S(1)}, bf16[384,128]{1,0:T(8,128)(2,1)S(1)}, u32[]{:S(2)}, u32[]{:S(2)}) collective-permute-start(bf16[384,128]{1,0:T(8,128)(2,1)S(1)} %get-tuple-element.44), channel_id=1, source_target_pairs={{0,8},{4,12},{8,0},{12,4},{16,24},{20,28},{24,16},{28,20},{1,9},{5... | collective-permute-start | bytes 294920 | tf_op jit(solution)/shard_map/ppermute | solution.py:292
  9.2 0.5 %collective-permute-start.1 = (bf16[384,128]{1,0:T(8,128)(2,1)S(1)}, bf16[384,128]{1,0:T(8,128)(2,1)S(1)}, u32[]{:S(2)}, u32[]{:S(2)}) collective-permute-start(bf16[384,128]{1,0:T(8,128)(2,1)S(1)} %get-tuple-element.43), channel_id=1, source_target_pairs={{0,2},{1,3},{2,0},{3,1},{4,6},{5,7},{6,4},{7,5},{8,10},{9,11},{10,... | collective-permute-start | bytes 294920 | tf_op jit(solution)/shard_map/ppermute | solution.py:289
  9.8 2.6 %collective-permute-start.6 = (bf16[384,128]{1,0:T(8,128)(2,1)S(1)}, bf16[384,128]{1,0:T(8,128)(2,1)S(1)}, u32[]{:S(2)}, u32[]{:S(2)}) collective-permute-start(bf16[384,128]{1,0:T(8,128)(2,1)S(1)} %get-tuple-element.51), channel_id=1, source_target_pairs={{0,16},{4,20},{8,24},{12,28},{16,0},{20,4},{24,8},{28,12},{1,17},{... | collective-permute-start | bytes 294920 | tf_op jit(solution)/shard_map/ppermute | solution.py:292
  12.3 0.0 collective-permute-done.4.rest_1_.rest_0_.rest_2_
  12.4 0.0 copy-start.1
  12.4 0.0 copy-start.2
  12.4 1.6 %collective-permute-start.5 = (bf16[192,768]{1,0:T(8,128)(2,1)S(1)}, bf16[192,768]{1,0:T(8,128)(2,1)S(1)}, u32[]{:S(2)}, u32[]{:S(2)}) collective-permute-start(bf16[192,768]{1,0:T(8,128)(2,1)S(1)} %cross_output_rows.1), channel_id=1, source_target_pairs={{0,2},{1,3},{2,0},{3,1},{4,6},{5,7},{6,4},{7,5},{8,10},{9,11},{10,... | collective-permute-start | bytes 884744 | tf_op jit(solution)/shard_map/ppermute | solution.py:289
  14.0 0.0 collective-permute-done.3.rest_0_.rest_1_
  14.0 2.5 %collective-permute-start.8 = (bf16[384,128]{1,0:T(8,128)(2,1)S(1)}, bf16[384,128]{1,0:T(8,128)(2,1)S(1)}, u32[]{:S(2)}, u32[]{:S(2)}) collective-permute-start(bf16[384,128]{1,0:T(8,128)(2,1)S(1)} %get-tuple-element.52), channel_id=1, source_target_pairs={{0,24},{4,28},{8,16},{12,20},{16,8},{20,12},{24,0},{28,4},{1,25},{... | collective-permute-start | bytes 294920 | tf_op jit(solution)/shard_map/ppermute | solution.py:292
  16.5 1.3 %collective-permute-start.9 = (bf16[384,128]{1,0:T(8,128)(2,1)S(1)}, bf16[384,128]{1,0:T(8,128)(2,1)S(1)}, u32[]{:S(2)}, u32[]{:S(2)}) collective-permute-start(bf16[384,128]{1,0:T(8,128)(2,1)S(1)} %get-tuple-element.53), channel_id=1, source_target_pairs={{0,28},{4,8},{8,4},{12,16},{16,12},{20,24},{24,20},{28,0},{1,29},{... | collective-permute-start | bytes 294920 | tf_op jit(solution)/shard_map/ppermute | solution.py:292
  17.8 0.0 collective-permute-done.1
  17.8 2.8 %conditional.1 = ((f32[2,32,768]{2,1,0:T(8,128)S(1)}, bf16[2,128,192]{2,1,0:T(8,128)(2,1)S(1)})) conditional(s32[]{:T(128)} %convert_element_type.3, () %tuple.12, (bf16[2,128,768]{2,1,0:T(8,128)(2,1)S(1)}, bf16[384,128]{1,0:T(8,128)(2,1)S(1)}, bf16[384,128]{1,0:T(8,128)(2,1)S(1)}, bf16[192,768]{1,0:T(8,128)(2,1)S(1)}, ...), branch_computations={%region_0.0_spmd, %region_1.0_spmd} | conditional | flops 2 | bytes 1572914 | solution.py:389
  17.8 0.4 %self_output_share.1 = (f32[256,768]{1,0:T(8,128)S(1)}, bf16[256,768]{1,0:T(8,128)(2,1)S(1)}) custom-call(bf16[2,128,768]{2,1,0:T(8,128)(2,1)S(1)} %get-tuple-element.19.states, bf16[384,128]{1,0:T(8,128)(2,1)S(1)} %get-tuple-element.20.own, bf16[384,128]{1,0:T(8,128)(2,1)S(1)} %get-tuple-element.21.got, bf16[192,768]{1,0:T(8,128)(2,1)S(1)} %get-tuple-element.22.own_weight, ...), custom_call_target="tpu_custom_call" | custom-call | flops 1 | bytes 1 | tf_op jit(solution)/shard_map/cond/branch_1_fun/self_output_share/pallas_call | solution.py:296
  18.3 0.1 collective-permute-start
  18.4 1.7 %collective-permute-done.got = bf16[256,768]{1,0:T(8,128)(2,1)S(1)} collective-permute-done((bf16[256,768]{1,0:T(8,128)(2,1)S(1)}, bf16[256,768]{1,0:T(8,128)(2,1)S(1)}, u32[]{:S(2)}, u32[]{:S(2)}) %collective-permute-start) | collective-permute-done | bytes 393248 | tf_op jit(solution)/shard_map/cond/branch_1_fun/ppermute | solution.py:289
  20.1 0.5 %mixed_and_queries.1 = (f32[2,32,768]{2,1,0:T(8,128)S(1)}, bf16[2,128,192]{2,1,0:T(8,128)(2,1)S(1)}) custom-call(f32[256,768]{1,0:T(8,128)S(1)} %get-tuple-element.24.base, bf16[256,768]{1,0:T(8,128)(2,1)S(1)} %collective-permute-done.got, f32[3,768]{1,0:T(4,128)S(1)} %get-tuple-element.26.gains, bf16[192,768]{1,0:T(8,128)(2,1)S(1)} %get-tuple-element.27.weight), custom_call_target="tpu_custom_call" | custom-call | flops 1 | bytes 1 | tf_op jit(solution)/shard_map/cond/branch_1_fun/mixed_and_queries/pallas_call | solution.py:296
  20.6 0.0 copy-start
  20.6 1.2 %early_cross_attention.1.waited.before = bf16[4,3,48,128]{3,2,1,0:T(8,128)(2,1)S(1)} custom-call(bf16[2,128,192]{2,1,0:T(8,128)(2,1)S(1)} %get-tuple-element.50.queries, s32[11,128]{1,0:T(8,128)S(1)} %get-tuple-element.48.table, bf16[384,128]{1,0:T(8,128)(2,1)S(1)} %collective-permute-done.6.rest_0_, ...), custom_call_target="tpu_custom_call" | custom-call | flops 3000000000 | bytes 1 | tf_op jit(solution)/shard_map/early_cross_attention/pallas_call | solution.py:296
  21.9 0.1 cross_output_both_rows.1.own_weights
  22.0 0.2 collective-permute-start.7
  22.2 0.0 collective-permute-done.8.rest_0_
  22.2 1.6 %collective-permute-done.9.rest_1_ = bf16[384,128]{1,0:T(8,128)(2,1)S(1)} collective-permute-done((bf16[384,128]{1,0:T(8,128)(2,1)S(1)}, bf16[384,128]{1,0:T(8,128)(2,1)S(1)}, u32[]{:S(2)}, u32[]{:S(2)}) %collective-permute-start.9) | collective-permute-done | bytes 98336 | tf_op jit(solution)/shard_map/ppermute | solution.py:292
  23.9 0.9 %late_cross_attention.1 = (bf16[5,48,128]{2,1,0:T(8,128)(2,1)S(1)}, bf16[5,48,128]{2,1,0:T(8,128)(2,1)S(1)}, bf16[5,48,128]{2,1,0:T(8,128)(2,1)S(1)}, bf16[5,48,128]{2,1,0:T(8,128)(2,1)S(1)}) custom-call(bf16[2,128,192]{2,1,0:T(8,128)(2,1)S(1)} %get-tuple-element.50.queries, s32[11,128]{1,0:T(8,128)S(1)} %get-tuple-element.48.table, ...), custom_call_target="tpu_custom_call" | custom-call | flops 99999997952 | bytes 1 | tf_op jit(solution)/shard_map/late_cross_attention/pallas_call | solution.py:296
  24.7 1.0 %collective-permute-start.10 = (bf16[5,48,128]{2,1,0:T(8,128)(2,1)S(1)}, bf16[5,48,128]{2,1,0:T(8,128)(2,1)S(1)}, u32[]{:S(2)}, u32[]{:S(2)}) collective-permute-start(bf16[5,48,128]{2,1,0:T(8,128)(2,1)S(1)} %get-tuple-element.55), channel_id=1, source_target_pairs={{0,2},{1,3},{2,0},{3,1},{4,6},{5,7},{6,4},{7,5},{8,10},{9,11},{10,... | collective-permute-start | bytes 184328 | tf_op jit(solution)/shard_map/ppermute | solution.py:289
  25.7 0.0 collective-permute-start.11
  25.7 1.2 %collective-permute-start.12 = (bf16[5,48,128]{2,1,0:T(8,128)(2,1)S(1)}, bf16[5,48,128]{2,1,0:T(8,128)(2,1)S(1)}, u32[]{:S(2)}, u32[]{:S(2)}) collective-permute-start(bf16[5,48,128]{2,1,0:T(8,128)(2,1)S(1)} %get-tuple-element.57), channel_id=1, source_target_pairs={{0,1},{1,0},{2,3},{3,2},{4,5},{5,4},{6,7},{7,6},{8,9},{9,8},{10,11... | collective-permute-start | bytes 184328 | tf_op jit(solution)/shard_map/ppermute | solution.py:289
  26.9 2.4 %collective-permute-done.10.rest_1_ = bf16[5,48,128]{2,1,0:T(8,128)(2,1)S(1)} collective-permute-done((bf16[5,48,128]{2,1,0:T(8,128)(2,1)S(1)}, bf16[5,48,128]{2,1,0:T(8,128)(2,1)S(1)}, u32[]{:S(2)}, u32[]{:S(2)}) %collective-permute-start.10) | collective-permute-done | bytes 61472 | tf_op jit(solution)/shard_map/ppermute | solution.py:289
  29.3 0.7 %collective-permute-done.11.rest_2_ = bf16[5,48,128]{2,1,0:T(8,128)(2,1)S(1)} collective-permute-done((bf16[5,48,128]{2,1,0:T(8,128)(2,1)S(1)}, bf16[5,48,128]{2,1,0:T(8,128)(2,1)S(1)}, u32[]{:S(2)}, u32[]{:S(2)}) %collective-permute-start.11) | collective-permute-done | bytes 61472 | tf_op jit(solution)/shard_map/ppermute | solution.py:289
  30.0 1.4 %pair_output.1 = bf16[2,5,32,768]{3,2,1,0:T(8,128)(2,1)} custom-call(f32[2,32,768]{2,1,0:T(8,128)S(1)} %get-tuple-element.47.own_rows, s32[11,128]{1,0:T(8,128)S(1)} %get-tuple-element.48.table, bf16[384,768]{1,0:T(8,128)(2,1)S(1)} %cross_output_both_rows.1.own_weights, bf16[384,768]{1,0:T(8,128)(2,1)S(1)} %collective-permute-done.7.core_weights, ...), custom_call_target="tpu_custom_call" | custom-call | flops 1 | bytes 1 | tf_op jit(solution)/shard_map/pair_output/pallas_call | solution.py:296
  (12 shorter events, 0.0 us)
Async XLA Ops:
  0.0 16.5 %collective-permute-start.2 = (bf16[192,768]{1,0:T(8,128)(2,1)}, bf16[192,768]{1,0:T(8,128)(2,1)S(1)}, u32[]{:S(2)}, u32[]{:S(2)}) collective-permute-start(bf16[192,768]{1,0:T(8,128)(2,1)} %param.12), channel_id=1, source_target_pairs={{0,2},{1,3},{2,0},{3,1},{4,6},{5,7},{6,4},{7,5},{8,10},{9,11},{10,... | collective-permute-start | bytes 884744 | tf_op jit(solution)/shard_map/ppermute | solution.py:289
  6.1 6.3 %collective-permute-start.4 = (bf16[384,128]{1,0:T(8,128)(2,1)S(1)}, bf16[384,128]{1,0:T(8,128)(2,1)S(1)}, u32[]{:S(2)}, u32[]{:S(2)}) collective-permute-start(bf16[384,128]{1,0:T(8,128)(2,1)S(1)} %get-tuple-element.45), channel_id=1, source_target_pairs={{0,4},{4,0},{8,12},{12,8},{16,20},{20,16},{24,28},{28,24},{1,5},{5... | collective-permute-start | bytes 294920 | tf_op jit(solution)/shard_map/ppermute | solution.py:292
  7.7 6.3 %collective-permute-start.3 = (bf16[384,128]{1,0:T(8,128)(2,1)S(1)}, bf16[384,128]{1,0:T(8,128)(2,1)S(1)}, u32[]{:S(2)}, u32[]{:S(2)}) collective-permute-start(bf16[384,128]{1,0:T(8,128)(2,1)S(1)} %get-tuple-element.44), channel_id=1, source_target_pairs={{0,8},{4,12},{8,0},{12,4},{16,24},{20,28},{24,16},{28,20},{1,9},{5... | collective-permute-start | bytes 294920 | tf_op jit(solution)/shard_map/ppermute | solution.py:292
  9.2 8.6 %collective-permute-start.1 = (bf16[384,128]{1,0:T(8,128)(2,1)S(1)}, bf16[384,128]{1,0:T(8,128)(2,1)S(1)}, u32[]{:S(2)}, u32[]{:S(2)}) collective-permute-start(bf16[384,128]{1,0:T(8,128)(2,1)S(1)} %get-tuple-element.43), channel_id=1, source_target_pairs={{0,2},{1,3},{2,0},{3,1},{4,6},{5,7},{6,4},{7,5},{8,10},{9,11},{10,... | collective-permute-start | bytes 294920 | tf_op jit(solution)/shard_map/ppermute | solution.py:289
  9.8 10.8 %collective-permute-start.6 = (bf16[384,128]{1,0:T(8,128)(2,1)S(1)}, bf16[384,128]{1,0:T(8,128)(2,1)S(1)}, u32[]{:S(2)}, u32[]{:S(2)}) collective-permute-start(bf16[384,128]{1,0:T(8,128)(2,1)S(1)} %get-tuple-element.51), channel_id=1, source_target_pairs={{0,16},{4,20},{8,24},{12,28},{16,0},{20,4},{24,8},{28,12},{1,17},{... | collective-permute-start | bytes 294920 | tf_op jit(solution)/shard_map/ppermute | solution.py:292
  12.4 5.5 %copy-start.3 = (bf16[192,768]{1,0:T(8,128)(2,1)S(1)}, bf16[192,768]{1,0:T(8,128)(2,1)}, u32[]{:S(2)}) copy-start(bf16[192,768]{1,0:T(8,128)(2,1)} %param.12) | copy-start | bytes 884740
  12.4 5.4 %copy-start.1 = (f32[3,768]{1,0:T(4,128)S(1)}, f32[3,768]{1,0:T(4,128)}, u32[]{:S(2)}) copy-start(f32[3,768]{1,0:T(4,128)} %value.1) | copy-start | bytes 27652
  12.4 5.4 %copy-start.2 = (bf16[2,128,768]{2,1,0:T(8,128)(2,1)S(1)}, bf16[2,128,768]{2,1,0:T(8,128)(2,1)}, u32[]{:S(2)}) copy-start(bf16[2,128,768]{2,1,0:T(8,128)(2,1)} %states.1) | copy-start | bytes 1179652
  12.4 9.5 %collective-permute-start.5 = (bf16[192,768]{1,0:T(8,128)(2,1)S(1)}, bf16[192,768]{1,0:T(8,128)(2,1)S(1)}, u32[]{:S(2)}, u32[]{:S(2)}) collective-permute-start(bf16[192,768]{1,0:T(8,128)(2,1)S(1)} %cross_output_rows.1), channel_id=1, source_target_pairs={{0,2},{1,3},{2,0},{3,1},{4,6},{5,7},{6,4},{7,5},{8,10},{9,11},{10,... | collective-permute-start | bytes 884744 | tf_op jit(solution)/shard_map/ppermute | solution.py:289
  14.0 8.2 %collective-permute-start.8 = (bf16[384,128]{1,0:T(8,128)(2,1)S(1)}, bf16[384,128]{1,0:T(8,128)(2,1)S(1)}, u32[]{:S(2)}, u32[]{:S(2)}) collective-permute-start(bf16[384,128]{1,0:T(8,128)(2,1)S(1)} %get-tuple-element.52), channel_id=1, source_target_pairs={{0,24},{4,28},{8,16},{12,20},{16,8},{20,12},{24,0},{28,4},{1,25},{... | collective-permute-start | bytes 294920 | tf_op jit(solution)/shard_map/ppermute | solution.py:292
  16.5 7.3 %collective-permute-start.9 = (bf16[384,128]{1,0:T(8,128)(2,1)S(1)}, bf16[384,128]{1,0:T(8,128)(2,1)S(1)}, u32[]{:S(2)}, u32[]{:S(2)}) collective-permute-start(bf16[384,128]{1,0:T(8,128)(2,1)S(1)} %get-tuple-element.53), channel_id=1, source_target_pairs={{0,28},{4,8},{8,4},{12,16},{16,12},{20,24},{24,20},{28,0},{1,29},{... | collective-permute-start | bytes 294920 | tf_op jit(solution)/shard_map/ppermute | solution.py:292
  18.3 1.8 %collective-permute-start = (bf16[256,768]{1,0:T(8,128)(2,1)S(1)}, bf16[256,768]{1,0:T(8,128)(2,1)S(1)}, u32[]{:S(2)}, u32[]{:S(2)}) collective-permute-start(bf16[256,768]{1,0:T(8,128)(2,1)S(1)} %get-tuple-element.25), channel_id=1, source_target_pairs={{0,1},{1,0},{2,3},{3,2},{4,5},{5,4},{6,7},{7,6},{8,9},{9,8},{10,11... | collective-permute-start | bytes 1179656 | tf_op jit(solution)/shard_map/cond/branch_1_fun/ppermute | solution.py:289
  20.6 1.3 %copy-start = (bf16[192,768]{1,0:T(8,128)(2,1)S(1)}, bf16[192,768]{1,0:T(8,128)(2,1)}, u32[]{:S(2)}) copy-start(bf16[192,768]{1,0:T(8,128)(2,1)} %own.1) | copy-start | bytes 884740
  22.0 8.0 %collective-permute-start.7 = (bf16[384,768]{1,0:T(8,128)(2,1)S(1)}, bf16[384,768]{1,0:T(8,128)(2,1)S(1)}, u32[]{:S(2)}, u32[]{:S(2)}) collective-permute-start(bf16[384,768]{1,0:T(8,128)(2,1)S(1)} %cross_output_both_rows.1.own_weights), channel_id=1, source_target_pairs={{0,1},{1,0},{2,3},{3,2},{4,5},{5,4},{6,7},{7,6},{8,9},{9,8},{10,11... | collective-permute-start | bytes 1769480 | tf_op jit(solution)/shard_map/ppermute | solution.py:289
  24.7 4.6 %collective-permute-start.10 = (bf16[5,48,128]{2,1,0:T(8,128)(2,1)S(1)}, bf16[5,48,128]{2,1,0:T(8,128)(2,1)S(1)}, u32[]{:S(2)}, u32[]{:S(2)}) collective-permute-start(bf16[5,48,128]{2,1,0:T(8,128)(2,1)S(1)} %get-tuple-element.55), channel_id=1, source_target_pairs={{0,2},{1,3},{2,0},{3,1},{4,6},{5,7},{6,4},{7,5},{8,10},{9,11},{10,... | collective-permute-start | bytes 184328 | tf_op jit(solution)/shard_map/ppermute | solution.py:289
  25.7 4.3 %collective-permute-start.11 = (bf16[5,48,128]{2,1,0:T(8,128)(2,1)S(1)}, bf16[5,48,128]{2,1,0:T(8,128)(2,1)S(1)}, u32[]{:S(2)}, u32[]{:S(2)}) collective-permute-start(bf16[5,48,128]{2,1,0:T(8,128)(2,1)S(1)} %get-tuple-element.56), channel_id=1, source_target_pairs={{0,3},{1,2},{2,1},{3,0},{4,7},{5,6},{6,5},{7,4},{8,11},{9,10},{10,... | collective-permute-start | bytes 184328 | tf_op jit(solution)/shard_map/ppermute | solution.py:289
  25.7 4.3 %collective-permute-start.12 = (bf16[5,48,128]{2,1,0:T(8,128)(2,1)S(1)}, bf16[5,48,128]{2,1,0:T(8,128)(2,1)S(1)}, u32[]{:S(2)}, u32[]{:S(2)}) collective-permute-start(bf16[5,48,128]{2,1,0:T(8,128)(2,1)S(1)} %get-tuple-element.57), channel_id=1, source_target_pairs={{0,1},{1,0},{2,3},{3,2},{4,5},{5,4},{6,7},{7,6},{8,9},{9,8},{10,11... | collective-permute-start | bytes 184328 | tf_op jit(solution)/shard_map/ppermute | solution.py:289

commit v13 on v11

--- a/solution.py
+++ b/solution.py
@@ -343,9 +343,9 @@
         "cross_output_rows",
         hand_on_kernel,
         shape(cross_out.shape, BF16),
-        [VMEM] + [ANY] * len([arrived[short[0]]]),
+        [VMEM] + [ANY] * len([self_out_got]),
         [],
-        cross_out_own, *[arrived[short[0]]],
+        cross_out_own, *[self_out_got],
     )
     cross_out_got = across(cross_out_sent, chip_hop)
     before = [arrived[at] for at in short] + [self_out_got]

time: 30.4 us -> 30.9 us (1.016)
  waiting for transfers between devices: 5.55 us -> 5.97 us
    ppermute x5, waiting for transfers between devices: 0.44 us -> 1.94 us  [exchange(): lax.ppermute(value, 'owner', [(o, swap_target(o, swap, owner_n)) for o in...]
    ppermute x8, waiting for transfers between devices: 5.12 us -> 4.03 us  [across(): return lax.ppermute(value, 'helper', [(j, j ^ k) for j in range(helper_n)])]
  transfers between devices with their start and end apart: 13 -> 13, of which waited for: 4 -> 3; matrix products, arithmetic and copies ran while one was open for 0% -> 0% of each run, Pallas kernels for 20% -> 20%
where the time goes in v13:
time: 30.9 us; the launch traced here: 30.8 us
  starting transfers between devices  17.2 us (56%)
  Pallas kernels  7.45 us (24%)
  waiting for transfers between devices  5.97 us (19%)
    ppermute x5, starting transfers between devices, exchange(): lax.ppermute(value, 'owner', [(o, swap_target(o, swap, owner_n)) for o in...  9.67 us
    ppermute x8, starting transfers between devices, across(): return lax.ppermute(value, 'helper', [(j, j ^ k) for j in range(helper_n)])  7.52 us
    pallas_call x9, Pallas kernels, call(): pl.pallas_call(kernel, out_shape=out_shape, in_specs=in_specs, out_specs=...  7.45 us
    ppermute x8, waiting for transfers between devices, across(): return lax.ppermute(value, 'helper', [(j, j ^ k) for j in range(helper_n)])  4.03 us
    ppermute x5, waiting for transfers between devices, exchange(): lax.ppermute(value, 'owner', [(o, swap_target(o, swap, owner_n)) for o in...  1.94 us
  transfers between devices with their start and end apart: 13, of which 3 were waited for; matrix products, arithmetic and copies ran while one was open for 0% of the time, Pallas kernels for 20%

profile of v13, /device:TPU:0, one launch (start us, length us, event | category | flops | bytes accessed | tf_op | source)
XLA Modules:
  0.0 30.8 jit_solution(10921531240870965148)
XLA Ops:
  0.0 3.0 %collective-permute-start.2 = (bf16[192,768]{1,0:T(8,128)(2,1)}, bf16[192,768]{1,0:T(8,128)(2,1)S(1)}, u32[]{:S(2)}, u32[]{:S(2)}) collective-permute-start(bf16[192,768]{1,0:T(8,128)(2,1)} %param.12), channel_id=1, source_target_pairs={{0,2},{1,3},{2,0},{3,1},{4,6},{5,7},{6,4},{7,5},{8,10},{9,11},{10,... | collective-permute-start | bytes 884744 | tf_op jit(solution)/shard_map/ppermute | solution.py:288
  3.0 3.1 %own_images.1 = (bf16[384,128]{1,0:T(8,128)(2,1)S(1)}, bf16[384,128]{1,0:T(8,128)(2,1)S(1)}, bf16[384,128]{1,0:T(8,128)(2,1)S(1)}, bf16[384,128]{1,0:T(8,128)(2,...) custom-call(bf16[2,128,768]{2,1,0:T(8,128)(2,1)} %states.1, ...), custom_call_target="tpu_custom_call" | custom-call | flops 1 | bytes 1 | tf_op jit(solution)/shard_map/own_images/pallas_call | solution.py:295
  6.0 1.6 %collective-permute-start.3 = (bf16[384,128]{1,0:T(8,128)(2,1)S(1)}, bf16[384,128]{1,0:T(8,128)(2,1)S(1)}, u32[]{:S(2)}, u32[]{:S(2)}) collective-permute-start(bf16[384,128]{1,0:T(8,128)(2,1)S(1)} %get-tuple-element.44), channel_id=1, source_target_pairs={{0,8},{4,12},{8,0},{12,4},{16,24},{20,28},{24,16},{28,20},{1,9},{5... | collective-permute-start | bytes 294920 | tf_op jit(solution)/shard_map/ppermute | solution.py:291
  7.7 1.5 %collective-permute-start.4 = (bf16[384,128]{1,0:T(8,128)(2,1)S(1)}, bf16[384,128]{1,0:T(8,128)(2,1)S(1)}, u32[]{:S(2)}, u32[]{:S(2)}) collective-permute-start(bf16[384,128]{1,0:T(8,128)(2,1)S(1)} %get-tuple-element.45), channel_id=1, source_target_pairs={{0,4},{4,0},{8,12},{12,8},{16,20},{20,16},{24,28},{28,24},{1,5},{5... | collective-permute-start | bytes 294920 | tf_op jit(solution)/shard_map/ppermute | solution.py:291
  9.2 0.5 %collective-permute-start.1 = (bf16[384,128]{1,0:T(8,128)(2,1)S(1)}, bf16[384,128]{1,0:T(8,128)(2,1)S(1)}, u32[]{:S(2)}, u32[]{:S(2)}) collective-permute-start(bf16[384,128]{1,0:T(8,128)(2,1)S(1)} %get-tuple-element.43), channel_id=1, source_target_pairs={{0,2},{1,3},{2,0},{3,1},{4,6},{5,7},{6,4},{7,5},{8,10},{9,11},{10,... | collective-permute-start | bytes 294920 | tf_op jit(solution)/shard_map/ppermute | solution.py:288
  9.7 2.6 %collective-permute-start.6 = (bf16[384,128]{1,0:T(8,128)(2,1)S(1)}, bf16[384,128]{1,0:T(8,128)(2,1)S(1)}, u32[]{:S(2)}, u32[]{:S(2)}) collective-permute-start(bf16[384,128]{1,0:T(8,128)(2,1)S(1)} %get-tuple-element.51), channel_id=1, source_target_pairs={{0,16},{4,20},{8,24},{12,28},{16,0},{20,4},{24,8},{28,12},{1,17},{... | collective-permute-start | bytes 294920 | tf_op jit(solution)/shard_map/ppermute | solution.py:291
  12.3 0.0 collective-permute-done.2.rest_2_.rest_0_
  12.3 0.0 copy-start.1
  12.3 0.0 copy-start.2
  12.3 1.6 %collective-permute-start.5 = (bf16[192,768]{1,0:T(8,128)(2,1)S(1)}, bf16[192,768]{1,0:T(8,128)(2,1)S(1)}, u32[]{:S(2)}, u32[]{:S(2)}) collective-permute-start(bf16[192,768]{1,0:T(8,128)(2,1)S(1)} %cross_output_rows.1), channel_id=1, source_target_pairs={{0,2},{1,3},{2,0},{3,1},{4,6},{5,7},{6,4},{7,5},{8,10},{9,11},{10,... | collective-permute-start | bytes 884744 | tf_op jit(solution)/shard_map/ppermute | solution.py:288
  13.9 0.0 collective-permute-done.3.rest_0_.rest_1_
  13.9 2.8 %collective-permute-start.8 = (bf16[384,128]{1,0:T(8,128)(2,1)S(1)}, bf16[384,128]{1,0:T(8,128)(2,1)S(1)}, u32[]{:S(2)}, u32[]{:S(2)}) collective-permute-start(bf16[384,128]{1,0:T(8,128)(2,1)S(1)} %get-tuple-element.52), channel_id=1, source_target_pairs={{0,24},{4,28},{8,16},{12,20},{16,8},{20,12},{24,0},{28,4},{1,25},{... | collective-permute-start | bytes 294920 | tf_op jit(solution)/shard_map/ppermute | solution.py:291
  16.7 1.1 %collective-permute-start.9 = (bf16[384,128]{1,0:T(8,128)(2,1)S(1)}, bf16[384,128]{1,0:T(8,128)(2,1)S(1)}, u32[]{:S(2)}, u32[]{:S(2)}) collective-permute-start(bf16[384,128]{1,0:T(8,128)(2,1)S(1)} %get-tuple-element.53), channel_id=1, source_target_pairs={{0,28},{4,8},{8,4},{12,16},{16,12},{20,24},{24,20},{28,0},{1,29},{... | collective-permute-start | bytes 294920 | tf_op jit(solution)/shard_map/ppermute | solution.py:291
  17.9 0.0 collective-permute-done.1
  17.9 2.8 %conditional.1 = ((f32[2,32,768]{2,1,0:T(8,128)S(1)}, bf16[2,128,192]{2,1,0:T(8,128)(2,1)S(1)})) conditional(s32[]{:T(128)} %convert_element_type.3, () %tuple.12, (bf16[2,128,768]{2,1,0:T(8,128)(2,1)S(1)}, bf16[384,128]{1,0:T(8,128)(2,1)S(1)}, bf16[384,128]{1,0:T(8,128)(2,1)S(1)}, bf16[192,768]{1,0:T(8,128)(2,1)S(1)}, ...), branch_computations={%region_0.0_spmd, %region_1.0_spmd} | conditional | flops 2 | bytes 1572914 | solution.py:388
  17.9 0.4 %self_output_share.1 = (f32[256,768]{1,0:T(8,128)S(1)}, bf16[256,768]{1,0:T(8,128)(2,1)S(1)}) custom-call(bf16[2,128,768]{2,1,0:T(8,128)(2,1)S(1)} %get-tuple-element.19.states, bf16[384,128]{1,0:T(8,128)(2,1)S(1)} %get-tuple-element.20.own, bf16[384,128]{1,0:T(8,128)(2,1)S(1)} %get-tuple-element.21.got, bf16[192,768]{1,0:T(8,128)(2,1)S(1)} %get-tuple-element.22.own_weight, ...), custom_call_target="tpu_custom_call" | custom-call | flops 1 | bytes 1 | tf_op jit(solution)/shard_map/cond/branch_1_fun/self_output_share/pallas_call | solution.py:295
  18.3 0.1 collective-permute-start
  18.4 1.7 %collective-permute-done.got = bf16[256,768]{1,0:T(8,128)(2,1)S(1)} collective-permute-done((bf16[256,768]{1,0:T(8,128)(2,1)S(1)}, bf16[256,768]{1,0:T(8,128)(2,1)S(1)}, u32[]{:S(2)}, u32[]{:S(2)}) %collective-permute-start) | collective-permute-done | bytes 393248 | tf_op jit(solution)/shard_map/cond/branch_1_fun/ppermute | solution.py:288
  20.1 0.5 %mixed_and_queries.1 = (f32[2,32,768]{2,1,0:T(8,128)S(1)}, bf16[2,128,192]{2,1,0:T(8,128)(2,1)S(1)}) custom-call(f32[256,768]{1,0:T(8,128)S(1)} %get-tuple-element.24.base, bf16[256,768]{1,0:T(8,128)(2,1)S(1)} %collective-permute-done.got, f32[3,768]{1,0:T(4,128)S(1)} %get-tuple-element.26.gains, bf16[192,768]{1,0:T(8,128)(2,1)S(1)} %get-tuple-element.27.weight), custom_call_target="tpu_custom_call" | custom-call | flops 1 | bytes 1 | tf_op jit(solution)/shard_map/cond/branch_1_fun/mixed_and_queries/pallas_call | solution.py:295
  20.7 0.0 collective-permute-done.6.rest_0_
  20.7 0.0 copy-start
  20.7 1.0 %early_cross_attention.1.waited.before = bf16[4,3,48,128]{3,2,1,0:T(8,128)(2,1)S(1)} custom-call(bf16[2,128,192]{2,1,0:T(8,128)(2,1)S(1)} %get-tuple-element.50.queries, s32[11,128]{1,0:T(8,128)S(1)} %get-tuple-element.48.table, bf16[384,128]{1,0:T(8,128)(2,1)S(1)} %collective-permute-done.6.rest_0_, ...), custom_call_target="tpu_custom_call" | custom-call | flops 3000000000 | bytes 1 | tf_op jit(solution)/shard_map/early_cross_attention/pallas_call | solution.py:295
  21.7 0.1 cross_output_both_rows.1.own_weights
  21.9 0.2 collective-permute-start.7
  22.1 0.0 collective-permute-done.8.rest_0_
  22.1 1.9 %collective-permute-done.9.rest_1_ = bf16[384,128]{1,0:T(8,128)(2,1)S(1)} collective-permute-done((bf16[384,128]{1,0:T(8,128)(2,1)S(1)}, bf16[384,128]{1,0:T(8,128)(2,1)S(1)}, u32[]{:S(2)}, u32[]{:S(2)}) %collective-permute-start.9) | collective-permute-done | bytes 98336 | tf_op jit(solution)/shard_map/ppermute | solution.py:291
  24.0 0.9 %late_cross_attention.1 = (bf16[5,48,128]{2,1,0:T(8,128)(2,1)S(1)}, bf16[5,48,128]{2,1,0:T(8,128)(2,1)S(1)}, bf16[5,48,128]{2,1,0:T(8,128)(2,1)S(1)}, bf16[5,48,128]{2,1,0:T(8,128)(2,1)S(1)}) custom-call(bf16[2,128,192]{2,1,0:T(8,128)(2,1)S(1)} %get-tuple-element.50.queries, s32[11,128]{1,0:T(8,128)S(1)} %get-tuple-element.48.table, ...), custom_call_target="tpu_custom_call" | custom-call | flops 99999997952 | bytes 1 | tf_op jit(solution)/shard_map/late_cross_attention/pallas_call | solution.py:295
  24.9 0.2 collective-permute-start.10
  25.1 0.0 collective-permute-start.11
  25.1 2.0 %collective-permute-start.12 = (bf16[5,48,128]{2,1,0:T(8,128)(2,1)S(1)}, bf16[5,48,128]{2,1,0:T(8,128)(2,1)S(1)}, u32[]{:S(2)}, u32[]{:S(2)}) collective-permute-start(bf16[5,48,128]{2,1,0:T(8,128)(2,1)S(1)} %get-tuple-element.57), channel_id=1, source_target_pairs={{0,1},{1,0},{2,3},{3,2},{4,5},{5,4},{6,7},{7,6},{8,9},{9,8},{10,11... | collective-permute-start | bytes 184328 | tf_op jit(solution)/shard_map/ppermute | solution.py:288
  27.1 2.3 %collective-permute-done.10.rest_1_ = bf16[5,48,128]{2,1,0:T(8,128)(2,1)S(1)} collective-permute-done((bf16[5,48,128]{2,1,0:T(8,128)(2,1)S(1)}, bf16[5,48,128]{2,1,0:T(8,128)(2,1)S(1)}, u32[]{:S(2)}, u32[]{:S(2)}) %collective-permute-start.10) | collective-permute-done | bytes 61472 | tf_op jit(solution)/shard_map/ppermute | solution.py:288
  29.4 1.4 %pair_output.1 = bf16[2,5,32,768]{3,2,1,0:T(8,128)(2,1)} custom-call(f32[2,32,768]{2,1,0:T(8,128)S(1)} %get-tuple-element.47.own_rows, s32[11,128]{1,0:T(8,128)S(1)} %get-tuple-element.48.table, bf16[384,768]{1,0:T(8,128)(2,1)S(1)} %cross_output_both_rows.1.own_weights, bf16[384,768]{1,0:T(8,128)(2,1)S(1)} %collective-permute-done.7.core_weights, ...), custom_call_target="tpu_custom_call" | custom-call | flops 1 | bytes 1 | tf_op jit(solution)/shard_map/pair_output/pallas_call | solution.py:295
  (12 shorter events, 0.0 us)
Async XLA Ops:
  0.0 12.3 %collective-permute-start.2 = (bf16[192,768]{1,0:T(8,128)(2,1)}, bf16[192,768]{1,0:T(8,128)(2,1)S(1)}, u32[]{:S(2)}, u32[]{:S(2)}) collective-permute-start(bf16[192,768]{1,0:T(8,128)(2,1)} %param.12), channel_id=1, source_target_pairs={{0,2},{1,3},{2,0},{3,1},{4,6},{5,7},{6,4},{7,5},{8,10},{9,11},{10,... | collective-permute-start | bytes 884744 | tf_op jit(solution)/shard_map/ppermute | solution.py:288
  6.0 7.9 %collective-permute-start.3 = (bf16[384,128]{1,0:T(8,128)(2,1)S(1)}, bf16[384,128]{1,0:T(8,128)(2,1)S(1)}, u32[]{:S(2)}, u32[]{:S(2)}) collective-permute-start(bf16[384,128]{1,0:T(8,128)(2,1)S(1)} %get-tuple-element.44), channel_id=1, source_target_pairs={{0,8},{4,12},{8,0},{12,4},{16,24},{20,28},{24,16},{28,20},{1,9},{5... | collective-permute-start | bytes 294920 | tf_op jit(solution)/shard_map/ppermute | solution.py:291
  7.7 9.0 %collective-permute-start.4 = (bf16[384,128]{1,0:T(8,128)(2,1)S(1)}, bf16[384,128]{1,0:T(8,128)(2,1)S(1)}, u32[]{:S(2)}, u32[]{:S(2)}) collective-permute-start(bf16[384,128]{1,0:T(8,128)(2,1)S(1)} %get-tuple-element.45), channel_id=1, source_target_pairs={{0,4},{4,0},{8,12},{12,8},{16,20},{20,16},{24,28},{28,24},{1,5},{5... | collective-permute-start | bytes 294920 | tf_op jit(solution)/shard_map/ppermute | solution.py:291
  9.2 8.7 %collective-permute-start.1 = (bf16[384,128]{1,0:T(8,128)(2,1)S(1)}, bf16[384,128]{1,0:T(8,128)(2,1)S(1)}, u32[]{:S(2)}, u32[]{:S(2)}) collective-permute-start(bf16[384,128]{1,0:T(8,128)(2,1)S(1)} %get-tuple-element.43), channel_id=1, source_target_pairs={{0,2},{1,3},{2,0},{3,1},{4,6},{5,7},{6,4},{7,5},{8,10},{9,11},{10,... | collective-permute-start | bytes 294920 | tf_op jit(solution)/shard_map/ppermute | solution.py:288
  9.7 11.0 %collective-permute-start.6 = (bf16[384,128]{1,0:T(8,128)(2,1)S(1)}, bf16[384,128]{1,0:T(8,128)(2,1)S(1)}, u32[]{:S(2)}, u32[]{:S(2)}) collective-permute-start(bf16[384,128]{1,0:T(8,128)(2,1)S(1)} %get-tuple-element.51), channel_id=1, source_target_pairs={{0,16},{4,20},{8,24},{12,28},{16,0},{20,4},{24,8},{28,12},{1,17},{... | collective-permute-start | bytes 294920 | tf_op jit(solution)/shard_map/ppermute | solution.py:291
  12.3 5.6 %copy-start.3 = (bf16[192,768]{1,0:T(8,128)(2,1)S(1)}, bf16[192,768]{1,0:T(8,128)(2,1)}, u32[]{:S(2)}) copy-start(bf16[192,768]{1,0:T(8,128)(2,1)} %param.12) | copy-start | bytes 884740
  12.3 5.5 %copy-start.1 = (f32[3,768]{1,0:T(4,128)S(1)}, f32[3,768]{1,0:T(4,128)}, u32[]{:S(2)}) copy-start(f32[3,768]{1,0:T(4,128)} %value.1) | copy-start | bytes 27652
  12.3 5.6 %copy-start.2 = (bf16[2,128,768]{2,1,0:T(8,128)(2,1)S(1)}, bf16[2,128,768]{2,1,0:T(8,128)(2,1)}, u32[]{:S(2)}) copy-start(bf16[2,128,768]{2,1,0:T(8,128)(2,1)} %states.1) | copy-start | bytes 1179652
  12.3 9.4 %collective-permute-start.5 = (bf16[192,768]{1,0:T(8,128)(2,1)S(1)}, bf16[192,768]{1,0:T(8,128)(2,1)S(1)}, u32[]{:S(2)}, u32[]{:S(2)}) collective-permute-start(bf16[192,768]{1,0:T(8,128)(2,1)S(1)} %cross_output_rows.1), channel_id=1, source_target_pairs={{0,2},{1,3},{2,0},{3,1},{4,6},{5,7},{6,4},{7,5},{8,10},{9,11},{10,... | collective-permute-start | bytes 884744 | tf_op jit(solution)/shard_map/ppermute | solution.py:288
  13.9 8.2 %collective-permute-start.8 = (bf16[384,128]{1,0:T(8,128)(2,1)S(1)}, bf16[384,128]{1,0:T(8,128)(2,1)S(1)}, u32[]{:S(2)}, u32[]{:S(2)}) collective-permute-start(bf16[384,128]{1,0:T(8,128)(2,1)S(1)} %get-tuple-element.52), channel_id=1, source_target_pairs={{0,24},{4,28},{8,16},{12,20},{16,8},{20,12},{24,0},{28,4},{1,25},{... | collective-permute-start | bytes 294920 | tf_op jit(solution)/shard_map/ppermute | solution.py:291
  16.7 7.3 %collective-permute-start.9 = (bf16[384,128]{1,0:T(8,128)(2,1)S(1)}, bf16[384,128]{1,0:T(8,128)(2,1)S(1)}, u32[]{:S(2)}, u32[]{:S(2)}) collective-permute-start(bf16[384,128]{1,0:T(8,128)(2,1)S(1)} %get-tuple-element.53), channel_id=1, source_target_pairs={{0,28},{4,8},{8,4},{12,16},{16,12},{20,24},{24,20},{28,0},{1,29},{... | collective-permute-start | bytes 294920 | tf_op jit(solution)/shard_map/ppermute | solution.py:291
  18.3 1.8 %collective-permute-start = (bf16[256,768]{1,0:T(8,128)(2,1)S(1)}, bf16[256,768]{1,0:T(8,128)(2,1)S(1)}, u32[]{:S(2)}, u32[]{:S(2)}) collective-permute-start(bf16[256,768]{1,0:T(8,128)(2,1)S(1)} %get-tuple-element.25), channel_id=1, source_target_pairs={{0,1},{1,0},{2,3},{3,2},{4,5},{5,4},{6,7},{7,6},{8,9},{9,8},{10,11... | collective-permute-start | bytes 1179656 | tf_op jit(solution)/shard_map/cond/branch_1_fun/ppermute | solution.py:288
  20.7 1.1 %copy-start = (bf16[192,768]{1,0:T(8,128)(2,1)S(1)}, bf16[192,768]{1,0:T(8,128)(2,1)}, u32[]{:S(2)}) copy-start(bf16[192,768]{1,0:T(8,128)(2,1)} %own.1) | copy-start | bytes 884740
  21.9 7.5 %collective-permute-start.7 = (bf16[384,768]{1,0:T(8,128)(2,1)S(1)}, bf16[384,768]{1,0:T(8,128)(2,1)S(1)}, u32[]{:S(2)}, u32[]{:S(2)}) collective-permute-start(bf16[384,768]{1,0:T(8,128)(2,1)S(1)} %cross_output_both_rows.1.own_weights), channel_id=1, source_target_pairs={{0,1},{1,0},{2,3},{3,2},{4,5},{5,4},{6,7},{7,6},{8,9},{9,8},{10,11... | collective-permute-start | bytes 1769480 | tf_op jit(solution)/shard_map/ppermute | solution.py:288
  24.9 4.5 %collective-permute-start.10 = (bf16[5,48,128]{2,1,0:T(8,128)(2,1)S(1)}, bf16[5,48,128]{2,1,0:T(8,128)(2,1)S(1)}, u32[]{:S(2)}, u32[]{:S(2)}) collective-permute-start(bf16[5,48,128]{2,1,0:T(8,128)(2,1)S(1)} %get-tuple-element.55), channel_id=1, source_target_pairs={{0,2},{1,3},{2,0},{3,1},{4,6},{5,7},{6,4},{7,5},{8,10},{9,11},{10,... | collective-permute-start | bytes 184328 | tf_op jit(solution)/shard_map/ppermute | solution.py:288
  25.1 4.3 %collective-permute-start.11 = (bf16[5,48,128]{2,1,0:T(8,128)(2,1)S(1)}, bf16[5,48,128]{2,1,0:T(8,128)(2,1)S(1)}, u32[]{:S(2)}, u32[]{:S(2)}) collective-permute-start(bf16[5,48,128]{2,1,0:T(8,128)(2,1)S(1)} %get-tuple-element.56), channel_id=1, source_target_pairs={{0,3},{1,2},{2,1},{3,0},{4,7},{5,6},{6,5},{7,4},{8,11},{9,10},{10,... | collective-permute-start | bytes 184328 | tf_op jit(solution)/shard_map/ppermute | solution.py:288
  25.1 4.3 %collective-permute-start.12 = (bf16[5,48,128]{2,1,0:T(8,128)(2,1)S(1)}, bf16[5,48,128]{2,1,0:T(8,128)(2,1)S(1)}, u32[]{:S(2)}, u32[]{:S(2)}) collective-permute-start(bf16[5,48,128]{2,1,0:T(8,128)(2,1)S(1)} %get-tuple-element.57), channel_id=1, source_target_pairs={{0,1},{1,0},{2,3},{3,2},{4,5},{5,4},{6,7},{7,6},{8,9},{9,8},{10,11... | collective-permute-start | bytes 184328 | tf_op jit(solution)/shard_map/ppermute | solution.py:288

commit v14 on v11

--- a/solution.py
+++ b/solution.py
@@ -238,26 +238,30 @@
     return jnp.concatenate([main.reshape(-1, LANES), tail.reshape(-1, HEAD)], 1)
 
 
-def out_kernel(order, own_rows, table, own_weights, core_weights, *rest):
-    own, across_chip, across_both, across_core, out, out_v, sems = rest
-    sides = [own, across_chip, across_core, across_both]
-    row_n, width = own_rows.shape[1:]
+def placed_rows(sides, order, table):
     pair_n = len(order)
-    placed = []
+    rows = []
     for side in sides:
         pairs = [side[at].astype(F32) for at in range(pair_n)]
+        placed = []
         for position in range(pair_n):
             block = pairs[0]
             for at in range(1, pair_n):
                 row = pair_n + order[at]
                 block = jnp.where(table[row : row + 1, 0:1] == position, pairs[at], block)
             placed.append(block.astype(BF16)[None])
-    rows = [
-        side_rows(jnp.concatenate(placed[at * pair_n : (at + 1) * pair_n], 0)) for at in range(len(sides))
-    ]
-    half = len(sides) // 2
-    terms = nn(jnp.concatenate(rows[:half], 1), own_weights[...])
-    terms = terms + nn(jnp.concatenate(rows[half:], 1), core_weights[...])
+        rows.append(side_rows(jnp.concatenate(placed, 0)))
+    return jnp.concatenate(rows, 1)
+
+
+def first_terms_kernel(order, table, weights, own, across_chip, terms):
+    terms[...] = nn(placed_rows((own, across_chip), order, table), weights[...])
+
+
+def out_kernel(order, own_rows, table, weights, first, across_both, across_core, out, out_v, sems):
+    row_n, width = own_rows.shape[1:]
+    pair_n = len(order)
+    terms = first[...] + nn(placed_rows((across_core, across_both), order, table), weights[...])
     first_n = table[2 * pair_n :, 0:1]
     zero = jnp.zeros((row_n, width), F32)
     for position in range(pair_n):
@@ -418,14 +422,22 @@
         cross_out, cross_out_got, early_sides,
     )
     cross_out_core = across(cross_out_both, core_hop)
+    order = early + late
+    first_terms = call(
+        "first_terms",
+        functools.partial(first_terms_kernel, order),
+        shape((pair_n * row_n, width), F32),
+        [VMEM] * 4,
+        [],
+        table, cross_out_both, sides[0], sides[chip_hop],
+    )
     return call(
         "pair_output",
-        functools.partial(out_kernel, early + late),
+        functools.partial(out_kernel, order),
         shape((image_n, slot_n, row_n, width), BF16),
-        [VMEM] * (4 + helper_n),
+        [VMEM] * 6,
         [pltpu.VMEM((image_n, slot_n, row_n, width), BF16), dma((image_n,))],
-        own_rows, table, cross_out_both, cross_out_core,
-        *[sides[k] for k in (0, chip_hop, chip_hop ^ core_hop, core_hop)],
+        own_rows, table, cross_out_core, first_terms, sides[chip_hop ^ core_hop], sides[core_hop],
         out_specs=HBM,
     )
 

time: 30.4 us -> 30.3 us (level)
  waiting for transfers between devices: 5.55 us -> 5.12 us
  Pallas kernels: 7.46 us -> 7.77 us
    ppermute x8, waiting for transfers between devices: 5.12 us -> 4.69 us  [across(): return lax.ppermute(value, 'helper', [(j, j ^ k) for j in range(helper_n)])]
    pallas_call x9 -> x10, Pallas kernels: 7.46 us -> 7.77 us  [call(): pl.pallas_call(kernel, out_shape=out_shape, in_specs=in_specs, out_specs=...]
  transfers between devices with their start and end apart: 13 -> 13, of which waited for: 4 -> 4; matrix products, arithmetic and copies ran while one was open for 0% -> 0% of each run, Pallas kernels for 20% -> 22%
where the time goes in v14:
time: 30.3 us; the launch traced here: 30.1 us
  starting transfers between devices  17.1 us (56%)
  Pallas kernels  7.77 us (26%)
  waiting for transfers between devices  5.12 us (17%)
    ppermute x5, starting transfers between devices, exchange(): lax.ppermute(value, 'owner', [(o, swap_target(o, swap, owner_n)) for o in...  9.52 us
    pallas_call x10, Pallas kernels, call(): pl.pallas_call(kernel, out_shape=out_shape, in_specs=in_specs, out_specs=...  7.77 us
    ppermute x8, starting transfers between devices, across(): return lax.ppermute(value, 'helper', [(j, j ^ k) for j in range(helper_n)])  7.55 us
    ppermute x8, waiting for transfers between devices, across(): return lax.ppermute(value, 'helper', [(j, j ^ k) for j in range(helper_n)])  4.69 us
  transfers between devices with their start and end apart: 13, of which 4 were waited for; matrix products, arithmetic and copies ran while one was open for 0% of the time, Pallas kernels for 22%

profile of v14, /device:TPU:0, one launch (start us, length us, event | category | flops | bytes accessed | tf_op | source)
XLA Modules:
  0.0 30.1 jit_solution(10709893326886977888)
XLA Ops:
  0.0 3.0 %collective-permute-start.2 = (bf16[192,768]{1,0:T(8,128)(2,1)}, bf16[192,768]{1,0:T(8,128)(2,1)S(1)}, u32[]{:S(2)}, u32[]{:S(2)}) collective-permute-start(bf16[192,768]{1,0:T(8,128)(2,1)} %param.12), channel_id=1, source_target_pairs={{0,2},{1,3},{2,0},{3,1},{4,6},{5,7},{6,4},{7,5},{8,10},{9,11},{10,... | collective-permute-start | bytes 884744 | tf_op jit(solution)/shard_map/ppermute | solution.py:292
  3.0 3.1 %own_images.1 = (bf16[384,128]{1,0:T(8,128)(2,1)S(1)}, bf16[384,128]{1,0:T(8,128)(2,1)S(1)}, bf16[384,128]{1,0:T(8,128)(2,1)S(1)}, bf16[384,128]{1,0:T(8,128)(2,...) custom-call(bf16[2,128,768]{2,1,0:T(8,128)(2,1)} %states.1, ...), custom_call_target="tpu_custom_call" | custom-call | flops 1 | bytes 1 | tf_op jit(solution)/shard_map/own_images/pallas_call | solution.py:299
  6.0 1.7 %collective-permute-start.3 = (bf16[384,128]{1,0:T(8,128)(2,1)S(1)}, bf16[384,128]{1,0:T(8,128)(2,1)S(1)}, u32[]{:S(2)}, u32[]{:S(2)}) collective-permute-start(bf16[384,128]{1,0:T(8,128)(2,1)S(1)} %get-tuple-element.44), channel_id=1, source_target_pairs={{0,8},{4,12},{8,0},{12,4},{16,24},{20,28},{24,16},{28,20},{1,9},{5... | collective-permute-start | bytes 294920 | tf_op jit(solution)/shard_map/ppermute | solution.py:295
  7.7 1.5 %collective-permute-start.4 = (bf16[384,128]{1,0:T(8,128)(2,1)S(1)}, bf16[384,128]{1,0:T(8,128)(2,1)S(1)}, u32[]{:S(2)}, u32[]{:S(2)}) collective-permute-start(bf16[384,128]{1,0:T(8,128)(2,1)S(1)} %get-tuple-element.45), channel_id=1, source_target_pairs={{0,4},{4,0},{8,12},{12,8},{16,20},{20,16},{24,28},{28,24},{1,5},{5... | collective-permute-start | bytes 294920 | tf_op jit(solution)/shard_map/ppermute | solution.py:295
  9.2 0.5 %collective-permute-start.1 = (bf16[384,128]{1,0:T(8,128)(2,1)S(1)}, bf16[384,128]{1,0:T(8,128)(2,1)S(1)}, u32[]{:S(2)}, u32[]{:S(2)}) collective-permute-start(bf16[384,128]{1,0:T(8,128)(2,1)S(1)} %get-tuple-element.43), channel_id=1, source_target_pairs={{0,2},{1,3},{2,0},{3,1},{4,6},{5,7},{6,4},{7,5},{8,10},{9,11},{10,... | collective-permute-start | bytes 294920 | tf_op jit(solution)/shard_map/ppermute | solution.py:292
  9.7 2.6 %collective-permute-start.6 = (bf16[384,128]{1,0:T(8,128)(2,1)S(1)}, bf16[384,128]{1,0:T(8,128)(2,1)S(1)}, u32[]{:S(2)}, u32[]{:S(2)}) collective-permute-start(bf16[384,128]{1,0:T(8,128)(2,1)S(1)} %get-tuple-element.51), channel_id=1, source_target_pairs={{0,16},{4,20},{8,24},{12,28},{16,0},{20,4},{24,8},{28,12},{1,17},{... | collective-permute-start | bytes 294920 | tf_op jit(solution)/shard_map/ppermute | solution.py:295
  12.3 0.0 copy-start.1
  12.3 0.0 copy-start.2
  12.3 1.6 %collective-permute-start.5 = (bf16[192,768]{1,0:T(8,128)(2,1)S(1)}, bf16[192,768]{1,0:T(8,128)(2,1)S(1)}, u32[]{:S(2)}, u32[]{:S(2)}) collective-permute-start(bf16[192,768]{1,0:T(8,128)(2,1)S(1)} %cross_output_rows.1), channel_id=1, source_target_pairs={{0,2},{1,3},{2,0},{3,1},{4,6},{5,7},{6,4},{7,5},{8,10},{9,11},{10,... | collective-permute-start | bytes 884744 | tf_op jit(solution)/shard_map/ppermute | solution.py:292
  13.9 0.0 collective-permute-done.4.rest_1_.rest_2_
  13.9 1.0 %collective-permute-start.8 = (bf16[384,128]{1,0:T(8,128)(2,1)S(1)}, bf16[384,128]{1,0:T(8,128)(2,1)S(1)}, u32[]{:S(2)}, u32[]{:S(2)}) collective-permute-start(bf16[384,128]{1,0:T(8,128)(2,1)S(1)} %get-tuple-element.52), channel_id=1, source_target_pairs={{0,24},{4,28},{8,16},{12,20},{16,8},{20,12},{24,0},{28,4},{1,25},{... | collective-permute-start | bytes 294920 | tf_op jit(solution)/shard_map/ppermute | solution.py:295
  15.0 0.0 collective-permute-done.2.rest_2_
  15.0 2.8 %collective-permute-start.9 = (bf16[384,128]{1,0:T(8,128)(2,1)S(1)}, bf16[384,128]{1,0:T(8,128)(2,1)S(1)}, u32[]{:S(2)}, u32[]{:S(2)}) collective-permute-start(bf16[384,128]{1,0:T(8,128)(2,1)S(1)} %get-tuple-element.53), channel_id=1, source_target_pairs={{0,28},{4,8},{8,4},{12,16},{16,12},{20,24},{24,20},{28,0},{1,29},{... | collective-permute-start | bytes 294920 | tf_op jit(solution)/shard_map/ppermute | solution.py:295
  17.8 2.8 %conditional.1 = ((f32[2,32,768]{2,1,0:T(8,128)S(1)}, bf16[2,128,192]{2,1,0:T(8,128)(2,1)S(1)})) conditional(s32[]{:T(128)} %convert_element_type.3, () %tuple.12, (bf16[2,128,768]{2,1,0:T(8,128)(2,1)S(1)}, bf16[384,128]{1,0:T(8,128)(2,1)S(1)}, bf16[384,128]{1,0:T(8,128)(2,1)S(1)}, bf16[192,768]{1,0:T(8,128)(2,1)S(1)}, ...), branch_computations={%region_0.0_spmd, %region_1.0_spmd} | conditional | flops 2 | bytes 1572914 | solution.py:392
  17.8 0.4 %self_output_share.1 = (f32[256,768]{1,0:T(8,128)S(1)}, bf16[256,768]{1,0:T(8,128)(2,1)S(1)}) custom-call(bf16[2,128,768]{2,1,0:T(8,128)(2,1)S(1)} %get-tuple-element.19.states, bf16[384,128]{1,0:T(8,128)(2,1)S(1)} %get-tuple-element.20.own, bf16[384,128]{1,0:T(8,128)(2,1)S(1)} %get-tuple-element.21.got, bf16[192,768]{1,0:T(8,128)(2,1)S(1)} %get-tuple-element.22.own_weight, ...), custom_call_target="tpu_custom_call" | custom-call | flops 1 | bytes 1 | tf_op jit(solution)/shard_map/cond/branch_1_fun/self_output_share/pallas_call | solution.py:299
  18.2 0.1 collective-permute-start
  18.3 1.7 %collective-permute-done.got = bf16[256,768]{1,0:T(8,128)(2,1)S(1)} collective-permute-done((bf16[256,768]{1,0:T(8,128)(2,1)S(1)}, bf16[256,768]{1,0:T(8,128)(2,1)S(1)}, u32[]{:S(2)}, u32[]{:S(2)}) %collective-permute-start) | collective-permute-done | bytes 393248 | tf_op jit(solution)/shard_map/cond/branch_1_fun/ppermute | solution.py:292
  20.0 0.5 %mixed_and_queries.1 = (f32[2,32,768]{2,1,0:T(8,128)S(1)}, bf16[2,128,192]{2,1,0:T(8,128)(2,1)S(1)}) custom-call(f32[256,768]{1,0:T(8,128)S(1)} %get-tuple-element.24.base, bf16[256,768]{1,0:T(8,128)(2,1)S(1)} %collective-permute-done.got, f32[3,768]{1,0:T(4,128)S(1)} %get-tuple-element.26.gains, bf16[192,768]{1,0:T(8,128)(2,1)S(1)} %get-tuple-element.27.weight), custom_call_target="tpu_custom_call" | custom-call | flops 1 | bytes 1 | tf_op jit(solution)/shard_map/cond/branch_1_fun/mixed_and_queries/pallas_call | solution.py:299
  20.5 0.0 copy-start
  20.6 1.0 %early_cross_attention.1.waited.before = bf16[4,3,48,128]{3,2,1,0:T(8,128)(2,1)S(1)} custom-call(bf16[2,128,192]{2,1,0:T(8,128)(2,1)S(1)} %get-tuple-element.50.queries, s32[11,128]{1,0:T(8,128)S(1)} %get-tuple-element.48.table, bf16[384,128]{1,0:T(8,128)(2,1)S(1)} %collective-permute-done.6.rest_0_, ...), custom_call_target="tpu_custom_call" | custom-call | flops 3000000000 | bytes 1 | tf_op jit(solution)/shard_map/early_cross_attention/pallas_call | solution.py:299
  21.6 0.1 cross_output_both_rows.1.weights
  21.8 0.2 collective-permute-start.7
  22.0 0.4 %collective-permute-done.9.rest_1_ = bf16[384,128]{1,0:T(8,128)(2,1)S(1)} collective-permute-done((bf16[384,128]{1,0:T(8,128)(2,1)S(1)}, bf16[384,128]{1,0:T(8,128)(2,1)S(1)}, u32[]{:S(2)}, u32[]{:S(2)}) %collective-permute-start.9) | collective-permute-done | bytes 98336 | tf_op jit(solution)/shard_map/ppermute | solution.py:295
  22.4 0.9 %late_cross_attention.1 = (bf16[5,48,128]{2,1,0:T(8,128)(2,1)S(1)}, bf16[5,48,128]{2,1,0:T(8,128)(2,1)S(1)}, bf16[5,48,128]{2,1,0:T(8,128)(2,1)S(1)}, bf16[5,48,128]{2,1,0:T(8,128)(2,1)S(1)}) custom-call(bf16[2,128,192]{2,1,0:T(8,128)(2,1)S(1)} %get-tuple-element.50.queries, s32[11,128]{1,0:T(8,128)S(1)} %get-tuple-element.48.table, ...), custom_call_target="tpu_custom_call" | custom-call | flops 99999997952 | bytes 1 | tf_op jit(solution)/shard_map/late_cross_attention/pallas_call | solution.py:299
  23.2 1.6 %collective-permute-start.10 = (bf16[5,48,128]{2,1,0:T(8,128)(2,1)S(1)}, bf16[5,48,128]{2,1,0:T(8,128)(2,1)S(1)}, u32[]{:S(2)}, u32[]{:S(2)}) collective-permute-start(bf16[5,48,128]{2,1,0:T(8,128)(2,1)S(1)} %get-tuple-element.55), channel_id=1, source_target_pairs={{0,2},{1,3},{2,0},{3,1},{4,6},{5,7},{6,4},{7,5},{8,10},{9,11},{10,... | collective-permute-start | bytes 184328 | tf_op jit(solution)/shard_map/ppermute | solution.py:292
  24.8 0.0 collective-permute-start.11
  24.8 0.6 %collective-permute-start.12 = (bf16[5,48,128]{2,1,0:T(8,128)(2,1)S(1)}, bf16[5,48,128]{2,1,0:T(8,128)(2,1)S(1)}, u32[]{:S(2)}, u32[]{:S(2)}) collective-permute-start(bf16[5,48,128]{2,1,0:T(8,128)(2,1)S(1)} %get-tuple-element.57), channel_id=1, source_target_pairs={{0,1},{1,0},{2,3},{3,2},{4,5},{5,4},{6,7},{7,6},{8,9},{9,8},{10,11... | collective-permute-start | bytes 184328 | tf_op jit(solution)/shard_map/ppermute | solution.py:292
  25.4 2.1 %collective-permute-done.10.across_chip = bf16[5,48,128]{2,1,0:T(8,128)(2,1)S(1)} collective-permute-done((bf16[5,48,128]{2,1,0:T(8,128)(2,1)S(1)}, bf16[5,48,128]{2,1,0:T(8,128)(2,1)S(1)}, u32[]{:S(2)}, u32[]{:S(2)}) %collective-permute-start.10) | collective-permute-done | bytes 61472 | tf_op jit(solution)/shard_map/ppermute | solution.py:292
  27.5 0.4 %first_terms.1.first = f32[160,768]{1,0:T(8,128)S(1)} custom-call(s32[11,128]{1,0:T(8,128)S(1)} %get-tuple-element.48.table, bf16[384,768]{1,0:T(8,128)(2,1)S(1)} %cross_output_both_rows.1.weights, bf16[5,48,128]{2,1,0:T(8,128)(2,1)S(1)} %get-tuple-element.54.own, bf16[5,48,128]{2,1,0:T(8,128)(2,1)S(1)} %collective-permute-done.10.across_chip), custom_call_target="tpu_custom_call" | custom-call | flops 1 | bytes 1 | tf_op jit(solution)/shard_map/first_terms/pallas_call | solution.py:299
  28.0 0.9 %collective-permute-done.11.across_both = bf16[5,48,128]{2,1,0:T(8,128)(2,1)S(1)} collective-permute-done((bf16[5,48,128]{2,1,0:T(8,128)(2,1)S(1)}, bf16[5,48,128]{2,1,0:T(8,128)(2,1)S(1)}, u32[]{:S(2)}, u32[]{:S(2)}) %collective-permute-start.11) | collective-permute-done | bytes 61472 | tf_op jit(solution)/shard_map/ppermute | solution.py:292
  28.8 0.0 collective-permute-done.12.across_core
  28.8 1.3 %pair_output.1 = bf16[2,5,32,768]{3,2,1,0:T(8,128)(2,1)} custom-call(f32[2,32,768]{2,1,0:T(8,128)S(1)} %get-tuple-element.47.own_rows, s32[11,128]{1,0:T(8,128)S(1)} %get-tuple-element.48.table, bf16[384,768]{1,0:T(8,128)(2,1)S(1)} %collective-permute-done.7.weights, f32[160,768]{1,0:T(8,128)S(1)} %first_terms.1.first, ...), custom_call_target="tpu_custom_call" | custom-call | flops 1 | bytes 1 | tf_op jit(solution)/shard_map/pair_output/pallas_call | solution.py:299
  (13 shorter events, 0.0 us)
Async XLA Ops:
  0.0 15.0 %collective-permute-start.2 = (bf16[192,768]{1,0:T(8,128)(2,1)}, bf16[192,768]{1,0:T(8,128)(2,1)S(1)}, u32[]{:S(2)}, u32[]{:S(2)}) collective-permute-start(bf16[192,768]{1,0:T(8,128)(2,1)} %param.12), channel_id=1, source_target_pairs={{0,2},{1,3},{2,0},{3,1},{4,6},{5,7},{6,4},{7,5},{8,10},{9,11},{10,... | collective-permute-start | bytes 884744 | tf_op jit(solution)/shard_map/ppermute | solution.py:292
  6.0 6.2 %collective-permute-start.3 = (bf16[384,128]{1,0:T(8,128)(2,1)S(1)}, bf16[384,128]{1,0:T(8,128)(2,1)S(1)}, u32[]{:S(2)}, u32[]{:S(2)}) collective-permute-start(bf16[384,128]{1,0:T(8,128)(2,1)S(1)} %get-tuple-element.44), channel_id=1, source_target_pairs={{0,8},{4,12},{8,0},{12,4},{16,24},{20,28},{24,16},{28,20},{1,9},{5... | collective-permute-start | bytes 294920 | tf_op jit(solution)/shard_map/ppermute | solution.py:295
  7.7 6.2 %collective-permute-start.4 = (bf16[384,128]{1,0:T(8,128)(2,1)S(1)}, bf16[384,128]{1,0:T(8,128)(2,1)S(1)}, u32[]{:S(2)}, u32[]{:S(2)}) collective-permute-start(bf16[384,128]{1,0:T(8,128)(2,1)S(1)} %get-tuple-element.45), channel_id=1, source_target_pairs={{0,4},{4,0},{8,12},{12,8},{16,20},{20,16},{24,28},{28,24},{1,5},{5... | collective-permute-start | bytes 294920 | tf_op jit(solution)/shard_map/ppermute | solution.py:295
  9.2 8.6 %collective-permute-start.1 = (bf16[384,128]{1,0:T(8,128)(2,1)S(1)}, bf16[384,128]{1,0:T(8,128)(2,1)S(1)}, u32[]{:S(2)}, u32[]{:S(2)}) collective-permute-start(bf16[384,128]{1,0:T(8,128)(2,1)S(1)} %get-tuple-element.43), channel_id=1, source_target_pairs={{0,2},{1,3},{2,0},{3,1},{4,6},{5,7},{6,4},{7,5},{8,10},{9,11},{10,... | collective-permute-start | bytes 294920 | tf_op jit(solution)/shard_map/ppermute | solution.py:292
  9.7 10.8 %collective-permute-start.6 = (bf16[384,128]{1,0:T(8,128)(2,1)S(1)}, bf16[384,128]{1,0:T(8,128)(2,1)S(1)}, u32[]{:S(2)}, u32[]{:S(2)}) collective-permute-start(bf16[384,128]{1,0:T(8,128)(2,1)S(1)} %get-tuple-element.51), channel_id=1, source_target_pairs={{0,16},{4,20},{8,24},{12,28},{16,0},{20,4},{24,8},{28,12},{1,17},{... | collective-permute-start | bytes 294920 | tf_op jit(solution)/shard_map/ppermute | solution.py:295
  12.3 5.5 %copy-start.3 = (bf16[192,768]{1,0:T(8,128)(2,1)S(1)}, bf16[192,768]{1,0:T(8,128)(2,1)}, u32[]{:S(2)}) copy-start(bf16[192,768]{1,0:T(8,128)(2,1)} %param.12) | copy-start | bytes 884740
  12.3 5.4 %copy-start.1 = (f32[3,768]{1,0:T(4,128)S(1)}, f32[3,768]{1,0:T(4,128)}, u32[]{:S(2)}) copy-start(f32[3,768]{1,0:T(4,128)} %value.1) | copy-start | bytes 27652
  12.3 5.4 %copy-start.2 = (bf16[2,128,768]{2,1,0:T(8,128)(2,1)S(1)}, bf16[2,128,768]{2,1,0:T(8,128)(2,1)}, u32[]{:S(2)}) copy-start(bf16[2,128,768]{2,1,0:T(8,128)(2,1)} %states.1) | copy-start | bytes 1179652
  12.3 9.3 %collective-permute-start.5 = (bf16[192,768]{1,0:T(8,128)(2,1)S(1)}, bf16[192,768]{1,0:T(8,128)(2,1)S(1)}, u32[]{:S(2)}, u32[]{:S(2)}) collective-permute-start(bf16[192,768]{1,0:T(8,128)(2,1)S(1)} %cross_output_rows.1), channel_id=1, source_target_pairs={{0,2},{1,3},{2,0},{3,1},{4,6},{5,7},{6,4},{7,5},{8,10},{9,11},{10,... | collective-permute-start | bytes 884744 | tf_op jit(solution)/shard_map/ppermute | solution.py:292
  13.9 8.0 %collective-permute-start.8 = (bf16[384,128]{1,0:T(8,128)(2,1)S(1)}, bf16[384,128]{1,0:T(8,128)(2,1)S(1)}, u32[]{:S(2)}, u32[]{:S(2)}) collective-permute-start(bf16[384,128]{1,0:T(8,128)(2,1)S(1)} %get-tuple-element.52), channel_id=1, source_target_pairs={{0,24},{4,28},{8,16},{12,20},{16,8},{20,12},{24,0},{28,4},{1,25},{... | collective-permute-start | bytes 294920 | tf_op jit(solution)/shard_map/ppermute | solution.py:295
  15.0 7.4 %collective-permute-start.9 = (bf16[384,128]{1,0:T(8,128)(2,1)S(1)}, bf16[384,128]{1,0:T(8,128)(2,1)S(1)}, u32[]{:S(2)}, u32[]{:S(2)}) collective-permute-start(bf16[384,128]{1,0:T(8,128)(2,1)S(1)} %get-tuple-element.53), channel_id=1, source_target_pairs={{0,28},{4,8},{8,4},{12,16},{16,12},{20,24},{24,20},{28,0},{1,29},{... | collective-permute-start | bytes 294920 | tf_op jit(solution)/shard_map/ppermute | solution.py:295
  18.2 1.8 %collective-permute-start = (bf16[256,768]{1,0:T(8,128)(2,1)S(1)}, bf16[256,768]{1,0:T(8,128)(2,1)S(1)}, u32[]{:S(2)}, u32[]{:S(2)}) collective-permute-start(bf16[256,768]{1,0:T(8,128)(2,1)S(1)} %get-tuple-element.25), channel_id=1, source_target_pairs={{0,1},{1,0},{2,3},{3,2},{4,5},{5,4},{6,7},{7,6},{8,9},{9,8},{10,11... | collective-permute-start | bytes 1179656 | tf_op jit(solution)/shard_map/cond/branch_1_fun/ppermute | solution.py:292
  20.5 1.1 %copy-start = (bf16[192,768]{1,0:T(8,128)(2,1)S(1)}, bf16[192,768]{1,0:T(8,128)(2,1)}, u32[]{:S(2)}) copy-start(bf16[192,768]{1,0:T(8,128)(2,1)} %own.1) | copy-start | bytes 884740
  21.8 7.1 %collective-permute-start.7 = (bf16[384,768]{1,0:T(8,128)(2,1)S(1)}, bf16[384,768]{1,0:T(8,128)(2,1)S(1)}, u32[]{:S(2)}, u32[]{:S(2)}) collective-permute-start(bf16[384,768]{1,0:T(8,128)(2,1)S(1)} %cross_output_both_rows.1.weights), channel_id=1, source_target_pairs={{0,1},{1,0},{2,3},{3,2},{4,5},{5,4},{6,7},{7,6},{8,9},{9,8},{10,11... | collective-permute-start | bytes 1769480 | tf_op jit(solution)/shard_map/ppermute | solution.py:292
  23.2 4.3 %collective-permute-start.10 = (bf16[5,48,128]{2,1,0:T(8,128)(2,1)S(1)}, bf16[5,48,128]{2,1,0:T(8,128)(2,1)S(1)}, u32[]{:S(2)}, u32[]{:S(2)}) collective-permute-start(bf16[5,48,128]{2,1,0:T(8,128)(2,1)S(1)} %get-tuple-element.55), channel_id=1, source_target_pairs={{0,2},{1,3},{2,0},{3,1},{4,6},{5,7},{6,4},{7,5},{8,10},{9,11},{10,... | collective-permute-start | bytes 184328 | tf_op jit(solution)/shard_map/ppermute | solution.py:292
  24.8 4.0 %collective-permute-start.11 = (bf16[5,48,128]{2,1,0:T(8,128)(2,1)S(1)}, bf16[5,48,128]{2,1,0:T(8,128)(2,1)S(1)}, u32[]{:S(2)}, u32[]{:S(2)}) collective-permute-start(bf16[5,48,128]{2,1,0:T(8,128)(2,1)S(1)} %get-tuple-element.56), channel_id=1, source_target_pairs={{0,3},{1,2},{2,1},{3,0},{4,7},{5,6},{6,5},{7,4},{8,11},{9,10},{10,... | collective-permute-start | bytes 184328 | tf_op jit(solution)/shard_map/ppermute | solution.py:292
  24.8 4.0 %collective-permute-start.12 = (bf16[5,48,128]{2,1,0:T(8,128)(2,1)S(1)}, bf16[5,48,128]{2,1,0:T(8,128)(2,1)S(1)}, u32[]{:S(2)}, u32[]{:S(2)}) collective-permute-start(bf16[5,48,128]{2,1,0:T(8,128)(2,1)S(1)} %get-tuple-element.57), channel_id=1, source_target_pairs={{0,1},{1,0},{2,3},{3,2},{4,5},{5,4},{6,7},{7,6},{8,9},{9,8},{10,11... | collective-permute-start | bytes 184328 | tf_op jit(solution)/shard_map/ppermute | solution.py:292

commit v15 on v14

--- a/solution.py
+++ b/solution.py
@@ -264,14 +264,17 @@
     terms = first[...] + nn(placed_rows((across_core, across_both), order, table), weights[...])
     first_n = table[2 * pair_n :, 0:1]
     zero = jnp.zeros((row_n, width), F32)
+    copies = []
     for position in range(pair_n):
         term = terms[position * row_n : (position + 1) * row_n]
         is_first = first_n > position
         out_v[0, position] = jnp.where(is_first, own_rows[0] + term, zero).astype(BF16)
         out_v[1, pair_n - 1 - position] = jnp.where(is_first, zero, own_rows[1] + term).astype(BF16)
-    copies = [pltpu.make_async_copy(out_v.at[image], out.at[image], sems.at[image]) for image in range(2)]
-    for copy in copies:
-        copy.start()
+        for image, slot in ((0, position), (1, pair_n - 1 - position)):
+            copies.append(
+                pltpu.make_async_copy(out_v.at[image, slot], out.at[image, slot], sems.at[image, slot])
+            )
+            copies[-1].start()
     for copy in copies:
         copy.wait()
 
@@ -340,9 +343,9 @@
     arrived = [exchange(value, swap) for value, swap in zip(outgoing, swaps)]
     context_got = across(context, chip_hop)
     near = (slot_n - 1) // 2
-    late = [at for at, (_, colour) in enumerate(swaps) if colour]
-    early = [at for at in range(pair_n) if at not in late]
-    short = [2 * near - 2, 2 * near - 1]
+    early = [2 * near - 2, 2 * near - 1]
+    late = [at for at in range(pair_n) if at not in early]
+    short = early
     cross_out_sent = call(
         "cross_output_rows",
         hand_on_kernel,
@@ -401,6 +404,14 @@
         [VMEM] * (2 + len(early)),
         [],
         queries, table, *[arrived[at] for at in early],
+    )
+    arrived[0] = call(
+        "half_way",
+        hand_on_kernel,
+        block,
+        [VMEM, ANY],
+        [],
+        arrived[0], early_sides,
         flops=EARLY_WEIGHT,
     )
     sides = call(
@@ -436,7 +447,7 @@
         functools.partial(out_kernel, order),
         shape((image_n, slot_n, row_n, width), BF16),
         [VMEM] * 6,
-        [pltpu.VMEM((image_n, slot_n, row_n, width), BF16), dma((image_n,))],
+        [pltpu.VMEM((image_n, slot_n, row_n, width), BF16), dma((image_n, slot_n))],
         own_rows, table, cross_out_core, first_terms, sides[chip_hop ^ core_hop], sides[core_hop],
         out_specs=HBM,
     )

time: 30.3 us -> 30.7 us (1.013)
  local copies, waits for them, and re-layouts: 0.02 us -> 0.95 us
  waiting for transfers between devices: 5.12 us -> 4.6 us
    unnamed x8, local copies, waits for them, and re-layouts: 0.02 us -> 0.95 us
    ppermute x5, waiting for transfers between devices: 0.44 us -> 0.01 us  [exchange(): lax.ppermute(value, 'owner', [(o, swap_target(o, swap, owner_n)) for o in...]
    pallas_call x10 -> x11, Pallas kernels: 7.77 us -> 7.78 us  [call(): pl.pallas_call(kernel, out_shape=out_shape, in_specs=in_specs, out_specs=...]
  transfers between devices with their start and end apart: 13 -> 13, of which waited for: 4 -> 3; matrix products, arithmetic and copies ran while one was open for 0% -> 0% of each run, Pallas kernels for 22% -> 21%
where the time goes in v15:
time: 30.7 us; the launch traced here: 30.5 us
  starting transfers between devices  17.1 us (56%)
  Pallas kernels  7.78 us (25%)
  waiting for transfers between devices  4.6 us (15%)
  local copies, waits for them, and re-layouts  0.95 us (3%)
    ppermute x5, starting transfers between devices, exchange(): lax.ppermute(value, 'owner', [(o, swap_target(o, swap, owner_n)) for o in...  9.5 us
    pallas_call x11, Pallas kernels, call(): pl.pallas_call(kernel, out_shape=out_shape, in_specs=in_specs, out_specs=...  7.78 us
    ppermute x8, starting transfers between devices, across(): return lax.ppermute(value, 'helper', [(j, j ^ k) for j in range(helper_n)])  7.58 us
    ppermute x8, waiting for transfers between devices, across(): return lax.ppermute(value, 'helper', [(j, j ^ k) for j in range(helper_n)])  4.59 us
    unnamed x8, local copies, waits for them, and re-layouts  0.95 us
  transfers between devices with their start and end apart: 13, of which 3 were waited for; matrix products, arithmetic and copies ran while one was open for 0% of the time, Pallas kernels for 21%

profile of v15, /device:TPU:0, one launch (start us, length us, event | category | flops | bytes accessed | tf_op | source)
XLA Modules:
  0.0 30.5 jit_solution(14884138230581789579)
XLA Ops:
  0.0 3.0 %collective-permute-start.2 = (bf16[192,768]{1,0:T(8,128)(2,1)}, bf16[192,768]{1,0:T(8,128)(2,1)S(1)}, u32[]{:S(2)}, u32[]{:S(2)}) collective-permute-start(bf16[192,768]{1,0:T(8,128)(2,1)} %param.12), channel_id=1, source_target_pairs={{0,2},{1,3},{2,0},{3,1},{4,6},{5,7},{6,4},{7,5},{8,10},{9,11},{10,... | collective-permute-start | bytes 884744 | tf_op jit(solution)/shard_map/ppermute | solution.py:295
  3.0 3.1 %own_images.1 = (bf16[384,128]{1,0:T(8,128)(2,1)S(1)}, bf16[384,128]{1,0:T(8,128)(2,1)S(1)}, bf16[384,128]{1,0:T(8,128)(2,1)S(1)}, bf16[384,128]{1,0:T(8,128)(2,...) custom-call(bf16[2,128,768]{2,1,0:T(8,128)(2,1)} %states.1, ...), custom_call_target="tpu_custom_call" | custom-call | flops 1 | bytes 1 | tf_op jit(solution)/shard_map/own_images/pallas_call | solution.py:302
  6.0 1.7 %collective-permute-start.3 = (bf16[384,128]{1,0:T(8,128)(2,1)S(1)}, bf16[384,128]{1,0:T(8,128)(2,1)S(1)}, u32[]{:S(2)}, u32[]{:S(2)}) collective-permute-start(bf16[384,128]{1,0:T(8,128)(2,1)S(1)} %get-tuple-element.44), channel_id=1, source_target_pairs={{0,8},{4,12},{8,0},{12,4},{16,24},{20,28},{24,16},{28,20},{1,9},{5... | collective-permute-start | bytes 294920 | tf_op jit(solution)/shard_map/ppermute | solution.py:298
  7.7 1.5 %collective-permute-start.4 = (bf16[384,128]{1,0:T(8,128)(2,1)S(1)}, bf16[384,128]{1,0:T(8,128)(2,1)S(1)}, u32[]{:S(2)}, u32[]{:S(2)}) collective-permute-start(bf16[384,128]{1,0:T(8,128)(2,1)S(1)} %get-tuple-element.45), channel_id=1, source_target_pairs={{0,4},{4,0},{8,12},{12,8},{16,20},{20,16},{24,28},{28,24},{1,5},{5... | collective-permute-start | bytes 294920 | tf_op jit(solution)/shard_map/ppermute | solution.py:298
  9.2 0.5 %collective-permute-start.1 = (bf16[384,128]{1,0:T(8,128)(2,1)S(1)}, bf16[384,128]{1,0:T(8,128)(2,1)S(1)}, u32[]{:S(2)}, u32[]{:S(2)}) collective-permute-start(bf16[384,128]{1,0:T(8,128)(2,1)S(1)} %get-tuple-element.43), channel_id=1, source_target_pairs={{0,2},{1,3},{2,0},{3,1},{4,6},{5,7},{6,4},{7,5},{8,10},{9,11},{10,... | collective-permute-start | bytes 294920 | tf_op jit(solution)/shard_map/ppermute | solution.py:295
  9.7 2.6 %collective-permute-start.7 = (bf16[384,128]{1,0:T(8,128)(2,1)S(1)}, bf16[384,128]{1,0:T(8,128)(2,1)S(1)}, u32[]{:S(2)}, u32[]{:S(2)}) collective-permute-start(bf16[384,128]{1,0:T(8,128)(2,1)S(1)} %get-tuple-element.51), channel_id=1, source_target_pairs={{0,16},{4,20},{8,24},{12,28},{16,0},{20,4},{24,8},{28,12},{1,17},{... | collective-permute-start | bytes 294920 | tf_op jit(solution)/shard_map/ppermute | solution.py:298
  12.3 0.0 copy-start.1
  12.3 0.0 copy-start.2
  12.3 1.6 %collective-permute-start.5 = (bf16[192,768]{1,0:T(8,128)(2,1)S(1)}, bf16[192,768]{1,0:T(8,128)(2,1)S(1)}, u32[]{:S(2)}, u32[]{:S(2)}) collective-permute-start(bf16[192,768]{1,0:T(8,128)(2,1)S(1)} %cross_output_rows.1), channel_id=1, source_target_pairs={{0,2},{1,3},{2,0},{3,1},{4,6},{5,7},{6,4},{7,5},{8,10},{9,11},{10,... | collective-permute-start | bytes 884744 | tf_op jit(solution)/shard_map/ppermute | solution.py:295
  13.9 0.0 collective-permute-done.4.rest_1_
  13.9 1.0 %collective-permute-start.8 = (bf16[384,128]{1,0:T(8,128)(2,1)S(1)}, bf16[384,128]{1,0:T(8,128)(2,1)S(1)}, u32[]{:S(2)}, u32[]{:S(2)}) collective-permute-start(bf16[384,128]{1,0:T(8,128)(2,1)S(1)} %get-tuple-element.52), channel_id=1, source_target_pairs={{0,24},{4,28},{8,16},{12,20},{16,8},{20,12},{24,0},{28,4},{1,25},{... | collective-permute-start | bytes 294920 | tf_op jit(solution)/shard_map/ppermute | solution.py:298
  15.0 0.0 collective-permute-done.2.rest_2_
  15.0 2.8 %collective-permute-start.9 = (bf16[384,128]{1,0:T(8,128)(2,1)S(1)}, bf16[384,128]{1,0:T(8,128)(2,1)S(1)}, u32[]{:S(2)}, u32[]{:S(2)}) collective-permute-start(bf16[384,128]{1,0:T(8,128)(2,1)S(1)} %get-tuple-element.53), channel_id=1, source_target_pairs={{0,28},{4,8},{8,4},{12,16},{16,12},{20,24},{24,20},{28,0},{1,29},{... | collective-permute-start | bytes 294920 | tf_op jit(solution)/shard_map/ppermute | solution.py:298
  17.7 0.0 collective-permute-done.1
  17.7 2.8 %conditional.1 = ((f32[2,32,768]{2,1,0:T(8,128)S(1)}, bf16[2,128,192]{2,1,0:T(8,128)(2,1)S(1)})) conditional(s32[]{:T(128)} %convert_element_type.3, () %tuple.12, (bf16[2,128,768]{2,1,0:T(8,128)(2,1)S(1)}, bf16[384,128]{1,0:T(8,128)(2,1)S(1)}, bf16[384,128]{1,0:T(8,128)(2,1)S(1)}, bf16[192,768]{1,0:T(8,128)(2,1)S(1)}, ...), branch_computations={%region_0.0_spmd, %region_1.0_spmd} | conditional | flops 2 | bytes 1572914 | solution.py:395
  17.8 0.4 %self_output_share.1 = (f32[256,768]{1,0:T(8,128)S(1)}, bf16[256,768]{1,0:T(8,128)(2,1)S(1)}) custom-call(bf16[2,128,768]{2,1,0:T(8,128)(2,1)S(1)} %get-tuple-element.19.states, bf16[384,128]{1,0:T(8,128)(2,1)S(1)} %get-tuple-element.20.own, bf16[384,128]{1,0:T(8,128)(2,1)S(1)} %get-tuple-element.21.got, bf16[192,768]{1,0:T(8,128)(2,1)S(1)} %get-tuple-element.22.own_weight, ...), custom_call_target="tpu_custom_call" | custom-call | flops 1 | bytes 1 | tf_op jit(solution)/shard_map/cond/branch_1_fun/self_output_share/pallas_call | solution.py:302
  18.2 0.1 collective-permute-start
  18.3 1.7 %collective-permute-done.got = bf16[256,768]{1,0:T(8,128)(2,1)S(1)} collective-permute-done((bf16[256,768]{1,0:T(8,128)(2,1)S(1)}, bf16[256,768]{1,0:T(8,128)(2,1)S(1)}, u32[]{:S(2)}, u32[]{:S(2)}) %collective-permute-start) | collective-permute-done | bytes 393248 | tf_op jit(solution)/shard_map/cond/branch_1_fun/ppermute | solution.py:295
  20.0 0.5 %mixed_and_queries.1 = (f32[2,32,768]{2,1,0:T(8,128)S(1)}, bf16[2,128,192]{2,1,0:T(8,128)(2,1)S(1)}) custom-call(f32[256,768]{1,0:T(8,128)S(1)} %get-tuple-element.24.base, bf16[256,768]{1,0:T(8,128)(2,1)S(1)} %collective-permute-done.got, f32[3,768]{1,0:T(4,128)S(1)} %get-tuple-element.26.gains, bf16[192,768]{1,0:T(8,128)(2,1)S(1)} %get-tuple-element.27.weight), custom_call_target="tpu_custom_call" | custom-call | flops 1 | bytes 1 | tf_op jit(solution)/shard_map/cond/branch_1_fun/mixed_and_queries/pallas_call | solution.py:302
  20.5 0.8 %early_cross_attention.1.waited.rest_0_.before = bf16[4,2,48,128]{3,2,1,0:T(8,128)(2,1)S(1)} custom-call(bf16[2,128,192]{2,1,0:T(8,128)(2,1)S(1)} %get-tuple-element.50.queries, s32[11,128]{1,0:T(8,128)S(1)} %get-tuple-element.48.table, bf16[384,128]{1,0:T(8,128)(2,1)S(1)} %collective-permute-done.3.rest_0_, bf16[384,128]{1,0:T(8,128)(2,1)S(1)} %collective-permute-done.4.rest_1_), custom_call_target="tpu_custom_call" | custom-call | flops 1 | bytes 1 | tf_op jit(solution)/shard_map/early_cross_attention/pallas_call | solution.py:302
  21.4 0.0 collective-permute-done.7.value
  21.4 0.9 %copy-done = bf16[192,768]{1,0:T(8,128)(2,1)S(1)} copy-done((bf16[192,768]{1,0:T(8,128)(2,1)S(1)}, bf16[192,768]{1,0:T(8,128)(2,1)}, u32[]{:S(2)}) %copy-start) | copy-done | bytes 294936
  22.3 0.1 cross_output_both_rows.1.weights
  22.5 0.2 collective-permute-start.6
  22.7 1.1 %late_cross_attention.1 = (bf16[5,48,128]{2,1,0:T(8,128)(2,1)S(1)}, bf16[5,48,128]{2,1,0:T(8,128)(2,1)S(1)}, bf16[5,48,128]{2,1,0:T(8,128)(2,1)S(1)}, bf16[5,48,128]{2,1,0:T(8,128)(2,1)S(1)}) custom-call(bf16[2,128,192]{2,1,0:T(8,128)(2,1)S(1)} %get-tuple-element.50.queries, s32[11,128]{1,0:T(8,128)S(1)} %get-tuple-element.48.table, ...), custom_call_target="tpu_custom_call" | custom-call | flops 99999997952 | bytes 1 | tf_op jit(solution)/shard_map/late_cross_attention/pallas_call | solution.py:302
  23.7 1.3 %collective-permute-start.10 = (bf16[5,48,128]{2,1,0:T(8,128)(2,1)S(1)}, bf16[5,48,128]{2,1,0:T(8,128)(2,1)S(1)}, u32[]{:S(2)}, u32[]{:S(2)}) collective-permute-start(bf16[5,48,128]{2,1,0:T(8,128)(2,1)S(1)} %get-tuple-element.55), channel_id=1, source_target_pairs={{0,2},{1,3},{2,0},{3,1},{4,6},{5,7},{6,4},{7,5},{8,10},{9,11},{10,... | collective-permute-start | bytes 184328 | tf_op jit(solution)/shard_map/ppermute | solution.py:295
  25.0 0.5 %collective-permute-start.11 = (bf16[5,48,128]{2,1,0:T(8,128)(2,1)S(1)}, bf16[5,48,128]{2,1,0:T(8,128)(2,1)S(1)}, u32[]{:S(2)}, u32[]{:S(2)}) collective-permute-start(bf16[5,48,128]{2,1,0:T(8,128)(2,1)S(1)} %get-tuple-element.56), channel_id=1, source_target_pairs={{0,3},{1,2},{2,1},{3,0},{4,7},{5,6},{6,5},{7,4},{8,11},{9,10},{10,... | collective-permute-start | bytes 184328 | tf_op jit(solution)/shard_map/ppermute | solution.py:295
  25.5 0.4 %collective-permute-start.12 = (bf16[5,48,128]{2,1,0:T(8,128)(2,1)S(1)}, bf16[5,48,128]{2,1,0:T(8,128)(2,1)S(1)}, u32[]{:S(2)}, u32[]{:S(2)}) collective-permute-start(bf16[5,48,128]{2,1,0:T(8,128)(2,1)S(1)} %get-tuple-element.57), channel_id=1, source_target_pairs={{0,1},{1,0},{2,3},{3,2},{4,5},{5,4},{6,7},{7,6},{8,9},{9,8},{10,11... | collective-permute-start | bytes 184328 | tf_op jit(solution)/shard_map/ppermute | solution.py:295
  26.0 2.3 %collective-permute-done.10.across_chip = bf16[5,48,128]{2,1,0:T(8,128)(2,1)S(1)} collective-permute-done((bf16[5,48,128]{2,1,0:T(8,128)(2,1)S(1)}, bf16[5,48,128]{2,1,0:T(8,128)(2,1)S(1)}, u32[]{:S(2)}, u32[]{:S(2)}) %collective-permute-start.10) | collective-permute-done | bytes 61472 | tf_op jit(solution)/shard_map/ppermute | solution.py:295
  28.2 0.4 %first_terms.1.first = f32[160,768]{1,0:T(8,128)S(1)} custom-call(s32[11,128]{1,0:T(8,128)S(1)} %get-tuple-element.48.table, bf16[384,768]{1,0:T(8,128)(2,1)S(1)} %cross_output_both_rows.1.weights, bf16[5,48,128]{2,1,0:T(8,128)(2,1)S(1)} %get-tuple-element.54.own, bf16[5,48,128]{2,1,0:T(8,128)(2,1)S(1)} %collective-permute-done.10.across_chip), custom_call_target="tpu_custom_call" | custom-call | flops 1 | bytes 1 | tf_op jit(solution)/shard_map/first_terms/pallas_call | solution.py:302
  28.7 0.6 %collective-permute-done.11.across_both = bf16[5,48,128]{2,1,0:T(8,128)(2,1)S(1)} collective-permute-done((bf16[5,48,128]{2,1,0:T(8,128)(2,1)S(1)}, bf16[5,48,128]{2,1,0:T(8,128)(2,1)S(1)}, u32[]{:S(2)}, u32[]{:S(2)}) %collective-permute-start.11) | collective-permute-done | bytes 61472 | tf_op jit(solution)/shard_map/ppermute | solution.py:295
  29.3 1.3 %pair_output.1 = bf16[2,5,32,768]{3,2,1,0:T(8,128)(2,1)} custom-call(f32[2,32,768]{2,1,0:T(8,128)S(1)} %get-tuple-element.47.own_rows, s32[11,128]{1,0:T(8,128)S(1)} %get-tuple-element.48.table, bf16[384,768]{1,0:T(8,128)(2,1)S(1)} %collective-permute-done.6.weights, f32[160,768]{1,0:T(8,128)S(1)} %first_terms.1.first, ...), custom_call_target="tpu_custom_call" | custom-call | flops 1 | bytes 1 | tf_op jit(solution)/shard_map/pair_output/pallas_call | solution.py:302
  (14 shorter events, 0.1 us)
Async XLA Ops:
  0.0 15.0 %collective-permute-start.2 = (bf16[192,768]{1,0:T(8,128)(2,1)}, bf16[192,768]{1,0:T(8,128)(2,1)S(1)}, u32[]{:S(2)}, u32[]{:S(2)}) collective-permute-start(bf16[192,768]{1,0:T(8,128)(2,1)} %param.12), channel_id=1, source_target_pairs={{0,2},{1,3},{2,0},{3,1},{4,6},{5,7},{6,4},{7,5},{8,10},{9,11},{10,... | collective-permute-start | bytes 884744 | tf_op jit(solution)/shard_map/ppermute | solution.py:295
  6.0 6.2 %collective-permute-start.3 = (bf16[384,128]{1,0:T(8,128)(2,1)S(1)}, bf16[384,128]{1,0:T(8,128)(2,1)S(1)}, u32[]{:S(2)}, u32[]{:S(2)}) collective-permute-start(bf16[384,128]{1,0:T(8,128)(2,1)S(1)} %get-tuple-element.44), channel_id=1, source_target_pairs={{0,8},{4,12},{8,0},{12,4},{16,24},{20,28},{24,16},{28,20},{1,9},{5... | collective-permute-start | bytes 294920 | tf_op jit(solution)/shard_map/ppermute | solution.py:298
  7.7 6.2 %collective-permute-start.4 = (bf16[384,128]{1,0:T(8,128)(2,1)S(1)}, bf16[384,128]{1,0:T(8,128)(2,1)S(1)}, u32[]{:S(2)}, u32[]{:S(2)}) collective-permute-start(bf16[384,128]{1,0:T(8,128)(2,1)S(1)} %get-tuple-element.45), channel_id=1, source_target_pairs={{0,4},{4,0},{8,12},{12,8},{16,20},{20,16},{24,28},{28,24},{1,5},{5... | collective-permute-start | bytes 294920 | tf_op jit(solution)/shard_map/ppermute | solution.py:298
  9.2 8.6 %collective-permute-start.1 = (bf16[384,128]{1,0:T(8,128)(2,1)S(1)}, bf16[384,128]{1,0:T(8,128)(2,1)S(1)}, u32[]{:S(2)}, u32[]{:S(2)}) collective-permute-start(bf16[384,128]{1,0:T(8,128)(2,1)S(1)} %get-tuple-element.43), channel_id=1, source_target_pairs={{0,2},{1,3},{2,0},{3,1},{4,6},{5,7},{6,4},{7,5},{8,10},{9,11},{10,... | collective-permute-start | bytes 294920 | tf_op jit(solution)/shard_map/ppermute | solution.py:295
  9.7 11.7 %collective-permute-start.7 = (bf16[384,128]{1,0:T(8,128)(2,1)S(1)}, bf16[384,128]{1,0:T(8,128)(2,1)S(1)}, u32[]{:S(2)}, u32[]{:S(2)}) collective-permute-start(bf16[384,128]{1,0:T(8,128)(2,1)S(1)} %get-tuple-element.51), channel_id=1, source_target_pairs={{0,16},{4,20},{8,24},{12,28},{16,0},{20,4},{24,8},{28,12},{1,17},{... | collective-permute-start | bytes 294920 | tf_op jit(solution)/shard_map/ppermute | solution.py:298
  12.3 5.5 %copy-start.3 = (bf16[192,768]{1,0:T(8,128)(2,1)S(1)}, bf16[192,768]{1,0:T(8,128)(2,1)}, u32[]{:S(2)}) copy-start(bf16[192,768]{1,0:T(8,128)(2,1)} %param.12) | copy-start | bytes 884740
  12.3 5.4 %copy-start.1 = (f32[3,768]{1,0:T(4,128)S(1)}, f32[3,768]{1,0:T(4,128)}, u32[]{:S(2)}) copy-start(f32[3,768]{1,0:T(4,128)} %value.1) | copy-start | bytes 27652
  12.3 5.4 %copy-start.2 = (bf16[2,128,768]{2,1,0:T(8,128)(2,1)S(1)}, bf16[2,128,768]{2,1,0:T(8,128)(2,1)}, u32[]{:S(2)}) copy-start(bf16[2,128,768]{2,1,0:T(8,128)(2,1)} %states.1) | copy-start | bytes 1179652
  12.3 9.1 %collective-permute-start.5 = (bf16[192,768]{1,0:T(8,128)(2,1)S(1)}, bf16[192,768]{1,0:T(8,128)(2,1)S(1)}, u32[]{:S(2)}, u32[]{:S(2)}) collective-permute-start(bf16[192,768]{1,0:T(8,128)(2,1)S(1)} %cross_output_rows.1), channel_id=1, source_target_pairs={{0,2},{1,3},{2,0},{3,1},{4,6},{5,7},{6,4},{7,5},{8,10},{9,11},{10,... | collective-permute-start | bytes 884744 | tf_op jit(solution)/shard_map/ppermute | solution.py:295
  13.9 8.8 %collective-permute-start.8 = (bf16[384,128]{1,0:T(8,128)(2,1)S(1)}, bf16[384,128]{1,0:T(8,128)(2,1)S(1)}, u32[]{:S(2)}, u32[]{:S(2)}) collective-permute-start(bf16[384,128]{1,0:T(8,128)(2,1)S(1)} %get-tuple-element.52), channel_id=1, source_target_pairs={{0,24},{4,28},{8,16},{12,20},{16,8},{20,12},{24,0},{28,4},{1,25},{... | collective-permute-start | bytes 294920 | tf_op jit(solution)/shard_map/ppermute | solution.py:298
  15.0 7.7 %collective-permute-start.9 = (bf16[384,128]{1,0:T(8,128)(2,1)S(1)}, bf16[384,128]{1,0:T(8,128)(2,1)S(1)}, u32[]{:S(2)}, u32[]{:S(2)}) collective-permute-start(bf16[384,128]{1,0:T(8,128)(2,1)S(1)} %get-tuple-element.53), channel_id=1, source_target_pairs={{0,28},{4,8},{8,4},{12,16},{16,12},{20,24},{24,20},{28,0},{1,29},{... | collective-permute-start | bytes 294920 | tf_op jit(solution)/shard_map/ppermute | solution.py:298
  18.2 1.8 %collective-permute-start = (bf16[256,768]{1,0:T(8,128)(2,1)S(1)}, bf16[256,768]{1,0:T(8,128)(2,1)S(1)}, u32[]{:S(2)}, u32[]{:S(2)}) collective-permute-start(bf16[256,768]{1,0:T(8,128)(2,1)S(1)} %get-tuple-element.25), channel_id=1, source_target_pairs={{0,1},{1,0},{2,3},{3,2},{4,5},{5,4},{6,7},{7,6},{8,9},{9,8},{10,11... | collective-permute-start | bytes 1179656 | tf_op jit(solution)/shard_map/cond/branch_1_fun/ppermute | solution.py:295
  21.4 1.0 %copy-start = (bf16[192,768]{1,0:T(8,128)(2,1)S(1)}, bf16[192,768]{1,0:T(8,128)(2,1)}, u32[]{:S(2)}) copy-start(bf16[192,768]{1,0:T(8,128)(2,1)} %own.1) | copy-start | bytes 884740
  22.5 6.8 %collective-permute-start.6 = (bf16[384,768]{1,0:T(8,128)(2,1)S(1)}, bf16[384,768]{1,0:T(8,128)(2,1)S(1)}, u32[]{:S(2)}, u32[]{:S(2)}) collective-permute-start(bf16[384,768]{1,0:T(8,128)(2,1)S(1)} %cross_output_both_rows.1.weights), channel_id=1, source_target_pairs={{0,1},{1,0},{2,3},{3,2},{4,5},{5,4},{6,7},{7,6},{8,9},{9,8},{10,11... | collective-permute-start | bytes 1769480 | tf_op jit(solution)/shard_map/ppermute | solution.py:295
  23.7 4.5 %collective-permute-start.10 = (bf16[5,48,128]{2,1,0:T(8,128)(2,1)S(1)}, bf16[5,48,128]{2,1,0:T(8,128)(2,1)S(1)}, u32[]{:S(2)}, u32[]{:S(2)}) collective-permute-start(bf16[5,48,128]{2,1,0:T(8,128)(2,1)S(1)} %get-tuple-element.55), channel_id=1, source_target_pairs={{0,2},{1,3},{2,0},{3,1},{4,6},{5,7},{6,4},{7,5},{8,10},{9,11},{10,... | collective-permute-start | bytes 184328 | tf_op jit(solution)/shard_map/ppermute | solution.py:295
  25.0 4.2 %collective-permute-start.11 = (bf16[5,48,128]{2,1,0:T(8,128)(2,1)S(1)}, bf16[5,48,128]{2,1,0:T(8,128)(2,1)S(1)}, u32[]{:S(2)}, u32[]{:S(2)}) collective-permute-start(bf16[5,48,128]{2,1,0:T(8,128)(2,1)S(1)} %get-tuple-element.56), channel_id=1, source_target_pairs={{0,3},{1,2},{2,1},{3,0},{4,7},{5,6},{6,5},{7,4},{8,11},{9,10},{10,... | collective-permute-start | bytes 184328 | tf_op jit(solution)/shard_map/ppermute | solution.py:295
  25.5 3.7 %collective-permute-start.12 = (bf16[5,48,128]{2,1,0:T(8,128)(2,1)S(1)}, bf16[5,48,128]{2,1,0:T(8,128)(2,1)S(1)}, u32[]{:S(2)}, u32[]{:S(2)}) collective-permute-start(bf16[5,48,128]{2,1,0:T(8,128)(2,1)S(1)} %get-tuple-element.57), channel_id=1, source_target_pairs={{0,1},{1,0},{2,3},{3,2},{4,5},{5,4},{6,7},{7,6},{8,9},{9,8},{10,11... | collective-permute-start | bytes 184328 | tf_op jit(solution)/shard_map/ppermute | solution.py:295

commit v16 on v15

--- a/solution.py
+++ b/solution.py
@@ -430,7 +430,7 @@
         shape((2 * columns, width), BF16),
         [VMEM, ANY, ANY],
         [dma((2,))],
-        cross_out, cross_out_got, early_sides,
+        cross_out_sent, cross_out_got, early_sides,
     )
     cross_out_core = across(cross_out_both, core_hop)
     order = early + late

time: 30.7 us -> 30.5 us (level)
  local copies, waits for them, and re-layouts: 0.95 us -> 0.02 us
  waiting for transfers between devices: 4.6 us -> 5.32 us
    unnamed x8 -> x6, local copies, waits for them, and re-layouts: 0.95 us -> 0.02 us
    ppermute x5, waiting for transfers between devices: 0.01 us -> 0.63 us  [exchange(): lax.ppermute(value, 'owner', [(o, swap_target(o, swap, owner_n)) for o in...]
  transfers between devices with their start and end apart: 13 -> 13, of which waited for: 3 -> 4; matrix products, arithmetic and copies ran while one was open for 0% -> 0% of each run, Pallas kernels for 21% -> 21%
where the time goes in v16:
time: 30.5 us; the launch traced here: 30.3 us
  starting transfers between devices  17.1 us (56%)
  Pallas kernels  7.78 us (26%)
  waiting for transfers between devices  5.32 us (17%)
    ppermute x5, starting transfers between devices, exchange(): lax.ppermute(value, 'owner', [(o, swap_target(o, swap, owner_n)) for o in...  9.53 us
    pallas_call x11, Pallas kernels, call(): pl.pallas_call(kernel, out_shape=out_shape, in_specs=in_specs, out_specs=...  7.78 us
    ppermute x8, starting transfers between devices, across(): return lax.ppermute(value, 'helper', [(j, j ^ k) for j in range(helper_n)])  7.55 us
    ppermute x8, waiting for transfers between devices, across(): return lax.ppermute(value, 'helper', [(j, j ^ k) for j in range(helper_n)])  4.69 us
    ppermute x5, waiting for transfers between devices, exchange(): lax.ppermute(value, 'owner', [(o, swap_target(o, swap, owner_n)) for o in...  0.63 us
  transfers between devices with their start and end apart: 13, of which 4 were waited for; matrix products, arithmetic and copies ran while one was open for 0% of the time, Pallas kernels for 21%

profile of v16, /device:TPU:0, one launch (start us, length us, event | category | flops | bytes accessed | tf_op | source)
XLA Modules:
  0.0 30.3 jit_solution(5423129986024623583)
XLA Ops:
  0.0 3.0 %collective-permute-start.2 = (bf16[192,768]{1,0:T(8,128)(2,1)}, bf16[192,768]{1,0:T(8,128)(2,1)S(1)}, u32[]{:S(2)}, u32[]{:S(2)}) collective-permute-start(bf16[192,768]{1,0:T(8,128)(2,1)} %param.12), channel_id=1, source_target_pairs={{0,2},{1,3},{2,0},{3,1},{4,6},{5,7},{6,4},{7,5},{8,10},{9,11},{10,... | collective-permute-start | bytes 884744 | tf_op jit(solution)/shard_map/ppermute | solution.py:295
  3.0 3.1 %own_images.1 = (bf16[384,128]{1,0:T(8,128)(2,1)S(1)}, bf16[384,128]{1,0:T(8,128)(2,1)S(1)}, bf16[384,128]{1,0:T(8,128)(2,1)S(1)}, bf16[384,128]{1,0:T(8,128)(2,...) custom-call(bf16[2,128,768]{2,1,0:T(8,128)(2,1)} %states.1, ...), custom_call_target="tpu_custom_call" | custom-call | flops 1 | bytes 1 | tf_op jit(solution)/shard_map/own_images/pallas_call | solution.py:302
  6.0 1.7 %collective-permute-start.3 = (bf16[384,128]{1,0:T(8,128)(2,1)S(1)}, bf16[384,128]{1,0:T(8,128)(2,1)S(1)}, u32[]{:S(2)}, u32[]{:S(2)}) collective-permute-start(bf16[384,128]{1,0:T(8,128)(2,1)S(1)} %get-tuple-element.44), channel_id=1, source_target_pairs={{0,8},{4,12},{8,0},{12,4},{16,24},{20,28},{24,16},{28,20},{1,9},{5... | collective-permute-start | bytes 294920 | tf_op jit(solution)/shard_map/ppermute | solution.py:298
  7.7 1.5 %collective-permute-start.4 = (bf16[384,128]{1,0:T(8,128)(2,1)S(1)}, bf16[384,128]{1,0:T(8,128)(2,1)S(1)}, u32[]{:S(2)}, u32[]{:S(2)}) collective-permute-start(bf16[384,128]{1,0:T(8,128)(2,1)S(1)} %get-tuple-element.45), channel_id=1, source_target_pairs={{0,4},{4,0},{8,12},{12,8},{16,20},{20,16},{24,28},{28,24},{1,5},{5... | collective-permute-start | bytes 294920 | tf_op jit(solution)/shard_map/ppermute | solution.py:298
  9.2 0.5 %collective-permute-start.1 = (bf16[384,128]{1,0:T(8,128)(2,1)S(1)}, bf16[384,128]{1,0:T(8,128)(2,1)S(1)}, u32[]{:S(2)}, u32[]{:S(2)}) collective-permute-start(bf16[384,128]{1,0:T(8,128)(2,1)S(1)} %get-tuple-element.43), channel_id=1, source_target_pairs={{0,2},{1,3},{2,0},{3,1},{4,6},{5,7},{6,4},{7,5},{8,10},{9,11},{10,... | collective-permute-start | bytes 294920 | tf_op jit(solution)/shard_map/ppermute | solution.py:295
  9.7 2.6 %collective-permute-start.7 = (bf16[384,128]{1,0:T(8,128)(2,1)S(1)}, bf16[384,128]{1,0:T(8,128)(2,1)S(1)}, u32[]{:S(2)}, u32[]{:S(2)}) collective-permute-start(bf16[384,128]{1,0:T(8,128)(2,1)S(1)} %get-tuple-element.51), channel_id=1, source_target_pairs={{0,16},{4,20},{8,24},{12,28},{16,0},{20,4},{24,8},{28,12},{1,17},{... | collective-permute-start | bytes 294920 | tf_op jit(solution)/shard_map/ppermute | solution.py:298
  12.3 0.0 copy-start
  12.3 0.0 copy-start.1
  12.3 1.6 %collective-permute-start.5 = (bf16[192,768]{1,0:T(8,128)(2,1)S(1)}, bf16[192,768]{1,0:T(8,128)(2,1)S(1)}, u32[]{:S(2)}, u32[]{:S(2)}) collective-permute-start(bf16[192,768]{1,0:T(8,128)(2,1)S(1)} %cross_output_rows.1.own), channel_id=1, source_target_pairs={{0,2},{1,3},{2,0},{3,1},{4,6},{5,7},{6,4},{7,5},{8,10},{9,11},{10,... | collective-permute-start | bytes 884744 | tf_op jit(solution)/shard_map/ppermute | solution.py:295
  13.9 1.0 %collective-permute-start.8 = (bf16[384,128]{1,0:T(8,128)(2,1)S(1)}, bf16[384,128]{1,0:T(8,128)(2,1)S(1)}, u32[]{:S(2)}, u32[]{:S(2)}) collective-permute-start(bf16[384,128]{1,0:T(8,128)(2,1)S(1)} %get-tuple-element.52), channel_id=1, source_target_pairs={{0,24},{4,28},{8,16},{12,20},{16,8},{20,12},{24,0},{28,4},{1,25},{... | collective-permute-start | bytes 294920 | tf_op jit(solution)/shard_map/ppermute | solution.py:298
  15.0 0.0 collective-permute-done.2.rest_2_
  15.0 2.8 %collective-permute-start.9 = (bf16[384,128]{1,0:T(8,128)(2,1)S(1)}, bf16[384,128]{1,0:T(8,128)(2,1)S(1)}, u32[]{:S(2)}, u32[]{:S(2)}) collective-permute-start(bf16[384,128]{1,0:T(8,128)(2,1)S(1)} %get-tuple-element.53), channel_id=1, source_target_pairs={{0,28},{4,8},{8,4},{12,16},{16,12},{20,24},{24,20},{28,0},{1,29},{... | collective-permute-start | bytes 294920 | tf_op jit(solution)/shard_map/ppermute | solution.py:298
  17.8 2.8 %conditional.1 = ((f32[2,32,768]{2,1,0:T(8,128)S(1)}, bf16[2,128,192]{2,1,0:T(8,128)(2,1)S(1)})) conditional(s32[]{:T(128)} %convert_element_type.3, () %tuple.12, (bf16[2,128,768]{2,1,0:T(8,128)(2,1)S(1)}, bf16[384,128]{1,0:T(8,128)(2,1)S(1)}, bf16[384,128]{1,0:T(8,128)(2,1)S(1)}, bf16[192,768]{1,0:T(8,128)(2,1)S(1)}, ...), branch_computations={%region_0.0_spmd, %region_1.0_spmd} | conditional | flops 2 | bytes 1572914 | solution.py:395
  17.8 0.4 %self_output_share.1 = (f32[256,768]{1,0:T(8,128)S(1)}, bf16[256,768]{1,0:T(8,128)(2,1)S(1)}) custom-call(bf16[2,128,768]{2,1,0:T(8,128)(2,1)S(1)} %get-tuple-element.19.states, bf16[384,128]{1,0:T(8,128)(2,1)S(1)} %get-tuple-element.20.own, bf16[384,128]{1,0:T(8,128)(2,1)S(1)} %get-tuple-element.21.got, bf16[192,768]{1,0:T(8,128)(2,1)S(1)} %get-tuple-element.22.own_weight, ...), custom_call_target="tpu_custom_call" | custom-call | flops 1 | bytes 1 | tf_op jit(solution)/shard_map/cond/branch_1_fun/self_output_share/pallas_call | solution.py:302
  18.2 0.1 collective-permute-start
  18.3 1.7 %collective-permute-done.got = bf16[256,768]{1,0:T(8,128)(2,1)S(1)} collective-permute-done((bf16[256,768]{1,0:T(8,128)(2,1)S(1)}, bf16[256,768]{1,0:T(8,128)(2,1)S(1)}, u32[]{:S(2)}, u32[]{:S(2)}) %collective-permute-start) | collective-permute-done | bytes 393248 | tf_op jit(solution)/shard_map/cond/branch_1_fun/ppermute | solution.py:295
  20.0 0.5 %mixed_and_queries.1 = (f32[2,32,768]{2,1,0:T(8,128)S(1)}, bf16[2,128,192]{2,1,0:T(8,128)(2,1)S(1)}) custom-call(f32[256,768]{1,0:T(8,128)S(1)} %get-tuple-element.24.base, bf16[256,768]{1,0:T(8,128)(2,1)S(1)} %collective-permute-done.got, f32[3,768]{1,0:T(4,128)S(1)} %get-tuple-element.26.gains, bf16[192,768]{1,0:T(8,128)(2,1)S(1)} %get-tuple-element.27.weight), custom_call_target="tpu_custom_call" | custom-call | flops 1 | bytes 1 | tf_op jit(solution)/shard_map/cond/branch_1_fun/mixed_and_queries/pallas_call | solution.py:302
  20.5 0.8 %early_cross_attention.1.waited.rest_0_.before = bf16[4,2,48,128]{3,2,1,0:T(8,128)(2,1)S(1)} custom-call(bf16[2,128,192]{2,1,0:T(8,128)(2,1)S(1)} %get-tuple-element.50.queries, s32[11,128]{1,0:T(8,128)S(1)} %get-tuple-element.48.table, bf16[384,128]{1,0:T(8,128)(2,1)S(1)} %collective-permute-done.3.rest_0_, bf16[384,128]{1,0:T(8,128)(2,1)S(1)} %collective-permute-done.4.rest_1_), custom_call_target="tpu_custom_call" | custom-call | flops 1 | bytes 1 | tf_op jit(solution)/shard_map/early_cross_attention/pallas_call | solution.py:302
  21.4 0.0 collective-permute-done.7.value
  21.4 0.0 collective-permute-done.5.got
  21.4 0.1 cross_output_both_rows.1.weights
  21.6 0.2 collective-permute-start.6
  21.8 0.0 collective-permute-done.8.rest_1_
  21.8 0.6 %collective-permute-done.9.rest_2_ = bf16[384,128]{1,0:T(8,128)(2,1)S(1)} collective-permute-done((bf16[384,128]{1,0:T(8,128)(2,1)S(1)}, bf16[384,128]{1,0:T(8,128)(2,1)S(1)}, u32[]{:S(2)}, u32[]{:S(2)}) %collective-permute-start.9) | collective-permute-done | bytes 98336 | tf_op jit(solution)/shard_map/ppermute | solution.py:298
  22.4 1.1 %late_cross_attention.1 = (bf16[5,48,128]{2,1,0:T(8,128)(2,1)S(1)}, bf16[5,48,128]{2,1,0:T(8,128)(2,1)S(1)}, bf16[5,48,128]{2,1,0:T(8,128)(2,1)S(1)}, bf16[5,48,128]{2,1,0:T(8,128)(2,1)S(1)}) custom-call(bf16[2,128,192]{2,1,0:T(8,128)(2,1)S(1)} %get-tuple-element.50.queries, s32[11,128]{1,0:T(8,128)S(1)} %get-tuple-element.48.table, ...), custom_call_target="tpu_custom_call" | custom-call | flops 99999997952 | bytes 1 | tf_op jit(solution)/shard_map/late_cross_attention/pallas_call | solution.py:302
  23.4 1.6 %collective-permute-start.10 = (bf16[5,48,128]{2,1,0:T(8,128)(2,1)S(1)}, bf16[5,48,128]{2,1,0:T(8,128)(2,1)S(1)}, u32[]{:S(2)}, u32[]{:S(2)}) collective-permute-start(bf16[5,48,128]{2,1,0:T(8,128)(2,1)S(1)} %get-tuple-element.55), channel_id=1, source_target_pairs={{0,2},{1,3},{2,0},{3,1},{4,6},{5,7},{6,4},{7,5},{8,10},{9,11},{10,... | collective-permute-start | bytes 184328 | tf_op jit(solution)/shard_map/ppermute | solution.py:295
  25.0 0.6 %collective-permute-start.12 = (bf16[5,48,128]{2,1,0:T(8,128)(2,1)S(1)}, bf16[5,48,128]{2,1,0:T(8,128)(2,1)S(1)}, u32[]{:S(2)}, u32[]{:S(2)}) collective-permute-start(bf16[5,48,128]{2,1,0:T(8,128)(2,1)S(1)} %get-tuple-element.57), channel_id=1, source_target_pairs={{0,1},{1,0},{2,3},{3,2},{4,5},{5,4},{6,7},{7,6},{8,9},{9,8},{10,11... | collective-permute-start | bytes 184328 | tf_op jit(solution)/shard_map/ppermute | solution.py:295
  25.7 2.1 %collective-permute-done.10.across_chip = bf16[5,48,128]{2,1,0:T(8,128)(2,1)S(1)} collective-permute-done((bf16[5,48,128]{2,1,0:T(8,128)(2,1)S(1)}, bf16[5,48,128]{2,1,0:T(8,128)(2,1)S(1)}, u32[]{:S(2)}, u32[]{:S(2)}) %collective-permute-start.10) | collective-permute-done | bytes 61472 | tf_op jit(solution)/shard_map/ppermute | solution.py:295
  27.7 0.4 %first_terms.1.first = f32[160,768]{1,0:T(8,128)S(1)} custom-call(s32[11,128]{1,0:T(8,128)S(1)} %get-tuple-element.48.table, bf16[384,768]{1,0:T(8,128)(2,1)S(1)} %cross_output_both_rows.1.weights, bf16[5,48,128]{2,1,0:T(8,128)(2,1)S(1)} %get-tuple-element.54.own, bf16[5,48,128]{2,1,0:T(8,128)(2,1)S(1)} %collective-permute-done.10.across_chip), custom_call_target="tpu_custom_call" | custom-call | flops 1 | bytes 1 | tf_op jit(solution)/shard_map/first_terms/pallas_call | solution.py:302
  28.2 0.9 %collective-permute-done.11.across_both = bf16[5,48,128]{2,1,0:T(8,128)(2,1)S(1)} collective-permute-done((bf16[5,48,128]{2,1,0:T(8,128)(2,1)S(1)}, bf16[5,48,128]{2,1,0:T(8,128)(2,1)S(1)}, u32[]{:S(2)}, u32[]{:S(2)}) %collective-permute-start.11) | collective-permute-done | bytes 61472 | tf_op jit(solution)/shard_map/ppermute | solution.py:295
  29.0 0.0 collective-permute-done.12.across_core
  29.1 1.3 %pair_output.1 = bf16[2,5,32,768]{3,2,1,0:T(8,128)(2,1)} custom-call(f32[2,32,768]{2,1,0:T(8,128)S(1)} %get-tuple-element.47.own_rows, s32[11,128]{1,0:T(8,128)S(1)} %get-tuple-element.48.table, bf16[384,768]{1,0:T(8,128)(2,1)S(1)} %collective-permute-done.6.weights, f32[160,768]{1,0:T(8,128)S(1)} %first_terms.1.first, ...), custom_call_target="tpu_custom_call" | custom-call | flops 1 | bytes 1 | tf_op jit(solution)/shard_map/pair_output/pallas_call | solution.py:302
  (12 shorter events, 0.1 us)
Async XLA Ops:
  0.0 15.0 %collective-permute-start.2 = (bf16[192,768]{1,0:T(8,128)(2,1)}, bf16[192,768]{1,0:T(8,128)(2,1)S(1)}, u32[]{:S(2)}, u32[]{:S(2)}) collective-permute-start(bf16[192,768]{1,0:T(8,128)(2,1)} %param.12), channel_id=1, source_target_pairs={{0,2},{1,3},{2,0},{3,1},{4,6},{5,7},{6,4},{7,5},{8,10},{9,11},{10,... | collective-permute-start | bytes 884744 | tf_op jit(solution)/shard_map/ppermute | solution.py:295
  6.0 6.2 %collective-permute-start.3 = (bf16[384,128]{1,0:T(8,128)(2,1)S(1)}, bf16[384,128]{1,0:T(8,128)(2,1)S(1)}, u32[]{:S(2)}, u32[]{:S(2)}) collective-permute-start(bf16[384,128]{1,0:T(8,128)(2,1)S(1)} %get-tuple-element.44), channel_id=1, source_target_pairs={{0,8},{4,12},{8,0},{12,4},{16,24},{20,28},{24,16},{28,20},{1,9},{5... | collective-permute-start | bytes 294920 | tf_op jit(solution)/shard_map/ppermute | solution.py:298
  7.7 6.2 %collective-permute-start.4 = (bf16[384,128]{1,0:T(8,128)(2,1)S(1)}, bf16[384,128]{1,0:T(8,128)(2,1)S(1)}, u32[]{:S(2)}, u32[]{:S(2)}) collective-permute-start(bf16[384,128]{1,0:T(8,128)(2,1)S(1)} %get-tuple-element.45), channel_id=1, source_target_pairs={{0,4},{4,0},{8,12},{12,8},{16,20},{20,16},{24,28},{28,24},{1,5},{5... | collective-permute-start | bytes 294920 | tf_op jit(solution)/shard_map/ppermute | solution.py:298
  9.2 8.6 %collective-permute-start.1 = (bf16[384,128]{1,0:T(8,128)(2,1)S(1)}, bf16[384,128]{1,0:T(8,128)(2,1)S(1)}, u32[]{:S(2)}, u32[]{:S(2)}) collective-permute-start(bf16[384,128]{1,0:T(8,128)(2,1)S(1)} %get-tuple-element.43), channel_id=1, source_target_pairs={{0,2},{1,3},{2,0},{3,1},{4,6},{5,7},{6,4},{7,5},{8,10},{9,11},{10,... | collective-permute-start | bytes 294920 | tf_op jit(solution)/shard_map/ppermute | solution.py:295
  9.7 11.7 %collective-permute-start.7 = (bf16[384,128]{1,0:T(8,128)(2,1)S(1)}, bf16[384,128]{1,0:T(8,128)(2,1)S(1)}, u32[]{:S(2)}, u32[]{:S(2)}) collective-permute-start(bf16[384,128]{1,0:T(8,128)(2,1)S(1)} %get-tuple-element.51), channel_id=1, source_target_pairs={{0,16},{4,20},{8,24},{12,28},{16,0},{20,4},{24,8},{28,12},{1,17},{... | collective-permute-start | bytes 294920 | tf_op jit(solution)/shard_map/ppermute | solution.py:298
  12.3 5.5 %copy-start.2 = (bf16[192,768]{1,0:T(8,128)(2,1)S(1)}, bf16[192,768]{1,0:T(8,128)(2,1)}, u32[]{:S(2)}) copy-start(bf16[192,768]{1,0:T(8,128)(2,1)} %param.12) | copy-start | bytes 884740
  12.3 5.4 %copy-start = (f32[3,768]{1,0:T(4,128)S(1)}, f32[3,768]{1,0:T(4,128)}, u32[]{:S(2)}) copy-start(f32[3,768]{1,0:T(4,128)} %value.1) | copy-start | bytes 27652
  12.3 5.4 %copy-start.1 = (bf16[2,128,768]{2,1,0:T(8,128)(2,1)S(1)}, bf16[2,128,768]{2,1,0:T(8,128)(2,1)}, u32[]{:S(2)}) copy-start(bf16[2,128,768]{2,1,0:T(8,128)(2,1)} %states.1) | copy-start | bytes 1179652
  12.3 9.1 %collective-permute-start.5 = (bf16[192,768]{1,0:T(8,128)(2,1)S(1)}, bf16[192,768]{1,0:T(8,128)(2,1)S(1)}, u32[]{:S(2)}, u32[]{:S(2)}) collective-permute-start(bf16[192,768]{1,0:T(8,128)(2,1)S(1)} %cross_output_rows.1.own), channel_id=1, source_target_pairs={{0,2},{1,3},{2,0},{3,1},{4,6},{5,7},{6,4},{7,5},{8,10},{9,11},{10,... | collective-permute-start | bytes 884744 | tf_op jit(solution)/shard_map/ppermute | solution.py:295
  13.9 7.8 %collective-permute-start.8 = (bf16[384,128]{1,0:T(8,128)(2,1)S(1)}, bf16[384,128]{1,0:T(8,128)(2,1)S(1)}, u32[]{:S(2)}, u32[]{:S(2)}) collective-permute-start(bf16[384,128]{1,0:T(8,128)(2,1)S(1)} %get-tuple-element.52), channel_id=1, source_target_pairs={{0,24},{4,28},{8,16},{12,20},{16,8},{20,12},{24,0},{28,4},{1,25},{... | collective-permute-start | bytes 294920 | tf_op jit(solution)/shard_map/ppermute | solution.py:298
  15.0 7.4 %collective-permute-start.9 = (bf16[384,128]{1,0:T(8,128)(2,1)S(1)}, bf16[384,128]{1,0:T(8,128)(2,1)S(1)}, u32[]{:S(2)}, u32[]{:S(2)}) collective-permute-start(bf16[384,128]{1,0:T(8,128)(2,1)S(1)} %get-tuple-element.53), channel_id=1, source_target_pairs={{0,28},{4,8},{8,4},{12,16},{16,12},{20,24},{24,20},{28,0},{1,29},{... | collective-permute-start | bytes 294920 | tf_op jit(solution)/shard_map/ppermute | solution.py:298
  18.2 1.8 %collective-permute-start = (bf16[256,768]{1,0:T(8,128)(2,1)S(1)}, bf16[256,768]{1,0:T(8,128)(2,1)S(1)}, u32[]{:S(2)}, u32[]{:S(2)}) collective-permute-start(bf16[256,768]{1,0:T(8,128)(2,1)S(1)} %get-tuple-element.25), channel_id=1, source_target_pairs={{0,1},{1,0},{2,3},{3,2},{4,5},{5,4},{6,7},{7,6},{8,9},{9,8},{10,11... | collective-permute-start | bytes 1179656 | tf_op jit(solution)/shard_map/cond/branch_1_fun/ppermute | solution.py:295
  21.6 7.5 %collective-permute-start.6 = (bf16[384,768]{1,0:T(8,128)(2,1)S(1)}, bf16[384,768]{1,0:T(8,128)(2,1)S(1)}, u32[]{:S(2)}, u32[]{:S(2)}) collective-permute-start(bf16[384,768]{1,0:T(8,128)(2,1)S(1)} %cross_output_both_rows.1.weights), channel_id=1, source_target_pairs={{0,1},{1,0},{2,3},{3,2},{4,5},{5,4},{6,7},{7,6},{8,9},{9,8},{10,11... | collective-permute-start | bytes 1769480 | tf_op jit(solution)/shard_map/ppermute | solution.py:295
  23.4 4.3 %collective-permute-start.10 = (bf16[5,48,128]{2,1,0:T(8,128)(2,1)S(1)}, bf16[5,48,128]{2,1,0:T(8,128)(2,1)S(1)}, u32[]{:S(2)}, u32[]{:S(2)}) collective-permute-start(bf16[5,48,128]{2,1,0:T(8,128)(2,1)S(1)} %get-tuple-element.55), channel_id=1, source_target_pairs={{0,2},{1,3},{2,0},{3,1},{4,6},{5,7},{6,4},{7,5},{8,10},{9,11},{10,... | collective-permute-start | bytes 184328 | tf_op jit(solution)/shard_map/ppermute | solution.py:295
  25.0 4.0 %collective-permute-start.11 = (bf16[5,48,128]{2,1,0:T(8,128)(2,1)S(1)}, bf16[5,48,128]{2,1,0:T(8,128)(2,1)S(1)}, u32[]{:S(2)}, u32[]{:S(2)}) collective-permute-start(bf16[5,48,128]{2,1,0:T(8,128)(2,1)S(1)} %get-tuple-element.56), channel_id=1, source_target_pairs={{0,3},{1,2},{2,1},{3,0},{4,7},{5,6},{6,5},{7,4},{8,11},{9,10},{10,... | collective-permute-start | bytes 184328 | tf_op jit(solution)/shard_map/ppermute | solution.py:295
  25.0 4.0 %collective-permute-start.12 = (bf16[5,48,128]{2,1,0:T(8,128)(2,1)S(1)}, bf16[5,48,128]{2,1,0:T(8,128)(2,1)S(1)}, u32[]{:S(2)}, u32[]{:S(2)}) collective-permute-start(bf16[5,48,128]{2,1,0:T(8,128)(2,1)S(1)} %get-tuple-element.57), channel_id=1, source_target_pairs={{0,1},{1,0},{2,3},{3,2},{4,5},{5,4},{6,7},{7,6},{8,9},{9,8},{10,11... | collective-permute-start | bytes 184328 | tf_op jit(solution)/shard_map/ppermute | solution.py:295

commit v17 on v14

--- a/solution.py
+++ b/solution.py
@@ -258,7 +258,7 @@
     terms[...] = nn(placed_rows((own, across_chip), order, table), weights[...])
 
 
-def out_kernel(order, own_rows, table, weights, first, across_both, across_core, out, out_v, sems):
+def out_kernel(order, own_rows, table, weights, first, across_core, across_both, out, out_v, sems):
     row_n, width = own_rows.shape[1:]
     pair_n = len(order)
     terms = first[...] + nn(placed_rows((across_core, across_both), order, table), weights[...])
@@ -419,7 +419,7 @@
         shape((2 * columns, width), BF16),
         [VMEM, ANY, ANY],
         [dma((2,))],
-        cross_out, cross_out_got, early_sides,
+        cross_out_sent, cross_out_got, early_sides,
     )
     cross_out_core = across(cross_out_both, core_hop)
     order = early + late
@@ -437,7 +437,7 @@
         shape((image_n, slot_n, row_n, width), BF16),
         [VMEM] * 6,
         [pltpu.VMEM((image_n, slot_n, row_n, width), BF16), dma((image_n,))],
-        own_rows, table, cross_out_core, first_terms, sides[chip_hop ^ core_hop], sides[core_hop],
+        own_rows, table, cross_out_core, first_terms, sides[core_hop], sides[chip_hop ^ core_hop],
         out_specs=HBM,
     )
 

time: 30.3 us -> 29.9 us (0.987)
  waiting for transfers between devices: 5.12 us -> 4.77 us
    ppermute x8, waiting for transfers between devices: 4.69 us -> 4.31 us  [across(): return lax.ppermute(value, 'helper', [(j, j ^ k) for j in range(helper_n)])]
where the time goes in v17:
time: 29.9 us; the launch traced here: 29.7 us
  starting transfers between devices  17.1 us (57%)
  Pallas kernels  7.77 us (26%)
  waiting for transfers between devices  4.77 us (16%)
    ppermute x5, starting transfers between devices, exchange(): lax.ppermute(value, 'owner', [(o, swap_target(o, swap, owner_n)) for o in...  9.52 us
    pallas_call x10, Pallas kernels, call(): pl.pallas_call(kernel, out_shape=out_shape, in_specs=in_specs, out_specs=...  7.77 us
    ppermute x8, starting transfers between devices, across(): return lax.ppermute(value, 'helper', [(j, j ^ k) for j in range(helper_n)])  7.55 us
    ppermute x8, waiting for transfers between devices, across(): return lax.ppermute(value, 'helper', [(j, j ^ k) for j in range(helper_n)])  4.31 us
  transfers between devices with their start and end apart: 13, of which 4 were waited for; matrix products, arithmetic and copies ran while one was open for 0% of the time, Pallas kernels for 22%

profile of v17, /device:TPU:0, one launch (start us, length us, event | category | flops | bytes accessed | tf_op | source)
XLA Modules:
  0.0 29.7 jit_solution(9919822370721321728)
XLA Ops:
  0.0 3.0 %collective-permute-start.2 = (bf16[192,768]{1,0:T(8,128)(2,1)}, bf16[192,768]{1,0:T(8,128)(2,1)S(1)}, u32[]{:S(2)}, u32[]{:S(2)}) collective-permute-start(bf16[192,768]{1,0:T(8,128)(2,1)} %param.12), channel_id=1, source_target_pairs={{0,2},{1,3},{2,0},{3,1},{4,6},{5,7},{6,4},{7,5},{8,10},{9,11},{10,... | collective-permute-start | bytes 884744 | tf_op jit(solution)/shard_map/ppermute | solution.py:292
  3.0 3.1 %own_images.1 = (bf16[384,128]{1,0:T(8,128)(2,1)S(1)}, bf16[384,128]{1,0:T(8,128)(2,1)S(1)}, bf16[384,128]{1,0:T(8,128)(2,1)S(1)}, bf16[384,128]{1,0:T(8,128)(2,...) custom-call(bf16[2,128,768]{2,1,0:T(8,128)(2,1)} %states.1, ...), custom_call_target="tpu_custom_call" | custom-call | flops 1 | bytes 1 | tf_op jit(solution)/shard_map/own_images/pallas_call | solution.py:299
  6.0 1.6 %collective-permute-start.3 = (bf16[384,128]{1,0:T(8,128)(2,1)S(1)}, bf16[384,128]{1,0:T(8,128)(2,1)S(1)}, u32[]{:S(2)}, u32[]{:S(2)}) collective-permute-start(bf16[384,128]{1,0:T(8,128)(2,1)S(1)} %get-tuple-element.44), channel_id=1, source_target_pairs={{0,8},{4,12},{8,0},{12,4},{16,24},{20,28},{24,16},{28,20},{1,9},{5... | collective-permute-start | bytes 294920 | tf_op jit(solution)/shard_map/ppermute | solution.py:295
  7.7 1.5 %collective-permute-start.4 = (bf16[384,128]{1,0:T(8,128)(2,1)S(1)}, bf16[384,128]{1,0:T(8,128)(2,1)S(1)}, u32[]{:S(2)}, u32[]{:S(2)}) collective-permute-start(bf16[384,128]{1,0:T(8,128)(2,1)S(1)} %get-tuple-element.45), channel_id=1, source_target_pairs={{0,4},{4,0},{8,12},{12,8},{16,20},{20,16},{24,28},{28,24},{1,5},{5... | collective-permute-start | bytes 294920 | tf_op jit(solution)/shard_map/ppermute | solution.py:295
  9.2 0.5 %collective-permute-start.1 = (bf16[384,128]{1,0:T(8,128)(2,1)S(1)}, bf16[384,128]{1,0:T(8,128)(2,1)S(1)}, u32[]{:S(2)}, u32[]{:S(2)}) collective-permute-start(bf16[384,128]{1,0:T(8,128)(2,1)S(1)} %get-tuple-element.43), channel_id=1, source_target_pairs={{0,2},{1,3},{2,0},{3,1},{4,6},{5,7},{6,4},{7,5},{8,10},{9,11},{10,... | collective-permute-start | bytes 294920 | tf_op jit(solution)/shard_map/ppermute | solution.py:292
  9.7 2.6 %collective-permute-start.6 = (bf16[384,128]{1,0:T(8,128)(2,1)S(1)}, bf16[384,128]{1,0:T(8,128)(2,1)S(1)}, u32[]{:S(2)}, u32[]{:S(2)}) collective-permute-start(bf16[384,128]{1,0:T(8,128)(2,1)S(1)} %get-tuple-element.51), channel_id=1, source_target_pairs={{0,16},{4,20},{8,24},{12,28},{16,0},{20,4},{24,8},{28,12},{1,17},{... | collective-permute-start | bytes 294920 | tf_op jit(solution)/shard_map/ppermute | solution.py:295
  12.3 0.0 collective-permute-done.3.rest_0_.rest_1_
  12.3 0.0 copy-start
  12.3 0.0 copy-start.1
  12.3 1.6 %collective-permute-start.5 = (bf16[192,768]{1,0:T(8,128)(2,1)S(1)}, bf16[192,768]{1,0:T(8,128)(2,1)S(1)}, u32[]{:S(2)}, u32[]{:S(2)}) collective-permute-start(bf16[192,768]{1,0:T(8,128)(2,1)S(1)} %cross_output_rows.1.own), channel_id=1, source_target_pairs={{0,2},{1,3},{2,0},{3,1},{4,6},{5,7},{6,4},{7,5},{8,10},{9,11},{10,... | collective-permute-start | bytes 884744 | tf_op jit(solution)/shard_map/ppermute | solution.py:292
  13.9 1.0 %collective-permute-start.8 = (bf16[384,128]{1,0:T(8,128)(2,1)S(1)}, bf16[384,128]{1,0:T(8,128)(2,1)S(1)}, u32[]{:S(2)}, u32[]{:S(2)}) collective-permute-start(bf16[384,128]{1,0:T(8,128)(2,1)S(1)} %get-tuple-element.52), channel_id=1, source_target_pairs={{0,24},{4,28},{8,16},{12,20},{16,8},{20,12},{24,0},{28,4},{1,25},{... | collective-permute-start | bytes 294920 | tf_op jit(solution)/shard_map/ppermute | solution.py:295
  15.0 0.0 collective-permute-done.2.rest_2_
  15.0 2.8 %collective-permute-start.9 = (bf16[384,128]{1,0:T(8,128)(2,1)S(1)}, bf16[384,128]{1,0:T(8,128)(2,1)S(1)}, u32[]{:S(2)}, u32[]{:S(2)}) collective-permute-start(bf16[384,128]{1,0:T(8,128)(2,1)S(1)} %get-tuple-element.53), channel_id=1, source_target_pairs={{0,28},{4,8},{8,4},{12,16},{16,12},{20,24},{24,20},{28,0},{1,29},{... | collective-permute-start | bytes 294920 | tf_op jit(solution)/shard_map/ppermute | solution.py:295
  17.7 0.0 collective-permute-done.1
  17.8 2.8 %conditional.1 = ((f32[2,32,768]{2,1,0:T(8,128)S(1)}, bf16[2,128,192]{2,1,0:T(8,128)(2,1)S(1)})) conditional(s32[]{:T(128)} %convert_element_type.3, () %tuple.12, (bf16[2,128,768]{2,1,0:T(8,128)(2,1)S(1)}, bf16[384,128]{1,0:T(8,128)(2,1)S(1)}, bf16[384,128]{1,0:T(8,128)(2,1)S(1)}, bf16[192,768]{1,0:T(8,128)(2,1)S(1)}, ...), branch_computations={%region_0.0_spmd, %region_1.0_spmd} | conditional | flops 2 | bytes 1572914 | solution.py:392
  17.8 0.4 %self_output_share.1 = (f32[256,768]{1,0:T(8,128)S(1)}, bf16[256,768]{1,0:T(8,128)(2,1)S(1)}) custom-call(bf16[2,128,768]{2,1,0:T(8,128)(2,1)S(1)} %get-tuple-element.19.states, bf16[384,128]{1,0:T(8,128)(2,1)S(1)} %get-tuple-element.20.own, bf16[384,128]{1,0:T(8,128)(2,1)S(1)} %get-tuple-element.21.got, bf16[192,768]{1,0:T(8,128)(2,1)S(1)} %get-tuple-element.22.own_weight, ...), custom_call_target="tpu_custom_call" | custom-call | flops 1 | bytes 1 | tf_op jit(solution)/shard_map/cond/branch_1_fun/self_output_share/pallas_call | solution.py:299
  18.2 0.1 collective-permute-start
  18.3 1.7 %collective-permute-done.got = bf16[256,768]{1,0:T(8,128)(2,1)S(1)} collective-permute-done((bf16[256,768]{1,0:T(8,128)(2,1)S(1)}, bf16[256,768]{1,0:T(8,128)(2,1)S(1)}, u32[]{:S(2)}, u32[]{:S(2)}) %collective-permute-start) | collective-permute-done | bytes 393248 | tf_op jit(solution)/shard_map/cond/branch_1_fun/ppermute | solution.py:292
  20.0 0.5 %mixed_and_queries.1 = (f32[2,32,768]{2,1,0:T(8,128)S(1)}, bf16[2,128,192]{2,1,0:T(8,128)(2,1)S(1)}) custom-call(f32[256,768]{1,0:T(8,128)S(1)} %get-tuple-element.24.base, bf16[256,768]{1,0:T(8,128)(2,1)S(1)} %collective-permute-done.got, f32[3,768]{1,0:T(4,128)S(1)} %get-tuple-element.26.gains, bf16[192,768]{1,0:T(8,128)(2,1)S(1)} %get-tuple-element.27.weight), custom_call_target="tpu_custom_call" | custom-call | flops 1 | bytes 1 | tf_op jit(solution)/shard_map/cond/branch_1_fun/mixed_and_queries/pallas_call | solution.py:299
  20.5 0.0 collective-permute-done.6.rest_0_
  20.5 1.0 %early_cross_attention.1.waited.before = bf16[4,3,48,128]{3,2,1,0:T(8,128)(2,1)S(1)} custom-call(bf16[2,128,192]{2,1,0:T(8,128)(2,1)S(1)} %get-tuple-element.50.queries, s32[11,128]{1,0:T(8,128)S(1)} %get-tuple-element.48.table, bf16[384,128]{1,0:T(8,128)(2,1)S(1)} %collective-permute-done.6.rest_0_, ...), custom_call_target="tpu_custom_call" | custom-call | flops 3000000000 | bytes 1 | tf_op jit(solution)/shard_map/early_cross_attention/pallas_call | solution.py:299
  21.6 0.1 cross_output_both_rows.1.weights
  21.7 0.2 collective-permute-start.7
  21.9 0.4 %collective-permute-done.9.rest_1_ = bf16[384,128]{1,0:T(8,128)(2,1)S(1)} collective-permute-done((bf16[384,128]{1,0:T(8,128)(2,1)S(1)}, bf16[384,128]{1,0:T(8,128)(2,1)S(1)}, u32[]{:S(2)}, u32[]{:S(2)}) %collective-permute-start.9) | collective-permute-done | bytes 98336 | tf_op jit(solution)/shard_map/ppermute | solution.py:295
  22.4 0.9 %late_cross_attention.1 = (bf16[5,48,128]{2,1,0:T(8,128)(2,1)S(1)}, bf16[5,48,128]{2,1,0:T(8,128)(2,1)S(1)}, bf16[5,48,128]{2,1,0:T(8,128)(2,1)S(1)}, bf16[5,48,128]{2,1,0:T(8,128)(2,1)S(1)}) custom-call(bf16[2,128,192]{2,1,0:T(8,128)(2,1)S(1)} %get-tuple-element.50.queries, s32[11,128]{1,0:T(8,128)S(1)} %get-tuple-element.48.table, ...), custom_call_target="tpu_custom_call" | custom-call | flops 99999997952 | bytes 1 | tf_op jit(solution)/shard_map/late_cross_attention/pallas_call | solution.py:299
  23.2 1.6 %collective-permute-start.10 = (bf16[5,48,128]{2,1,0:T(8,128)(2,1)S(1)}, bf16[5,48,128]{2,1,0:T(8,128)(2,1)S(1)}, u32[]{:S(2)}, u32[]{:S(2)}) collective-permute-start(bf16[5,48,128]{2,1,0:T(8,128)(2,1)S(1)} %get-tuple-element.55), channel_id=1, source_target_pairs={{0,2},{1,3},{2,0},{3,1},{4,6},{5,7},{6,4},{7,5},{8,10},{9,11},{10,... | collective-permute-start | bytes 184328 | tf_op jit(solution)/shard_map/ppermute | solution.py:292
  24.8 0.6 %collective-permute-start.12 = (bf16[5,48,128]{2,1,0:T(8,128)(2,1)S(1)}, bf16[5,48,128]{2,1,0:T(8,128)(2,1)S(1)}, u32[]{:S(2)}, u32[]{:S(2)}) collective-permute-start(bf16[5,48,128]{2,1,0:T(8,128)(2,1)S(1)} %get-tuple-element.57), channel_id=1, source_target_pairs={{0,3},{1,2},{2,1},{3,0},{4,7},{5,6},{6,5},{7,4},{8,11},{9,10},{10,... | collective-permute-start | bytes 184328 | tf_op jit(solution)/shard_map/ppermute | solution.py:292
  25.4 2.1 %collective-permute-done.10.across_chip = bf16[5,48,128]{2,1,0:T(8,128)(2,1)S(1)} collective-permute-done((bf16[5,48,128]{2,1,0:T(8,128)(2,1)S(1)}, bf16[5,48,128]{2,1,0:T(8,128)(2,1)S(1)}, u32[]{:S(2)}, u32[]{:S(2)}) %collective-permute-start.10) | collective-permute-done | bytes 61472 | tf_op jit(solution)/shard_map/ppermute | solution.py:292
  27.5 0.4 %first_terms.1.first = f32[160,768]{1,0:T(8,128)S(1)} custom-call(s32[11,128]{1,0:T(8,128)S(1)} %get-tuple-element.48.table, bf16[384,768]{1,0:T(8,128)(2,1)S(1)} %cross_output_both_rows.1.weights, bf16[5,48,128]{2,1,0:T(8,128)(2,1)S(1)} %get-tuple-element.54.own, bf16[5,48,128]{2,1,0:T(8,128)(2,1)S(1)} %collective-permute-done.10.across_chip), custom_call_target="tpu_custom_call" | custom-call | flops 1 | bytes 1 | tf_op jit(solution)/shard_map/first_terms/pallas_call | solution.py:299
  28.0 0.5 %collective-permute-done.12.across_both = bf16[5,48,128]{2,1,0:T(8,128)(2,1)S(1)} collective-permute-done((bf16[5,48,128]{2,1,0:T(8,128)(2,1)S(1)}, bf16[5,48,128]{2,1,0:T(8,128)(2,1)S(1)}, u32[]{:S(2)}, u32[]{:S(2)}) %collective-permute-start.12) | collective-permute-done | bytes 61472 | tf_op jit(solution)/shard_map/ppermute | solution.py:292
  28.5 0.0 collective-permute-done.7.weights
  28.5 1.3 %pair_output.1 = bf16[2,5,32,768]{3,2,1,0:T(8,128)(2,1)} custom-call(f32[2,32,768]{2,1,0:T(8,128)S(1)} %get-tuple-element.47.own_rows, s32[11,128]{1,0:T(8,128)S(1)} %get-tuple-element.48.table, bf16[384,768]{1,0:T(8,128)(2,1)S(1)} %collective-permute-done.7.weights, f32[160,768]{1,0:T(8,128)S(1)} %first_terms.1.first, ...), custom_call_target="tpu_custom_call" | custom-call | flops 1 | bytes 1 | tf_op jit(solution)/shard_map/pair_output/pallas_call | solution.py:299
  (11 shorter events, 0.0 us)
Async XLA Ops:
  0.0 15.0 %collective-permute-start.2 = (bf16[192,768]{1,0:T(8,128)(2,1)}, bf16[192,768]{1,0:T(8,128)(2,1)S(1)}, u32[]{:S(2)}, u32[]{:S(2)}) collective-permute-start(bf16[192,768]{1,0:T(8,128)(2,1)} %param.12), channel_id=1, source_target_pairs={{0,2},{1,3},{2,0},{3,1},{4,6},{5,7},{6,4},{7,5},{8,10},{9,11},{10,... | collective-permute-start | bytes 884744 | tf_op jit(solution)/shard_map/ppermute | solution.py:292
  6.0 6.2 %collective-permute-start.3 = (bf16[384,128]{1,0:T(8,128)(2,1)S(1)}, bf16[384,128]{1,0:T(8,128)(2,1)S(1)}, u32[]{:S(2)}, u32[]{:S(2)}) collective-permute-start(bf16[384,128]{1,0:T(8,128)(2,1)S(1)} %get-tuple-element.44), channel_id=1, source_target_pairs={{0,8},{4,12},{8,0},{12,4},{16,24},{20,28},{24,16},{28,20},{1,9},{5... | collective-permute-start | bytes 294920 | tf_op jit(solution)/shard_map/ppermute | solution.py:295
  7.7 6.3 %collective-permute-start.4 = (bf16[384,128]{1,0:T(8,128)(2,1)S(1)}, bf16[384,128]{1,0:T(8,128)(2,1)S(1)}, u32[]{:S(2)}, u32[]{:S(2)}) collective-permute-start(bf16[384,128]{1,0:T(8,128)(2,1)S(1)} %get-tuple-element.45), channel_id=1, source_target_pairs={{0,4},{4,0},{8,12},{12,8},{16,20},{20,16},{24,28},{28,24},{1,5},{5... | collective-permute-start | bytes 294920 | tf_op jit(solution)/shard_map/ppermute | solution.py:295
  9.2 8.6 %collective-permute-start.1 = (bf16[384,128]{1,0:T(8,128)(2,1)S(1)}, bf16[384,128]{1,0:T(8,128)(2,1)S(1)}, u32[]{:S(2)}, u32[]{:S(2)}) collective-permute-start(bf16[384,128]{1,0:T(8,128)(2,1)S(1)} %get-tuple-element.43), channel_id=1, source_target_pairs={{0,2},{1,3},{2,0},{3,1},{4,6},{5,7},{6,4},{7,5},{8,10},{9,11},{10,... | collective-permute-start | bytes 294920 | tf_op jit(solution)/shard_map/ppermute | solution.py:292
  9.7 10.9 %collective-permute-start.6 = (bf16[384,128]{1,0:T(8,128)(2,1)S(1)}, bf16[384,128]{1,0:T(8,128)(2,1)S(1)}, u32[]{:S(2)}, u32[]{:S(2)}) collective-permute-start(bf16[384,128]{1,0:T(8,128)(2,1)S(1)} %get-tuple-element.51), channel_id=1, source_target_pairs={{0,16},{4,20},{8,24},{12,28},{16,0},{20,4},{24,8},{28,12},{1,17},{... | collective-permute-start | bytes 294920 | tf_op jit(solution)/shard_map/ppermute | solution.py:295
  12.3 5.5 %copy-start.2 = (bf16[192,768]{1,0:T(8,128)(2,1)S(1)}, bf16[192,768]{1,0:T(8,128)(2,1)}, u32[]{:S(2)}) copy-start(bf16[192,768]{1,0:T(8,128)(2,1)} %param.12) | copy-start | bytes 884740
  12.3 5.4 %copy-start = (f32[3,768]{1,0:T(4,128)S(1)}, f32[3,768]{1,0:T(4,128)}, u32[]{:S(2)}) copy-start(f32[3,768]{1,0:T(4,128)} %value.1) | copy-start | bytes 27652
  12.3 5.4 %copy-start.1 = (bf16[2,128,768]{2,1,0:T(8,128)(2,1)S(1)}, bf16[2,128,768]{2,1,0:T(8,128)(2,1)}, u32[]{:S(2)}) copy-start(bf16[2,128,768]{2,1,0:T(8,128)(2,1)} %states.1) | copy-start | bytes 1179652
  12.3 9.3 %collective-permute-start.5 = (bf16[192,768]{1,0:T(8,128)(2,1)S(1)}, bf16[192,768]{1,0:T(8,128)(2,1)S(1)}, u32[]{:S(2)}, u32[]{:S(2)}) collective-permute-start(bf16[192,768]{1,0:T(8,128)(2,1)S(1)} %cross_output_rows.1.own), channel_id=1, source_target_pairs={{0,2},{1,3},{2,0},{3,1},{4,6},{5,7},{6,4},{7,5},{8,10},{9,11},{10,... | collective-permute-start | bytes 884744 | tf_op jit(solution)/shard_map/ppermute | solution.py:292
  13.9 8.0 %collective-permute-start.8 = (bf16[384,128]{1,0:T(8,128)(2,1)S(1)}, bf16[384,128]{1,0:T(8,128)(2,1)S(1)}, u32[]{:S(2)}, u32[]{:S(2)}) collective-permute-start(bf16[384,128]{1,0:T(8,128)(2,1)S(1)} %get-tuple-element.52), channel_id=1, source_target_pairs={{0,24},{4,28},{8,16},{12,20},{16,8},{20,12},{24,0},{28,4},{1,25},{... | collective-permute-start | bytes 294920 | tf_op jit(solution)/shard_map/ppermute | solution.py:295
  15.0 7.4 %collective-permute-start.9 = (bf16[384,128]{1,0:T(8,128)(2,1)S(1)}, bf16[384,128]{1,0:T(8,128)(2,1)S(1)}, u32[]{:S(2)}, u32[]{:S(2)}) collective-permute-start(bf16[384,128]{1,0:T(8,128)(2,1)S(1)} %get-tuple-element.53), channel_id=1, source_target_pairs={{0,28},{4,8},{8,4},{12,16},{16,12},{20,24},{24,20},{28,0},{1,29},{... | collective-permute-start | bytes 294920 | tf_op jit(solution)/shard_map/ppermute | solution.py:295
  18.2 1.8 %collective-permute-start = (bf16[256,768]{1,0:T(8,128)(2,1)S(1)}, bf16[256,768]{1,0:T(8,128)(2,1)S(1)}, u32[]{:S(2)}, u32[]{:S(2)}) collective-permute-start(bf16[256,768]{1,0:T(8,128)(2,1)S(1)} %get-tuple-element.25), channel_id=1, source_target_pairs={{0,1},{1,0},{2,3},{3,2},{4,5},{5,4},{6,7},{7,6},{8,9},{9,8},{10,11... | collective-permute-start | bytes 1179656 | tf_op jit(solution)/shard_map/cond/branch_1_fun/ppermute | solution.py:292
  21.7 6.7 %collective-permute-start.7 = (bf16[384,768]{1,0:T(8,128)(2,1)S(1)}, bf16[384,768]{1,0:T(8,128)(2,1)S(1)}, u32[]{:S(2)}, u32[]{:S(2)}) collective-permute-start(bf16[384,768]{1,0:T(8,128)(2,1)S(1)} %cross_output_both_rows.1.weights), channel_id=1, source_target_pairs={{0,1},{1,0},{2,3},{3,2},{4,5},{5,4},{6,7},{7,6},{8,9},{9,8},{10,11... | collective-permute-start | bytes 1769480 | tf_op jit(solution)/shard_map/ppermute | solution.py:292
  23.2 4.3 %collective-permute-start.10 = (bf16[5,48,128]{2,1,0:T(8,128)(2,1)S(1)}, bf16[5,48,128]{2,1,0:T(8,128)(2,1)S(1)}, u32[]{:S(2)}, u32[]{:S(2)}) collective-permute-start(bf16[5,48,128]{2,1,0:T(8,128)(2,1)S(1)} %get-tuple-element.55), channel_id=1, source_target_pairs={{0,2},{1,3},{2,0},{3,1},{4,6},{5,7},{6,4},{7,5},{8,10},{9,11},{10,... | collective-permute-start | bytes 184328 | tf_op jit(solution)/shard_map/ppermute | solution.py:292
  24.8 3.1 %collective-permute-start.11 = (bf16[5,48,128]{2,1,0:T(8,128)(2,1)S(1)}, bf16[5,48,128]{2,1,0:T(8,128)(2,1)S(1)}, u32[]{:S(2)}, u32[]{:S(2)}) collective-permute-start(bf16[5,48,128]{2,1,0:T(8,128)(2,1)S(1)} %get-tuple-element.56), channel_id=1, source_target_pairs={{0,1},{1,0},{2,3},{3,2},{4,5},{5,4},{6,7},{7,6},{8,9},{9,8},{10,11... | collective-permute-start | bytes 184328 | tf_op jit(solution)/shard_map/ppermute | solution.py:292
  24.8 3.6 %collective-permute-start.12 = (bf16[5,48,128]{2,1,0:T(8,128)(2,1)S(1)}, bf16[5,48,128]{2,1,0:T(8,128)(2,1)S(1)}, u32[]{:S(2)}, u32[]{:S(2)}) collective-permute-start(bf16[5,48,128]{2,1,0:T(8,128)(2,1)S(1)} %get-tuple-element.57), channel_id=1, source_target_pairs={{0,3},{1,2},{2,1},{3,0},{4,7},{5,6},{6,5},{7,4},{8,11},{9,10},{10,... | collective-permute-start | bytes 184328 | tf_op jit(solution)/shard_map/ppermute | solution.py:292

commit v18 on v17

--- a/solution.py
+++ b/solution.py
@@ -254,14 +254,17 @@
     return jnp.concatenate(rows, 1)
 
 
-def first_terms_kernel(order, table, weights, own, across_chip, terms):
-    terms[...] = nn(placed_rows((own, across_chip), order, table), weights[...])
-
-
-def out_kernel(order, own_rows, table, weights, first, across_core, across_both, out, out_v, sems):
+def first_terms_kernel(order, table, weights, core_weights, own, across_chip, across_core, terms):
+    columns = core_weights.shape[0] // 2
+    both = nn(placed_rows((own, across_chip), order, table), weights[...])
+    terms[...] = both + nn(placed_rows((across_core,), order, table), core_weights[:columns, :])
+
+
+def out_kernel(order, own_rows, table, weights, first, across_both, out, out_v, sems):
     row_n, width = own_rows.shape[1:]
     pair_n = len(order)
-    terms = first[...] + nn(placed_rows((across_core, across_both), order, table), weights[...])
+    columns = weights.shape[0] // 2
+    terms = first[...] + nn(placed_rows((across_both,), order, table), weights[columns:, :])
     first_n = table[2 * pair_n :, 0:1]
     zero = jnp.zeros((row_n, width), F32)
     for position in range(pair_n):
@@ -427,17 +430,17 @@
         "first_terms",
         functools.partial(first_terms_kernel, order),
         shape((pair_n * row_n, width), F32),
-        [VMEM] * 4,
+        [VMEM] * 6,
         [],
-        table, cross_out_both, sides[0], sides[chip_hop],
+        table, cross_out_both, cross_out_core, sides[0], sides[chip_hop], sides[core_hop],
     )
     return call(
         "pair_output",
         functools.partial(out_kernel, order),
         shape((image_n, slot_n, row_n, width), BF16),
-        [VMEM] * 6,
+        [VMEM] * 5,
         [pltpu.VMEM((image_n, slot_n, row_n, width), BF16), dma((image_n,))],
-        own_rows, table, cross_out_core, first_terms, sides[core_hop], sides[chip_hop ^ core_hop],
+        own_rows, table, cross_out_core, first_terms, sides[chip_hop ^ core_hop],
         out_specs=HBM,
     )
 

time: 29.9 us -> 29.8 us (level)
  no operation moved by 1% of the time
where the time goes in v18:
time: 29.8 us; the launch traced here: 29.6 us
  starting transfers between devices  17.1 us (57%)
  Pallas kernels  7.65 us (26%)
  waiting for transfers between devices  4.74 us (16%)
    ppermute x5, starting transfers between devices, exchange(): lax.ppermute(value, 'owner', [(o, swap_target(o, swap, owner_n)) for o in...  9.51 us
    pallas_call x10, Pallas kernels, call(): pl.pallas_call(kernel, out_shape=out_shape, in_specs=in_specs, out_specs=...  7.65 us
    ppermute x8, starting transfers between devices, across(): return lax.ppermute(value, 'helper', [(j, j ^ k) for j in range(helper_n)])  7.54 us
    ppermute x8, waiting for transfers between devices, across(): return lax.ppermute(value, 'helper', [(j, j ^ k) for j in range(helper_n)])  4.28 us
  transfers between devices with their start and end apart: 13, of which 4 were waited for; matrix products, arithmetic and copies ran while one was open for 0% of the time, Pallas kernels for 22%

profile of v18, /device:TPU:0, one launch (start us, length us, event | category | flops | bytes accessed | tf_op | source)
XLA Modules:
  0.0 29.6 jit_solution(917996585727774872)
XLA Ops:
  0.0 3.0 %collective-permute-start.2 = (bf16[192,768]{1,0:T(8,128)(2,1)}, bf16[192,768]{1,0:T(8,128)(2,1)S(1)}, u32[]{:S(2)}, u32[]{:S(2)}) collective-permute-start(bf16[192,768]{1,0:T(8,128)(2,1)} %param.12), channel_id=1, source_target_pairs={{0,2},{1,3},{2,0},{3,1},{4,6},{5,7},{6,4},{7,5},{8,10},{9,11},{10,... | collective-permute-start | bytes 884744 | tf_op jit(solution)/shard_map/ppermute | solution.py:295
  3.0 3.1 %own_images.1 = (bf16[384,128]{1,0:T(8,128)(2,1)S(1)}, bf16[384,128]{1,0:T(8,128)(2,1)S(1)}, bf16[384,128]{1,0:T(8,128)(2,1)S(1)}, bf16[384,128]{1,0:T(8,128)(2,...) custom-call(bf16[2,128,768]{2,1,0:T(8,128)(2,1)} %states.1, ...), custom_call_target="tpu_custom_call" | custom-call | flops 1 | bytes 1 | tf_op jit(solution)/shard_map/own_images/pallas_call | solution.py:302
  6.0 1.7 %collective-permute-start.3 = (bf16[384,128]{1,0:T(8,128)(2,1)S(1)}, bf16[384,128]{1,0:T(8,128)(2,1)S(1)}, u32[]{:S(2)}, u32[]{:S(2)}) collective-permute-start(bf16[384,128]{1,0:T(8,128)(2,1)S(1)} %get-tuple-element.44), channel_id=1, source_target_pairs={{0,8},{4,12},{8,0},{12,4},{16,24},{20,28},{24,16},{28,20},{1,9},{5... | collective-permute-start | bytes 294920 | tf_op jit(solution)/shard_map/ppermute | solution.py:298
  7.7 1.5 %collective-permute-start.4 = (bf16[384,128]{1,0:T(8,128)(2,1)S(1)}, bf16[384,128]{1,0:T(8,128)(2,1)S(1)}, u32[]{:S(2)}, u32[]{:S(2)}) collective-permute-start(bf16[384,128]{1,0:T(8,128)(2,1)S(1)} %get-tuple-element.45), channel_id=1, source_target_pairs={{0,4},{4,0},{8,12},{12,8},{16,20},{20,16},{24,28},{28,24},{1,5},{5... | collective-permute-start | bytes 294920 | tf_op jit(solution)/shard_map/ppermute | solution.py:298
  9.2 0.5 %collective-permute-start.1 = (bf16[384,128]{1,0:T(8,128)(2,1)S(1)}, bf16[384,128]{1,0:T(8,128)(2,1)S(1)}, u32[]{:S(2)}, u32[]{:S(2)}) collective-permute-start(bf16[384,128]{1,0:T(8,128)(2,1)S(1)} %get-tuple-element.43), channel_id=1, source_target_pairs={{0,2},{1,3},{2,0},{3,1},{4,6},{5,7},{6,4},{7,5},{8,10},{9,11},{10,... | collective-permute-start | bytes 294920 | tf_op jit(solution)/shard_map/ppermute | solution.py:295
  9.7 2.6 %collective-permute-start.6 = (bf16[384,128]{1,0:T(8,128)(2,1)S(1)}, bf16[384,128]{1,0:T(8,128)(2,1)S(1)}, u32[]{:S(2)}, u32[]{:S(2)}) collective-permute-start(bf16[384,128]{1,0:T(8,128)(2,1)S(1)} %get-tuple-element.51), channel_id=1, source_target_pairs={{0,16},{4,20},{8,24},{12,28},{16,0},{20,4},{24,8},{28,12},{1,17},{... | collective-permute-start | bytes 294920 | tf_op jit(solution)/shard_map/ppermute | solution.py:298
  12.3 0.0 collective-permute-done.3.rest_0_.rest_1_
  12.3 0.0 copy-start
  12.3 0.0 copy-start.1
  12.3 1.6 %collective-permute-start.5 = (bf16[192,768]{1,0:T(8,128)(2,1)S(1)}, bf16[192,768]{1,0:T(8,128)(2,1)S(1)}, u32[]{:S(2)}, u32[]{:S(2)}) collective-permute-start(bf16[192,768]{1,0:T(8,128)(2,1)S(1)} %cross_output_rows.1.own), channel_id=1, source_target_pairs={{0,2},{1,3},{2,0},{3,1},{4,6},{5,7},{6,4},{7,5},{8,10},{9,11},{10,... | collective-permute-start | bytes 884744 | tf_op jit(solution)/shard_map/ppermute | solution.py:295
  13.9 0.0 collective-permute-done.4.rest_1_.rest_2_
  13.9 1.0 %collective-permute-start.8 = (bf16[384,128]{1,0:T(8,128)(2,1)S(1)}, bf16[384,128]{1,0:T(8,128)(2,1)S(1)}, u32[]{:S(2)}, u32[]{:S(2)}) collective-permute-start(bf16[384,128]{1,0:T(8,128)(2,1)S(1)} %get-tuple-element.52), channel_id=1, source_target_pairs={{0,24},{4,28},{8,16},{12,20},{16,8},{20,12},{24,0},{28,4},{1,25},{... | collective-permute-start | bytes 294920 | tf_op jit(solution)/shard_map/ppermute | solution.py:298
  15.0 0.0 collective-permute-done.2.rest_2_
  15.0 2.8 %collective-permute-start.9 = (bf16[384,128]{1,0:T(8,128)(2,1)S(1)}, bf16[384,128]{1,0:T(8,128)(2,1)S(1)}, u32[]{:S(2)}, u32[]{:S(2)}) collective-permute-start(bf16[384,128]{1,0:T(8,128)(2,1)S(1)} %get-tuple-element.53), channel_id=1, source_target_pairs={{0,28},{4,8},{8,4},{12,16},{16,12},{20,24},{24,20},{28,0},{1,29},{... | collective-permute-start | bytes 294920 | tf_op jit(solution)/shard_map/ppermute | solution.py:298
  17.7 0.0 collective-permute-done.1
  17.7 2.8 %conditional.1 = ((f32[2,32,768]{2,1,0:T(8,128)S(1)}, bf16[2,128,192]{2,1,0:T(8,128)(2,1)S(1)})) conditional(s32[]{:T(128)} %convert_element_type.3, () %tuple.12, (bf16[2,128,768]{2,1,0:T(8,128)(2,1)S(1)}, bf16[384,128]{1,0:T(8,128)(2,1)S(1)}, bf16[384,128]{1,0:T(8,128)(2,1)S(1)}, bf16[192,768]{1,0:T(8,128)(2,1)S(1)}, ...), branch_computations={%region_0.0_spmd, %region_1.0_spmd} | conditional | flops 2 | bytes 1572914 | solution.py:395
  17.8 0.4 %self_output_share.1 = (f32[256,768]{1,0:T(8,128)S(1)}, bf16[256,768]{1,0:T(8,128)(2,1)S(1)}) custom-call(bf16[2,128,768]{2,1,0:T(8,128)(2,1)S(1)} %get-tuple-element.19.states, bf16[384,128]{1,0:T(8,128)(2,1)S(1)} %get-tuple-element.20.own, bf16[384,128]{1,0:T(8,128)(2,1)S(1)} %get-tuple-element.21.got, bf16[192,768]{1,0:T(8,128)(2,1)S(1)} %get-tuple-element.22.own_weight, ...), custom_call_target="tpu_custom_call" | custom-call | flops 1 | bytes 1 | tf_op jit(solution)/shard_map/cond/branch_1_fun/self_output_share/pallas_call | solution.py:302
  18.2 0.1 collective-permute-start
  18.3 1.7 %collective-permute-done.got = bf16[256,768]{1,0:T(8,128)(2,1)S(1)} collective-permute-done((bf16[256,768]{1,0:T(8,128)(2,1)S(1)}, bf16[256,768]{1,0:T(8,128)(2,1)S(1)}, u32[]{:S(2)}, u32[]{:S(2)}) %collective-permute-start) | collective-permute-done | bytes 393248 | tf_op jit(solution)/shard_map/cond/branch_1_fun/ppermute | solution.py:295
  20.0 0.5 %mixed_and_queries.1 = (f32[2,32,768]{2,1,0:T(8,128)S(1)}, bf16[2,128,192]{2,1,0:T(8,128)(2,1)S(1)}) custom-call(f32[256,768]{1,0:T(8,128)S(1)} %get-tuple-element.24.base, bf16[256,768]{1,0:T(8,128)(2,1)S(1)} %collective-permute-done.got, f32[3,768]{1,0:T(4,128)S(1)} %get-tuple-element.26.gains, bf16[192,768]{1,0:T(8,128)(2,1)S(1)} %get-tuple-element.27.weight), custom_call_target="tpu_custom_call" | custom-call | flops 1 | bytes 1 | tf_op jit(solution)/shard_map/cond/branch_1_fun/mixed_and_queries/pallas_call | solution.py:302
  20.5 1.0 %early_cross_attention.1.waited.before = bf16[4,3,48,128]{3,2,1,0:T(8,128)(2,1)S(1)} custom-call(bf16[2,128,192]{2,1,0:T(8,128)(2,1)S(1)} %get-tuple-element.50.queries, s32[11,128]{1,0:T(8,128)S(1)} %get-tuple-element.48.table, bf16[384,128]{1,0:T(8,128)(2,1)S(1)} %collective-permute-done.6.rest_0_, ...), custom_call_target="tpu_custom_call" | custom-call | flops 3000000000 | bytes 1 | tf_op jit(solution)/shard_map/early_cross_attention/pallas_call | solution.py:302
  21.6 0.1 cross_output_both_rows.1.weights
  21.7 0.2 collective-permute-start.7
  21.9 0.0 collective-permute-done.8.rest_0_
  21.9 0.5 %collective-permute-done.9.rest_1_ = bf16[384,128]{1,0:T(8,128)(2,1)S(1)} collective-permute-done((bf16[384,128]{1,0:T(8,128)(2,1)S(1)}, bf16[384,128]{1,0:T(8,128)(2,1)S(1)}, u32[]{:S(2)}, u32[]{:S(2)}) %collective-permute-start.9) | collective-permute-done | bytes 98336 | tf_op jit(solution)/shard_map/ppermute | solution.py:298
  22.4 0.9 %late_cross_attention.1 = (bf16[5,48,128]{2,1,0:T(8,128)(2,1)S(1)}, bf16[5,48,128]{2,1,0:T(8,128)(2,1)S(1)}, bf16[5,48,128]{2,1,0:T(8,128)(2,1)S(1)}, bf16[5,48,128]{2,1,0:T(8,128)(2,1)S(1)}) custom-call(bf16[2,128,192]{2,1,0:T(8,128)(2,1)S(1)} %get-tuple-element.50.queries, s32[11,128]{1,0:T(8,128)S(1)} %get-tuple-element.48.table, ...), custom_call_target="tpu_custom_call" | custom-call | flops 99999997952 | bytes 1 | tf_op jit(solution)/shard_map/late_cross_attention/pallas_call | solution.py:302
  23.2 1.6 %collective-permute-start.10 = (bf16[5,48,128]{2,1,0:T(8,128)(2,1)S(1)}, bf16[5,48,128]{2,1,0:T(8,128)(2,1)S(1)}, u32[]{:S(2)}, u32[]{:S(2)}) collective-permute-start(bf16[5,48,128]{2,1,0:T(8,128)(2,1)S(1)} %get-tuple-element.55), channel_id=1, source_target_pairs={{0,2},{1,3},{2,0},{3,1},{4,6},{5,7},{6,4},{7,5},{8,10},{9,11},{10,... | collective-permute-start | bytes 184328 | tf_op jit(solution)/shard_map/ppermute | solution.py:295
  24.8 0.6 %collective-permute-start.12 = (bf16[5,48,128]{2,1,0:T(8,128)(2,1)S(1)}, bf16[5,48,128]{2,1,0:T(8,128)(2,1)S(1)}, u32[]{:S(2)}, u32[]{:S(2)}) collective-permute-start(bf16[5,48,128]{2,1,0:T(8,128)(2,1)S(1)} %get-tuple-element.57), channel_id=1, source_target_pairs={{0,3},{1,2},{2,1},{3,0},{4,7},{5,6},{6,5},{7,4},{8,11},{9,10},{10,... | collective-permute-start | bytes 184328 | tf_op jit(solution)/shard_map/ppermute | solution.py:295
  25.4 2.1 %collective-permute-done.10.across_chip = bf16[5,48,128]{2,1,0:T(8,128)(2,1)S(1)} collective-permute-done((bf16[5,48,128]{2,1,0:T(8,128)(2,1)S(1)}, bf16[5,48,128]{2,1,0:T(8,128)(2,1)S(1)}, u32[]{:S(2)}, u32[]{:S(2)}) %collective-permute-start.10) | collective-permute-done | bytes 61472 | tf_op jit(solution)/shard_map/ppermute | solution.py:295
  27.5 0.4 %first_terms.1.first = f32[160,768]{1,0:T(8,128)S(1)} custom-call(s32[11,128]{1,0:T(8,128)S(1)} %get-tuple-element.48.table, bf16[384,768]{1,0:T(8,128)(2,1)S(1)} %cross_output_both_rows.1.weights, bf16[384,768]{1,0:T(8,128)(2,1)S(1)} %collective-permute-done.7.core_weights.weights, bf16[5,48,128]{2,1,0:T(8,128)(2,1)S(1)} %get-tuple-element.54.own, ...), custom_call_target="tpu_custom_call" | custom-call | flops 1 | bytes 1 | tf_op jit(solution)/shard_map/first_terms/pallas_call | solution.py:302
  28.0 0.5 %collective-permute-done.12.across_both = bf16[5,48,128]{2,1,0:T(8,128)(2,1)S(1)} collective-permute-done((bf16[5,48,128]{2,1,0:T(8,128)(2,1)S(1)}, bf16[5,48,128]{2,1,0:T(8,128)(2,1)S(1)}, u32[]{:S(2)}, u32[]{:S(2)}) %collective-permute-start.12) | collective-permute-done | bytes 61472 | tf_op jit(solution)/shard_map/ppermute | solution.py:295
  28.5 1.1 %pair_output.1 = bf16[2,5,32,768]{3,2,1,0:T(8,128)(2,1)} custom-call(f32[2,32,768]{2,1,0:T(8,128)S(1)} %get-tuple-element.47.own_rows, s32[11,128]{1,0:T(8,128)S(1)} %get-tuple-element.48.table, bf16[384,768]{1,0:T(8,128)(2,1)S(1)} %collective-permute-done.7.core_weights.weights, f32[160,768]{1,0:T(8,128)S(1)} %first_terms.1.first, ...), custom_call_target="tpu_custom_call" | custom-call | flops 1 | bytes 1 | tf_op jit(solution)/shard_map/pair_output/pallas_call | solution.py:302
  (11 shorter events, 0.0 us)
Async XLA Ops:
  0.0 15.0 %collective-permute-start.2 = (bf16[192,768]{1,0:T(8,128)(2,1)}, bf16[192,768]{1,0:T(8,128)(2,1)S(1)}, u32[]{:S(2)}, u32[]{:S(2)}) collective-permute-start(bf16[192,768]{1,0:T(8,128)(2,1)} %param.12), channel_id=1, source_target_pairs={{0,2},{1,3},{2,0},{3,1},{4,6},{5,7},{6,4},{7,5},{8,10},{9,11},{10,... | collective-permute-start | bytes 884744 | tf_op jit(solution)/shard_map/ppermute | solution.py:295
  6.0 6.3 %collective-permute-start.3 = (bf16[384,128]{1,0:T(8,128)(2,1)S(1)}, bf16[384,128]{1,0:T(8,128)(2,1)S(1)}, u32[]{:S(2)}, u32[]{:S(2)}) collective-permute-start(bf16[384,128]{1,0:T(8,128)(2,1)S(1)} %get-tuple-element.44), channel_id=1, source_target_pairs={{0,8},{4,12},{8,0},{12,4},{16,24},{20,28},{24,16},{28,20},{1,9},{5... | collective-permute-start | bytes 294920 | tf_op jit(solution)/shard_map/ppermute | solution.py:298
  7.7 6.2 %collective-permute-start.4 = (bf16[384,128]{1,0:T(8,128)(2,1)S(1)}, bf16[384,128]{1,0:T(8,128)(2,1)S(1)}, u32[]{:S(2)}, u32[]{:S(2)}) collective-permute-start(bf16[384,128]{1,0:T(8,128)(2,1)S(1)} %get-tuple-element.45), channel_id=1, source_target_pairs={{0,4},{4,0},{8,12},{12,8},{16,20},{20,16},{24,28},{28,24},{1,5},{5... | collective-permute-start | bytes 294920 | tf_op jit(solution)/shard_map/ppermute | solution.py:298
  9.2 8.5 %collective-permute-start.1 = (bf16[384,128]{1,0:T(8,128)(2,1)S(1)}, bf16[384,128]{1,0:T(8,128)(2,1)S(1)}, u32[]{:S(2)}, u32[]{:S(2)}) collective-permute-start(bf16[384,128]{1,0:T(8,128)(2,1)S(1)} %get-tuple-element.43), channel_id=1, source_target_pairs={{0,2},{1,3},{2,0},{3,1},{4,6},{5,7},{6,4},{7,5},{8,10},{9,11},{10,... | collective-permute-start | bytes 294920 | tf_op jit(solution)/shard_map/ppermute | solution.py:295
  9.7 10.8 %collective-permute-start.6 = (bf16[384,128]{1,0:T(8,128)(2,1)S(1)}, bf16[384,128]{1,0:T(8,128)(2,1)S(1)}, u32[]{:S(2)}, u32[]{:S(2)}) collective-permute-start(bf16[384,128]{1,0:T(8,128)(2,1)S(1)} %get-tuple-element.51), channel_id=1, source_target_pairs={{0,16},{4,20},{8,24},{12,28},{16,0},{20,4},{24,8},{28,12},{1,17},{... | collective-permute-start | bytes 294920 | tf_op jit(solution)/shard_map/ppermute | solution.py:298
  12.3 5.4 %copy-start.2 = (bf16[192,768]{1,0:T(8,128)(2,1)S(1)}, bf16[192,768]{1,0:T(8,128)(2,1)}, u32[]{:S(2)}) copy-start(bf16[192,768]{1,0:T(8,128)(2,1)} %param.12) | copy-start | bytes 884740
  12.3 5.4 %copy-start = (f32[3,768]{1,0:T(4,128)S(1)}, f32[3,768]{1,0:T(4,128)}, u32[]{:S(2)}) copy-start(f32[3,768]{1,0:T(4,128)} %value.1) | copy-start | bytes 27652
  12.3 5.4 %copy-start.1 = (bf16[2,128,768]{2,1,0:T(8,128)(2,1)S(1)}, bf16[2,128,768]{2,1,0:T(8,128)(2,1)}, u32[]{:S(2)}) copy-start(bf16[2,128,768]{2,1,0:T(8,128)(2,1)} %states.1) | copy-start | bytes 1179652
  12.3 9.2 %collective-permute-start.5 = (bf16[192,768]{1,0:T(8,128)(2,1)S(1)}, bf16[192,768]{1,0:T(8,128)(2,1)S(1)}, u32[]{:S(2)}, u32[]{:S(2)}) collective-permute-start(bf16[192,768]{1,0:T(8,128)(2,1)S(1)} %cross_output_rows.1.own), channel_id=1, source_target_pairs={{0,2},{1,3},{2,0},{3,1},{4,6},{5,7},{6,4},{7,5},{8,10},{9,11},{10,... | collective-permute-start | bytes 884744 | tf_op jit(solution)/shard_map/ppermute | solution.py:295
  13.9 8.0 %collective-permute-start.8 = (bf16[384,128]{1,0:T(8,128)(2,1)S(1)}, bf16[384,128]{1,0:T(8,128)(2,1)S(1)}, u32[]{:S(2)}, u32[]{:S(2)}) collective-permute-start(bf16[384,128]{1,0:T(8,128)(2,1)S(1)} %get-tuple-element.52), channel_id=1, source_target_pairs={{0,24},{4,28},{8,16},{12,20},{16,8},{20,12},{24,0},{28,4},{1,25},{... | collective-permute-start | bytes 294920 | tf_op jit(solution)/shard_map/ppermute | solution.py:298
  15.0 7.4 %collective-permute-start.9 = (bf16[384,128]{1,0:T(8,128)(2,1)S(1)}, bf16[384,128]{1,0:T(8,128)(2,1)S(1)}, u32[]{:S(2)}, u32[]{:S(2)}) collective-permute-start(bf16[384,128]{1,0:T(8,128)(2,1)S(1)} %get-tuple-element.53), channel_id=1, source_target_pairs={{0,28},{4,8},{8,4},{12,16},{16,12},{20,24},{24,20},{28,0},{1,29},{... | collective-permute-start | bytes 294920 | tf_op jit(solution)/shard_map/ppermute | solution.py:298
  18.2 1.8 %collective-permute-start = (bf16[256,768]{1,0:T(8,128)(2,1)S(1)}, bf16[256,768]{1,0:T(8,128)(2,1)S(1)}, u32[]{:S(2)}, u32[]{:S(2)}) collective-permute-start(bf16[256,768]{1,0:T(8,128)(2,1)S(1)} %get-tuple-element.25), channel_id=1, source_target_pairs={{0,1},{1,0},{2,3},{3,2},{4,5},{5,4},{6,7},{7,6},{8,9},{9,8},{10,11... | collective-permute-start | bytes 1179656 | tf_op jit(solution)/shard_map/cond/branch_1_fun/ppermute | solution.py:295
  21.7 5.8 %collective-permute-start.7 = (bf16[384,768]{1,0:T(8,128)(2,1)S(1)}, bf16[384,768]{1,0:T(8,128)(2,1)S(1)}, u32[]{:S(2)}, u32[]{:S(2)}) collective-permute-start(bf16[384,768]{1,0:T(8,128)(2,1)S(1)} %cross_output_both_rows.1.weights), channel_id=1, source_target_pairs={{0,1},{1,0},{2,3},{3,2},{4,5},{5,4},{6,7},{7,6},{8,9},{9,8},{10,11... | collective-permute-start | bytes 1769480 | tf_op jit(solution)/shard_map/ppermute | solution.py:295
  23.2 4.3 %collective-permute-start.10 = (bf16[5,48,128]{2,1,0:T(8,128)(2,1)S(1)}, bf16[5,48,128]{2,1,0:T(8,128)(2,1)S(1)}, u32[]{:S(2)}, u32[]{:S(2)}) collective-permute-start(bf16[5,48,128]{2,1,0:T(8,128)(2,1)S(1)} %get-tuple-element.55), channel_id=1, source_target_pairs={{0,2},{1,3},{2,0},{3,1},{4,6},{5,7},{6,4},{7,5},{8,10},{9,11},{10,... | collective-permute-start | bytes 184328 | tf_op jit(solution)/shard_map/ppermute | solution.py:295
  24.8 2.7 %collective-permute-start.11 = (bf16[5,48,128]{2,1,0:T(8,128)(2,1)S(1)}, bf16[5,48,128]{2,1,0:T(8,128)(2,1)S(1)}, u32[]{:S(2)}, u32[]{:S(2)}) collective-permute-start(bf16[5,48,128]{2,1,0:T(8,128)(2,1)S(1)} %get-tuple-element.56), channel_id=1, source_target_pairs={{0,1},{1,0},{2,3},{3,2},{4,5},{5,4},{6,7},{7,6},{8,9},{9,8},{10,11... | collective-permute-start | bytes 184328 | tf_op jit(solution)/shard_map/ppermute | solution.py:295
  24.8 3.6 %collective-permute-start.12 = (bf16[5,48,128]{2,1,0:T(8,128)(2,1)S(1)}, bf16[5,48,128]{2,1,0:T(8,128)(2,1)S(1)}, u32[]{:S(2)}, u32[]{:S(2)}) collective-permute-start(bf16[5,48,128]{2,1,0:T(8,128)(2,1)S(1)} %get-tuple-element.57), channel_id=1, source_target_pairs={{0,3},{1,2},{2,1},{3,0},{4,7},{5,6},{6,5},{7,4},{8,11},{9,10},{10,... | collective-permute-start | bytes 184328 | tf_op jit(solution)/shard_map/ppermute | solution.py:295
